TPU v7x, 256 devices: a whole 4x4x8 slice. The times are simulated.
256 devices in a mesh: tile: 32 (over y, z), head: 8 (over x, core).
Axes of the slice: x: 4, y: 4, z: 8, core: 2. Of those that a mesh axis runs over, the one named last changes fastest.
Arguments:
- query_slab: bfloat16 [32, 8, 32, 5120], P('tile', None, 'head'), may hold values from -30 to 30
- key_slab: bfloat16 [32, 8, 32, 5120], P('tile', None, 'head'), may hold values from -5 to 5
- value_slab: bfloat16 [32, 8, 32, 5120], P('tile', None, 'head'), may hold values from -5 to 5
- upstream: bfloat16 [8192, 5120], P('tile', 'head'), may hold values from -5 to 5
Outputs:
- attended: bfloat16 [8192, 5120], P('tile', 'head')
- query_grad: bfloat16 [8192, 5120], P('tile', 'head')
- key_grad: bfloat16 [8192, 5120], P('tile', 'head')
- value_grad: bfloat16 [8192, 5120], P('tile', 'head')
All inputs are finite; a program needn't handle non-finite values.
Results may differ from a plain program's by a relative error of at most 0.012.
Values may be sent and summed in bfloat16 or wider, within the bound.
No kernel may reach another device: no remote copies, remote signals or barrier semaphores. Data moves between devices by JAX's collectives and lax.ppermute only.
A program may use at most 128 MiB of HBM per device.

v0:
```python
import functools
import math

import jax
import jax.numpy as jnp
import numpy as np
from jax import lax
from jax.experimental import pallas as pl
from jax.experimental.pallas import tpu as pltpu
from jax.sharding import PartitionSpec as P

HEAD_DIM = 128
HEADS_HERE = 5
STRIPS = 4
SLOTS = 8
TILE = 128
LOW = jnp.bfloat16
WIDE = jnp.float32
NEVER = -1e30


def route(step):
    pairs = []
    for strip in range(STRIPS):
        for slot in range(SLOTS):
            goal = step(strip, slot)
            if goal is not None:
                pairs.append((strip * SLOTS + slot, goal[0] * SLOTS + goal[1]))
    return pairs


def shifted(rows, columns):
    def step(strip, slot):
        there = (strip + rows, slot + columns)
        return there if 0 <= there[0] < STRIPS and 0 <= there[1] < SLOTS else None

    return route(step)


def owner_of(which, turn):
    def step(strip, slot):
        odd = slot % 2
        if which == 2:
            unit = 5 * slot + (0 if odd else 4)
        else:
            unit = 5 * slot + odd + 2 * which
        return (strip, ((turn + odd) % 2) * 4 + (unit % 8) // 2)

    return route(step)


def flipped(pairs):
    return [(target, source) for source, target in pairs]


HALO_STEPS = ((1, 0), (-1, 0), (0, 1), (0, -1), (1, 1), (1, -1), (-1, 1), (-1, -1))
OWNER_STEPS = tuple((which, turn) for which in range(3) for turn in range(2))


def whole(count):
    return [pl.BlockSpec(memory_space=pltpu.VMEM)] * count


def owner_table():
    slot = lax.axis_index("tile") % SLOTS
    row, pair = slot // 4, slot % 4
    heads = []
    for which, turn in OWNER_STEPS:
        odd = (row + turn) % 2
        if which == 2:
            unit = 10 * ((pair + 2) % 4) + 4
        else:
            even_unit = 10 * ((pair - which + 4) % 4) + 2 * which
            odd_unit = 10 * ((pair - 3 - which + 8) % 4) + 6 + 2 * which
            unit = jnp.where(odd == 1, odd_unit, even_unit)
        heads.append(unit // 8)
    return jnp.stack(heads + [row]).astype(jnp.int32)


def spread_kernel(table, upstream, *outs):
    line = lax.broadcasted_iota(jnp.int32, (2 * TILE, 2 * TILE), 0)
    col = lax.broadcasted_iota(jnp.int32, (2 * TILE, 2 * TILE), 1)
    source = ((line & 127) >> 2) * 8 + (line >> 7) * 4 + (line & 3)
    order = (col == source).astype(LOW)
    for at, (which, turn) in enumerate(OWNER_STEPS):
        head = pl.multiple_of(table[at] * HEAD_DIM, HEAD_DIM)
        tiles = jnp.dot(order, upstream[:, pl.ds(head, HEAD_DIM)], preferred_element_type=WIDE)
        tiles = tiles.astype(LOW)
        if which == 2:
            second = ((table[6] + turn) % 2) == 1
            outs[at][...] = jnp.where(second, tiles[TILE:], tiles[:TILE])
        else:
            outs[at][...] = tiles.reshape(2, TILE, HEAD_DIM)


def spread(table, upstream):
    shapes = [
        jax.ShapeDtypeStruct((TILE, HEAD_DIM) if which == 2 else (2, TILE, HEAD_DIM), LOW)
        for which, _ in OWNER_STEPS
    ]
    return pl.pallas_call(
        spread_kernel,
        out_shape=shapes,
        in_specs=[pl.BlockSpec(memory_space=pltpu.SMEM)] + whole(1),
        out_specs=whole(6),
        compiler_params=pltpu.CompilerParams(vmem_limit_bytes=16 << 20),
        name="spread",
    )(table, upstream)


def gather_kernel(table, *refs):
    first, second, outs = refs[:6], refs[6:12], refs[12:16]
    single = refs[16]
    line = lax.broadcasted_iota(jnp.int32, (2 * TILE, 2 * TILE), 0)
    col = lax.broadcasted_iota(jnp.int32, (2 * TILE, 2 * TILE), 1)
    source = ((line >> 2) & 1) * TILE + (line >> 3) * 4 + (line & 3)
    order = (col == source).astype(LOW)
    for group, received in enumerate((first, second)):
        for kind in range(2):
            out = outs[2 * group + kind]
            for at in range(4):
                head = pl.multiple_of(table[at] * HEAD_DIM, HEAD_DIM)
                tiles = received[at][kind].reshape(2 * TILE, HEAD_DIM)
                out[:, pl.ds(head, HEAD_DIM)] = jnp.dot(
                    order, tiles, preferred_element_type=WIDE
                ).astype(LOW)
            flip = table[6] == 1
            one, two = received[4][kind], received[5][kind]
            single[:TILE] = jnp.where(flip, two, one)
            single[TILE:] = jnp.where(flip, one, two)
            head = pl.multiple_of(table[4] * HEAD_DIM, HEAD_DIM)
            out[:, pl.ds(head, HEAD_DIM)] = jnp.dot(
                order, single[...], preferred_element_type=WIDE
            ).astype(LOW)


def gather(table, first, second):
    return pl.pallas_call(
        gather_kernel,
        out_shape=[jax.ShapeDtypeStruct((2 * TILE, HEADS_HERE * HEAD_DIM), LOW)] * 4,
        in_specs=[pl.BlockSpec(memory_space=pltpu.SMEM)] + whole(12),
        out_specs=whole(4),
        scratch_shapes=[pltpu.VMEM((2 * TILE, HEAD_DIM), LOW)],
        compiler_params=pltpu.CompilerParams(vmem_limit_bytes=16 << 20),
        name="gather",
    )(table, *first, *second)


def unit_table():
    place = lax.axis_index("tile")
    strip, slot = place // SLOTS, place % SLOTS
    cols = [(5 * slot + at) % 8 for at in range(5)]
    return jnp.stack([strip, slot % 2] + cols).astype(jnp.int32)


def nt(one, two):
    return lax.dot_general(one, two, (((1,), (1,)), ((), ())), preferred_element_type=WIDE)


def nn(one, two):
    return jnp.dot(one, two, preferred_element_type=WIDE)


def fill_outs(odd, held, outs):
    for at, (which, turn) in enumerate(OWNER_STEPS):
        row = (turn + odd) % 2
        for kind in range(2):
            if which == 2:
                outs[at][kind] = held[kind, row, 4 - 4 * odd]
            else:
                for part in range(2):
                    outs[at][kind, part] = held[kind, row, odd + 2 * which + part]


def owner_shapes():
    return [
        jax.ShapeDtypeStruct((2, TILE, HEAD_DIM) if which == 2 else (2, 2, TILE, HEAD_DIM), LOW)
        for which, _ in OWNER_STEPS
    ]


def attend_kernel(table, own, *refs):
    halos, grads = refs[:8], refs[8:14]
    outs, terms, edges = refs[14:20], refs[20], refs[21:29]
    pair, turned, grad, total, held = refs[29:]
    strip, odd = table[0], table[1]
    scaling = HEAD_DIM**-0.5
    rate = scaling * math.log2(math.e)

    for kind in range(2):
        for at in range(5):
            for row in range(2):
                pair[kind, at + 1, row] = own[kind + 1, row, at]
            pair[kind, at + 1, 2] = halos[0][kind, at]
            pair[kind, at + 1, 3] = halos[1][kind, at]
        for row in range(2):
            pair[kind, 0, row] = halos[2][kind, row]
            pair[kind, 6, row] = halos[3][kind, row]
        pair[kind, 0, 2] = halos[4][kind]
        pair[kind, 6, 2] = halos[5][kind]
        pair[kind, 0, 3] = halos[6][kind]
        pair[kind, 6, 3] = halos[7][kind]
    for kind in range(2):
        for at in range(7):
            for row in range(4):
                turned[kind, at, row] = pair[kind, at, row].T
    for at, (which, turn) in enumerate(OWNER_STEPS):
        row = (turn + odd) % 2
        if which == 2:
            grad[row, 4 - 4 * odd] = grads[at][...]
        else:
            for part in range(2):
                grad[row, odd + 2 * which + part] = grads[at][part]
    total[...] = jnp.zeros_like(total)

    def one_unit(unit, carry):
        column = table[2 + unit]
        queries = [own[0, row, unit] for row in range(2)]
        both = jnp.concatenate(queries, axis=0)
        ups = [grad[row, unit] for row in range(2)]
        up_both = jnp.concatenate(ups, axis=0)
        column_ok = (column > 0, None, column < 7)
        row_ok = (strip > 0, strip < STRIPS - 1)

        def products(kind, left, left_both):
            inner, outer = [], []
            for step in range(3):
                slot = unit + step
                near = pair[kind, slot, 0:2].reshape(2 * TILE, HEAD_DIM)
                inner.append(nt(near, left_both))
                outer.append(
                    jnp.concatenate(
                        [nt(pair[kind, slot, 2 + row], left[row]) for row in range(2)], axis=1
                    )
                )
            return inner, outer

        inner, outer = products(0, queries, both)
        lane = lax.broadcasted_iota(jnp.int32, (1, 2 * TILE), 1)
        row_bias = jnp.where(
            lane < TILE,
            jnp.where(row_ok[0], 0.0, NEVER),
            jnp.where(row_ok[1], 0.0, NEVER),
        )
        for step in range(3):
            if column_ok[step] is None:
                outer[step] = outer[step] + row_bias
            else:
                bias = jnp.where(column_ok[step], 0.0, NEVER)
                inner[step] = inner[step] + bias
                outer[step] = outer[step] + (row_bias + bias)
        highest = functools.reduce(
            jnp.maximum, [jnp.max(block, axis=0, keepdims=True) for block in inner + outer]
        )
        raised = [jnp.exp2((block - highest) * rate) for block in inner + outer]
        amount = sum(jnp.sum(block, axis=0, keepdims=True) for block in raised)
        inverse = 1.0 / amount
        weights = [block * inverse for block in raised]
        low = [block.astype(LOW) for block in weights]

        def mix(kind, parts):
            near = sum(
                nn(turned[kind, unit + step, row], parts[step][row * TILE : (row + 1) * TILE])
                for step in range(3)
                for row in range(2)
            )
            far = [
                sum(
                    nn(
                        turned[kind, unit + step, 2 + row],
                        parts[3 + step][:, row * TILE : (row + 1) * TILE],
                    )
                    for step in range(3)
                )
                for row in range(2)
            ]
            return near + jnp.concatenate(far, axis=1)

        def fold(kind, parts, right, right_both):
            for step in range(3):
                slot = unit + step
                near = nn(parts[step], right_both)
                for row in range(2):
                    total[kind, slot, row] += near[row * TILE : (row + 1) * TILE]
                    total[kind, slot, 2 + row] += nn(
                        parts[3 + step][:, row * TILE : (row + 1) * TILE], right[row]
                    )

        mixed = mix(1, low).T
        offsets = jnp.sum((up_both.astype(WIDE) * mixed).T, axis=0, keepdims=True)
        for row in range(2):
            held[0, row, unit] = mixed[row * TILE : (row + 1) * TILE].astype(LOW)
        fold(1, low, ups, up_both)
        inner, outer = products(1, ups, up_both)
        slopes = [
            (weight * (block - offsets)).astype(LOW)
            for weight, block in zip(weights, inner + outer)
        ]
        query_grad = mix(0, slopes).T * scaling
        for row in range(2):
            held[1, row, unit] = query_grad[row * TILE : (row + 1) * TILE].astype(LOW)
        fold(0, slopes, queries, both)
        return carry

    lax.fori_loop(0, 5, one_unit, 0)
    fill_outs(odd, held, outs)
    for kind, factor in ((0, scaling), (1, 1.0)):
        for at in range(5):
            for row in range(2):
                terms[kind, row, at] = total[kind, at + 1, row] * factor
            edges[0][kind, at] = (total[kind, at + 1, 3] * factor).astype(LOW)
            edges[1][kind, at] = (total[kind, at + 1, 2] * factor).astype(LOW)
        for row in range(2):
            edges[2][kind, row] = (total[kind, 6, row] * factor).astype(LOW)
            edges[3][kind, row] = (total[kind, 0, row] * factor).astype(LOW)
        edges[4][kind] = (total[kind, 6, 3] * factor).astype(LOW)
        edges[5][kind] = (total[kind, 0, 3] * factor).astype(LOW)
        edges[6][kind] = (total[kind, 6, 2] * factor).astype(LOW)
        edges[7][kind] = (total[kind, 0, 2] * factor).astype(LOW)


def halo_shapes():
    middle = [(5,), (5,), (2,), (2,), (), (), (), ()]
    return [jax.ShapeDtypeStruct((2,) + size + (TILE, HEAD_DIM), LOW) for size in middle]


def attend(table, own, halos, grads):
    return pl.pallas_call(
        attend_kernel,
        out_shape=owner_shapes()
        + [jax.ShapeDtypeStruct((2, 2, 5, TILE, HEAD_DIM), WIDE)]
        + halo_shapes(),
        in_specs=[pl.BlockSpec(memory_space=pltpu.SMEM)] + whole(15),
        out_specs=whole(15),
        scratch_shapes=[
            pltpu.VMEM((2, 7, 4, TILE, HEAD_DIM), LOW),
            pltpu.VMEM((2, 7, 4, HEAD_DIM, TILE), LOW),
            pltpu.VMEM((2, 5, TILE, HEAD_DIM), LOW),
            pltpu.VMEM((2, 7, 4, TILE, HEAD_DIM), WIDE),
            pltpu.VMEM((2, 2, 5, TILE, HEAD_DIM), LOW),
        ],
        compiler_params=pltpu.CompilerParams(vmem_limit_bytes=40 << 20),
        cost_estimate=pl.CostEstimate(
            flops=3_000_000_000, bytes_accessed=8_000_000, transcendentals=1_500_000
        ),
        name="attend",
    )(table, own, *halos, *grads)


def combine_kernel(table, terms, *refs):
    edges, outs, held = refs[:8], refs[8:14], refs[14]
    for kind in range(2):
        for row in range(2):
            for at in range(5):
                value = terms[kind, row, at] + edges[row][kind, at].astype(WIDE)
                if at == 0:
                    value = value + edges[2][kind, row].astype(WIDE)
                    value = value + edges[4 + 2 * row][kind].astype(WIDE)
                if at == 4:
                    value = value + edges[3][kind, row].astype(WIDE)
                    value = value + edges[5 + 2 * row][kind].astype(WIDE)
                held[kind, row, at] = value.astype(LOW)
    fill_outs(table[1], held, outs)


def combine(table, terms, edges):
    return pl.pallas_call(
        combine_kernel,
        out_shape=owner_shapes(),
        in_specs=[pl.BlockSpec(memory_space=pltpu.SMEM)] + whole(9),
        out_specs=whole(6),
        scratch_shapes=[pltpu.VMEM((2, 2, 5, TILE, HEAD_DIM), LOW)],
        compiler_params=pltpu.CompilerParams(vmem_limit_bytes=16 << 20),
        name="combine",
    )(table, terms, *edges)


def send_all(parts, routes):
    return [lax.ppermute(part, "tile", path) for part, path in zip(parts, routes)]


def local(query_slab, key_slab, value_slab, upstream):
    owners = owner_table()
    units = unit_table()
    to_owner = [owner_of(which, turn) for which, turn in OWNER_STEPS]
    halo_routes = [shifted(*step) for step in HALO_STEPS]

    with jax.named_scope("upstream_to_units"):
        grads = send_all(spread(owners, upstream), [flipped(path) for path in to_owner])

    with jax.named_scope("heads"):
        lines = [
            slab.reshape(8, 4, 40, 128).transpose(2, 0, 1, 3).reshape(8, 5, 32, 128)
            for slab in (query_slab, key_slab, value_slab)
        ]
        by_head = lax.all_to_all(jnp.stack(lines, axis=1), "head", 0, 0, tiled=True)
    with jax.named_scope("tiles"):
        shaped = by_head.reshape(8, 3, 5, 4, 8, 128).transpose(3, 2, 0, 1, 4, 5)
        got = lax.all_to_all(shaped.reshape(32, 5, 3, 8, 128), "tile", 0, 0, tiled=True)
        own = got.reshape(32, 5, 3, 2, 4, 128).transpose(2, 3, 1, 0, 4, 5)
        own = own.reshape(3, 2, 5, TILE, HEAD_DIM)
    with jax.named_scope("halos"):
        pair = own[1:]
        leaving = [
            pair[:, 1],
            pair[:, 0],
            pair[:, :, 4],
            pair[:, :, 0],
            pair[:, 1, 4],
            pair[:, 1, 0],
            pair[:, 0, 4],
            pair[:, 0, 0],
        ]
        halos = send_all(leaving, halo_routes)
    with jax.named_scope("attention"):
        results = attend(units, own, halos, grads)
    first, terms, edges = results[:6], results[6], results[7:]
    with jax.named_scope("terms"):
        edges = send_all(edges, halo_routes)
    with jax.named_scope("outputs_home"):
        first = send_all(first, to_owner)
    with jax.named_scope("key_terms_home"):
        second = send_all(combine(units, terms, edges), to_owner)
    with jax.named_scope("settle"):
        return tuple(gather(owners, first, second))


def solution(mesh):
    slab = P("tile", None, "head", None)
    block = P("tile", "head")
    return jax.shard_map(
        local,
        mesh=mesh,
        in_specs=(slab, slab, slab, block),
        out_specs=(block, block, block, block),
        check_vma=False,
    )
```

profile of v0, /device:TPU:40, one launch (start us, length us, event | category | flops | bytes accessed | tf_op | source)
XLA Modules:
  0.0 192.2 jit_solution(8149079170284368184)
XLA Ops:
  0.7 1.2 reshape.39
  2.7 19.5 %all_to_all.10 = bf16[8,3,5,32,128]{4,3,2,1,0:T(8,128)(2,1)S(1)} all-to-all(bf16[8,3,5,32,128]{4,3,2,1,0:T(8,128)(2,1)S(1)} %copy.38), channel_id=1, replica_groups=mesh['tile'=32,'head'=8] {'head'}, dimensions={0} | all-to-all | bytes 1966080 | tf_op jit(solution)/shard_map/heads/all_to_all | solution.py:396
  22.2 1.2 copy.39
  23.4 11.4 %all-to-all-start.1 = ((bf16[32,5,3,8,128]{4,3,2,1,0:T(8,128)(2,1)}), bf16[32,5,3,8,128]{4,3,2,1,0:T(8,128)(2,1)S(1)}, u32[]{:S(2)}, u32[]{:S(2)}) async-start(bf16[32,5,3,8,128]{4,3,2,1,0:T(8,128)(2,1)} %bitcast.21), calls=%async_computation.1 | async-start | bytes 1966080 | tf_op jit(solution)/shard_map/tiles/all_to_all | solution.py:399
  35.1 0.9 spread.1
  36.0 3.7 %collective-permute-start.12 = (bf16[128,128]{1,0:T(8,128)(2,1)S(1)}, bf16[128,128]{1,0:T(8,128)(2,1)S(1)}, u32[]{:S(2)}, u32[]{:S(2)}) collective-permute-start(bf16[128,128]{1,0:T(8,128)(2,1)S(1)} %get-tuple-element.35), channel_id=1, source_target_pairs={{16,0},{48,8},{24,16},{56,24},{0,32},{32,40},{8,48},{40,56},{80,64... | collective-permute-start | bytes 98312 | tf_op jit(solution)/shard_map/upstream_to_units/ppermute | solution.py:379
  39.7 4.2 %collective-permute-start.13 = (bf16[128,128]{1,0:T(8,128)(2,1)S(1)}, bf16[128,128]{1,0:T(8,128)(2,1)S(1)}, u32[]{:S(2)}, u32[]{:S(2)}) collective-permute-start(bf16[128,128]{1,0:T(8,128)(2,1)S(1)} %get-tuple-element.36), channel_id=1, source_target_pairs={{48,0},{16,8},{56,16},{24,24},{32,32},{0,40},{40,48},{8,56},{112,6... | collective-permute-start | bytes 98312 | tf_op jit(solution)/shard_map/upstream_to_units/ppermute | solution.py:379
  44.0 1.9 collective-permute-start.8
  46.0 17.3 %all-to-all-done.1 = bf16[32,5,3,8,128]{4,3,2,1,0:T(8,128)(2,1)S(1)} async-done(((bf16[32,5,3,8,128]{4,3,2,1,0:T(8,128)(2,1)}), bf16[32,5,3,8,128]{4,3,2,1,0:T(8,128)(2,1)S(1)}, u32[]{:S(2)}, u32[]{:S(2)}) %all-to-all-start.1) | async-done | bytes 983072 | tf_op jit(solution)/shard_map/tiles/all_to_all | solution.py:399
  63.5 0.3 copy.42
  63.9 2.8 %collective-permute-start.1 = (bf16[2,5,128,128]{3,2,0,1:T(8,128)(2,1)S(1)}, bf16[2,5,128,128]{3,2,0,1:T(8,128)(2,1)S(1)}, u32[]{:S(2)}, u32[]{:S(2)}) collective-permute-start(bf16[2,5,128,128]{3,2,0,1:T(8,128)(2,1)S(1)} %get-tuple-element.64), channel_id=1, source_target_pairs={{64,0},{72,8},{80,16},{88,24},{96,32},{104,40},{112,48},{120,56},{... | collective-permute-start | bytes 983048 | tf_op jit(solution)/shard_map/halos/ppermute | solution.py:379
  66.8 3.0 %collective-permute-start = (bf16[2,5,128,128]{3,2,0,1:T(8,128)(2,1)S(1)}, bf16[2,5,128,128]{3,2,0,1:T(8,128)(2,1)S(1)}, u32[]{:S(2)}, u32[]{:S(2)}) collective-permute-start(bf16[2,5,128,128]{3,2,0,1:T(8,128)(2,1)S(1)} %get-tuple-element.65), channel_id=1, source_target_pairs={{0,64},{8,72},{16,80},{24,88},{32,96},{40,104},{48,112},{56,120},{... | collective-permute-start | bytes 983048 | tf_op jit(solution)/shard_map/halos/ppermute | solution.py:379
  69.8 1.9 collective-permute-start.10
  71.8 2.6 %collective-permute-start.3 = (bf16[2,2,128,128]{3,2,0,1:T(8,128)(2,1)S(1)}, bf16[2,2,128,128]{3,2,0,1:T(8,128)(2,1)S(1)}, u32[]{:S(2)}, u32[]{:S(2)}) collective-permute-start(bf16[2,2,128,128]{3,2,0,1:T(8,128)(2,1)S(1)} %get-tuple-element.62), channel_id=1, source_target_pairs={{8,0},{16,8},{24,16},{32,24},{40,32},{48,40},{56,48},{72,64},{80,7... | collective-permute-start | bytes 393224 | tf_op jit(solution)/shard_map/halos/ppermute | solution.py:379
  74.4 3.3 %collective-permute-start.2 = (bf16[2,2,128,128]{3,2,0,1:T(8,128)(2,1)S(1)}, bf16[2,2,128,128]{3,2,0,1:T(8,128)(2,1)S(1)}, u32[]{:S(2)}, u32[]{:S(2)}) collective-permute-start(bf16[2,2,128,128]{3,2,0,1:T(8,128)(2,1)S(1)} %get-tuple-element.63), channel_id=1, source_target_pairs={{0,8},{8,16},{16,24},{24,32},{32,40},{40,48},{48,56},{64,72},{72,8... | collective-permute-start | bytes 393224 | tf_op jit(solution)/shard_map/halos/ppermute | solution.py:379
  77.7 1.7 collective-permute-done.10.refs_10_
  79.3 2.0 %collective-permute-start.11 = (bf16[2,128,128]{2,1,0:T(8,128)(2,1)S(1)}, bf16[2,128,128]{2,1,0:T(8,128)(2,1)S(1)}, u32[]{:S(2)}, u32[]{:S(2)}) collective-permute-start(bf16[2,128,128]{2,1,0:T(8,128)(2,1)S(1)} %get-tuple-element.34), channel_id=1, source_target_pairs={{40,0},{0,8},{48,16},{8,24},{56,32},{16,40},{32,48},{24,56},{104,6... | collective-permute-start | bytes 196616 | tf_op jit(solution)/shard_map/upstream_to_units/ppermute | solution.py:379
  81.3 2.6 %collective-permute-start.7 = (bf16[2,128,128]{2,1,0:T(8,128)(2,1)S(1)}, bf16[2,128,128]{2,1,0:T(8,128)(2,1)S(1)}, u32[]{:S(2)}, u32[]{:S(2)}) collective-permute-start(bf16[2,128,128]{2,1,0:T(8,128)(2,1)S(1)} %get-tuple-element.58), channel_id=1, source_target_pairs={{72,0},{80,8},{88,16},{96,24},{104,32},{112,40},{120,48},{136,64},... | collective-permute-start | bytes 196616 | tf_op jit(solution)/shard_map/halos/ppermute | solution.py:379
  84.0 2.8 %collective-permute-start.6 = (bf16[2,128,128]{2,1,0:T(8,128)(2,1)S(1)}, bf16[2,128,128]{2,1,0:T(8,128)(2,1)S(1)}, u32[]{:S(2)}, u32[]{:S(2)}) collective-permute-start(bf16[2,128,128]{2,1,0:T(8,128)(2,1)S(1)} %get-tuple-element.59), channel_id=1, source_target_pairs={{64,8},{72,16},{80,24},{88,32},{96,40},{104,48},{112,56},{128,72},... | collective-permute-start | bytes 196616 | tf_op jit(solution)/shard_map/halos/ppermute | solution.py:379
  86.8 3.9 %collective-permute-start.5 = (bf16[2,128,128]{2,1,0:T(8,128)(2,1)S(1)}, bf16[2,128,128]{2,1,0:T(8,128)(2,1)S(1)}, u32[]{:S(2)}, u32[]{:S(2)}) collective-permute-start(bf16[2,128,128]{2,1,0:T(8,128)(2,1)S(1)} %get-tuple-element.60), channel_id=1, source_target_pairs={{8,64},{16,72},{24,80},{32,88},{40,96},{48,104},{56,112},{72,128},... | collective-permute-start | bytes 196616 | tf_op jit(solution)/shard_map/halos/ppermute | solution.py:379
  90.7 4.1 %collective-permute-start.4 = (bf16[2,128,128]{2,1,0:T(8,128)(2,1)S(1)}, bf16[2,128,128]{2,1,0:T(8,128)(2,1)S(1)}, u32[]{:S(2)}, u32[]{:S(2)}) collective-permute-start(bf16[2,128,128]{2,1,0:T(8,128)(2,1)S(1)} %get-tuple-element.61), channel_id=1, source_target_pairs={{0,72},{8,80},{16,88},{24,96},{32,104},{40,112},{48,120},{64,136},... | collective-permute-start | bytes 196616 | tf_op jit(solution)/shard_map/halos/ppermute | solution.py:379
  95.1 0.5 copy.41
  95.7 2.1 %collective-permute-done.4.refs_4_ = bf16[2,128,128]{2,1,0:T(8,128)(2,1)S(1)} collective-permute-done((bf16[2,128,128]{2,1,0:T(8,128)(2,1)S(1)}, bf16[2,128,128]{2,1,0:T(8,128)(2,1)S(1)}, u32[]{:S(2)}, u32[]{:S(2)}) %collective-permute-start.4) | collective-permute-done | bytes 65568 | tf_op jit(solution)/shard_map/halos/ppermute | solution.py:379
  97.8 10.1 %attend.1 = (bf16[2,2,128,128]{3,2,1,0:T(8,128)(2,1)S(1)}, bf16[2,2,128,128]{3,2,1,0:T(8,128)(2,1)S(1)}, bf16[2,2,128,128]{3,2,1,0:T(8,128)(2,1)S(1)}, bf16[2,2,...) custom-call(s32[7]{0:T(128)S(1)} %stack.63.table, ...), custom_call_target="tpu_custom_call" | custom-call | flops 3000000000 | bytes 8000000 | tf_op jit(solution)/shard_map/attention/attend/pallas_call | solution.py:328
  107.9 2.7 %collective-permute-start.20 = (bf16[2,5,128,128]{3,2,1,0:T(8,128)(2,1)S(1)}, bf16[2,5,128,128]{3,2,1,0:T(8,128)(2,1)S(1)}, u32[]{:S(2)}, u32[]{:S(2)}) collective-permute-start(bf16[2,5,128,128]{3,2,1,0:T(8,128)(2,1)S(1)} %get-tuple-element.44), channel_id=1, source_target_pairs={{0,64},{8,72},{16,80},{24,88},{32,96},{40,104},{48,112},{56,120},{... | collective-permute-start | bytes 983048 | tf_op jit(solution)/shard_map/terms/ppermute | solution.py:379
  110.6 3.2 %collective-permute-start.21 = (bf16[2,5,128,128]{3,2,1,0:T(8,128)(2,1)S(1)}, bf16[2,5,128,128]{3,2,1,0:T(8,128)(2,1)S(1)}, u32[]{:S(2)}, u32[]{:S(2)}) collective-permute-start(bf16[2,5,128,128]{3,2,1,0:T(8,128)(2,1)S(1)} %get-tuple-element.45), channel_id=1, source_target_pairs={{64,0},{72,8},{80,16},{88,24},{96,32},{104,40},{112,48},{120,56},{... | collective-permute-start | bytes 983048 | tf_op jit(solution)/shard_map/terms/ppermute | solution.py:379
  113.8 2.5 %collective-permute-start.18 = (bf16[2,128,128]{2,1,0:T(8,128)(2,1)S(1)}, bf16[2,128,128]{2,1,0:T(8,128)(2,1)S(1)}, u32[]{:S(2)}, u32[]{:S(2)}) collective-permute-start(bf16[2,128,128]{2,1,0:T(8,128)(2,1)S(1)} %get-tuple-element.41), channel_id=1, source_target_pairs={{0,16},{8,48},{16,24},{24,56},{32,0},{40,32},{48,8},{56,40},{64,80... | collective-permute-start | bytes 196616 | tf_op jit(solution)/shard_map/outputs_home/ppermute | solution.py:379
  116.3 3.2 %collective-permute-start.24 = (bf16[2,128,128]{2,1,0:T(8,128)(2,1)S(1)}, bf16[2,128,128]{2,1,0:T(8,128)(2,1)S(1)}, u32[]{:S(2)}, u32[]{:S(2)}) collective-permute-start(bf16[2,128,128]{2,1,0:T(8,128)(2,1)S(1)} %get-tuple-element.48), channel_id=1, source_target_pairs={{0,72},{8,80},{16,88},{24,96},{32,104},{40,112},{48,120},{64,136},... | collective-permute-start | bytes 196616 | tf_op jit(solution)/shard_map/terms/ppermute | solution.py:379
  119.5 3.3 %collective-permute-start.25 = (bf16[2,128,128]{2,1,0:T(8,128)(2,1)S(1)}, bf16[2,128,128]{2,1,0:T(8,128)(2,1)S(1)}, u32[]{:S(2)}, u32[]{:S(2)}) collective-permute-start(bf16[2,128,128]{2,1,0:T(8,128)(2,1)S(1)} %get-tuple-element.49), channel_id=1, source_target_pairs={{8,64},{16,72},{24,80},{32,88},{40,96},{48,104},{56,112},{72,128},... | collective-permute-start | bytes 196616 | tf_op jit(solution)/shard_map/terms/ppermute | solution.py:379
  122.8 3.5 %collective-permute-start.26 = (bf16[2,128,128]{2,1,0:T(8,128)(2,1)S(1)}, bf16[2,128,128]{2,1,0:T(8,128)(2,1)S(1)}, u32[]{:S(2)}, u32[]{:S(2)}) collective-permute-start(bf16[2,128,128]{2,1,0:T(8,128)(2,1)S(1)} %get-tuple-element.50), channel_id=1, source_target_pairs={{64,8},{72,16},{80,24},{88,32},{96,40},{104,48},{112,56},{128,72},... | collective-permute-start | bytes 196616 | tf_op jit(solution)/shard_map/terms/ppermute | solution.py:379
  126.3 3.4 %collective-permute-start.22 = (bf16[2,2,128,128]{3,2,1,0:T(8,128)(2,1)S(1)}, bf16[2,2,128,128]{3,2,1,0:T(8,128)(2,1)S(1)}, u32[]{:S(2)}, u32[]{:S(2)}) collective-permute-start(bf16[2,2,128,128]{3,2,1,0:T(8,128)(2,1)S(1)} %get-tuple-element.46), channel_id=1, source_target_pairs={{0,8},{8,16},{16,24},{24,32},{32,40},{40,48},{48,56},{64,72},{72,8... | collective-permute-start | bytes 393224 | tf_op jit(solution)/shard_map/terms/ppermute | solution.py:379
  129.7 2.4 %collective-permute-start.23 = (bf16[2,2,128,128]{3,2,1,0:T(8,128)(2,1)S(1)}, bf16[2,2,128,128]{3,2,1,0:T(8,128)(2,1)S(1)}, u32[]{:S(2)}, u32[]{:S(2)}) collective-permute-start(bf16[2,2,128,128]{3,2,1,0:T(8,128)(2,1)S(1)} %get-tuple-element.47), channel_id=1, source_target_pairs={{8,0},{16,8},{24,16},{32,24},{40,32},{48,40},{56,48},{72,64},{80,7... | collective-permute-start | bytes 393224 | tf_op jit(solution)/shard_map/terms/ppermute | solution.py:379
  132.1 1.9 collective-permute-start.27
  134.1 6.6 %collective-permute-done.27.refs_7_ = bf16[2,128,128]{2,1,0:T(8,128)(2,1)S(1)} collective-permute-done((bf16[2,128,128]{2,1,0:T(8,128)(2,1)S(1)}, bf16[2,128,128]{2,1,0:T(8,128)(2,1)S(1)}, u32[]{:S(2)}, u32[]{:S(2)}) %collective-permute-start.27) | collective-permute-done | bytes 65568 | tf_op jit(solution)/shard_map/terms/ppermute | solution.py:379
  140.7 1.9 collective-permute-start.14
  142.6 7.7 %collective-permute-start.15 = (bf16[2,2,128,128]{3,2,1,0:T(8,128)(2,1)S(1)}, bf16[2,2,128,128]{3,2,1,0:T(8,128)(2,1)S(1)}, u32[]{:S(2)}, u32[]{:S(2)}) collective-permute-start(bf16[2,2,128,128]{3,2,1,0:T(8,128)(2,1)S(1)} %get-tuple-element.38), channel_id=1, source_target_pairs={{0,32},{8,24},{16,40},{24,0},{32,48},{40,8},{48,56},{56,16},{64,96... | collective-permute-start | bytes 393224 | tf_op jit(solution)/shard_map/outputs_home/ppermute | solution.py:379
  150.3 6.9 %collective-permute-start.16 = (bf16[2,2,128,128]{3,2,1,0:T(8,128)(2,1)S(1)}, bf16[2,2,128,128]{3,2,1,0:T(8,128)(2,1)S(1)}, u32[]{:S(2)}, u32[]{:S(2)}) collective-permute-start(bf16[2,2,128,128]{3,2,1,0:T(8,128)(2,1)S(1)} %get-tuple-element.39), channel_id=1, source_target_pairs={{0,8},{8,32},{16,16},{24,40},{32,24},{40,48},{48,0},{56,56},{64,72... | collective-permute-start | bytes 393224 | tf_op jit(solution)/shard_map/outputs_home/ppermute | solution.py:379
  157.5 2.9 %collective-permute-start.19 = (bf16[2,128,128]{2,1,0:T(8,128)(2,1)S(1)}, bf16[2,128,128]{2,1,0:T(8,128)(2,1)S(1)}, u32[]{:S(2)}, u32[]{:S(2)}) collective-permute-start(bf16[2,128,128]{2,1,0:T(8,128)(2,1)S(1)} %get-tuple-element.42), channel_id=1, source_target_pairs={{0,48},{8,16},{16,56},{24,24},{32,32},{40,0},{48,40},{56,8},{64,11... | collective-permute-start | bytes 196616 | tf_op jit(solution)/shard_map/outputs_home/ppermute | solution.py:379
  160.4 0.8 combine.1
  161.1 4.6 %collective-permute-done.19.refs_5_ = bf16[2,128,128]{2,1,0:T(8,128)(2,1)S(1)} collective-permute-done((bf16[2,128,128]{2,1,0:T(8,128)(2,1)S(1)}, bf16[2,128,128]{2,1,0:T(8,128)(2,1)S(1)}, u32[]{:S(2)}, u32[]{:S(2)}) %collective-permute-start.19) | collective-permute-done | bytes 65568 | tf_op jit(solution)/shard_map/outputs_home/ppermute | solution.py:379
  165.8 1.4 collective-permute-start.32
  167.2 4.2 %collective-permute-start.28 = (bf16[2,2,128,128]{3,2,1,0:T(8,128)(2,1)S(1)}, bf16[2,2,128,128]{3,2,1,0:T(8,128)(2,1)S(1)}, u32[]{:S(2)}, u32[]{:S(2)}) collective-permute-start(bf16[2,2,128,128]{3,2,1,0:T(8,128)(2,1)S(1)} %get-tuple-element.52), channel_id=1, source_target_pairs={{0,0},{8,56},{16,8},{24,32},{32,16},{40,40},{48,24},{56,48},{64,64... | collective-permute-start | bytes 393224 | tf_op jit(solution)/shard_map/key_terms_home/ppermute | solution.py:379
  171.5 5.5 %collective-permute-start.29 = (bf16[2,2,128,128]{3,2,1,0:T(8,128)(2,1)S(1)}, bf16[2,2,128,128]{3,2,1,0:T(8,128)(2,1)S(1)}, u32[]{:S(2)}, u32[]{:S(2)}) collective-permute-start(bf16[2,2,128,128]{3,2,1,0:T(8,128)(2,1)S(1)} %get-tuple-element.53), channel_id=1, source_target_pairs={{0,32},{8,24},{16,40},{24,0},{32,48},{40,8},{48,56},{56,16},{64,96... | collective-permute-start | bytes 393224 | tf_op jit(solution)/shard_map/key_terms_home/ppermute | solution.py:379
  177.0 3.2 %collective-permute-start.30 = (bf16[2,2,128,128]{3,2,1,0:T(8,128)(2,1)S(1)}, bf16[2,2,128,128]{3,2,1,0:T(8,128)(2,1)S(1)}, u32[]{:S(2)}, u32[]{:S(2)}) collective-permute-start(bf16[2,2,128,128]{3,2,1,0:T(8,128)(2,1)S(1)} %get-tuple-element.54), channel_id=1, source_target_pairs={{0,8},{8,32},{16,16},{24,40},{32,24},{40,48},{48,0},{56,56},{64,72... | collective-permute-start | bytes 393224 | tf_op jit(solution)/shard_map/key_terms_home/ppermute | solution.py:379
  180.3 0.8 collective-permute-start.31
  181.0 5.8 %collective-permute-start.33 = (bf16[2,128,128]{2,1,0:T(8,128)(2,1)S(1)}, bf16[2,128,128]{2,1,0:T(8,128)(2,1)S(1)}, u32[]{:S(2)}, u32[]{:S(2)}) collective-permute-start(bf16[2,128,128]{2,1,0:T(8,128)(2,1)S(1)} %get-tuple-element.57), channel_id=1, source_target_pairs={{0,48},{8,16},{16,56},{24,24},{32,32},{40,0},{48,40},{56,8},{64,11... | collective-permute-start | bytes 196616 | tf_op jit(solution)/shard_map/key_terms_home/ppermute | solution.py:379
  186.9 3.1 %collective-permute-done.33.refs_11_ = bf16[2,128,128]{2,1,0:T(8,128)(2,1)S(1)} collective-permute-done((bf16[2,128,128]{2,1,0:T(8,128)(2,1)S(1)}, bf16[2,128,128]{2,1,0:T(8,128)(2,1)S(1)}, u32[]{:S(2)}, u32[]{:S(2)}) %collective-permute-start.33) | collective-permute-done | bytes 65568 | tf_op jit(solution)/shard_map/key_terms_home/ppermute | solution.py:379
  190.0 2.2 %gather.1 = (bf16[256,640]{1,0:T(8,128)(2,1)}, bf16[256,640]{1,0:T(8,128)(2,1)}, bf16[256,640]{1,0:T(8,128)(2,1)}, bf16[256,640]{1,0:T(8,128)(2,1)}) custom-call(s32[7]{0:T(128)S(1)} %stack.55.table, bf16[2,2,128,128]{3,2,1,0:T(8,128)(2,1)S(1)} %collective-permute-done.14.refs_0_, bf16[2,2,128,128]{3,2,1,0:T(8,128)(2,1)S(1)} %collective-permute-done.15.refs_1_, ...), custom_call_target="tpu_custom_call" | custom-call | tf_op jit(solution)/shard_map/settle/gather/pallas_call | solution.py:138
  (55 shorter events, 1.8 us)
Async XLA Ops:
  0.6 1.3 copy-start.1
  0.6 1.6 copy-start.2
  23.4 11.7 %copy-start = (bf16[256,640]{1,0:T(8,128)(2,1)S(1)}, bf16[256,640]{1,0:T(8,128)(2,1)}, u32[]{:S(2)}) copy-start(bf16[256,640]{1,0:T(8,128)(2,1)} %upstream.1) | copy-start | bytes 983044
  23.4 39.9 %all-to-all-start.1 = ((bf16[32,5,3,8,128]{4,3,2,1,0:T(8,128)(2,1)}), bf16[32,5,3,8,128]{4,3,2,1,0:T(8,128)(2,1)S(1)}, u32[]{:S(2)}, u32[]{:S(2)}) async-start(bf16[32,5,3,8,128]{4,3,2,1,0:T(8,128)(2,1)} %bitcast.21), calls=%async_computation.1 | async-start | bytes 1966080 | tf_op jit(solution)/shard_map/tiles/all_to_all | solution.py:399
  36.0 30.7 %collective-permute-start.12 = (bf16[128,128]{1,0:T(8,128)(2,1)S(1)}, bf16[128,128]{1,0:T(8,128)(2,1)S(1)}, u32[]{:S(2)}, u32[]{:S(2)}) collective-permute-start(bf16[128,128]{1,0:T(8,128)(2,1)S(1)} %get-tuple-element.35), channel_id=1, source_target_pairs={{16,0},{48,8},{24,16},{56,24},{0,32},{32,40},{8,48},{40,56},{80,64... | collective-permute-start | bytes 98312 | tf_op jit(solution)/shard_map/upstream_to_units/ppermute | solution.py:379
  39.7 30.1 %collective-permute-start.13 = (bf16[128,128]{1,0:T(8,128)(2,1)S(1)}, bf16[128,128]{1,0:T(8,128)(2,1)S(1)}, u32[]{:S(2)}, u32[]{:S(2)}) collective-permute-start(bf16[128,128]{1,0:T(8,128)(2,1)S(1)} %get-tuple-element.36), channel_id=1, source_target_pairs={{48,0},{16,8},{56,16},{24,24},{32,32},{0,40},{40,48},{8,56},{112,6... | collective-permute-start | bytes 98312 | tf_op jit(solution)/shard_map/upstream_to_units/ppermute | solution.py:379
  44.0 27.8 %collective-permute-start.8 = (bf16[2,128,128]{2,1,0:T(8,128)(2,1)S(1)}, bf16[2,128,128]{2,1,0:T(8,128)(2,1)S(1)}, u32[]{:S(2)}, u32[]{:S(2)}) collective-permute-start(bf16[2,128,128]{2,1,0:T(8,128)(2,1)S(1)} %get-tuple-element.31), channel_id=1, source_target_pairs={{0,0},{56,8},{8,16},{32,24},{16,32},{40,40},{24,48},{48,56},{64,64... | collective-permute-start | bytes 196616 | tf_op jit(solution)/shard_map/upstream_to_units/ppermute | solution.py:379
  45.9 28.5 %collective-permute-start.9 = (bf16[2,128,128]{2,1,0:T(8,128)(2,1)S(1)}, bf16[2,128,128]{2,1,0:T(8,128)(2,1)S(1)}, u32[]{:S(2)}, u32[]{:S(2)}) collective-permute-start(bf16[2,128,128]{2,1,0:T(8,128)(2,1)S(1)} %get-tuple-element.32), channel_id=1, source_target_pairs={{32,0},{24,8},{40,16},{0,24},{48,32},{8,40},{56,48},{16,56},{96,64... | collective-permute-start | bytes 196616 | tf_op jit(solution)/shard_map/upstream_to_units/ppermute | solution.py:379
  63.9 22.9 %collective-permute-start.1 = (bf16[2,5,128,128]{3,2,0,1:T(8,128)(2,1)S(1)}, bf16[2,5,128,128]{3,2,0,1:T(8,128)(2,1)S(1)}, u32[]{:S(2)}, u32[]{:S(2)}) collective-permute-start(bf16[2,5,128,128]{3,2,0,1:T(8,128)(2,1)S(1)} %get-tuple-element.64), channel_id=1, source_target_pairs={{64,0},{72,8},{80,16},{88,24},{96,32},{104,40},{112,48},{120,56},{... | collective-permute-start | bytes 983048 | tf_op jit(solution)/shard_map/halos/ppermute | solution.py:379
  66.8 23.9 %collective-permute-start = (bf16[2,5,128,128]{3,2,0,1:T(8,128)(2,1)S(1)}, bf16[2,5,128,128]{3,2,0,1:T(8,128)(2,1)S(1)}, u32[]{:S(2)}, u32[]{:S(2)}) collective-permute-start(bf16[2,5,128,128]{3,2,0,1:T(8,128)(2,1)S(1)} %get-tuple-element.65), channel_id=1, source_target_pairs={{0,64},{8,72},{16,80},{24,88},{32,96},{40,104},{48,112},{56,120},{... | collective-permute-start | bytes 983048 | tf_op jit(solution)/shard_map/halos/ppermute | solution.py:379
  69.8 9.5 %collective-permute-start.10 = (bf16[2,128,128]{2,1,0:T(8,128)(2,1)S(1)}, bf16[2,128,128]{2,1,0:T(8,128)(2,1)S(1)}, u32[]{:S(2)}, u32[]{:S(2)}) collective-permute-start(bf16[2,128,128]{2,1,0:T(8,128)(2,1)S(1)} %get-tuple-element.33), channel_id=1, source_target_pairs={{8,0},{32,8},{16,16},{40,24},{24,32},{48,40},{0,48},{56,56},{72,64... | collective-permute-start | bytes 196616 | tf_op jit(solution)/shard_map/upstream_to_units/ppermute | solution.py:379
  71.8 9.6 %collective-permute-start.3 = (bf16[2,2,128,128]{3,2,0,1:T(8,128)(2,1)S(1)}, bf16[2,2,128,128]{3,2,0,1:T(8,128)(2,1)S(1)}, u32[]{:S(2)}, u32[]{:S(2)}) collective-permute-start(bf16[2,2,128,128]{3,2,0,1:T(8,128)(2,1)S(1)} %get-tuple-element.62), channel_id=1, source_target_pairs={{8,0},{16,8},{24,16},{32,24},{40,32},{48,40},{56,48},{72,64},{80,7... | collective-permute-start | bytes 393224 | tf_op jit(solution)/shard_map/halos/ppermute | solution.py:379
  74.4 9.6 %collective-permute-start.2 = (bf16[2,2,128,128]{3,2,0,1:T(8,128)(2,1)S(1)}, bf16[2,2,128,128]{3,2,0,1:T(8,128)(2,1)S(1)}, u32[]{:S(2)}, u32[]{:S(2)}) collective-permute-start(bf16[2,2,128,128]{3,2,0,1:T(8,128)(2,1)S(1)} %get-tuple-element.63), channel_id=1, source_target_pairs={{0,8},{8,16},{16,24},{24,32},{32,40},{40,48},{48,56},{64,72},{72,8... | collective-permute-start | bytes 393224 | tf_op jit(solution)/shard_map/halos/ppermute | solution.py:379
  79.3 16.3 %collective-permute-start.11 = (bf16[2,128,128]{2,1,0:T(8,128)(2,1)S(1)}, bf16[2,128,128]{2,1,0:T(8,128)(2,1)S(1)}, u32[]{:S(2)}, u32[]{:S(2)}) collective-permute-start(bf16[2,128,128]{2,1,0:T(8,128)(2,1)S(1)} %get-tuple-element.34), channel_id=1, source_target_pairs={{40,0},{0,8},{48,16},{8,24},{56,32},{16,40},{32,48},{24,56},{104,6... | collective-permute-start | bytes 196616 | tf_op jit(solution)/shard_map/upstream_to_units/ppermute | solution.py:379
  81.3 14.4 %collective-permute-start.7 = (bf16[2,128,128]{2,1,0:T(8,128)(2,1)S(1)}, bf16[2,128,128]{2,1,0:T(8,128)(2,1)S(1)}, u32[]{:S(2)}, u32[]{:S(2)}) collective-permute-start(bf16[2,128,128]{2,1,0:T(8,128)(2,1)S(1)} %get-tuple-element.58), channel_id=1, source_target_pairs={{72,0},{80,8},{88,16},{96,24},{104,32},{112,40},{120,48},{136,64},... | collective-permute-start | bytes 196616 | tf_op jit(solution)/shard_map/halos/ppermute | solution.py:379
  84.0 11.8 %collective-permute-start.6 = (bf16[2,128,128]{2,1,0:T(8,128)(2,1)S(1)}, bf16[2,128,128]{2,1,0:T(8,128)(2,1)S(1)}, u32[]{:S(2)}, u32[]{:S(2)}) collective-permute-start(bf16[2,128,128]{2,1,0:T(8,128)(2,1)S(1)} %get-tuple-element.59), channel_id=1, source_target_pairs={{64,8},{72,16},{80,24},{88,32},{96,40},{104,48},{112,56},{128,72},... | collective-permute-start | bytes 196616 | tf_op jit(solution)/shard_map/halos/ppermute | solution.py:379
  86.8 8.9 %collective-permute-start.5 = (bf16[2,128,128]{2,1,0:T(8,128)(2,1)S(1)}, bf16[2,128,128]{2,1,0:T(8,128)(2,1)S(1)}, u32[]{:S(2)}, u32[]{:S(2)}) collective-permute-start(bf16[2,128,128]{2,1,0:T(8,128)(2,1)S(1)} %get-tuple-element.60), channel_id=1, source_target_pairs={{8,64},{16,72},{24,80},{32,88},{40,96},{48,104},{56,112},{72,128},... | collective-permute-start | bytes 196616 | tf_op jit(solution)/shard_map/halos/ppermute | solution.py:379
  90.7 7.1 %collective-permute-start.4 = (bf16[2,128,128]{2,1,0:T(8,128)(2,1)S(1)}, bf16[2,128,128]{2,1,0:T(8,128)(2,1)S(1)}, u32[]{:S(2)}, u32[]{:S(2)}) collective-permute-start(bf16[2,128,128]{2,1,0:T(8,128)(2,1)S(1)} %get-tuple-element.61), channel_id=1, source_target_pairs={{0,72},{8,80},{16,88},{24,96},{32,104},{40,112},{48,120},{64,136},... | collective-permute-start | bytes 196616 | tf_op jit(solution)/shard_map/halos/ppermute | solution.py:379
  107.9 49.3 %collective-permute-start.20 = (bf16[2,5,128,128]{3,2,1,0:T(8,128)(2,1)S(1)}, bf16[2,5,128,128]{3,2,1,0:T(8,128)(2,1)S(1)}, u32[]{:S(2)}, u32[]{:S(2)}) collective-permute-start(bf16[2,5,128,128]{3,2,1,0:T(8,128)(2,1)S(1)} %get-tuple-element.44), channel_id=1, source_target_pairs={{0,64},{8,72},{16,80},{24,88},{32,96},{40,104},{48,112},{56,120},{... | collective-permute-start | bytes 983048 | tf_op jit(solution)/shard_map/terms/ppermute | solution.py:379
  110.6 46.9 %collective-permute-start.21 = (bf16[2,5,128,128]{3,2,1,0:T(8,128)(2,1)S(1)}, bf16[2,5,128,128]{3,2,1,0:T(8,128)(2,1)S(1)}, u32[]{:S(2)}, u32[]{:S(2)}) collective-permute-start(bf16[2,5,128,128]{3,2,1,0:T(8,128)(2,1)S(1)} %get-tuple-element.45), channel_id=1, source_target_pairs={{64,0},{72,8},{80,16},{88,24},{96,32},{104,40},{112,48},{120,56},{... | collective-permute-start | bytes 983048 | tf_op jit(solution)/shard_map/terms/ppermute | solution.py:379
  113.8 8.9 %collective-permute-start.18 = (bf16[2,128,128]{2,1,0:T(8,128)(2,1)S(1)}, bf16[2,128,128]{2,1,0:T(8,128)(2,1)S(1)}, u32[]{:S(2)}, u32[]{:S(2)}) collective-permute-start(bf16[2,128,128]{2,1,0:T(8,128)(2,1)S(1)} %get-tuple-element.41), channel_id=1, source_target_pairs={{0,16},{8,48},{16,24},{24,56},{32,0},{40,32},{48,8},{56,40},{64,80... | collective-permute-start | bytes 196616 | tf_op jit(solution)/shard_map/outputs_home/ppermute | solution.py:379
  116.3 10.0 %collective-permute-start.24 = (bf16[2,128,128]{2,1,0:T(8,128)(2,1)S(1)}, bf16[2,128,128]{2,1,0:T(8,128)(2,1)S(1)}, u32[]{:S(2)}, u32[]{:S(2)}) collective-permute-start(bf16[2,128,128]{2,1,0:T(8,128)(2,1)S(1)} %get-tuple-element.48), channel_id=1, source_target_pairs={{0,72},{8,80},{16,88},{24,96},{32,104},{40,112},{48,120},{64,136},... | collective-permute-start | bytes 196616 | tf_op jit(solution)/shard_map/terms/ppermute | solution.py:379
  119.5 10.2 %collective-permute-start.25 = (bf16[2,128,128]{2,1,0:T(8,128)(2,1)S(1)}, bf16[2,128,128]{2,1,0:T(8,128)(2,1)S(1)}, u32[]{:S(2)}, u32[]{:S(2)}) collective-permute-start(bf16[2,128,128]{2,1,0:T(8,128)(2,1)S(1)} %get-tuple-element.49), channel_id=1, source_target_pairs={{8,64},{16,72},{24,80},{32,88},{40,96},{48,104},{56,112},{72,128},... | collective-permute-start | bytes 196616 | tf_op jit(solution)/shard_map/terms/ppermute | solution.py:379
  122.8 9.4 %collective-permute-start.26 = (bf16[2,128,128]{2,1,0:T(8,128)(2,1)S(1)}, bf16[2,128,128]{2,1,0:T(8,128)(2,1)S(1)}, u32[]{:S(2)}, u32[]{:S(2)}) collective-permute-start(bf16[2,128,128]{2,1,0:T(8,128)(2,1)S(1)} %get-tuple-element.50), channel_id=1, source_target_pairs={{64,8},{72,16},{80,24},{88,32},{96,40},{104,48},{112,56},{128,72},... | collective-permute-start | bytes 196616 | tf_op jit(solution)/shard_map/terms/ppermute | solution.py:379
  126.3 16.4 %collective-permute-start.22 = (bf16[2,2,128,128]{3,2,1,0:T(8,128)(2,1)S(1)}, bf16[2,2,128,128]{3,2,1,0:T(8,128)(2,1)S(1)}, u32[]{:S(2)}, u32[]{:S(2)}) collective-permute-start(bf16[2,2,128,128]{3,2,1,0:T(8,128)(2,1)S(1)} %get-tuple-element.46), channel_id=1, source_target_pairs={{0,8},{8,16},{16,24},{24,32},{32,40},{40,48},{48,56},{64,72},{72,8... | collective-permute-start | bytes 393224 | tf_op jit(solution)/shard_map/terms/ppermute | solution.py:379
  129.7 20.6 %collective-permute-start.23 = (bf16[2,2,128,128]{3,2,1,0:T(8,128)(2,1)S(1)}, bf16[2,2,128,128]{3,2,1,0:T(8,128)(2,1)S(1)}, u32[]{:S(2)}, u32[]{:S(2)}) collective-permute-start(bf16[2,2,128,128]{3,2,1,0:T(8,128)(2,1)S(1)} %get-tuple-element.47), channel_id=1, source_target_pairs={{8,0},{16,8},{24,16},{32,24},{40,32},{48,40},{56,48},{72,64},{80,7... | collective-permute-start | bytes 393224 | tf_op jit(solution)/shard_map/terms/ppermute | solution.py:379
  132.1 8.6 %collective-permute-start.27 = (bf16[2,128,128]{2,1,0:T(8,128)(2,1)S(1)}, bf16[2,128,128]{2,1,0:T(8,128)(2,1)S(1)}, u32[]{:S(2)}, u32[]{:S(2)}) collective-permute-start(bf16[2,128,128]{2,1,0:T(8,128)(2,1)S(1)} %get-tuple-element.51), channel_id=1, source_target_pairs={{72,0},{80,8},{88,16},{96,24},{104,32},{112,40},{120,48},{136,64},... | collective-permute-start | bytes 196616 | tf_op jit(solution)/shard_map/terms/ppermute | solution.py:379
  140.7 26.5 %collective-permute-start.14 = (bf16[2,2,128,128]{3,2,1,0:T(8,128)(2,1)S(1)}, bf16[2,2,128,128]{3,2,1,0:T(8,128)(2,1)S(1)}, u32[]{:S(2)}, u32[]{:S(2)}) collective-permute-start(bf16[2,2,128,128]{3,2,1,0:T(8,128)(2,1)S(1)} %get-tuple-element.37), channel_id=1, source_target_pairs={{0,0},{8,56},{16,8},{24,32},{32,16},{40,40},{48,24},{56,48},{64,64... | collective-permute-start | bytes 393224 | tf_op jit(solution)/shard_map/outputs_home/ppermute | solution.py:379
  142.6 28.8 %collective-permute-start.15 = (bf16[2,2,128,128]{3,2,1,0:T(8,128)(2,1)S(1)}, bf16[2,2,128,128]{3,2,1,0:T(8,128)(2,1)S(1)}, u32[]{:S(2)}, u32[]{:S(2)}) collective-permute-start(bf16[2,2,128,128]{3,2,1,0:T(8,128)(2,1)S(1)} %get-tuple-element.38), channel_id=1, source_target_pairs={{0,32},{8,24},{16,40},{24,0},{32,48},{40,8},{48,56},{56,16},{64,96... | collective-permute-start | bytes 393224 | tf_op jit(solution)/shard_map/outputs_home/ppermute | solution.py:379
  150.3 26.7 %collective-permute-start.16 = (bf16[2,2,128,128]{3,2,1,0:T(8,128)(2,1)S(1)}, bf16[2,2,128,128]{3,2,1,0:T(8,128)(2,1)S(1)}, u32[]{:S(2)}, u32[]{:S(2)}) collective-permute-start(bf16[2,2,128,128]{3,2,1,0:T(8,128)(2,1)S(1)} %get-tuple-element.39), channel_id=1, source_target_pairs={{0,8},{8,32},{16,16},{24,40},{32,24},{40,48},{48,0},{56,56},{64,72... | collective-permute-start | bytes 393224 | tf_op jit(solution)/shard_map/outputs_home/ppermute | solution.py:379
  157.2 23.0 %collective-permute-start.17 = (bf16[2,2,128,128]{3,2,1,0:T(8,128)(2,1)S(1)}, bf16[2,2,128,128]{3,2,1,0:T(8,128)(2,1)S(1)}, u32[]{:S(2)}, u32[]{:S(2)}) collective-permute-start(bf16[2,2,128,128]{3,2,1,0:T(8,128)(2,1)S(1)} %get-tuple-element.40), channel_id=1, source_target_pairs={{0,40},{8,0},{16,48},{24,8},{32,56},{40,16},{48,32},{56,24},{64,10... | collective-permute-start | bytes 393224 | tf_op jit(solution)/shard_map/outputs_home/ppermute | solution.py:379
  157.5 8.3 %collective-permute-start.19 = (bf16[2,128,128]{2,1,0:T(8,128)(2,1)S(1)}, bf16[2,128,128]{2,1,0:T(8,128)(2,1)S(1)}, u32[]{:S(2)}, u32[]{:S(2)}) collective-permute-start(bf16[2,128,128]{2,1,0:T(8,128)(2,1)S(1)} %get-tuple-element.42), channel_id=1, source_target_pairs={{0,48},{8,16},{16,56},{24,24},{32,32},{40,0},{48,40},{56,8},{64,11... | collective-permute-start | bytes 196616 | tf_op jit(solution)/shard_map/outputs_home/ppermute | solution.py:379
  165.8 15.3 %collective-permute-start.32 = (bf16[2,128,128]{2,1,0:T(8,128)(2,1)S(1)}, bf16[2,128,128]{2,1,0:T(8,128)(2,1)S(1)}, u32[]{:S(2)}, u32[]{:S(2)}) collective-permute-start(bf16[2,128,128]{2,1,0:T(8,128)(2,1)S(1)} %get-tuple-element.56), channel_id=1, source_target_pairs={{0,16},{8,48},{16,24},{24,56},{32,0},{40,32},{48,8},{56,40},{64,80... | collective-permute-start | bytes 196616 | tf_op jit(solution)/shard_map/key_terms_home/ppermute | solution.py:379
  167.2 22.8 %collective-permute-start.28 = (bf16[2,2,128,128]{3,2,1,0:T(8,128)(2,1)S(1)}, bf16[2,2,128,128]{3,2,1,0:T(8,128)(2,1)S(1)}, u32[]{:S(2)}, u32[]{:S(2)}) collective-permute-start(bf16[2,2,128,128]{3,2,1,0:T(8,128)(2,1)S(1)} %get-tuple-element.52), channel_id=1, source_target_pairs={{0,0},{8,56},{16,8},{24,32},{32,16},{40,40},{48,24},{56,48},{64,64... | collective-permute-start | bytes 393224 | tf_op jit(solution)/shard_map/key_terms_home/ppermute | solution.py:379
  171.5 18.5 %collective-permute-start.29 = (bf16[2,2,128,128]{3,2,1,0:T(8,128)(2,1)S(1)}, bf16[2,2,128,128]{3,2,1,0:T(8,128)(2,1)S(1)}, u32[]{:S(2)}, u32[]{:S(2)}) collective-permute-start(bf16[2,2,128,128]{3,2,1,0:T(8,128)(2,1)S(1)} %get-tuple-element.53), channel_id=1, source_target_pairs={{0,32},{8,24},{16,40},{24,0},{32,48},{40,8},{48,56},{56,16},{64,96... | collective-permute-start | bytes 393224 | tf_op jit(solution)/shard_map/key_terms_home/ppermute | solution.py:379
  177.0 13.0 %collective-permute-start.30 = (bf16[2,2,128,128]{3,2,1,0:T(8,128)(2,1)S(1)}, bf16[2,2,128,128]{3,2,1,0:T(8,128)(2,1)S(1)}, u32[]{:S(2)}, u32[]{:S(2)}) collective-permute-start(bf16[2,2,128,128]{3,2,1,0:T(8,128)(2,1)S(1)} %get-tuple-element.54), channel_id=1, source_target_pairs={{0,8},{8,32},{16,16},{24,40},{32,24},{40,48},{48,0},{56,56},{64,72... | collective-permute-start | bytes 393224 | tf_op jit(solution)/shard_map/key_terms_home/ppermute | solution.py:379
  180.3 9.8 %collective-permute-start.31 = (bf16[2,2,128,128]{3,2,1,0:T(8,128)(2,1)S(1)}, bf16[2,2,128,128]{3,2,1,0:T(8,128)(2,1)S(1)}, u32[]{:S(2)}, u32[]{:S(2)}) collective-permute-start(bf16[2,2,128,128]{3,2,1,0:T(8,128)(2,1)S(1)} %get-tuple-element.55), channel_id=1, source_target_pairs={{0,40},{8,0},{16,48},{24,8},{32,56},{40,16},{48,32},{56,24},{64,10... | collective-permute-start | bytes 393224 | tf_op jit(solution)/shard_map/key_terms_home/ppermute | solution.py:379
  181.0 9.0 %collective-permute-start.33 = (bf16[2,128,128]{2,1,0:T(8,128)(2,1)S(1)}, bf16[2,128,128]{2,1,0:T(8,128)(2,1)S(1)}, u32[]{:S(2)}, u32[]{:S(2)}) collective-permute-start(bf16[2,128,128]{2,1,0:T(8,128)(2,1)S(1)} %get-tuple-element.57), channel_id=1, source_target_pairs={{0,48},{8,16},{16,56},{24,24},{32,32},{40,0},{48,40},{56,8},{64,11... | collective-permute-start | bytes 196616 | tf_op jit(solution)/shard_map/key_terms_home/ppermute | solution.py:379
where the time goes:
time: 194 us; the launch traced here: 192 us
  starting transfers between devices  117 us (60%)
  waiting for transfers between devices  35.5 us (18%)
  blocking collectives  19.5 us (10%)
  Pallas kernels  14 us (7%)
  local copies, waits for them, and re-layouts  4.5 us (2%)
    ppermute x34, starting transfers between devices, send_all(): lax.ppermute(part, 'tile', path)  106 us
    all_to_all x1, blocking collectives, local(): by_head = lax.all_to_all(jnp.stack(lines, axis=1), 'head', 0, 0, tiled=True)  19.5 us
    ppermute x34, waiting for transfers between devices, send_all(): lax.ppermute(part, 'tile', path)  18.2 us
    all_to_all x1, waiting for transfers between devices, local(): lax.all_to_all(shaped.reshape(32, 5, 3, 8, 128), 'tile', 0, 0, tiled=True)  17.3 us
    all_to_all x1, starting transfers between devices, local(): lax.all_to_all(shaped.reshape(32, 5, 3, 8, 128), 'tile', 0, 0, tiled=True)  11.4 us
    pallas_call x1, Pallas kernels, attend(): pl.pallas_call(attend_kernel, out_shape=owner_shapes() + [jax.ShapeDtypeS...  10.1 us
  transfers between devices with their start and end apart: 35, of which 6 were waited for; matrix products, arithmetic and copies ran while one was open for 1% of the time, Pallas kernels for 1%

commit v1 on v0

--- a/solution.py
+++ b/solution.py
@@ -53,7 +53,8 @@
     return [(target, source) for source, target in pairs]
 
 
-HALO_STEPS = ((1, 0), (-1, 0), (0, 1), (0, -1), (1, 1), (1, -1), (-1, 1), (-1, -1))
+ROW_STEPS = ((1, 0), (-1, 0))
+COLUMN_STEPS = ((0, 1), (0, -1))
 OWNER_STEPS = tuple((which, turn) for which in range(3) for turn in range(2))
 
 
@@ -179,10 +180,10 @@
     ]
 
 
-def attend_kernel(table, own, *refs):
-    halos, grads = refs[:8], refs[8:14]
-    outs, terms, edges = refs[14:20], refs[20], refs[21:29]
-    pair, turned, grad, total, held = refs[29:]
+def attend_kernel(table, own, near, *refs):
+    halos, grads = refs[:4], refs[4:10]
+    outs, terms, edges = refs[10:16], refs[16], refs[17:19]
+    pair, turned, grad, total, held = refs[19:]
     strip, odd = table[0], table[1]
     scaling = HEAD_DIM**-0.5
     rate = scaling * math.log2(math.e)
@@ -190,16 +191,13 @@
     for kind in range(2):
         for at in range(5):
             for row in range(2):
-                pair[kind, at + 1, row] = own[kind + 1, row, at]
-            pair[kind, at + 1, 2] = halos[0][kind, at]
-            pair[kind, at + 1, 3] = halos[1][kind, at]
+                pair[kind, at + 1, row] = near[kind, row, at]
         for row in range(2):
-            pair[kind, 0, row] = halos[2][kind, row]
-            pair[kind, 6, row] = halos[3][kind, row]
-        pair[kind, 0, 2] = halos[4][kind]
-        pair[kind, 6, 2] = halos[5][kind]
-        pair[kind, 0, 3] = halos[6][kind]
-        pair[kind, 6, 3] = halos[7][kind]
+            pair[kind, 0, row] = halos[0][kind, row]
+            pair[kind, 6, row] = halos[1][kind, row]
+        for at in range(7):
+            pair[kind, at, 2] = halos[2][kind, at]
+            pair[kind, at, 3] = halos[3][kind, at]
     for kind in range(2):
         for at in range(7):
             for row in range(4):
@@ -215,7 +213,7 @@
 
     def one_unit(unit, carry):
         column = table[2 + unit]
-        queries = [own[0, row, unit] for row in range(2)]
+        queries = [own[row, unit] for row in range(2)]
         both = jnp.concatenate(queries, axis=0)
         ups = [grad[row, unit] for row in range(2)]
         up_both = jnp.concatenate(ups, axis=0)
@@ -305,33 +303,24 @@
     lax.fori_loop(0, 5, one_unit, 0)
     fill_outs(odd, held, outs)
     for kind, factor in ((0, scaling), (1, 1.0)):
-        for at in range(5):
+        for at in range(7):
             for row in range(2):
-                terms[kind, row, at] = total[kind, at + 1, row] * factor
-            edges[0][kind, at] = (total[kind, at + 1, 3] * factor).astype(LOW)
-            edges[1][kind, at] = (total[kind, at + 1, 2] * factor).astype(LOW)
-        for row in range(2):
-            edges[2][kind, row] = (total[kind, 6, row] * factor).astype(LOW)
-            edges[3][kind, row] = (total[kind, 0, row] * factor).astype(LOW)
-        edges[4][kind] = (total[kind, 6, 3] * factor).astype(LOW)
-        edges[5][kind] = (total[kind, 0, 3] * factor).astype(LOW)
-        edges[6][kind] = (total[kind, 6, 2] * factor).astype(LOW)
-        edges[7][kind] = (total[kind, 0, 2] * factor).astype(LOW)
-
-
-def halo_shapes():
-    middle = [(5,), (5,), (2,), (2,), (), (), (), ()]
-    return [jax.ShapeDtypeStruct((2,) + size + (TILE, HEAD_DIM), LOW) for size in middle]
-
-
-def attend(table, own, halos, grads):
+                terms[kind, row, at] = total[kind, at, row] * factor
+                edges[row][kind, at] = (total[kind, at, 3 - row] * factor).astype(LOW)
+
+
+def column_shapes():
+    return [jax.ShapeDtypeStruct((2, 2, TILE, HEAD_DIM), LOW)] * 2
+
+
+def attend(table, own, pair, halos, grads):
     return pl.pallas_call(
         attend_kernel,
         out_shape=owner_shapes()
-        + [jax.ShapeDtypeStruct((2, 2, 5, TILE, HEAD_DIM), WIDE)]
-        + halo_shapes(),
-        in_specs=[pl.BlockSpec(memory_space=pltpu.SMEM)] + whole(15),
-        out_specs=whole(15),
+        + [jax.ShapeDtypeStruct((2, 2, 7, TILE, HEAD_DIM), WIDE)]
+        + [jax.ShapeDtypeStruct((2, 7, TILE, HEAD_DIM), LOW)] * 2,
+        in_specs=[pl.BlockSpec(memory_space=pltpu.SMEM)] + whole(12),
+        out_specs=whole(9),
         scratch_shapes=[
             pltpu.VMEM((2, 7, 4, TILE, HEAD_DIM), LOW),
             pltpu.VMEM((2, 7, 4, HEAD_DIM, TILE), LOW),
@@ -344,35 +333,51 @@
             flops=3_000_000_000, bytes_accessed=8_000_000, transcendentals=1_500_000
         ),
         name="attend",
-    )(table, own, *halos, *grads)
+    )(table, own, pair, *halos, *grads)
+
+
+def rims_kernel(terms, above, below, right, left):
+    for kind in range(2):
+        for row, edge in enumerate((above, below)):
+            for out, at in ((right, 6), (left, 0)):
+                out[kind, row] = (terms[kind, row, at] + edge[kind, at].astype(WIDE)).astype(LOW)
+
+
+def rims(terms, edges):
+    return pl.pallas_call(
+        rims_kernel,
+        out_shape=column_shapes(),
+        in_specs=whole(3),
+        out_specs=whole(2),
+        compiler_params=pltpu.CompilerParams(vmem_limit_bytes=16 << 20),
+        name="rims",
+    )(terms, *edges)
 
 
 def combine_kernel(table, terms, *refs):
-    edges, outs, held = refs[:8], refs[8:14], refs[14]
+    edges, columns, outs, held = refs[:2], refs[2:4], refs[4:10], refs[10]
     for kind in range(2):
         for row in range(2):
             for at in range(5):
-                value = terms[kind, row, at] + edges[row][kind, at].astype(WIDE)
+                value = terms[kind, row, at + 1] + edges[row][kind, at + 1].astype(WIDE)
                 if at == 0:
-                    value = value + edges[2][kind, row].astype(WIDE)
-                    value = value + edges[4 + 2 * row][kind].astype(WIDE)
+                    value = value + columns[0][kind, row].astype(WIDE)
                 if at == 4:
-                    value = value + edges[3][kind, row].astype(WIDE)
-                    value = value + edges[5 + 2 * row][kind].astype(WIDE)
+                    value = value + columns[1][kind, row].astype(WIDE)
                 held[kind, row, at] = value.astype(LOW)
     fill_outs(table[1], held, outs)
 
 
-def combine(table, terms, edges):
+def combine(table, terms, edges, columns):
     return pl.pallas_call(
         combine_kernel,
         out_shape=owner_shapes(),
-        in_specs=[pl.BlockSpec(memory_space=pltpu.SMEM)] + whole(9),
+        in_specs=[pl.BlockSpec(memory_space=pltpu.SMEM)] + whole(5),
         out_specs=whole(6),
         scratch_shapes=[pltpu.VMEM((2, 2, 5, TILE, HEAD_DIM), LOW)],
         compiler_params=pltpu.CompilerParams(vmem_limit_bytes=16 << 20),
         name="combine",
-    )(table, terms, *edges)
+    )(table, terms, *edges, *columns)
 
 
 def send_all(parts, routes):
@@ -383,44 +388,55 @@
     owners = owner_table()
     units = unit_table()
     to_owner = [owner_of(which, turn) for which, turn in OWNER_STEPS]
-    halo_routes = [shifted(*step) for step in HALO_STEPS]
+    row_routes = [shifted(*step) for step in ROW_STEPS]
+    column_routes = [shifted(*step) for step in COLUMN_STEPS]
 
     with jax.named_scope("upstream_to_units"):
         grads = send_all(spread(owners, upstream), [flipped(path) for path in to_owner])
 
-    with jax.named_scope("heads"):
+    def by_head(*slabs):
         lines = [
             slab.reshape(8, 4, 40, 128).transpose(2, 0, 1, 3).reshape(8, 5, 32, 128)
-            for slab in (query_slab, key_slab, value_slab)
+            for slab in slabs
         ]
-        by_head = lax.all_to_all(jnp.stack(lines, axis=1), "head", 0, 0, tiled=True)
-    with jax.named_scope("tiles"):
-        shaped = by_head.reshape(8, 3, 5, 4, 8, 128).transpose(3, 2, 0, 1, 4, 5)
-        got = lax.all_to_all(shaped.reshape(32, 5, 3, 8, 128), "tile", 0, 0, tiled=True)
-        own = got.reshape(32, 5, 3, 2, 4, 128).transpose(2, 3, 1, 0, 4, 5)
-        own = own.reshape(3, 2, 5, TILE, HEAD_DIM)
+        return jnp.stack(lines, axis=1)
+
+    def by_unit(swapped):
+        shaped = swapped.reshape(8, -1, 5, 4, 8, 128).transpose(3, 2, 0, 1, 4, 5)
+        return shaped.reshape(32, 5, -1, 8, 128)
+
+    def by_tile(got):
+        own = got.reshape(32, 5, -1, 2, 4, 128).transpose(2, 3, 1, 0, 4, 5)
+        return own.reshape(-1, 2, 5, TILE, HEAD_DIM)
+
+    with jax.named_scope("heads"):
+        lines = by_head(key_slab, value_slab, query_slab)
+        swapped = lax.all_to_all(lines, "head", 0, 0, tiled=True)
+    with jax.named_scope("key_value_tiles"):
+        shaped, grads = lax.optimization_barrier((by_unit(swapped[:, :2]), grads))
+        pair = by_tile(lax.all_to_all(shaped, "tile", 0, 0, tiled=True))
+    with jax.named_scope("query_tiles"):
+        own = by_tile(lax.all_to_all(by_unit(swapped[:, 2:]), "tile", 0, 0, tiled=True))[0]
     with jax.named_scope("halos"):
-        pair = own[1:]
+        sides = send_all([pair[:, :, 4], pair[:, :, 0]], column_routes)
         leaving = [
-            pair[:, 1],
-            pair[:, 0],
-            pair[:, :, 4],
-            pair[:, :, 0],
-            pair[:, 1, 4],
-            pair[:, 1, 0],
-            pair[:, 0, 4],
-            pair[:, 0, 0],
+            jnp.concatenate([sides[0][:, row, None], pair[:, row], sides[1][:, row, None]], axis=1)
+            for row in (1, 0)
         ]
-        halos = send_all(leaving, halo_routes)
+        halos = sides + send_all(leaving, row_routes)
     with jax.named_scope("attention"):
-        results = attend(units, own, halos, grads)
+        results = attend(units, own, pair, halos, grads)
     first, terms, edges = results[:6], results[6], results[7:]
     with jax.named_scope("terms"):
-        edges = send_all(edges, halo_routes)
-    with jax.named_scope("outputs_home"):
-        first = send_all(first, to_owner)
+        edges = send_all(edges, row_routes)
+        early = send_all(first[:3], to_owner[:3])
+        edges, early = lax.optimization_barrier((edges, early))
+        columns = send_all(rims(terms, edges), column_routes)
+        late = send_all(first[3:], to_owner[3:])
     with jax.named_scope("key_terms_home"):
-        second = send_all(combine(units, terms, edges), to_owner)
+        columns, late = lax.optimization_barrier((columns, late))
+        second = send_all(combine(units, terms, edges, columns), to_owner)
+    first = early + late
     with jax.named_scope("settle"):
         return tuple(gather(owners, first, second))
 

time: 194 us -> 176 us (0.907)
  blocking collectives: 19.5 us -> 0 us
  starting transfers between devices: 117 us -> 101 us
  waiting for transfers between devices: 35.5 us -> 50.2 us
  local copies, waits for them, and re-layouts: 4.5 us -> 6.79 us
    ppermute x34 -> x26, starting transfers between devices: 106 us -> 82.2 us  [send_all(): lax.ppermute(part, 'tile', path)]
    all_to_all x1 -> x0, blocking collectives: 19.5 us -> none  [local(): by_head = lax.all_to_all(jnp.stack(lines, axis=1), 'head', 0, 0, tiled=True)]
    ppermute x34 -> x26, waiting for transfers between devices: 18.2 us -> 33 us  [send_all(): lax.ppermute(part, 'tile', path)]
    all_to_all x1 -> x3, starting transfers between devices: 11.4 us -> 19.1 us  [the longest x1 9.11 us: local(): pair = by_tile(lax.all_to_all(shaped, 'tile', 0, 0, tiled=True))]
    all_to_all x1 -> x3, waiting for transfers between devices: 17.3 us -> 17.2 us  [the longest x1 17.2 us: local(): pair = by_tile(lax.all_to_all(shaped, 'tile', 0, 0, tiled=True))]
  transfers between devices with their start and end apart: 35 -> 29, of which waited for: 6 -> 12; matrix products, arithmetic and copies ran while one was open for 1% -> 2% of each run, Pallas kernels for 1% -> 1%
where the time goes in v1:
time: 176 us; the launch traced here: 174 us
  starting transfers between devices  101 us (57%)
  waiting for transfers between devices  50.2 us (29%)
  Pallas kernels  14 us (8%)
  local copies, waits for them, and re-layouts  6.79 us (4%)
    ppermute x26, starting transfers between devices, send_all(): lax.ppermute(part, 'tile', path)  82.2 us
    ppermute x26, waiting for transfers between devices, send_all(): lax.ppermute(part, 'tile', path)  33 us
    all_to_all x1, waiting for transfers between devices, local(): pair = by_tile(lax.all_to_all(shaped, 'tile', 0, 0, tiled=True))  17.2 us
    pallas_call x1, Pallas kernels, attend(): pl.pallas_call(attend_kernel, out_shape=owner_shapes() + [jax.ShapeDtypeS...  10.1 us
    all_to_all x1, starting transfers between devices, local(): pair = by_tile(lax.all_to_all(shaped, 'tile', 0, 0, tiled=True))  9.11 us
    all_to_all x1, starting transfers between devices, local(): lax.all_to_all(by_unit(swapped[:, 2:]), 'tile', 0, 0, tiled=True)  5.67 us
    all_to_all x1, starting transfers between devices, local(): swapped = lax.all_to_all(lines, 'head', 0, 0, tiled=True)  4.3 us
  transfers between devices with their start and end apart: 29, of which 12 were waited for; matrix products, arithmetic and copies ran while one was open for 2% of the time, Pallas kernels for 1%

profile of v1, /device:TPU:40, one launch (start us, length us, event | category | flops | bytes accessed | tf_op | source)
XLA Modules:
  0.0 173.7 jit_solution(690682982484650572)
XLA Ops:
  0.6 1.1 reshape.54
  1.9 1.1 reshape.50
  3.6 1.0 copy.50
  4.6 4.3 %all-to-all-start = ((bf16[8,3,5,32,128]{4,3,2,1,0:T(8,128)(2,1)}), bf16[8,3,5,32,128]{4,3,2,1,0:T(8,128)(2,1)S(1)}, u32[]{:S(2)}, u32[]{:S(2)}) async-start(bf16[8,3,5,32,128]{4,3,2,1,0:T(8,128)(2,1)} %copy.50), calls=%async_computation | async-start | bytes 1966080 | tf_op jit(solution)/shard_map/heads/all_to_all | solution.py:414
  9.0 0.9 spread.1
  9.9 5.9 %collective-permute-start.4 = (bf16[128,128]{1,0:T(8,128)(2,1)S(1)}, bf16[128,128]{1,0:T(8,128)(2,1)S(1)}, u32[]{:S(2)}, u32[]{:S(2)}) collective-permute-start(bf16[128,128]{1,0:T(8,128)(2,1)S(1)} %get-tuple-element.48), channel_id=1, source_target_pairs={{16,0},{48,8},{24,16},{56,24},{0,32},{32,40},{8,48},{40,56},{80,64... | collective-permute-start | bytes 98312 | tf_op jit(solution)/shard_map/upstream_to_units/ppermute | solution.py:384
  15.8 2.9 %collective-permute-start.5 = (bf16[128,128]{1,0:T(8,128)(2,1)S(1)}, bf16[128,128]{1,0:T(8,128)(2,1)S(1)}, u32[]{:S(2)}, u32[]{:S(2)}) collective-permute-start(bf16[128,128]{1,0:T(8,128)(2,1)S(1)} %get-tuple-element.49), channel_id=1, source_target_pairs={{48,0},{16,8},{56,16},{24,24},{32,32},{0,40},{40,48},{8,56},{112,6... | collective-permute-start | bytes 98312 | tf_op jit(solution)/shard_map/upstream_to_units/ppermute | solution.py:384
  18.7 3.0 %collective-permute-start = (bf16[2,128,128]{2,1,0:T(8,128)(2,1)S(1)}, bf16[2,128,128]{2,1,0:T(8,128)(2,1)S(1)}, u32[]{:S(2)}, u32[]{:S(2)}) collective-permute-start(bf16[2,128,128]{2,1,0:T(8,128)(2,1)S(1)} %get-tuple-element.44), channel_id=1, source_target_pairs={{0,0},{56,8},{8,16},{32,24},{16,32},{40,40},{24,48},{48,56},{64,64... | collective-permute-start | bytes 196616 | tf_op jit(solution)/shard_map/upstream_to_units/ppermute | solution.py:384
  21.8 7.8 %collective-permute-start.2 = (bf16[2,128,128]{2,1,0:T(8,128)(2,1)S(1)}, bf16[2,128,128]{2,1,0:T(8,128)(2,1)S(1)}, u32[]{:S(2)}, u32[]{:S(2)}) collective-permute-start(bf16[2,128,128]{2,1,0:T(8,128)(2,1)S(1)} %get-tuple-element.46), channel_id=1, source_target_pairs={{8,0},{32,8},{16,16},{40,24},{24,32},{48,40},{0,48},{56,56},{72,64... | collective-permute-start | bytes 196616 | tf_op jit(solution)/shard_map/upstream_to_units/ppermute | solution.py:384
  29.7 1.0 copy.56
  30.8 0.9 collective-permute-done.1.refs_5_
  31.6 0.6 collective-permute-done.2.refs_6_
  32.3 2.2 %collective-permute-done.3.refs_7_ = bf16[2,128,128]{2,1,0:T(8,128)(2,1)S(1)} collective-permute-done((bf16[2,128,128]{2,1,0:T(8,128)(2,1)S(1)}, bf16[2,128,128]{2,1,0:T(8,128)(2,1)S(1)}, u32[]{:S(2)}, u32[]{:S(2)}) %collective-permute-start.3) | collective-permute-done | bytes 65568 | tf_op jit(solution)/shard_map/upstream_to_units/ppermute | solution.py:384
  34.5 9.1 %all-to-all-start.2 = ((bf16[32,5,2,8,128]{4,3,2,1,0:T(8,128)(2,1)}), bf16[32,5,2,8,128]{4,3,2,1,0:T(8,128)(2,1)S(1)}, u32[]{:S(2)}, u32[]{:S(2)}) async-start(bf16[32,5,2,8,128]{4,3,2,1,0:T(8,128)(2,1)} %bitcast.28), calls=%async_computation.2 | async-start | bytes 1310720 | tf_op jit(solution)/shard_map/key_value_tiles/all_to_all | solution.py:417
  43.6 0.8 copy.52
  44.4 17.2 %all-to-all-done.2 = bf16[32,5,2,8,128]{4,3,2,1,0:T(8,128)(2,1)S(1)} async-done(((bf16[32,5,2,8,128]{4,3,2,1,0:T(8,128)(2,1)}), bf16[32,5,2,8,128]{4,3,2,1,0:T(8,128)(2,1)S(1)}, u32[]{:S(2)}, u32[]{:S(2)}) %all-to-all-start.2) | async-done | bytes 655392 | tf_op jit(solution)/shard_map/key_value_tiles/all_to_all | solution.py:417
  61.6 5.7 %all-to-all-start.1 = ((bf16[32,5,1,8,128]{4,3,1,2,0:T(8,128)(2,1)}), bf16[32,5,1,8,128]{4,3,1,2,0:T(8,128)(2,1)S(1)}, u32[]{:S(2)}, u32[]{:S(2)}) async-start(bf16[32,5,1,8,128]{4,3,1,2,0:T(8,128)(2,1)} %bitcast.22), calls=%async_computation.1 | async-start | bytes 655360 | tf_op jit(solution)/shard_map/query_tiles/all_to_all | solution.py:419
  67.3 0.2 copy.57
  67.5 0.3 copy.58
  67.9 3.4 %collective-permute-start.6 = (bf16[2,2,128,128]{3,2,0,1:T(8,128)(2,1)S(1)}, bf16[2,2,128,128]{3,2,0,1:T(8,128)(2,1)S(1)}, u32[]{:S(2)}, u32[]{:S(2)}) collective-permute-start(bf16[2,2,128,128]{3,2,0,1:T(8,128)(2,1)S(1)} %bitcast.66), channel_id=1, source_target_pairs={{0,8},{8,16},{16,24},{24,32},{32,40},{40,48},{48,56},{64,72},{72,8... | collective-permute-start | bytes 393224 | tf_op jit(solution)/shard_map/halos/ppermute | solution.py:384
  71.3 2.5 %collective-permute-start.7 = (bf16[2,2,128,128]{3,2,1,0:T(8,128)(2,1)S(1)}, bf16[2,2,128,128]{3,2,1,0:T(8,128)(2,1)S(1)}, u32[]{:S(2)}, u32[]{:S(2)}) collective-permute-start(bf16[2,2,128,128]{3,2,1,0:T(8,128)(2,1)S(1)} %get-tuple-element.86), channel_id=1, source_target_pairs={{8,0},{16,8},{24,16},{32,24},{40,32},{48,40},{56,48},{72,64},{80,7... | collective-permute-start | bytes 393224 | tf_op jit(solution)/shard_map/halos/ppermute | solution.py:384
  73.8 2.5 %collective-permute-done.6 = bf16[2,2,128,128]{3,2,0,1:T(8,128)(2,1)S(1)} collective-permute-done((bf16[2,2,128,128]{3,2,0,1:T(8,128)(2,1)S(1)}, bf16[2,2,128,128]{3,2,0,1:T(8,128)(2,1)S(1)}, u32[]{:S(2)}, u32[]{:S(2)}) %collective-permute-start.6) | collective-permute-done | bytes 131104 | tf_op jit(solution)/shard_map/halos/ppermute | solution.py:384
  76.4 1.8 %collective-permute-done.7.refs_1_ = bf16[2,2,128,128]{3,2,1,0:T(8,128)(2,1)S(1)} collective-permute-done((bf16[2,2,128,128]{3,2,1,0:T(8,128)(2,1)S(1)}, bf16[2,2,128,128]{3,2,1,0:T(8,128)(2,1)S(1)}, u32[]{:S(2)}, u32[]{:S(2)}) %collective-permute-start.7) | collective-permute-done | bytes 131104 | tf_op jit(solution)/shard_map/halos/ppermute | solution.py:384
  78.2 3.4 %collective-permute-start.8 = (bf16[2,7,128,128]{3,2,0,1:T(8,128)(2,1)S(1)}, bf16[2,7,128,128]{3,2,0,1:T(8,128)(2,1)S(1)}, u32[]{:S(2)}, u32[]{:S(2)}) collective-permute-start(bf16[2,7,128,128]{3,2,0,1:T(8,128)(2,1)S(1)} %pad_maximum_fusion.1), channel_id=1, source_target_pairs={{0,64},{8,72},{16,80},{24,88},{32,96},{40,104},{48,112},{56,120},{... | collective-permute-start | bytes 1376264 | tf_op jit(solution)/shard_map/halos/ppermute | solution.py:384
  81.6 2.5 %collective-permute-start.9 = (bf16[2,7,128,128]{3,2,1,0:T(8,128)(2,1)S(1)}, bf16[2,7,128,128]{3,2,1,0:T(8,128)(2,1)S(1)}, u32[]{:S(2)}, u32[]{:S(2)}) collective-permute-start(bf16[2,7,128,128]{3,2,1,0:T(8,128)(2,1)S(1)} %pad_maximum_fusion.2), channel_id=1, source_target_pairs={{64,0},{72,8},{80,16},{88,24},{96,32},{104,40},{112,48},{120,56},{... | collective-permute-start | bytes 1376264 | tf_op jit(solution)/shard_map/halos/ppermute | solution.py:384
  84.4 0.2 copy.55
  84.6 5.6 %collective-permute-done.8 = bf16[2,7,128,128]{3,2,0,1:T(8,128)(2,1)S(1)} collective-permute-done((bf16[2,7,128,128]{3,2,0,1:T(8,128)(2,1)S(1)}, bf16[2,7,128,128]{3,2,0,1:T(8,128)(2,1)S(1)}, u32[]{:S(2)}, u32[]{:S(2)}) %collective-permute-start.8) | collective-permute-done | bytes 458784 | tf_op jit(solution)/shard_map/halos/ppermute | solution.py:384
  90.3 3.1 %collective-permute-done.9.refs_3_ = bf16[2,7,128,128]{3,2,1,0:T(8,128)(2,1)S(1)} collective-permute-done((bf16[2,7,128,128]{3,2,1,0:T(8,128)(2,1)S(1)}, bf16[2,7,128,128]{3,2,1,0:T(8,128)(2,1)S(1)}, u32[]{:S(2)}, u32[]{:S(2)}) %collective-permute-start.9) | collective-permute-done | bytes 458784 | tf_op jit(solution)/shard_map/halos/ppermute | solution.py:384
  93.4 10.1 %attend.1 = (bf16[2,2,128,128]{3,2,1,0:T(8,128)(2,1)S(1)}, bf16[2,2,128,128]{3,2,1,0:T(8,128)(2,1)S(1)}, bf16[2,2,128,128]{3,2,1,0:T(8,128)(2,1)S(1)}, bf16[2,2,...) custom-call(s32[7]{0:T(128)S(1)} %stack.63.table, ...), custom_call_target="tpu_custom_call" | custom-call | flops 3000000000 | bytes 8000000 | tf_op jit(solution)/shard_map/attention/attend/pallas_call | solution.py:317
  103.5 3.1 %collective-permute-start.10 = (bf16[2,7,128,128]{3,2,1,0:T(8,128)(2,1)S(1)}, bf16[2,7,128,128]{3,2,1,0:T(8,128)(2,1)S(1)}, u32[]{:S(2)}, u32[]{:S(2)}) collective-permute-start(bf16[2,7,128,128]{3,2,1,0:T(8,128)(2,1)S(1)} %get-tuple-element.57), channel_id=1, source_target_pairs={{0,64},{8,72},{16,80},{24,88},{32,96},{40,104},{48,112},{56,120},{... | collective-permute-start | bytes 1376264 | tf_op jit(solution)/shard_map/terms/ppermute | solution.py:384
  106.7 2.8 %collective-permute-start.11 = (bf16[2,7,128,128]{3,2,1,0:T(8,128)(2,1)S(1)}, bf16[2,7,128,128]{3,2,1,0:T(8,128)(2,1)S(1)}, u32[]{:S(2)}, u32[]{:S(2)}) collective-permute-start(bf16[2,7,128,128]{3,2,1,0:T(8,128)(2,1)S(1)} %get-tuple-element.58), channel_id=1, source_target_pairs={{64,0},{72,8},{80,16},{88,24},{96,32},{104,40},{112,48},{120,56},{... | collective-permute-start | bytes 1376264 | tf_op jit(solution)/shard_map/terms/ppermute | solution.py:384
  109.4 2.2 %collective-permute-start.12 = (bf16[2,2,128,128]{3,2,1,0:T(8,128)(2,1)S(1)}, bf16[2,2,128,128]{3,2,1,0:T(8,128)(2,1)S(1)}, u32[]{:S(2)}, u32[]{:S(2)}) collective-permute-start(bf16[2,2,128,128]{3,2,1,0:T(8,128)(2,1)S(1)} %get-tuple-element.59), channel_id=1, source_target_pairs={{0,0},{8,56},{16,8},{24,32},{32,16},{40,40},{48,24},{56,48},{64,64... | collective-permute-start | bytes 393224 | tf_op jit(solution)/shard_map/terms/ppermute | solution.py:384
  111.7 3.5 %collective-permute-start.13 = (bf16[2,2,128,128]{3,2,1,0:T(8,128)(2,1)S(1)}, bf16[2,2,128,128]{3,2,1,0:T(8,128)(2,1)S(1)}, u32[]{:S(2)}, u32[]{:S(2)}) collective-permute-start(bf16[2,2,128,128]{3,2,1,0:T(8,128)(2,1)S(1)} %get-tuple-element.60), channel_id=1, source_target_pairs={{0,32},{8,24},{16,40},{24,0},{32,48},{40,8},{48,56},{56,16},{64,96... | collective-permute-start | bytes 393224 | tf_op jit(solution)/shard_map/terms/ppermute | solution.py:384
  115.2 6.6 %collective-permute-start.14 = (bf16[2,2,128,128]{3,2,1,0:T(8,128)(2,1)S(1)}, bf16[2,2,128,128]{3,2,1,0:T(8,128)(2,1)S(1)}, u32[]{:S(2)}, u32[]{:S(2)}) collective-permute-start(bf16[2,2,128,128]{3,2,1,0:T(8,128)(2,1)S(1)} %get-tuple-element.61), channel_id=1, source_target_pairs={{0,8},{8,32},{16,16},{24,40},{32,24},{40,48},{48,0},{56,56},{64,72... | collective-permute-start | bytes 393224 | tf_op jit(solution)/shard_map/terms/ppermute | solution.py:384
  121.9 2.8 %collective-permute-done.14.refs_2_ = bf16[2,2,128,128]{3,2,1,0:T(8,128)(2,1)S(1)} collective-permute-done((bf16[2,2,128,128]{3,2,1,0:T(8,128)(2,1)S(1)}, bf16[2,2,128,128]{3,2,1,0:T(8,128)(2,1)S(1)}, u32[]{:S(2)}, u32[]{:S(2)}) %collective-permute-start.14) | collective-permute-done | bytes 131104 | tf_op jit(solution)/shard_map/terms/ppermute | solution.py:384
  124.7 3.4 %collective-permute-start.15 = (bf16[2,2,128,128]{3,2,1,0:T(8,128)(2,1)S(1)}, bf16[2,2,128,128]{3,2,1,0:T(8,128)(2,1)S(1)}, u32[]{:S(2)}, u32[]{:S(2)}) collective-permute-start(bf16[2,2,128,128]{3,2,1,0:T(8,128)(2,1)S(1)} %get-tuple-element.68), channel_id=1, source_target_pairs={{0,8},{8,16},{16,24},{24,32},{32,40},{40,48},{48,56},{64,72},{72,8... | collective-permute-start | bytes 393224 | tf_op jit(solution)/shard_map/terms/ppermute | solution.py:384
  128.1 3.3 %collective-permute-start.16 = (bf16[2,2,128,128]{3,2,1,0:T(8,128)(2,1)S(1)}, bf16[2,2,128,128]{3,2,1,0:T(8,128)(2,1)S(1)}, u32[]{:S(2)}, u32[]{:S(2)}) collective-permute-start(bf16[2,2,128,128]{3,2,1,0:T(8,128)(2,1)S(1)} %get-tuple-element.69), channel_id=1, source_target_pairs={{8,0},{16,8},{24,16},{32,24},{40,32},{48,40},{56,48},{72,64},{80,7... | collective-permute-start | bytes 393224 | tf_op jit(solution)/shard_map/terms/ppermute | solution.py:384
  131.4 7.7 %collective-permute-start.18 = (bf16[2,128,128]{2,1,0:T(8,128)(2,1)S(1)}, bf16[2,128,128]{2,1,0:T(8,128)(2,1)S(1)}, u32[]{:S(2)}, u32[]{:S(2)}) collective-permute-start(bf16[2,128,128]{2,1,0:T(8,128)(2,1)S(1)} %get-tuple-element.71), channel_id=1, source_target_pairs={{0,16},{8,48},{16,24},{24,56},{32,0},{40,32},{48,8},{56,40},{64,80... | collective-permute-start | bytes 196616 | tf_op jit(solution)/shard_map/terms/ppermute | solution.py:384
  139.1 1.9 %collective-permute-start.19 = (bf16[2,128,128]{2,1,0:T(8,128)(2,1)S(1)}, bf16[2,128,128]{2,1,0:T(8,128)(2,1)S(1)}, u32[]{:S(2)}, u32[]{:S(2)}) collective-permute-start(bf16[2,128,128]{2,1,0:T(8,128)(2,1)S(1)} %get-tuple-element.72), channel_id=1, source_target_pairs={{0,48},{8,16},{16,56},{24,24},{32,32},{40,0},{48,40},{56,8},{64,11... | collective-permute-start | bytes 196616 | tf_op jit(solution)/shard_map/terms/ppermute | solution.py:384
  141.1 0.4 collective-permute-done.18.refs_4_
  141.5 6.7 %collective-permute-done.19.refs_5_ = bf16[2,128,128]{2,1,0:T(8,128)(2,1)S(1)} collective-permute-done((bf16[2,128,128]{2,1,0:T(8,128)(2,1)S(1)}, bf16[2,128,128]{2,1,0:T(8,128)(2,1)S(1)}, u32[]{:S(2)}, u32[]{:S(2)}) %collective-permute-start.19) | collective-permute-done | bytes 65568 | tf_op jit(solution)/shard_map/terms/ppermute | solution.py:384
  148.1 0.7 combine.1
  149.0 4.7 %collective-permute-start.20 = (bf16[2,2,128,128]{3,2,1,0:T(8,128)(2,1)S(1)}, bf16[2,2,128,128]{3,2,1,0:T(8,128)(2,1)S(1)}, u32[]{:S(2)}, u32[]{:S(2)}) collective-permute-start(bf16[2,2,128,128]{3,2,1,0:T(8,128)(2,1)S(1)} %get-tuple-element.78), channel_id=1, source_target_pairs={{0,0},{8,56},{16,8},{24,32},{32,16},{40,40},{48,24},{56,48},{64,64... | collective-permute-start | bytes 393224 | tf_op jit(solution)/shard_map/key_terms_home/ppermute | solution.py:384
  153.7 2.4 %collective-permute-start.21 = (bf16[2,2,128,128]{3,2,1,0:T(8,128)(2,1)S(1)}, bf16[2,2,128,128]{3,2,1,0:T(8,128)(2,1)S(1)}, u32[]{:S(2)}, u32[]{:S(2)}) collective-permute-start(bf16[2,2,128,128]{3,2,1,0:T(8,128)(2,1)S(1)} %get-tuple-element.79), channel_id=1, source_target_pairs={{0,32},{8,24},{16,40},{24,0},{32,48},{40,8},{48,56},{56,16},{64,96... | collective-permute-start | bytes 393224 | tf_op jit(solution)/shard_map/key_terms_home/ppermute | solution.py:384
  156.2 6.9 %collective-permute-start.22 = (bf16[2,2,128,128]{3,2,1,0:T(8,128)(2,1)S(1)}, bf16[2,2,128,128]{3,2,1,0:T(8,128)(2,1)S(1)}, u32[]{:S(2)}, u32[]{:S(2)}) collective-permute-start(bf16[2,2,128,128]{3,2,1,0:T(8,128)(2,1)S(1)} %get-tuple-element.80), channel_id=1, source_target_pairs={{0,8},{8,32},{16,16},{24,40},{32,24},{40,48},{48,0},{56,56},{64,72... | collective-permute-start | bytes 393224 | tf_op jit(solution)/shard_map/key_terms_home/ppermute | solution.py:384
  163.2 1.9 %collective-permute-start.25 = (bf16[2,128,128]{2,1,0:T(8,128)(2,1)S(1)}, bf16[2,128,128]{2,1,0:T(8,128)(2,1)S(1)}, u32[]{:S(2)}, u32[]{:S(2)}) collective-permute-start(bf16[2,128,128]{2,1,0:T(8,128)(2,1)S(1)} %get-tuple-element.83), channel_id=1, source_target_pairs={{0,48},{8,16},{16,56},{24,24},{32,32},{40,0},{48,40},{56,8},{64,11... | collective-permute-start | bytes 196616 | tf_op jit(solution)/shard_map/key_terms_home/ppermute | solution.py:384
  165.1 6.3 %collective-permute-done.25.refs_11_ = bf16[2,128,128]{2,1,0:T(8,128)(2,1)S(1)} collective-permute-done((bf16[2,128,128]{2,1,0:T(8,128)(2,1)S(1)}, bf16[2,128,128]{2,1,0:T(8,128)(2,1)S(1)}, u32[]{:S(2)}, u32[]{:S(2)}) %collective-permute-start.25) | collective-permute-done | bytes 65568 | tf_op jit(solution)/shard_map/key_terms_home/ppermute | solution.py:384
  171.5 2.2 %gather.1 = (bf16[256,640]{1,0:T(8,128)(2,1)}, bf16[256,640]{1,0:T(8,128)(2,1)}, bf16[256,640]{1,0:T(8,128)(2,1)}, bf16[256,640]{1,0:T(8,128)(2,1)}) custom-call(s32[7]{0:T(128)S(1)} %stack.55.table, bf16[2,2,128,128]{3,2,1,0:T(8,128)(2,1)S(1)} %collective-permute-done.12.refs_0_, bf16[2,2,128,128]{3,2,1,0:T(8,128)(2,1)S(1)} %collective-permute-done.13.refs_1_, ...), custom_call_target="tpu_custom_call" | custom-call | tf_op jit(solution)/shard_map/settle/gather/pallas_call | solution.py:139
  (47 shorter events, 1.7 us)
Async XLA Ops:
  0.6 2.5 %copy-start.1 = (bf16[1,8,4,5120]{3,2,1,0:T(4,128)(2,1)S(1)}, bf16[1,8,4,5120]{3,2,1,0:T(4,128)(2,1)}, u32[]{:S(2)}) copy-start(bf16[1,8,4,5120]{3,2,1,0:T(4,128)(2,1)} %param.6) | copy-start | bytes 983044
  3.6 5.4 %copy-start = (bf16[256,640]{1,0:T(8,128)(2,1)S(1)}, bf16[256,640]{1,0:T(8,128)(2,1)}, u32[]{:S(2)}) copy-start(bf16[256,640]{1,0:T(8,128)(2,1)} %upstream.1) | copy-start | bytes 983044
  4.6 25.1 %all-to-all-start = ((bf16[8,3,5,32,128]{4,3,2,1,0:T(8,128)(2,1)}), bf16[8,3,5,32,128]{4,3,2,1,0:T(8,128)(2,1)S(1)}, u32[]{:S(2)}, u32[]{:S(2)}) async-start(bf16[8,3,5,32,128]{4,3,2,1,0:T(8,128)(2,1)} %copy.50), calls=%async_computation | async-start | bytes 1966080 | tf_op jit(solution)/shard_map/heads/all_to_all | solution.py:414
  9.9 19.7 %collective-permute-start.4 = (bf16[128,128]{1,0:T(8,128)(2,1)S(1)}, bf16[128,128]{1,0:T(8,128)(2,1)S(1)}, u32[]{:S(2)}, u32[]{:S(2)}) collective-permute-start(bf16[128,128]{1,0:T(8,128)(2,1)S(1)} %get-tuple-element.48), channel_id=1, source_target_pairs={{16,0},{48,8},{24,16},{56,24},{0,32},{32,40},{8,48},{40,56},{80,64... | collective-permute-start | bytes 98312 | tf_op jit(solution)/shard_map/upstream_to_units/ppermute | solution.py:384
  15.8 14.9 %collective-permute-start.5 = (bf16[128,128]{1,0:T(8,128)(2,1)S(1)}, bf16[128,128]{1,0:T(8,128)(2,1)S(1)}, u32[]{:S(2)}, u32[]{:S(2)}) collective-permute-start(bf16[128,128]{1,0:T(8,128)(2,1)S(1)} %get-tuple-element.49), channel_id=1, source_target_pairs={{48,0},{16,8},{56,16},{24,24},{32,32},{0,40},{40,48},{8,56},{112,6... | collective-permute-start | bytes 98312 | tf_op jit(solution)/shard_map/upstream_to_units/ppermute | solution.py:384
  18.7 12.1 %collective-permute-start = (bf16[2,128,128]{2,1,0:T(8,128)(2,1)S(1)}, bf16[2,128,128]{2,1,0:T(8,128)(2,1)S(1)}, u32[]{:S(2)}, u32[]{:S(2)}) collective-permute-start(bf16[2,128,128]{2,1,0:T(8,128)(2,1)S(1)} %get-tuple-element.44), channel_id=1, source_target_pairs={{0,0},{56,8},{8,16},{32,24},{16,32},{40,40},{24,48},{48,56},{64,64... | collective-permute-start | bytes 196616 | tf_op jit(solution)/shard_map/upstream_to_units/ppermute | solution.py:384
  21.7 10.0 %collective-permute-start.1 = (bf16[2,128,128]{2,1,0:T(8,128)(2,1)S(1)}, bf16[2,128,128]{2,1,0:T(8,128)(2,1)S(1)}, u32[]{:S(2)}, u32[]{:S(2)}) collective-permute-start(bf16[2,128,128]{2,1,0:T(8,128)(2,1)S(1)} %get-tuple-element.45), channel_id=1, source_target_pairs={{32,0},{24,8},{40,16},{0,24},{48,32},{8,40},{56,48},{16,56},{96,64... | collective-permute-start | bytes 196616 | tf_op jit(solution)/shard_map/upstream_to_units/ppermute | solution.py:384
  21.8 10.5 %collective-permute-start.2 = (bf16[2,128,128]{2,1,0:T(8,128)(2,1)S(1)}, bf16[2,128,128]{2,1,0:T(8,128)(2,1)S(1)}, u32[]{:S(2)}, u32[]{:S(2)}) collective-permute-start(bf16[2,128,128]{2,1,0:T(8,128)(2,1)S(1)} %get-tuple-element.46), channel_id=1, source_target_pairs={{8,0},{32,8},{16,16},{40,24},{24,32},{48,40},{0,48},{56,56},{72,64... | collective-permute-start | bytes 196616 | tf_op jit(solution)/shard_map/upstream_to_units/ppermute | solution.py:384
  29.6 4.9 %collective-permute-start.3 = (bf16[2,128,128]{2,1,0:T(8,128)(2,1)S(1)}, bf16[2,128,128]{2,1,0:T(8,128)(2,1)S(1)}, u32[]{:S(2)}, u32[]{:S(2)}) collective-permute-start(bf16[2,128,128]{2,1,0:T(8,128)(2,1)S(1)} %get-tuple-element.47), channel_id=1, source_target_pairs={{40,0},{0,8},{48,16},{8,24},{56,32},{16,40},{32,48},{24,56},{104,6... | collective-permute-start | bytes 196616 | tf_op jit(solution)/shard_map/upstream_to_units/ppermute | solution.py:384
  34.5 27.2 %all-to-all-start.2 = ((bf16[32,5,2,8,128]{4,3,2,1,0:T(8,128)(2,1)}), bf16[32,5,2,8,128]{4,3,2,1,0:T(8,128)(2,1)S(1)}, u32[]{:S(2)}, u32[]{:S(2)}) async-start(bf16[32,5,2,8,128]{4,3,2,1,0:T(8,128)(2,1)} %bitcast.28), calls=%async_computation.2 | async-start | bytes 1310720 | tf_op jit(solution)/shard_map/key_value_tiles/all_to_all | solution.py:417
  61.6 22.7 %all-to-all-start.1 = ((bf16[32,5,1,8,128]{4,3,1,2,0:T(8,128)(2,1)}), bf16[32,5,1,8,128]{4,3,1,2,0:T(8,128)(2,1)S(1)}, u32[]{:S(2)}, u32[]{:S(2)}) async-start(bf16[32,5,1,8,128]{4,3,1,2,0:T(8,128)(2,1)} %bitcast.22), calls=%async_computation.1 | async-start | bytes 655360 | tf_op jit(solution)/shard_map/query_tiles/all_to_all | solution.py:419
  67.9 8.5 %collective-permute-start.6 = (bf16[2,2,128,128]{3,2,0,1:T(8,128)(2,1)S(1)}, bf16[2,2,128,128]{3,2,0,1:T(8,128)(2,1)S(1)}, u32[]{:S(2)}, u32[]{:S(2)}) collective-permute-start(bf16[2,2,128,128]{3,2,0,1:T(8,128)(2,1)S(1)} %bitcast.66), channel_id=1, source_target_pairs={{0,8},{8,16},{16,24},{24,32},{32,40},{40,48},{48,56},{64,72},{72,8... | collective-permute-start | bytes 393224 | tf_op jit(solution)/shard_map/halos/ppermute | solution.py:384
  71.3 6.9 %collective-permute-start.7 = (bf16[2,2,128,128]{3,2,1,0:T(8,128)(2,1)S(1)}, bf16[2,2,128,128]{3,2,1,0:T(8,128)(2,1)S(1)}, u32[]{:S(2)}, u32[]{:S(2)}) collective-permute-start(bf16[2,2,128,128]{3,2,1,0:T(8,128)(2,1)S(1)} %get-tuple-element.86), channel_id=1, source_target_pairs={{8,0},{16,8},{24,16},{32,24},{40,32},{48,40},{56,48},{72,64},{80,7... | collective-permute-start | bytes 393224 | tf_op jit(solution)/shard_map/halos/ppermute | solution.py:384
  78.2 12.1 %collective-permute-start.8 = (bf16[2,7,128,128]{3,2,0,1:T(8,128)(2,1)S(1)}, bf16[2,7,128,128]{3,2,0,1:T(8,128)(2,1)S(1)}, u32[]{:S(2)}, u32[]{:S(2)}) collective-permute-start(bf16[2,7,128,128]{3,2,0,1:T(8,128)(2,1)S(1)} %pad_maximum_fusion.1), channel_id=1, source_target_pairs={{0,64},{8,72},{16,80},{24,88},{32,96},{40,104},{48,112},{56,120},{... | collective-permute-start | bytes 1376264 | tf_op jit(solution)/shard_map/halos/ppermute | solution.py:384
  81.6 11.8 %collective-permute-start.9 = (bf16[2,7,128,128]{3,2,1,0:T(8,128)(2,1)S(1)}, bf16[2,7,128,128]{3,2,1,0:T(8,128)(2,1)S(1)}, u32[]{:S(2)}, u32[]{:S(2)}) collective-permute-start(bf16[2,7,128,128]{3,2,1,0:T(8,128)(2,1)S(1)} %pad_maximum_fusion.2), channel_id=1, source_target_pairs={{64,0},{72,8},{80,16},{88,24},{96,32},{104,40},{112,48},{120,56},{... | collective-permute-start | bytes 1376264 | tf_op jit(solution)/shard_map/halos/ppermute | solution.py:384
  103.5 21.1 %collective-permute-start.10 = (bf16[2,7,128,128]{3,2,1,0:T(8,128)(2,1)S(1)}, bf16[2,7,128,128]{3,2,1,0:T(8,128)(2,1)S(1)}, u32[]{:S(2)}, u32[]{:S(2)}) collective-permute-start(bf16[2,7,128,128]{3,2,1,0:T(8,128)(2,1)S(1)} %get-tuple-element.57), channel_id=1, source_target_pairs={{0,64},{8,72},{16,80},{24,88},{32,96},{40,104},{48,112},{56,120},{... | collective-permute-start | bytes 1376264 | tf_op jit(solution)/shard_map/terms/ppermute | solution.py:384
  106.7 18.0 %collective-permute-start.11 = (bf16[2,7,128,128]{3,2,1,0:T(8,128)(2,1)S(1)}, bf16[2,7,128,128]{3,2,1,0:T(8,128)(2,1)S(1)}, u32[]{:S(2)}, u32[]{:S(2)}) collective-permute-start(bf16[2,7,128,128]{3,2,1,0:T(8,128)(2,1)S(1)} %get-tuple-element.58), channel_id=1, source_target_pairs={{64,0},{72,8},{80,16},{88,24},{96,32},{104,40},{112,48},{120,56},{... | collective-permute-start | bytes 1376264 | tf_op jit(solution)/shard_map/terms/ppermute | solution.py:384
  109.4 12.3 %collective-permute-start.12 = (bf16[2,2,128,128]{3,2,1,0:T(8,128)(2,1)S(1)}, bf16[2,2,128,128]{3,2,1,0:T(8,128)(2,1)S(1)}, u32[]{:S(2)}, u32[]{:S(2)}) collective-permute-start(bf16[2,2,128,128]{3,2,1,0:T(8,128)(2,1)S(1)} %get-tuple-element.59), channel_id=1, source_target_pairs={{0,0},{8,56},{16,8},{24,32},{32,16},{40,40},{48,24},{56,48},{64,64... | collective-permute-start | bytes 393224 | tf_op jit(solution)/shard_map/terms/ppermute | solution.py:384
  111.7 10.2 %collective-permute-start.13 = (bf16[2,2,128,128]{3,2,1,0:T(8,128)(2,1)S(1)}, bf16[2,2,128,128]{3,2,1,0:T(8,128)(2,1)S(1)}, u32[]{:S(2)}, u32[]{:S(2)}) collective-permute-start(bf16[2,2,128,128]{3,2,1,0:T(8,128)(2,1)S(1)} %get-tuple-element.60), channel_id=1, source_target_pairs={{0,32},{8,24},{16,40},{24,0},{32,48},{40,8},{48,56},{56,16},{64,96... | collective-permute-start | bytes 393224 | tf_op jit(solution)/shard_map/terms/ppermute | solution.py:384
  115.2 9.5 %collective-permute-start.14 = (bf16[2,2,128,128]{3,2,1,0:T(8,128)(2,1)S(1)}, bf16[2,2,128,128]{3,2,1,0:T(8,128)(2,1)S(1)}, u32[]{:S(2)}, u32[]{:S(2)}) collective-permute-start(bf16[2,2,128,128]{3,2,1,0:T(8,128)(2,1)S(1)} %get-tuple-element.61), channel_id=1, source_target_pairs={{0,8},{8,32},{16,16},{24,40},{32,24},{40,48},{48,0},{56,56},{64,72... | collective-permute-start | bytes 393224 | tf_op jit(solution)/shard_map/terms/ppermute | solution.py:384
  121.7 26.4 %collective-permute-start.17 = (bf16[2,2,128,128]{3,2,1,0:T(8,128)(2,1)S(1)}, bf16[2,2,128,128]{3,2,1,0:T(8,128)(2,1)S(1)}, u32[]{:S(2)}, u32[]{:S(2)}) collective-permute-start(bf16[2,2,128,128]{3,2,1,0:T(8,128)(2,1)S(1)} %get-tuple-element.70), channel_id=1, source_target_pairs={{0,40},{8,0},{16,48},{24,8},{32,56},{40,16},{48,32},{56,24},{64,10... | collective-permute-start | bytes 393224 | tf_op jit(solution)/shard_map/terms/ppermute | solution.py:384
  124.7 23.4 %collective-permute-start.15 = (bf16[2,2,128,128]{3,2,1,0:T(8,128)(2,1)S(1)}, bf16[2,2,128,128]{3,2,1,0:T(8,128)(2,1)S(1)}, u32[]{:S(2)}, u32[]{:S(2)}) collective-permute-start(bf16[2,2,128,128]{3,2,1,0:T(8,128)(2,1)S(1)} %get-tuple-element.68), channel_id=1, source_target_pairs={{0,8},{8,16},{16,24},{24,32},{32,40},{40,48},{48,56},{64,72},{72,8... | collective-permute-start | bytes 393224 | tf_op jit(solution)/shard_map/terms/ppermute | solution.py:384
  128.1 20.0 %collective-permute-start.16 = (bf16[2,2,128,128]{3,2,1,0:T(8,128)(2,1)S(1)}, bf16[2,2,128,128]{3,2,1,0:T(8,128)(2,1)S(1)}, u32[]{:S(2)}, u32[]{:S(2)}) collective-permute-start(bf16[2,2,128,128]{3,2,1,0:T(8,128)(2,1)S(1)} %get-tuple-element.69), channel_id=1, source_target_pairs={{8,0},{16,8},{24,16},{32,24},{40,32},{48,40},{56,48},{72,64},{80,7... | collective-permute-start | bytes 393224 | tf_op jit(solution)/shard_map/terms/ppermute | solution.py:384
  131.4 10.1 %collective-permute-start.18 = (bf16[2,128,128]{2,1,0:T(8,128)(2,1)S(1)}, bf16[2,128,128]{2,1,0:T(8,128)(2,1)S(1)}, u32[]{:S(2)}, u32[]{:S(2)}) collective-permute-start(bf16[2,128,128]{2,1,0:T(8,128)(2,1)S(1)} %get-tuple-element.71), channel_id=1, source_target_pairs={{0,16},{8,48},{16,24},{24,56},{32,0},{40,32},{48,8},{56,40},{64,80... | collective-permute-start | bytes 196616 | tf_op jit(solution)/shard_map/terms/ppermute | solution.py:384
  139.1 9.0 %collective-permute-start.19 = (bf16[2,128,128]{2,1,0:T(8,128)(2,1)S(1)}, bf16[2,128,128]{2,1,0:T(8,128)(2,1)S(1)}, u32[]{:S(2)}, u32[]{:S(2)}) collective-permute-start(bf16[2,128,128]{2,1,0:T(8,128)(2,1)S(1)} %get-tuple-element.72), channel_id=1, source_target_pairs={{0,48},{8,16},{16,56},{24,24},{32,32},{40,0},{48,40},{56,8},{64,11... | collective-permute-start | bytes 196616 | tf_op jit(solution)/shard_map/terms/ppermute | solution.py:384
  148.9 14.3 %collective-permute-start.24 = (bf16[2,128,128]{2,1,0:T(8,128)(2,1)S(1)}, bf16[2,128,128]{2,1,0:T(8,128)(2,1)S(1)}, u32[]{:S(2)}, u32[]{:S(2)}) collective-permute-start(bf16[2,128,128]{2,1,0:T(8,128)(2,1)S(1)} %get-tuple-element.82), channel_id=1, source_target_pairs={{0,16},{8,48},{16,24},{24,56},{32,0},{40,32},{48,8},{56,40},{64,80... | collective-permute-start | bytes 196616 | tf_op jit(solution)/shard_map/key_terms_home/ppermute | solution.py:384
  149.0 22.5 %collective-permute-start.20 = (bf16[2,2,128,128]{3,2,1,0:T(8,128)(2,1)S(1)}, bf16[2,2,128,128]{3,2,1,0:T(8,128)(2,1)S(1)}, u32[]{:S(2)}, u32[]{:S(2)}) collective-permute-start(bf16[2,2,128,128]{3,2,1,0:T(8,128)(2,1)S(1)} %get-tuple-element.78), channel_id=1, source_target_pairs={{0,0},{8,56},{16,8},{24,32},{32,16},{40,40},{48,24},{56,48},{64,64... | collective-permute-start | bytes 393224 | tf_op jit(solution)/shard_map/key_terms_home/ppermute | solution.py:384
  153.7 17.7 %collective-permute-start.21 = (bf16[2,2,128,128]{3,2,1,0:T(8,128)(2,1)S(1)}, bf16[2,2,128,128]{3,2,1,0:T(8,128)(2,1)S(1)}, u32[]{:S(2)}, u32[]{:S(2)}) collective-permute-start(bf16[2,2,128,128]{3,2,1,0:T(8,128)(2,1)S(1)} %get-tuple-element.79), channel_id=1, source_target_pairs={{0,32},{8,24},{16,40},{24,0},{32,48},{40,8},{48,56},{56,16},{64,96... | collective-permute-start | bytes 393224 | tf_op jit(solution)/shard_map/key_terms_home/ppermute | solution.py:384
  156.2 15.3 %collective-permute-start.22 = (bf16[2,2,128,128]{3,2,1,0:T(8,128)(2,1)S(1)}, bf16[2,2,128,128]{3,2,1,0:T(8,128)(2,1)S(1)}, u32[]{:S(2)}, u32[]{:S(2)}) collective-permute-start(bf16[2,2,128,128]{3,2,1,0:T(8,128)(2,1)S(1)} %get-tuple-element.80), channel_id=1, source_target_pairs={{0,8},{8,32},{16,16},{24,40},{32,24},{40,48},{48,0},{56,56},{64,72... | collective-permute-start | bytes 393224 | tf_op jit(solution)/shard_map/key_terms_home/ppermute | solution.py:384
  163.1 8.4 %collective-permute-start.23 = (bf16[2,2,128,128]{3,2,1,0:T(8,128)(2,1)S(1)}, bf16[2,2,128,128]{3,2,1,0:T(8,128)(2,1)S(1)}, u32[]{:S(2)}, u32[]{:S(2)}) collective-permute-start(bf16[2,2,128,128]{3,2,1,0:T(8,128)(2,1)S(1)} %get-tuple-element.81), channel_id=1, source_target_pairs={{0,40},{8,0},{16,48},{24,8},{32,56},{40,16},{48,32},{56,24},{64,10... | collective-permute-start | bytes 393224 | tf_op jit(solution)/shard_map/key_terms_home/ppermute | solution.py:384
  163.2 8.3 %collective-permute-start.25 = (bf16[2,128,128]{2,1,0:T(8,128)(2,1)S(1)}, bf16[2,128,128]{2,1,0:T(8,128)(2,1)S(1)}, u32[]{:S(2)}, u32[]{:S(2)}) collective-permute-start(bf16[2,128,128]{2,1,0:T(8,128)(2,1)S(1)} %get-tuple-element.83), channel_id=1, source_target_pairs={{0,48},{8,16},{16,56},{24,24},{32,32},{40,0},{48,40},{56,8},{64,11... | collective-permute-start | bytes 196616 | tf_op jit(solution)/shard_map/key_terms_home/ppermute | solution.py:384

commit v2 on v1

--- a/solution.py
+++ b/solution.py
@@ -55,27 +55,48 @@
 
 ROW_STEPS = ((1, 0), (-1, 0))
 COLUMN_STEPS = ((0, 1), (0, -1))
+EARLY = 3
 OWNER_STEPS = tuple((which, turn) for which in range(3) for turn in range(2))
+
+
+def nt(one, two):
+    return lax.dot_general(one, two, (((1,), (1,)), ((), ())), preferred_element_type=WIDE)
+
+
+def nn(one, two):
+    return jnp.dot(one, two, preferred_element_type=WIDE)
 
 
 def whole(count):
     return [pl.BlockSpec(memory_space=pltpu.VMEM)] * count
 
 
-def owner_table():
-    slot = lax.axis_index("tile") % SLOTS
-    row, pair = slot // 4, slot % 4
-    heads = []
-    for which, turn in OWNER_STEPS:
-        odd = (row + turn) % 2
-        if which == 2:
-            unit = 10 * ((pair + 2) % 4) + 4
-        else:
-            even_unit = 10 * ((pair - which + 4) % 4) + 2 * which
-            odd_unit = 10 * ((pair - 3 - which + 8) % 4) + 6 + 2 * which
-            unit = jnp.where(odd == 1, odd_unit, even_unit)
-        heads.append(unit // 8)
-    return jnp.stack(heads + [row]).astype(jnp.int32)
+def owner_rows():
+    rows = []
+    for slot in range(SLOTS):
+        row, pair = slot // 4, slot % 4
+        heads = []
+        for which, turn in OWNER_STEPS:
+            if which == 2:
+                unit = 10 * ((pair + 2) % 4) + 4
+            elif (row + turn) % 2:
+                unit = 10 * ((pair - 3 - which) % 4) + 6 + 2 * which
+            else:
+                unit = 10 * ((pair - which) % 4) + 2 * which
+            heads.append(unit // 8)
+        rows.append(heads + [row])
+    return rows
+
+
+def place_table():
+    owners = owner_rows()
+    rows = [
+        owners[slot] + [strip, slot % 2] + [(5 * slot + at) % 8 for at in range(5)]
+        for strip in range(STRIPS)
+        for slot in range(SLOTS)
+    ]
+    every = jnp.asarray(np.array(rows, np.int32))
+    return lax.dynamic_index_in_dim(every, lax.axis_index("tile"), 0, keepdims=False)
 
 
 def spread_kernel(table, upstream, *outs):
@@ -110,94 +131,74 @@
 
 
 def gather_kernel(table, *refs):
-    first, second, outs = refs[:6], refs[6:12], refs[12:16]
-    single = refs[16]
+    received, outs, single = refs[:6], refs[6:10], refs[10]
     line = lax.broadcasted_iota(jnp.int32, (2 * TILE, 2 * TILE), 0)
     col = lax.broadcasted_iota(jnp.int32, (2 * TILE, 2 * TILE), 1)
     source = ((line >> 2) & 1) * TILE + (line >> 3) * 4 + (line & 3)
     order = (col == source).astype(LOW)
-    for group, received in enumerate((first, second)):
-        for kind in range(2):
-            out = outs[2 * group + kind]
-            for at in range(4):
-                head = pl.multiple_of(table[at] * HEAD_DIM, HEAD_DIM)
-                tiles = received[at][kind].reshape(2 * TILE, HEAD_DIM)
-                out[:, pl.ds(head, HEAD_DIM)] = jnp.dot(
-                    order, tiles, preferred_element_type=WIDE
-                ).astype(LOW)
-            flip = table[6] == 1
-            one, two = received[4][kind], received[5][kind]
-            single[:TILE] = jnp.where(flip, two, one)
-            single[TILE:] = jnp.where(flip, one, two)
-            head = pl.multiple_of(table[4] * HEAD_DIM, HEAD_DIM)
-            out[:, pl.ds(head, HEAD_DIM)] = jnp.dot(
-                order, single[...], preferred_element_type=WIDE
-            ).astype(LOW)
-
-
-def gather(table, first, second):
+    for kind, out in enumerate(outs):
+        for at in range(4):
+            head = pl.multiple_of(table[at] * HEAD_DIM, HEAD_DIM)
+            tiles = received[at][kind].reshape(2 * TILE, HEAD_DIM)
+            out[:, pl.ds(head, HEAD_DIM)] = nn(order, tiles).astype(LOW)
+        flip = table[6] == 1
+        one, two = received[4][kind], received[5][kind]
+        single[:TILE] = jnp.where(flip, two, one)
+        single[TILE:] = jnp.where(flip, one, two)
+        head = pl.multiple_of(table[4] * HEAD_DIM, HEAD_DIM)
+        out[:, pl.ds(head, HEAD_DIM)] = nn(order, single[...]).astype(LOW)
+
+
+def gather(table, received):
     return pl.pallas_call(
         gather_kernel,
         out_shape=[jax.ShapeDtypeStruct((2 * TILE, HEADS_HERE * HEAD_DIM), LOW)] * 4,
-        in_specs=[pl.BlockSpec(memory_space=pltpu.SMEM)] + whole(12),
+        in_specs=[pl.BlockSpec(memory_space=pltpu.SMEM)] + whole(6),
         out_specs=whole(4),
         scratch_shapes=[pltpu.VMEM((2 * TILE, HEAD_DIM), LOW)],
         compiler_params=pltpu.CompilerParams(vmem_limit_bytes=16 << 20),
         name="gather",
-    )(table, *first, *second)
-
-
-def unit_table():
-    place = lax.axis_index("tile")
-    strip, slot = place // SLOTS, place % SLOTS
-    cols = [(5 * slot + at) % 8 for at in range(5)]
-    return jnp.stack([strip, slot % 2] + cols).astype(jnp.int32)
-
-
-def nt(one, two):
-    return lax.dot_general(one, two, (((1,), (1,)), ((), ())), preferred_element_type=WIDE)
-
-
-def nn(one, two):
-    return jnp.dot(one, two, preferred_element_type=WIDE)
-
-
-def fill_outs(odd, held, outs):
-    for at, (which, turn) in enumerate(OWNER_STEPS):
-        row = (turn + odd) % 2
-        for kind in range(2):
-            if which == 2:
-                outs[at][kind] = held[kind, row, 4 - 4 * odd]
-            else:
-                for part in range(2):
-                    outs[at][kind, part] = held[kind, row, odd + 2 * which + part]
-
-
-def owner_shapes():
-    return [
-        jax.ShapeDtypeStruct((2, TILE, HEAD_DIM) if which == 2 else (2, 2, TILE, HEAD_DIM), LOW)
-        for which, _ in OWNER_STEPS
-    ]
-
-
-def attend_kernel(table, own, near, *refs):
-    halos, grads = refs[:4], refs[4:10]
-    outs, terms, edges = refs[10:16], refs[16], refs[17:19]
-    pair, turned, grad, total, held = refs[19:]
-    strip, odd = table[0], table[1]
+    )(table, *received)
+
+
+def deal_kernel(swapped, out):
+    for slot in range(SLOTS):
+        for at in range(7):
+            unit = min(max(5 * slot + at - 1, 0), 39)
+            head, column = unit // 8, unit % 8
+            for kind in range(3):
+                if kind == 0 and not 1 <= at <= 5:
+                    continue
+                place = at - 1 if kind == 0 else 7 * kind - 2 + at
+                lines = swapped[column, kind, head].reshape(STRIPS, 8, HEAD_DIM)
+                for strip in range(STRIPS):
+                    out[strip * SLOTS + slot, place] = lines[strip]
+
+
+def deal(swapped):
+    return pl.pallas_call(
+        deal_kernel,
+        out_shape=jax.ShapeDtypeStruct((STRIPS * SLOTS, 19, 8, HEAD_DIM), LOW),
+        in_specs=whole(1),
+        out_specs=whole(1)[0],
+        compiler_params=pltpu.CompilerParams(vmem_limit_bytes=16 << 20),
+        name="deal",
+    )(swapped)
+
+
+def attend_kernel(table, own, above, below, *refs):
+    grads, held, terms, edges = refs[:6], refs[6], refs[7], refs[8:10]
+    pair, turned, grad, total = refs[10:]
+    strip, odd = table[7], table[8]
     scaling = HEAD_DIM**-0.5
     rate = scaling * math.log2(math.e)
 
     for kind in range(2):
-        for at in range(5):
+        for at in range(7):
             for row in range(2):
-                pair[kind, at + 1, row] = near[kind, row, at]
-        for row in range(2):
-            pair[kind, 0, row] = halos[0][kind, row]
-            pair[kind, 6, row] = halos[1][kind, row]
-        for at in range(7):
-            pair[kind, at, 2] = halos[2][kind, at]
-            pair[kind, at, 3] = halos[3][kind, at]
+                pair[kind, at, row] = own[row, 5 + 7 * kind + at]
+            pair[kind, at, 2] = above[7 * kind + at]
+            pair[kind, at, 3] = below[7 * kind + at]
     for kind in range(2):
         for at in range(7):
             for row in range(4):
@@ -212,7 +213,7 @@
     total[...] = jnp.zeros_like(total)
 
     def one_unit(unit, carry):
-        column = table[2 + unit]
+        column = table[9 + unit]
         queries = [own[row, unit] for row in range(2)]
         both = jnp.concatenate(queries, axis=0)
         ups = [grad[row, unit] for row in range(2)]
@@ -301,7 +302,6 @@
         return carry
 
     lax.fori_loop(0, 5, one_unit, 0)
-    fill_outs(odd, held, outs)
     for kind, factor in ((0, scaling), (1, 1.0)):
         for at in range(7):
             for row in range(2):
@@ -313,27 +313,29 @@
     return [jax.ShapeDtypeStruct((2, 2, TILE, HEAD_DIM), LOW)] * 2
 
 
-def attend(table, own, pair, halos, grads):
+def attend(table, own, halos, grads):
     return pl.pallas_call(
         attend_kernel,
-        out_shape=owner_shapes()
-        + [jax.ShapeDtypeStruct((2, 2, 7, TILE, HEAD_DIM), WIDE)]
-        + [jax.ShapeDtypeStruct((2, 7, TILE, HEAD_DIM), LOW)] * 2,
-        in_specs=[pl.BlockSpec(memory_space=pltpu.SMEM)] + whole(12),
-        out_specs=whole(9),
+        out_shape=[
+            jax.ShapeDtypeStruct((2, 2, 5, TILE, HEAD_DIM), LOW),
+            jax.ShapeDtypeStruct((2, 2, 7, TILE, HEAD_DIM), WIDE),
+            jax.ShapeDtypeStruct((2, 7, TILE, HEAD_DIM), LOW),
+            jax.ShapeDtypeStruct((2, 7, TILE, HEAD_DIM), LOW),
+        ],
+        in_specs=[pl.BlockSpec(memory_space=pltpu.SMEM)] + whole(9),
+        out_specs=whole(4),
         scratch_shapes=[
             pltpu.VMEM((2, 7, 4, TILE, HEAD_DIM), LOW),
             pltpu.VMEM((2, 7, 4, HEAD_DIM, TILE), LOW),
             pltpu.VMEM((2, 5, TILE, HEAD_DIM), LOW),
             pltpu.VMEM((2, 7, 4, TILE, HEAD_DIM), WIDE),
-            pltpu.VMEM((2, 2, 5, TILE, HEAD_DIM), LOW),
         ],
         compiler_params=pltpu.CompilerParams(vmem_limit_bytes=40 << 20),
         cost_estimate=pl.CostEstimate(
             flops=3_000_000_000, bytes_accessed=8_000_000, transcendentals=1_500_000
         ),
         name="attend",
-    )(table, own, pair, *halos, *grads)
+    )(table, own, *halos, *grads)
 
 
 def rims_kernel(terms, above, below, right, left):
@@ -354,8 +356,9 @@
     )(terms, *edges)
 
 
-def combine_kernel(table, terms, *refs):
+def combine_kernel(table, first, terms, *refs):
     edges, columns, outs, held = refs[:2], refs[2:4], refs[4:10], refs[10]
+    odd = table[8]
     for kind in range(2):
         for row in range(2):
             for at in range(5):
@@ -365,19 +368,31 @@
                 if at == 4:
                     value = value + columns[1][kind, row].astype(WIDE)
                 held[kind, row, at] = value.astype(LOW)
-    fill_outs(table[1], held, outs)
-
-
-def combine(table, terms, edges, columns):
+    for at, (which, turn) in enumerate(OWNER_STEPS):
+        row = (turn + odd) % 2
+        for kind in range(4):
+            source = (first, held)[kind // 2]
+            if which == 2:
+                outs[at][kind] = source[kind % 2, row, 4 - 4 * odd]
+            else:
+                for part in range(2):
+                    outs[at][kind, part] = source[kind % 2, row, odd + 2 * which + part]
+
+
+def combine(table, first, terms, edges, columns):
+    shapes = [
+        jax.ShapeDtypeStruct((4, TILE, HEAD_DIM) if which == 2 else (4, 2, TILE, HEAD_DIM), LOW)
+        for which, _ in OWNER_STEPS
+    ]
     return pl.pallas_call(
         combine_kernel,
-        out_shape=owner_shapes(),
-        in_specs=[pl.BlockSpec(memory_space=pltpu.SMEM)] + whole(5),
+        out_shape=shapes,
+        in_specs=[pl.BlockSpec(memory_space=pltpu.SMEM)] + whole(6),
         out_specs=whole(6),
         scratch_shapes=[pltpu.VMEM((2, 2, 5, TILE, HEAD_DIM), LOW)],
         compiler_params=pltpu.CompilerParams(vmem_limit_bytes=16 << 20),
         name="combine",
-    )(table, terms, *edges, *columns)
+    )(table, first, terms, *edges, *columns)
 
 
 def send_all(parts, routes):
@@ -385,60 +400,37 @@
 
 
 def local(query_slab, key_slab, value_slab, upstream):
-    owners = owner_table()
-    units = unit_table()
+    place = place_table()
     to_owner = [owner_of(which, turn) for which, turn in OWNER_STEPS]
     row_routes = [shifted(*step) for step in ROW_STEPS]
     column_routes = [shifted(*step) for step in COLUMN_STEPS]
 
     with jax.named_scope("upstream_to_units"):
-        grads = send_all(spread(owners, upstream), [flipped(path) for path in to_owner])
-
-    def by_head(*slabs):
+        grads = send_all(spread(place, upstream), [flipped(path) for path in to_owner])
+
+    with jax.named_scope("heads"):
         lines = [
             slab.reshape(8, 4, 40, 128).transpose(2, 0, 1, 3).reshape(8, 5, 32, 128)
-            for slab in slabs
+            for slab in (query_slab, key_slab, value_slab)
         ]
-        return jnp.stack(lines, axis=1)
-
-    def by_unit(swapped):
-        shaped = swapped.reshape(8, -1, 5, 4, 8, 128).transpose(3, 2, 0, 1, 4, 5)
-        return shaped.reshape(32, 5, -1, 8, 128)
-
-    def by_tile(got):
-        own = got.reshape(32, 5, -1, 2, 4, 128).transpose(2, 3, 1, 0, 4, 5)
-        return own.reshape(-1, 2, 5, TILE, HEAD_DIM)
-
-    with jax.named_scope("heads"):
-        lines = by_head(key_slab, value_slab, query_slab)
-        swapped = lax.all_to_all(lines, "head", 0, 0, tiled=True)
-    with jax.named_scope("key_value_tiles"):
-        shaped, grads = lax.optimization_barrier((by_unit(swapped[:, :2]), grads))
-        pair = by_tile(lax.all_to_all(shaped, "tile", 0, 0, tiled=True))
-    with jax.named_scope("query_tiles"):
-        own = by_tile(lax.all_to_all(by_unit(swapped[:, 2:]), "tile", 0, 0, tiled=True))[0]
+        swapped = lax.all_to_all(jnp.stack(lines, axis=1), "head", 0, 0, tiled=True)
+    with jax.named_scope("tiles"):
+        dealt, early = lax.optimization_barrier((deal(swapped), grads[:EARLY]))
+        got = lax.all_to_all(dealt, "tile", 0, 0, tiled=True)
+        own = got.reshape(32, 19, 2, 4, 128).transpose(2, 1, 0, 3, 4)
+        own = own.reshape(2, 19, TILE, HEAD_DIM)
+        own, late = lax.optimization_barrier((own, grads[EARLY:]))
     with jax.named_scope("halos"):
-        sides = send_all([pair[:, :, 4], pair[:, :, 0]], column_routes)
-        leaving = [
-            jnp.concatenate([sides[0][:, row, None], pair[:, row], sides[1][:, row, None]], axis=1)
-            for row in (1, 0)
-        ]
-        halos = sides + send_all(leaving, row_routes)
+        halos = send_all([own[1, 5:], own[0, 5:]], row_routes)
     with jax.named_scope("attention"):
-        results = attend(units, own, pair, halos, grads)
-    first, terms, edges = results[:6], results[6], results[7:]
+        first, terms, *edges = attend(place, own, halos, early + late)
     with jax.named_scope("terms"):
         edges = send_all(edges, row_routes)
-        early = send_all(first[:3], to_owner[:3])
-        edges, early = lax.optimization_barrier((edges, early))
         columns = send_all(rims(terms, edges), column_routes)
-        late = send_all(first[3:], to_owner[3:])
-    with jax.named_scope("key_terms_home"):
-        columns, late = lax.optimization_barrier((columns, late))
-        second = send_all(combine(units, terms, edges, columns), to_owner)
-    first = early + late
+    with jax.named_scope("outputs_home"):
+        received = send_all(combine(place, first, terms, edges, columns), to_owner)
     with jax.named_scope("settle"):
-        return tuple(gather(owners, first, second))
+        return tuple(gather(place, received))
 
 
 def solution(mesh):

time: 176 us -> 160 us (0.909)
  the two profiles are of different devices: /device:TPU:40 before, /device:TPU:104 now
where the time goes in v2:
time: 160 us
  waiting for transfers between devices  81.4 us (51%)
  starting transfers between devices  57.8 us (36%)
  Pallas kernels  15.2 us (10%)
  local copies, waits for them, and re-layouts  3.23 us (2%)
    ppermute x18, waiting for transfers between devices, send_all(): lax.ppermute(part, 'tile', path)  47.9 us
    ppermute x18, starting transfers between devices, send_all(): lax.ppermute(part, 'tile', path)  43 us
    all_to_all x1, waiting for transfers between devices, local(): got = lax.all_to_all(dealt, 'tile', 0, 0, tiled=True)  27.8 us
    all_to_all x1, starting transfers between devices, local(): got = lax.all_to_all(dealt, 'tile', 0, 0, tiled=True)  10.4 us
    pallas_call x1, Pallas kernels, attend(): pl.pallas_call(attend_kernel, out_shape=[jax.ShapeDtypeStruct((2, 2, 5, T...  10.1 us
    all_to_all x1, waiting for transfers between devices, local(): swapped = lax.all_to_all(jnp.stack(lines, axis=1), 'head', 0, 0, tiled=True)  5.69 us
    all_to_all x1, starting transfers between devices, local(): swapped = lax.all_to_all(jnp.stack(lines, axis=1), 'head', 0, 0, tiled=True)  4.43 us
  transfers between devices with their start and end apart: 20, of which 11 were waited for; matrix products, arithmetic and copies ran while one was open for 1% of the time, Pallas kernels for 1%

profile of v2, /device:TPU:104, one launch (start us, length us, event | category | flops | bytes accessed | tf_op | source)
XLA Modules:
  0.0 159.7 jit_solution(262699959448827069)
XLA Ops:
  0.7 1.2 reshape.32
  1.8 0.1 copy.9
  2.0 0.1 reshape.34
  2.1 0.1 copy.10
  2.2 0.1 reshape.36
  2.4 0.1 copy.11
  2.5 1.1 pad_maximum_fusion
  3.6 4.4 %all-to-all-start = ((bf16[8,3,5,32,128]{4,3,2,1,0:T(8,128)(2,1)}), bf16[8,3,5,32,128]{4,3,2,1,0:T(8,128)(2,1)S(1)}, u32[]{:S(2)}, u32[]{:S(2)}) async-start(bf16[8,3,5,32,128]{4,3,2,1,0:T(8,128)(2,1)} %pad_maximum_fusion), calls=%async_computation | async-start | bytes 1966080 | tf_op jit(solution)/shard_map/heads/all_to_all | solution.py:416
  8.0 0.7 dynamic-slice_bitcast_fusion.table
  8.7 0.9 spread.1
  9.6 5.9 %collective-permute-start = (bf16[2,128,128]{2,1,0:T(8,128)(2,1)S(1)}, bf16[2,128,128]{2,1,0:T(8,128)(2,1)S(1)}, u32[]{:S(2)}, u32[]{:S(2)}) collective-permute-start(bf16[2,128,128]{2,1,0:T(8,128)(2,1)S(1)} %get-tuple-element.30), channel_id=1, source_target_pairs={{0,0},{56,8},{8,16},{32,24},{16,32},{40,40},{24,48},{48,56},{64,64... | collective-permute-start | bytes 196616 | tf_op jit(solution)/shard_map/upstream_to_units/ppermute | solution.py:399
  15.6 0.1 collective-permute-start.1
  15.7 1.9 %collective-permute-start.2 = (bf16[2,128,128]{2,1,0:T(8,128)(2,1)S(1)}, bf16[2,128,128]{2,1,0:T(8,128)(2,1)S(1)}, u32[]{:S(2)}, u32[]{:S(2)}) collective-permute-start(bf16[2,128,128]{2,1,0:T(8,128)(2,1)S(1)} %get-tuple-element.32), channel_id=1, source_target_pairs={{8,0},{32,8},{16,16},{40,24},{24,32},{48,40},{0,48},{56,56},{72,64... | collective-permute-start | bytes 196616 | tf_op jit(solution)/shard_map/upstream_to_units/ppermute | solution.py:399
  17.6 5.7 %all-to-all-done.swapped = bf16[8,3,5,32,128]{4,3,2,1,0:T(8,128)(2,1)S(1)} async-done(((bf16[8,3,5,32,128]{4,3,2,1,0:T(8,128)(2,1)}), bf16[8,3,5,32,128]{4,3,2,1,0:T(8,128)(2,1)S(1)}, u32[]{:S(2)}, u32[]{:S(2)}) %all-to-all-start) | async-done | bytes 983072 | tf_op jit(solution)/shard_map/heads/all_to_all | solution.py:416
  23.3 1.2 deal.1
  24.5 10.4 %all-to-all-start.1 = ((bf16[32,19,8,128]{3,2,1,0:T(8,128)(2,1)}), bf16[32,19,8,128]{3,2,1,0:T(8,128)(2,1)S(1)}, u32[]{:S(2)}, u32[]{:S(2)}) async-start(bf16[32,19,8,128]{3,2,1,0:T(8,128)(2,1)} %deal.1), calls=%async_computation.1 | async-start | bytes 2490368 | tf_op jit(solution)/shard_map/tiles/all_to_all | solution.py:419
  34.9 2.8 %collective-permute-start.3 = (bf16[2,128,128]{2,1,0:T(8,128)(2,1)S(1)}, bf16[2,128,128]{2,1,0:T(8,128)(2,1)S(1)}, u32[]{:S(2)}, u32[]{:S(2)}) collective-permute-start(bf16[2,128,128]{2,1,0:T(8,128)(2,1)S(1)} %get-tuple-element.34), channel_id=1, source_target_pairs={{40,0},{0,8},{48,16},{8,24},{56,32},{16,40},{32,48},{24,56},{104,6... | collective-permute-start | bytes 196616 | tf_op jit(solution)/shard_map/upstream_to_units/ppermute | solution.py:399
  37.6 1.5 collective-permute-start.4
  39.1 0.7 collective-permute-start.5
  39.8 27.8 %all-to-all-done.1 = bf16[32,19,8,128]{3,2,1,0:T(8,128)(2,1)S(1)} async-done(((bf16[32,19,8,128]{3,2,1,0:T(8,128)(2,1)}), bf16[32,19,8,128]{3,2,1,0:T(8,128)(2,1)S(1)}, u32[]{:S(2)}, u32[]{:S(2)}) %all-to-all-start.1) | async-done | bytes 1245216 | tf_op jit(solution)/shard_map/tiles/all_to_all | solution.py:419
  67.6 0.7 copy.12
  68.2 0.0 collective-permute-done.4.refs_4_
  68.2 0.0 collective-permute-done.5.refs_5_
  68.3 0.1 slice_bitcast_fusion
  68.3 2.3 %collective-permute-start.7 = (bf16[14,128,128]{2,1,0:T(8,128)(2,1)S(1)}, bf16[14,128,128]{2,1,0:T(8,128)(2,1)S(1)}, u32[]{:S(2)}, u32[]{:S(2)}) collective-permute-start(bf16[14,128,128]{2,1,0:T(8,128)(2,1)S(1)} %get-tuple-element.56), channel_id=1, source_target_pairs={{64,0},{72,8},{80,16},{88,24},{96,32},{104,40},{112,48},{120,56},{... | collective-permute-start | bytes 1376264 | tf_op jit(solution)/shard_map/halos/ppermute | solution.py:399
  70.7 3.5 %collective-permute-start.6 = (bf16[14,128,128]{2,1,0:T(8,128)(2,1)S(1)}, bf16[14,128,128]{2,1,0:T(8,128)(2,1)S(1)}, u32[]{:S(2)}, u32[]{:S(2)}) collective-permute-start(bf16[14,128,128]{2,1,0:T(8,128)(2,1)S(1)} %get-tuple-element.57), channel_id=1, source_target_pairs={{0,64},{8,72},{16,80},{24,88},{32,96},{40,104},{48,112},{56,120},{... | collective-permute-start | bytes 1376264 | tf_op jit(solution)/shard_map/halos/ppermute | solution.py:399
  74.2 7.8 %collective-permute-done.7.below = bf16[14,128,128]{2,1,0:T(8,128)(2,1)S(1)} collective-permute-done((bf16[14,128,128]{2,1,0:T(8,128)(2,1)S(1)}, bf16[14,128,128]{2,1,0:T(8,128)(2,1)S(1)}, u32[]{:S(2)}, u32[]{:S(2)}) %collective-permute-start.7) | collective-permute-done | bytes 458784 | tf_op jit(solution)/shard_map/halos/ppermute | solution.py:399
  82.0 1.9 %collective-permute-done.6.above = bf16[14,128,128]{2,1,0:T(8,128)(2,1)S(1)} collective-permute-done((bf16[14,128,128]{2,1,0:T(8,128)(2,1)S(1)}, bf16[14,128,128]{2,1,0:T(8,128)(2,1)S(1)}, u32[]{:S(2)}, u32[]{:S(2)}) %collective-permute-start.6) | collective-permute-done | bytes 458784 | tf_op jit(solution)/shard_map/halos/ppermute | solution.py:399
  83.9 10.1 %attend.1 = (bf16[2,2,5,128,128]{4,3,2,1,0:T(8,128)(2,1)S(1)}, f32[2,2,7,128,128]{4,3,2,1,0:T(8,128)S(1)}, bf16[2,7,128,128]{3,2,1,0:T(8,128)(2,1)S(1)}, bf16[2,7,128,128]{3,2,1,0:T(8,128)(2,1)S(1)}) custom-call(s32[14]{0:T(128)S(1)} %dynamic-slice_bitcast_fusion.table, bf16[2,19,128,128]{3,2,1,0:T(8,128)(2,1)S(1)} %bitcast.20, ...), custom_call_target="tpu_custom_call" | custom-call | flops 3000000000 | bytes 8000000 | tf_op jit(solution)/shard_map/attention/attend/pallas_call | solution.py:317
  94.0 3.6 %collective-permute-start.8 = (bf16[2,7,128,128]{3,2,1,0:T(8,128)(2,1)S(1)}, bf16[2,7,128,128]{3,2,1,0:T(8,128)(2,1)S(1)}, u32[]{:S(2)}, u32[]{:S(2)}) collective-permute-start(bf16[2,7,128,128]{3,2,1,0:T(8,128)(2,1)S(1)} %get-tuple-element.46), channel_id=1, source_target_pairs={{0,64},{8,72},{16,80},{24,88},{32,96},{40,104},{48,112},{56,120},{... | collective-permute-start | bytes 1376264 | tf_op jit(solution)/shard_map/terms/ppermute | solution.py:399
  97.7 2.2 %collective-permute-start.9 = (bf16[2,7,128,128]{3,2,1,0:T(8,128)(2,1)S(1)}, bf16[2,7,128,128]{3,2,1,0:T(8,128)(2,1)S(1)}, u32[]{:S(2)}, u32[]{:S(2)}) collective-permute-start(bf16[2,7,128,128]{3,2,1,0:T(8,128)(2,1)S(1)} %get-tuple-element.47), channel_id=1, source_target_pairs={{64,0},{72,8},{80,16},{88,24},{96,32},{104,40},{112,48},{120,56},{... | collective-permute-start | bytes 1376264 | tf_op jit(solution)/shard_map/terms/ppermute | solution.py:399
  99.9 6.5 %collective-permute-done.8.above.refs_0_ = bf16[2,7,128,128]{3,2,1,0:T(8,128)(2,1)S(1)} collective-permute-done((bf16[2,7,128,128]{3,2,1,0:T(8,128)(2,1)S(1)}, bf16[2,7,128,128]{3,2,1,0:T(8,128)(2,1)S(1)}, u32[]{:S(2)}, u32[]{:S(2)}) %collective-permute-start.8) | collective-permute-done | bytes 458784 | tf_op jit(solution)/shard_map/terms/ppermute | solution.py:399
  106.4 3.5 %collective-permute-done.9.below.refs_1_ = bf16[2,7,128,128]{3,2,1,0:T(8,128)(2,1)S(1)} collective-permute-done((bf16[2,7,128,128]{3,2,1,0:T(8,128)(2,1)S(1)}, bf16[2,7,128,128]{3,2,1,0:T(8,128)(2,1)S(1)}, u32[]{:S(2)}, u32[]{:S(2)}) %collective-permute-start.9) | collective-permute-done | bytes 458784 | tf_op jit(solution)/shard_map/terms/ppermute | solution.py:399
  109.9 1.9 %collective-permute-start.10 = (bf16[2,2,128,128]{3,2,1,0:T(8,128)(2,1)S(1)}, bf16[2,2,128,128]{3,2,1,0:T(8,128)(2,1)S(1)}, u32[]{:S(2)}, u32[]{:S(2)}) collective-permute-start(bf16[2,2,128,128]{3,2,1,0:T(8,128)(2,1)S(1)} %get-tuple-element.48), channel_id=1, source_target_pairs={{0,8},{8,16},{16,24},{24,32},{32,40},{40,48},{48,56},{64,72},{72,8... | collective-permute-start | bytes 393224 | tf_op jit(solution)/shard_map/terms/ppermute | solution.py:399
  111.8 3.9 %collective-permute-start.11 = (bf16[2,2,128,128]{3,2,1,0:T(8,128)(2,1)S(1)}, bf16[2,2,128,128]{3,2,1,0:T(8,128)(2,1)S(1)}, u32[]{:S(2)}, u32[]{:S(2)}) collective-permute-start(bf16[2,2,128,128]{3,2,1,0:T(8,128)(2,1)S(1)} %get-tuple-element.49), channel_id=1, source_target_pairs={{8,0},{16,8},{24,16},{32,24},{40,32},{48,40},{56,48},{72,64},{80,7... | collective-permute-start | bytes 393224 | tf_op jit(solution)/shard_map/terms/ppermute | solution.py:399
  115.7 1.0 collective-permute-done.10.refs_2_
  116.8 3.1 %collective-permute-done.11.refs_3_ = bf16[2,2,128,128]{3,2,1,0:T(8,128)(2,1)S(1)} collective-permute-done((bf16[2,2,128,128]{3,2,1,0:T(8,128)(2,1)S(1)}, bf16[2,2,128,128]{3,2,1,0:T(8,128)(2,1)S(1)}, u32[]{:S(2)}, u32[]{:S(2)}) %collective-permute-start.11) | collective-permute-done | bytes 131104 | tf_op jit(solution)/shard_map/terms/ppermute | solution.py:399
  119.9 0.8 combine.1
  120.7 0.1 collective-permute-start.16
  120.7 3.6 %collective-permute-start.12 = (bf16[4,2,128,128]{3,2,1,0:T(8,128)(2,1)S(1)}, bf16[4,2,128,128]{3,2,1,0:T(8,128)(2,1)S(1)}, u32[]{:S(2)}, u32[]{:S(2)}) collective-permute-start(bf16[4,2,128,128]{3,2,1,0:T(8,128)(2,1)S(1)} %get-tuple-element.50), channel_id=1, source_target_pairs={{0,0},{8,56},{16,8},{24,32},{32,16},{40,40},{48,24},{56,48},{64,64... | collective-permute-start | bytes 786440 | tf_op jit(solution)/shard_map/outputs_home/ppermute | solution.py:399
  124.4 1.3 collective-permute-start.13
  125.7 6.6 %collective-permute-start.14 = (bf16[4,2,128,128]{3,2,1,0:T(8,128)(2,1)S(1)}, bf16[4,2,128,128]{3,2,1,0:T(8,128)(2,1)S(1)}, u32[]{:S(2)}, u32[]{:S(2)}) collective-permute-start(bf16[4,2,128,128]{3,2,1,0:T(8,128)(2,1)S(1)} %get-tuple-element.52), channel_id=1, source_target_pairs={{0,8},{8,32},{16,16},{24,40},{32,24},{40,48},{48,0},{56,56},{64,72... | collective-permute-start | bytes 786440 | tf_op jit(solution)/shard_map/outputs_home/ppermute | solution.py:399
  132.2 0.4 collective-permute-start.15
  132.7 0.7 collective-permute-start.17
  133.4 8.1 %collective-permute-done.12.refs_0_ = bf16[4,2,128,128]{3,2,1,0:T(8,128)(2,1)S(1)} collective-permute-done((bf16[4,2,128,128]{3,2,1,0:T(8,128)(2,1)S(1)}, bf16[4,2,128,128]{3,2,1,0:T(8,128)(2,1)S(1)}, u32[]{:S(2)}, u32[]{:S(2)}) %collective-permute-start.12) | collective-permute-done | bytes 262176 | tf_op jit(solution)/shard_map/outputs_home/ppermute | solution.py:399
  141.4 3.7 %collective-permute-done.13.refs_1_ = bf16[4,2,128,128]{3,2,1,0:T(8,128)(2,1)S(1)} collective-permute-done((bf16[4,2,128,128]{3,2,1,0:T(8,128)(2,1)S(1)}, bf16[4,2,128,128]{3,2,1,0:T(8,128)(2,1)S(1)}, u32[]{:S(2)}, u32[]{:S(2)}) %collective-permute-start.13) | collective-permute-done | bytes 262176 | tf_op jit(solution)/shard_map/outputs_home/ppermute | solution.py:399
  145.2 12.3 %collective-permute-done.14.refs_2_ = bf16[4,2,128,128]{3,2,1,0:T(8,128)(2,1)S(1)} collective-permute-done((bf16[4,2,128,128]{3,2,1,0:T(8,128)(2,1)S(1)}, bf16[4,2,128,128]{3,2,1,0:T(8,128)(2,1)S(1)}, u32[]{:S(2)}, u32[]{:S(2)}) %collective-permute-start.14) | collective-permute-done | bytes 262176 | tf_op jit(solution)/shard_map/outputs_home/ppermute | solution.py:399
  157.5 2.2 %gather.1 = (bf16[256,640]{1,0:T(8,128)(2,1)}, bf16[256,640]{1,0:T(8,128)(2,1)}, bf16[256,640]{1,0:T(8,128)(2,1)}, bf16[256,640]{1,0:T(8,128)(2,1)}) custom-call(s32[14]{0:T(128)S(1)} %dynamic-slice_bitcast_fusion.table, bf16[4,2,128,128]{3,2,1,0:T(8,128)(2,1)S(1)} %collective-permute-done.12.refs_0_, ...), custom_call_target="tpu_custom_call" | custom-call | tf_op jit(solution)/shard_map/settle/gather/pallas_call | solution.py:153
  (14 shorter events, 0.1 us)
Async XLA Ops:
  0.6 1.3 copy-start.1
  0.6 1.6 copy-start.2
  3.6 5.1 %copy-start = (bf16[256,640]{1,0:T(8,128)(2,1)S(1)}, bf16[256,640]{1,0:T(8,128)(2,1)}, u32[]{:S(2)}) copy-start(bf16[256,640]{1,0:T(8,128)(2,1)} %upstream.1) | copy-start | bytes 983044
  3.6 19.7 %all-to-all-start = ((bf16[8,3,5,32,128]{4,3,2,1,0:T(8,128)(2,1)}), bf16[8,3,5,32,128]{4,3,2,1,0:T(8,128)(2,1)S(1)}, u32[]{:S(2)}, u32[]{:S(2)}) async-start(bf16[8,3,5,32,128]{4,3,2,1,0:T(8,128)(2,1)} %pad_maximum_fusion), calls=%async_computation | async-start | bytes 1966080 | tf_op jit(solution)/shard_map/heads/all_to_all | solution.py:416
  9.6 14.9 %collective-permute-start = (bf16[2,128,128]{2,1,0:T(8,128)(2,1)S(1)}, bf16[2,128,128]{2,1,0:T(8,128)(2,1)S(1)}, u32[]{:S(2)}, u32[]{:S(2)}) collective-permute-start(bf16[2,128,128]{2,1,0:T(8,128)(2,1)S(1)} %get-tuple-element.30), channel_id=1, source_target_pairs={{0,0},{56,8},{8,16},{32,24},{16,32},{40,40},{24,48},{48,56},{64,64... | collective-permute-start | bytes 196616 | tf_op jit(solution)/shard_map/upstream_to_units/ppermute | solution.py:399
  15.6 9.0 %collective-permute-start.1 = (bf16[2,128,128]{2,1,0:T(8,128)(2,1)S(1)}, bf16[2,128,128]{2,1,0:T(8,128)(2,1)S(1)}, u32[]{:S(2)}, u32[]{:S(2)}) collective-permute-start(bf16[2,128,128]{2,1,0:T(8,128)(2,1)S(1)} %get-tuple-element.31), channel_id=1, source_target_pairs={{32,0},{24,8},{40,16},{0,24},{48,32},{8,40},{56,48},{16,56},{96,64... | collective-permute-start | bytes 196616 | tf_op jit(solution)/shard_map/upstream_to_units/ppermute | solution.py:399
  15.7 8.9 %collective-permute-start.2 = (bf16[2,128,128]{2,1,0:T(8,128)(2,1)S(1)}, bf16[2,128,128]{2,1,0:T(8,128)(2,1)S(1)}, u32[]{:S(2)}, u32[]{:S(2)}) collective-permute-start(bf16[2,128,128]{2,1,0:T(8,128)(2,1)S(1)} %get-tuple-element.32), channel_id=1, source_target_pairs={{8,0},{32,8},{16,16},{40,24},{24,32},{48,40},{0,48},{56,56},{72,64... | collective-permute-start | bytes 196616 | tf_op jit(solution)/shard_map/upstream_to_units/ppermute | solution.py:399
  24.5 43.0 %all-to-all-start.1 = ((bf16[32,19,8,128]{3,2,1,0:T(8,128)(2,1)}), bf16[32,19,8,128]{3,2,1,0:T(8,128)(2,1)S(1)}, u32[]{:S(2)}, u32[]{:S(2)}) async-start(bf16[32,19,8,128]{3,2,1,0:T(8,128)(2,1)} %deal.1), calls=%async_computation.1 | async-start | bytes 2490368 | tf_op jit(solution)/shard_map/tiles/all_to_all | solution.py:419
  34.9 33.4 %collective-permute-start.3 = (bf16[2,128,128]{2,1,0:T(8,128)(2,1)S(1)}, bf16[2,128,128]{2,1,0:T(8,128)(2,1)S(1)}, u32[]{:S(2)}, u32[]{:S(2)}) collective-permute-start(bf16[2,128,128]{2,1,0:T(8,128)(2,1)S(1)} %get-tuple-element.34), channel_id=1, source_target_pairs={{40,0},{0,8},{48,16},{8,24},{56,32},{16,40},{32,48},{24,56},{104,6... | collective-permute-start | bytes 196616 | tf_op jit(solution)/shard_map/upstream_to_units/ppermute | solution.py:399
  37.6 30.6 %collective-permute-start.4 = (bf16[128,128]{1,0:T(8,128)(2,1)S(1)}, bf16[128,128]{1,0:T(8,128)(2,1)S(1)}, u32[]{:S(2)}, u32[]{:S(2)}) collective-permute-start(bf16[128,128]{1,0:T(8,128)(2,1)S(1)} %get-tuple-element.35), channel_id=1, source_target_pairs={{16,0},{48,8},{24,16},{56,24},{0,32},{32,40},{8,48},{40,56},{80,64... | collective-permute-start | bytes 98312 | tf_op jit(solution)/shard_map/upstream_to_units/ppermute | solution.py:399
  39.1 29.1 %collective-permute-start.5 = (bf16[128,128]{1,0:T(8,128)(2,1)S(1)}, bf16[128,128]{1,0:T(8,128)(2,1)S(1)}, u32[]{:S(2)}, u32[]{:S(2)}) collective-permute-start(bf16[128,128]{1,0:T(8,128)(2,1)S(1)} %get-tuple-element.36), channel_id=1, source_target_pairs={{48,0},{16,8},{56,16},{24,24},{32,32},{0,40},{40,48},{8,56},{112,6... | collective-permute-start | bytes 98312 | tf_op jit(solution)/shard_map/upstream_to_units/ppermute | solution.py:399
  68.3 13.7 %collective-permute-start.7 = (bf16[14,128,128]{2,1,0:T(8,128)(2,1)S(1)}, bf16[14,128,128]{2,1,0:T(8,128)(2,1)S(1)}, u32[]{:S(2)}, u32[]{:S(2)}) collective-permute-start(bf16[14,128,128]{2,1,0:T(8,128)(2,1)S(1)} %get-tuple-element.56), channel_id=1, source_target_pairs={{64,0},{72,8},{80,16},{88,24},{96,32},{104,40},{112,48},{120,56},{... | collective-permute-start | bytes 1376264 | tf_op jit(solution)/shard_map/halos/ppermute | solution.py:399
  70.7 13.3 %collective-permute-start.6 = (bf16[14,128,128]{2,1,0:T(8,128)(2,1)S(1)}, bf16[14,128,128]{2,1,0:T(8,128)(2,1)S(1)}, u32[]{:S(2)}, u32[]{:S(2)}) collective-permute-start(bf16[14,128,128]{2,1,0:T(8,128)(2,1)S(1)} %get-tuple-element.57), channel_id=1, source_target_pairs={{0,64},{8,72},{16,80},{24,88},{32,96},{40,104},{48,112},{56,120},{... | collective-permute-start | bytes 1376264 | tf_op jit(solution)/shard_map/halos/ppermute | solution.py:399
  94.0 12.4 %collective-permute-start.8 = (bf16[2,7,128,128]{3,2,1,0:T(8,128)(2,1)S(1)}, bf16[2,7,128,128]{3,2,1,0:T(8,128)(2,1)S(1)}, u32[]{:S(2)}, u32[]{:S(2)}) collective-permute-start(bf16[2,7,128,128]{3,2,1,0:T(8,128)(2,1)S(1)} %get-tuple-element.46), channel_id=1, source_target_pairs={{0,64},{8,72},{16,80},{24,88},{32,96},{40,104},{48,112},{56,120},{... | collective-permute-start | bytes 1376264 | tf_op jit(solution)/shard_map/terms/ppermute | solution.py:399
  97.7 12.2 %collective-permute-start.9 = (bf16[2,7,128,128]{3,2,1,0:T(8,128)(2,1)S(1)}, bf16[2,7,128,128]{3,2,1,0:T(8,128)(2,1)S(1)}, u32[]{:S(2)}, u32[]{:S(2)}) collective-permute-start(bf16[2,7,128,128]{3,2,1,0:T(8,128)(2,1)S(1)} %get-tuple-element.47), channel_id=1, source_target_pairs={{64,0},{72,8},{80,16},{88,24},{96,32},{104,40},{112,48},{120,56},{... | collective-permute-start | bytes 1376264 | tf_op jit(solution)/shard_map/terms/ppermute | solution.py:399
  109.9 6.9 %collective-permute-start.10 = (bf16[2,2,128,128]{3,2,1,0:T(8,128)(2,1)S(1)}, bf16[2,2,128,128]{3,2,1,0:T(8,128)(2,1)S(1)}, u32[]{:S(2)}, u32[]{:S(2)}) collective-permute-start(bf16[2,2,128,128]{3,2,1,0:T(8,128)(2,1)S(1)} %get-tuple-element.48), channel_id=1, source_target_pairs={{0,8},{8,16},{16,24},{24,32},{32,40},{40,48},{48,56},{64,72},{72,8... | collective-permute-start | bytes 393224 | tf_op jit(solution)/shard_map/terms/ppermute | solution.py:399
  111.8 8.1 %collective-permute-start.11 = (bf16[2,2,128,128]{3,2,1,0:T(8,128)(2,1)S(1)}, bf16[2,2,128,128]{3,2,1,0:T(8,128)(2,1)S(1)}, u32[]{:S(2)}, u32[]{:S(2)}) collective-permute-start(bf16[2,2,128,128]{3,2,1,0:T(8,128)(2,1)S(1)} %get-tuple-element.49), channel_id=1, source_target_pairs={{8,0},{16,8},{24,16},{32,24},{40,32},{48,40},{56,48},{72,64},{80,7... | collective-permute-start | bytes 393224 | tf_op jit(solution)/shard_map/terms/ppermute | solution.py:399
  120.7 12.0 %collective-permute-start.16 = (bf16[4,128,128]{2,1,0:T(8,128)(2,1)S(1)}, bf16[4,128,128]{2,1,0:T(8,128)(2,1)S(1)}, u32[]{:S(2)}, u32[]{:S(2)}) collective-permute-start(bf16[4,128,128]{2,1,0:T(8,128)(2,1)S(1)} %get-tuple-element.54), channel_id=1, source_target_pairs={{0,16},{8,48},{16,24},{24,56},{32,0},{40,32},{48,8},{56,40},{64,80... | collective-permute-start | bytes 393224 | tf_op jit(solution)/shard_map/outputs_home/ppermute | solution.py:399
  120.7 20.7 %collective-permute-start.12 = (bf16[4,2,128,128]{3,2,1,0:T(8,128)(2,1)S(1)}, bf16[4,2,128,128]{3,2,1,0:T(8,128)(2,1)S(1)}, u32[]{:S(2)}, u32[]{:S(2)}) collective-permute-start(bf16[4,2,128,128]{3,2,1,0:T(8,128)(2,1)S(1)} %get-tuple-element.50), channel_id=1, source_target_pairs={{0,0},{8,56},{16,8},{24,32},{32,16},{40,40},{48,24},{56,48},{64,64... | collective-permute-start | bytes 786440 | tf_op jit(solution)/shard_map/outputs_home/ppermute | solution.py:399
  124.4 20.8 %collective-permute-start.13 = (bf16[4,2,128,128]{3,2,1,0:T(8,128)(2,1)S(1)}, bf16[4,2,128,128]{3,2,1,0:T(8,128)(2,1)S(1)}, u32[]{:S(2)}, u32[]{:S(2)}) collective-permute-start(bf16[4,2,128,128]{3,2,1,0:T(8,128)(2,1)S(1)} %get-tuple-element.51), channel_id=1, source_target_pairs={{0,32},{8,24},{16,40},{24,0},{32,48},{40,8},{48,56},{56,16},{64,96... | collective-permute-start | bytes 786440 | tf_op jit(solution)/shard_map/outputs_home/ppermute | solution.py:399
  125.7 31.8 %collective-permute-start.14 = (bf16[4,2,128,128]{3,2,1,0:T(8,128)(2,1)S(1)}, bf16[4,2,128,128]{3,2,1,0:T(8,128)(2,1)S(1)}, u32[]{:S(2)}, u32[]{:S(2)}) collective-permute-start(bf16[4,2,128,128]{3,2,1,0:T(8,128)(2,1)S(1)} %get-tuple-element.52), channel_id=1, source_target_pairs={{0,8},{8,32},{16,16},{24,40},{32,24},{40,48},{48,0},{56,56},{64,72... | collective-permute-start | bytes 786440 | tf_op jit(solution)/shard_map/outputs_home/ppermute | solution.py:399
  132.2 25.2 %collective-permute-start.15 = (bf16[4,2,128,128]{3,2,1,0:T(8,128)(2,1)S(1)}, bf16[4,2,128,128]{3,2,1,0:T(8,128)(2,1)S(1)}, u32[]{:S(2)}, u32[]{:S(2)}) collective-permute-start(bf16[4,2,128,128]{3,2,1,0:T(8,128)(2,1)S(1)} %get-tuple-element.53), channel_id=1, source_target_pairs={{0,40},{8,0},{16,48},{24,8},{32,56},{40,16},{48,32},{56,24},{64,10... | collective-permute-start | bytes 786440 | tf_op jit(solution)/shard_map/outputs_home/ppermute | solution.py:399
  132.7 0.7 collective-permute-start.17

commit v3 on v2

--- a/solution.py
+++ b/solution.py
@@ -131,7 +131,7 @@
 
 
 def gather_kernel(table, *refs):
-    received, outs, single = refs[:6], refs[6:10], refs[10]
+    firsts, seconds, singles, outs, single = refs[:4], refs[4:8], refs[8:10], refs[10:14], refs[14]
     line = lax.broadcasted_iota(jnp.int32, (2 * TILE, 2 * TILE), 0)
     col = lax.broadcasted_iota(jnp.int32, (2 * TILE, 2 * TILE), 1)
     source = ((line >> 2) & 1) * TILE + (line >> 3) * 4 + (line & 3)
@@ -139,26 +139,26 @@
     for kind, out in enumerate(outs):
         for at in range(4):
             head = pl.multiple_of(table[at] * HEAD_DIM, HEAD_DIM)
-            tiles = received[at][kind].reshape(2 * TILE, HEAD_DIM)
+            tiles = (firsts, seconds)[kind // 2][at][kind % 2].reshape(2 * TILE, HEAD_DIM)
             out[:, pl.ds(head, HEAD_DIM)] = nn(order, tiles).astype(LOW)
         flip = table[6] == 1
-        one, two = received[4][kind], received[5][kind]
+        one, two = singles[0][kind], singles[1][kind]
         single[:TILE] = jnp.where(flip, two, one)
         single[TILE:] = jnp.where(flip, one, two)
         head = pl.multiple_of(table[4] * HEAD_DIM, HEAD_DIM)
         out[:, pl.ds(head, HEAD_DIM)] = nn(order, single[...]).astype(LOW)
 
 
-def gather(table, received):
+def gather(table, first, second):
     return pl.pallas_call(
         gather_kernel,
         out_shape=[jax.ShapeDtypeStruct((2 * TILE, HEADS_HERE * HEAD_DIM), LOW)] * 4,
-        in_specs=[pl.BlockSpec(memory_space=pltpu.SMEM)] + whole(6),
+        in_specs=[pl.BlockSpec(memory_space=pltpu.SMEM)] + whole(10),
         out_specs=whole(4),
         scratch_shapes=[pltpu.VMEM((2 * TILE, HEAD_DIM), LOW)],
         compiler_params=pltpu.CompilerParams(vmem_limit_bytes=16 << 20),
         name="gather",
-    )(table, *received)
+    )(table, *first, *second)
 
 
 def deal_kernel(swapped, out):
@@ -186,9 +186,21 @@
     )(swapped)
 
 
+def send_pairs(odd, held, outs):
+    for out, (which, turn) in zip(outs, OWNER_STEPS):
+        row = (turn + odd) % 2
+        for kind in range(2):
+            for part in range(2):
+                out[kind, part] = held[kind, row, odd + 2 * which + part]
+
+
+def pair_shapes():
+    return [jax.ShapeDtypeStruct((2, 2, TILE, HEAD_DIM), LOW)] * 4
+
+
 def attend_kernel(table, own, above, below, *refs):
-    grads, held, terms, edges = refs[:6], refs[6], refs[7], refs[8:10]
-    pair, turned, grad, total = refs[10:]
+    grads, firsts, rest, terms, edges = refs[:6], refs[6:10], refs[10], refs[11], refs[12:14]
+    pair, turned, grad, total, held = refs[14:]
     strip, odd = table[7], table[8]
     scaling = HEAD_DIM**-0.5
     rate = scaling * math.log2(math.e)
@@ -302,6 +314,10 @@
         return carry
 
     lax.fori_loop(0, 5, one_unit, 0)
+    send_pairs(odd, held, firsts)
+    for kind in range(2):
+        for row in range(2):
+            rest[kind, row] = held[kind, row, 4 - 4 * odd]
     for kind, factor in ((0, scaling), (1, 1.0)):
         for at in range(7):
             for row in range(2):
@@ -316,19 +332,21 @@
 def attend(table, own, halos, grads):
     return pl.pallas_call(
         attend_kernel,
-        out_shape=[
-            jax.ShapeDtypeStruct((2, 2, 5, TILE, HEAD_DIM), LOW),
+        out_shape=pair_shapes()
+        + [
+            jax.ShapeDtypeStruct((2, 2, TILE, HEAD_DIM), LOW),
             jax.ShapeDtypeStruct((2, 2, 7, TILE, HEAD_DIM), WIDE),
             jax.ShapeDtypeStruct((2, 7, TILE, HEAD_DIM), LOW),
             jax.ShapeDtypeStruct((2, 7, TILE, HEAD_DIM), LOW),
         ],
         in_specs=[pl.BlockSpec(memory_space=pltpu.SMEM)] + whole(9),
-        out_specs=whole(4),
+        out_specs=whole(8),
         scratch_shapes=[
             pltpu.VMEM((2, 7, 4, TILE, HEAD_DIM), LOW),
             pltpu.VMEM((2, 7, 4, HEAD_DIM, TILE), LOW),
             pltpu.VMEM((2, 5, TILE, HEAD_DIM), LOW),
             pltpu.VMEM((2, 7, 4, TILE, HEAD_DIM), WIDE),
+            pltpu.VMEM((2, 2, 5, TILE, HEAD_DIM), LOW),
         ],
         compiler_params=pltpu.CompilerParams(vmem_limit_bytes=40 << 20),
         cost_estimate=pl.CostEstimate(
@@ -356,7 +374,7 @@
     )(terms, *edges)
 
 
-def combine_kernel(table, first, terms, *refs):
+def combine_kernel(table, rest, terms, *refs):
     edges, columns, outs, held = refs[:2], refs[2:4], refs[4:10], refs[10]
     odd = table[8]
     for kind in range(2):
@@ -368,31 +386,24 @@
                 if at == 4:
                     value = value + columns[1][kind, row].astype(WIDE)
                 held[kind, row, at] = value.astype(LOW)
-    for at, (which, turn) in enumerate(OWNER_STEPS):
+    send_pairs(odd, held, outs[:4])
+    for turn in range(2):
         row = (turn + odd) % 2
-        for kind in range(4):
-            source = (first, held)[kind // 2]
-            if which == 2:
-                outs[at][kind] = source[kind % 2, row, 4 - 4 * odd]
-            else:
-                for part in range(2):
-                    outs[at][kind, part] = source[kind % 2, row, odd + 2 * which + part]
-
-
-def combine(table, first, terms, edges, columns):
-    shapes = [
-        jax.ShapeDtypeStruct((4, TILE, HEAD_DIM) if which == 2 else (4, 2, TILE, HEAD_DIM), LOW)
-        for which, _ in OWNER_STEPS
-    ]
+        for kind in range(2):
+            outs[4 + turn][kind] = rest[kind, row]
+            outs[4 + turn][2 + kind] = held[kind, row, 4 - 4 * odd]
+
+
+def combine(table, rest, terms, edges, columns):
     return pl.pallas_call(
         combine_kernel,
-        out_shape=shapes,
+        out_shape=pair_shapes() + [jax.ShapeDtypeStruct((4, TILE, HEAD_DIM), LOW)] * 2,
         in_specs=[pl.BlockSpec(memory_space=pltpu.SMEM)] + whole(6),
         out_specs=whole(6),
         scratch_shapes=[pltpu.VMEM((2, 2, 5, TILE, HEAD_DIM), LOW)],
         compiler_params=pltpu.CompilerParams(vmem_limit_bytes=16 << 20),
         name="combine",
-    )(table, first, terms, *edges, *columns)
+    )(table, rest, terms, *edges, *columns)
 
 
 def send_all(parts, routes):
@@ -423,14 +434,18 @@
     with jax.named_scope("halos"):
         halos = send_all([own[1, 5:], own[0, 5:]], row_routes)
     with jax.named_scope("attention"):
-        first, terms, *edges = attend(place, own, halos, early + late)
+        *first, rest, terms, above, below = attend(place, own, halos, early + late)
     with jax.named_scope("terms"):
-        edges = send_all(edges, row_routes)
+        edges = send_all([above, below], row_routes)
+        early = send_all(first[:2], to_owner[:2])
+        edges, early = lax.optimization_barrier((edges, early))
         columns = send_all(rims(terms, edges), column_routes)
+        late = send_all(first[2:], to_owner[2:])
+        columns, late = lax.optimization_barrier((columns, late))
     with jax.named_scope("outputs_home"):
-        received = send_all(combine(place, first, terms, edges, columns), to_owner)
+        second = send_all(combine(place, rest, terms, edges, columns), to_owner)
     with jax.named_scope("settle"):
-        return tuple(gather(place, received))
+        return tuple(gather(place, early + late, second))
 
 
 def solution(mesh):

time: 160 us -> 160 us (level)
  the two profiles are of different devices: /device:TPU:104 before, /device:TPU:60 now
where the time goes in v3:
time: 160 us
  starting transfers between devices  85.6 us (54%)
  waiting for transfers between devices  53.7 us (34%)
  Pallas kernels  15.3 us (10%)
  local copies, waits for them, and re-layouts  3.23 us (2%)
    ppermute x22, starting transfers between devices, send_all(): lax.ppermute(part, 'tile', path)  74.9 us
    ppermute x22, waiting for transfers between devices, send_all(): lax.ppermute(part, 'tile', path)  31.7 us
    all_to_all x1, waiting for transfers between devices, local(): got = lax.all_to_all(dealt, 'tile', 0, 0, tiled=True)  21.9 us
    pallas_call x1, Pallas kernels, attend(): pl.pallas_call(attend_kernel, out_shape=pair_shapes() + [jax.ShapeDtypeSt...  10.1 us
    all_to_all x1, starting transfers between devices, local(): got = lax.all_to_all(dealt, 'tile', 0, 0, tiled=True)  5.8 us
    all_to_all x1, starting transfers between devices, local(): swapped = lax.all_to_all(jnp.stack(lines, axis=1), 'head', 0, 0, tiled=True)  4.93 us
  transfers between devices with their start and end apart: 24, of which 11 were waited for; matrix products, arithmetic and copies ran while one was open for 1% of the time, Pallas kernels for 1%

profile of v3, /device:TPU:60, one launch (start us, length us, event | category | flops | bytes accessed | tf_op | source)
XLA Modules:
  0.0 159.8 jit_solution(12097058984466735099)
XLA Ops:
  0.7 1.2 reshape.32
  1.8 0.1 copy.9
  2.0 0.1 reshape.34
  2.1 0.1 copy.10
  2.2 0.1 reshape.36
  2.4 0.1 copy.11
  2.5 1.1 pad_maximum_fusion
  3.6 4.9 %all-to-all-start = ((bf16[8,3,5,32,128]{4,3,2,1,0:T(8,128)(2,1)}), bf16[8,3,5,32,128]{4,3,2,1,0:T(8,128)(2,1)S(1)}, u32[]{:S(2)}, u32[]{:S(2)}) async-start(bf16[8,3,5,32,128]{4,3,2,1,0:T(8,128)(2,1)} %pad_maximum_fusion), calls=%async_computation | async-start | bytes 1966080 | tf_op jit(solution)/shard_map/heads/all_to_all | solution.py:427
  8.5 0.7 dynamic-slice_bitcast_fusion.table
  9.2 0.9 spread.1
  10.1 3.8 %collective-permute-start = (bf16[2,128,128]{2,1,0:T(8,128)(2,1)S(1)}, bf16[2,128,128]{2,1,0:T(8,128)(2,1)S(1)}, u32[]{:S(2)}, u32[]{:S(2)}) collective-permute-start(bf16[2,128,128]{2,1,0:T(8,128)(2,1)S(1)} %get-tuple-element.42), channel_id=1, source_target_pairs={{0,0},{56,8},{8,16},{32,24},{16,32},{40,40},{24,48},{48,56},{64,64... | collective-permute-start | bytes 196616 | tf_op jit(solution)/shard_map/upstream_to_units/ppermute | solution.py:410
  13.9 3.2 %collective-permute-start.1 = (bf16[2,128,128]{2,1,0:T(8,128)(2,1)S(1)}, bf16[2,128,128]{2,1,0:T(8,128)(2,1)S(1)}, u32[]{:S(2)}, u32[]{:S(2)}) collective-permute-start(bf16[2,128,128]{2,1,0:T(8,128)(2,1)S(1)} %get-tuple-element.43), channel_id=1, source_target_pairs={{32,0},{24,8},{40,16},{0,24},{48,32},{8,40},{56,48},{16,56},{96,64... | collective-permute-start | bytes 196616 | tf_op jit(solution)/shard_map/upstream_to_units/ppermute | solution.py:410
  17.1 5.6 %collective-permute-start.2 = (bf16[2,128,128]{2,1,0:T(8,128)(2,1)S(1)}, bf16[2,128,128]{2,1,0:T(8,128)(2,1)S(1)}, u32[]{:S(2)}, u32[]{:S(2)}) collective-permute-start(bf16[2,128,128]{2,1,0:T(8,128)(2,1)S(1)} %get-tuple-element.44), channel_id=1, source_target_pairs={{8,0},{32,8},{16,16},{40,24},{24,32},{48,40},{0,48},{56,56},{72,64... | collective-permute-start | bytes 196616 | tf_op jit(solution)/shard_map/upstream_to_units/ppermute | solution.py:410
  22.8 1.3 deal.1
  24.0 4.0 %collective-permute-done.2.refs_2_ = bf16[2,128,128]{2,1,0:T(8,128)(2,1)S(1)} collective-permute-done((bf16[2,128,128]{2,1,0:T(8,128)(2,1)S(1)}, bf16[2,128,128]{2,1,0:T(8,128)(2,1)S(1)}, u32[]{:S(2)}, u32[]{:S(2)}) %collective-permute-start.2) | collective-permute-done | bytes 65568 | tf_op jit(solution)/shard_map/upstream_to_units/ppermute | solution.py:410
  28.0 5.8 %all-to-all-start.1 = ((bf16[32,19,8,128]{3,2,1,0:T(8,128)(2,1)}), bf16[32,19,8,128]{3,2,1,0:T(8,128)(2,1)S(1)}, u32[]{:S(2)}, u32[]{:S(2)}) async-start(bf16[32,19,8,128]{3,2,1,0:T(8,128)(2,1)} %deal.1), calls=%async_computation.1 | async-start | bytes 2490368 | tf_op jit(solution)/shard_map/tiles/all_to_all | solution.py:430
  33.8 2.5 %collective-permute-start.3 = (bf16[2,128,128]{2,1,0:T(8,128)(2,1)S(1)}, bf16[2,128,128]{2,1,0:T(8,128)(2,1)S(1)}, u32[]{:S(2)}, u32[]{:S(2)}) collective-permute-start(bf16[2,128,128]{2,1,0:T(8,128)(2,1)S(1)} %get-tuple-element.46), channel_id=1, source_target_pairs={{40,0},{0,8},{48,16},{8,24},{56,32},{16,40},{32,48},{24,56},{104,6... | collective-permute-start | bytes 196616 | tf_op jit(solution)/shard_map/upstream_to_units/ppermute | solution.py:410
  36.3 3.6 %collective-permute-start.4 = (bf16[128,128]{1,0:T(8,128)(2,1)S(1)}, bf16[128,128]{1,0:T(8,128)(2,1)S(1)}, u32[]{:S(2)}, u32[]{:S(2)}) collective-permute-start(bf16[128,128]{1,0:T(8,128)(2,1)S(1)} %get-tuple-element.47), channel_id=1, source_target_pairs={{16,0},{48,8},{24,16},{56,24},{0,32},{32,40},{8,48},{40,56},{80,64... | collective-permute-start | bytes 98312 | tf_op jit(solution)/shard_map/upstream_to_units/ppermute | solution.py:410
  39.8 4.6 %collective-permute-start.5 = (bf16[128,128]{1,0:T(8,128)(2,1)S(1)}, bf16[128,128]{1,0:T(8,128)(2,1)S(1)}, u32[]{:S(2)}, u32[]{:S(2)}) collective-permute-start(bf16[128,128]{1,0:T(8,128)(2,1)S(1)} %get-tuple-element.48), channel_id=1, source_target_pairs={{48,0},{16,8},{56,16},{24,24},{32,32},{0,40},{40,48},{8,56},{112,6... | collective-permute-start | bytes 98312 | tf_op jit(solution)/shard_map/upstream_to_units/ppermute | solution.py:410
  44.4 21.9 %all-to-all-done.1 = bf16[32,19,8,128]{3,2,1,0:T(8,128)(2,1)S(1)} async-done(((bf16[32,19,8,128]{3,2,1,0:T(8,128)(2,1)}), bf16[32,19,8,128]{3,2,1,0:T(8,128)(2,1)S(1)}, u32[]{:S(2)}, u32[]{:S(2)}) %all-to-all-start.1) | async-done | bytes 1245216 | tf_op jit(solution)/shard_map/tiles/all_to_all | solution.py:430
  66.4 0.7 copy.12
  67.0 1.3 collective-permute-done.4.refs_4_
  68.3 0.1 slice_bitcast_fusion
  68.4 2.7 %collective-permute-start.7 = (bf16[14,128,128]{2,1,0:T(8,128)(2,1)S(1)}, bf16[14,128,128]{2,1,0:T(8,128)(2,1)S(1)}, u32[]{:S(2)}, u32[]{:S(2)}) collective-permute-start(bf16[14,128,128]{2,1,0:T(8,128)(2,1)S(1)} %get-tuple-element.80), channel_id=1, source_target_pairs={{64,0},{72,8},{80,16},{88,24},{96,32},{104,40},{112,48},{120,56},{... | collective-permute-start | bytes 1376264 | tf_op jit(solution)/shard_map/halos/ppermute | solution.py:410
  71.1 1.3 collective-permute-start.6
  72.4 6.5 %collective-permute-done.7.below = bf16[14,128,128]{2,1,0:T(8,128)(2,1)S(1)} collective-permute-done((bf16[14,128,128]{2,1,0:T(8,128)(2,1)S(1)}, bf16[14,128,128]{2,1,0:T(8,128)(2,1)S(1)}, u32[]{:S(2)}, u32[]{:S(2)}) %collective-permute-start.7) | collective-permute-done | bytes 458784 | tf_op jit(solution)/shard_map/halos/ppermute | solution.py:410
  79.0 4.1 %collective-permute-done.6.above = bf16[14,128,128]{2,1,0:T(8,128)(2,1)S(1)} collective-permute-done((bf16[14,128,128]{2,1,0:T(8,128)(2,1)S(1)}, bf16[14,128,128]{2,1,0:T(8,128)(2,1)S(1)}, u32[]{:S(2)}, u32[]{:S(2)}) %collective-permute-start.6) | collective-permute-done | bytes 458784 | tf_op jit(solution)/shard_map/halos/ppermute | solution.py:410
  83.1 10.1 %attend.1 = (bf16[2,2,128,128]{3,2,1,0:T(8,128)(2,1)S(1)}, bf16[2,2,128,128]{3,2,1,0:T(8,128)(2,1)S(1)}, bf16[2,2,128,128]{3,2,1,0:T(8,128)(2,1)S(1)}, bf16[2,2,...) custom-call(s32[14]{0:T(128)S(1)} %dynamic-slice_bitcast_fusion.tabl, ...), custom_call_target="tpu_custom_call" | custom-call | flops 3000000000 | bytes 8000000 | tf_op jit(solution)/shard_map/attention/attend/pallas_call | solution.py:333
  93.3 1.3 collective-permute-start.8
  94.6 4.6 %collective-permute-start.9 = (bf16[2,7,128,128]{3,2,1,0:T(8,128)(2,1)S(1)}, bf16[2,7,128,128]{3,2,1,0:T(8,128)(2,1)S(1)}, u32[]{:S(2)}, u32[]{:S(2)}) collective-permute-start(bf16[2,7,128,128]{3,2,1,0:T(8,128)(2,1)S(1)} %get-tuple-element.57), channel_id=1, source_target_pairs={{64,0},{72,8},{80,16},{88,24},{96,32},{104,40},{112,48},{120,56},{... | collective-permute-start | bytes 1376264 | tf_op jit(solution)/shard_map/terms/ppermute | solution.py:410
  99.1 3.7 %collective-permute-start.10 = (bf16[2,2,128,128]{3,2,1,0:T(8,128)(2,1)S(1)}, bf16[2,2,128,128]{3,2,1,0:T(8,128)(2,1)S(1)}, u32[]{:S(2)}, u32[]{:S(2)}) collective-permute-start(bf16[2,2,128,128]{3,2,1,0:T(8,128)(2,1)S(1)} %get-tuple-element.58), channel_id=1, source_target_pairs={{0,0},{8,56},{16,8},{24,32},{32,16},{40,40},{48,24},{56,48},{64,64... | collective-permute-start | bytes 393224 | tf_op jit(solution)/shard_map/terms/ppermute | solution.py:410
  102.8 1.1 collective-permute-start.11
  103.9 6.9 %collective-permute-start.14 = (bf16[2,2,128,128]{3,2,1,0:T(8,128)(2,1)S(1)}, bf16[2,2,128,128]{3,2,1,0:T(8,128)(2,1)S(1)}, u32[]{:S(2)}, u32[]{:S(2)}) collective-permute-start(bf16[2,2,128,128]{3,2,1,0:T(8,128)(2,1)S(1)} %get-tuple-element.67), channel_id=1, source_target_pairs={{0,8},{8,32},{16,16},{24,40},{32,24},{40,48},{48,0},{56,56},{64,72... | collective-permute-start | bytes 393224 | tf_op jit(solution)/shard_map/terms/ppermute | solution.py:410
  110.9 3.6 %collective-permute-done.11.refs_1_ = bf16[2,2,128,128]{3,2,1,0:T(8,128)(2,1)S(1)} collective-permute-done((bf16[2,2,128,128]{3,2,1,0:T(8,128)(2,1)S(1)}, bf16[2,2,128,128]{3,2,1,0:T(8,128)(2,1)S(1)}, u32[]{:S(2)}, u32[]{:S(2)}) %collective-permute-start.11) | collective-permute-done | bytes 131104 | tf_op jit(solution)/shard_map/terms/ppermute | solution.py:410
  114.5 4.6 %collective-permute-start.12 = (bf16[2,2,128,128]{3,2,1,0:T(8,128)(2,1)S(1)}, bf16[2,2,128,128]{3,2,1,0:T(8,128)(2,1)S(1)}, u32[]{:S(2)}, u32[]{:S(2)}) collective-permute-start(bf16[2,2,128,128]{3,2,1,0:T(8,128)(2,1)S(1)} %get-tuple-element.65), channel_id=1, source_target_pairs={{0,8},{8,16},{16,24},{24,32},{32,40},{40,48},{48,56},{64,72},{72,8... | collective-permute-start | bytes 393224 | tf_op jit(solution)/shard_map/terms/ppermute | solution.py:410
  119.1 1.9 %collective-permute-start.13 = (bf16[2,2,128,128]{3,2,1,0:T(8,128)(2,1)S(1)}, bf16[2,2,128,128]{3,2,1,0:T(8,128)(2,1)S(1)}, u32[]{:S(2)}, u32[]{:S(2)}) collective-permute-start(bf16[2,2,128,128]{3,2,1,0:T(8,128)(2,1)S(1)} %get-tuple-element.66), channel_id=1, source_target_pairs={{8,0},{16,8},{24,16},{32,24},{40,32},{48,40},{56,48},{72,64},{80,7... | collective-permute-start | bytes 393224 | tf_op jit(solution)/shard_map/terms/ppermute | solution.py:410
  121.1 0.6 collective-permute-done.12.refs_2_
  121.6 4.8 %collective-permute-done.13.refs_3_ = bf16[2,2,128,128]{3,2,1,0:T(8,128)(2,1)S(1)} collective-permute-done((bf16[2,2,128,128]{3,2,1,0:T(8,128)(2,1)S(1)}, bf16[2,2,128,128]{3,2,1,0:T(8,128)(2,1)S(1)}, u32[]{:S(2)}, u32[]{:S(2)}) %collective-permute-start.13) | collective-permute-done | bytes 131104 | tf_op jit(solution)/shard_map/terms/ppermute | solution.py:410
  126.4 0.7 combine.1
  127.1 3.8 %collective-permute-start.16 = (bf16[2,2,128,128]{3,2,1,0:T(8,128)(2,1)S(1)}, bf16[2,2,128,128]{3,2,1,0:T(8,128)(2,1)S(1)}, u32[]{:S(2)}, u32[]{:S(2)}) collective-permute-start(bf16[2,2,128,128]{3,2,1,0:T(8,128)(2,1)S(1)} %get-tuple-element.74), channel_id=1, source_target_pairs={{0,0},{8,56},{16,8},{24,32},{32,16},{40,40},{48,24},{56,48},{64,64... | collective-permute-start | bytes 393224 | tf_op jit(solution)/shard_map/outputs_home/ppermute | solution.py:410
  130.9 7.4 %collective-permute-start.17 = (bf16[2,2,128,128]{3,2,1,0:T(8,128)(2,1)S(1)}, bf16[2,2,128,128]{3,2,1,0:T(8,128)(2,1)S(1)}, u32[]{:S(2)}, u32[]{:S(2)}) collective-permute-start(bf16[2,2,128,128]{3,2,1,0:T(8,128)(2,1)S(1)} %get-tuple-element.75), channel_id=1, source_target_pairs={{0,32},{8,24},{16,40},{24,0},{32,48},{40,8},{48,56},{56,16},{64,96... | collective-permute-start | bytes 393224 | tf_op jit(solution)/shard_map/outputs_home/ppermute | solution.py:410
  138.3 6.9 %collective-permute-start.18 = (bf16[2,2,128,128]{3,2,1,0:T(8,128)(2,1)S(1)}, bf16[2,2,128,128]{3,2,1,0:T(8,128)(2,1)S(1)}, u32[]{:S(2)}, u32[]{:S(2)}) collective-permute-start(bf16[2,2,128,128]{3,2,1,0:T(8,128)(2,1)S(1)} %get-tuple-element.76), channel_id=1, source_target_pairs={{0,8},{8,32},{16,16},{24,40},{32,24},{40,48},{48,0},{56,56},{64,72... | collective-permute-start | bytes 393224 | tf_op jit(solution)/shard_map/outputs_home/ppermute | solution.py:410
  145.3 1.5 collective-permute-start.20
  146.7 3.9 %collective-permute-start.21 = (bf16[4,128,128]{2,1,0:T(8,128)(2,1)S(1)}, bf16[4,128,128]{2,1,0:T(8,128)(2,1)S(1)}, u32[]{:S(2)}, u32[]{:S(2)}) collective-permute-start(bf16[4,128,128]{2,1,0:T(8,128)(2,1)S(1)} %get-tuple-element.79), channel_id=1, source_target_pairs={{0,48},{8,16},{16,56},{24,24},{32,32},{40,0},{48,40},{56,8},{64,11... | collective-permute-start | bytes 393224 | tf_op jit(solution)/shard_map/outputs_home/ppermute | solution.py:410
  150.7 0.6 collective-permute-done.19.refs_7_
  151.3 3.5 %collective-permute-done.20.refs_8_ = bf16[4,128,128]{2,1,0:T(8,128)(2,1)S(1)} collective-permute-done((bf16[4,128,128]{2,1,0:T(8,128)(2,1)S(1)}, bf16[4,128,128]{2,1,0:T(8,128)(2,1)S(1)}, u32[]{:S(2)}, u32[]{:S(2)}) %collective-permute-start.20) | collective-permute-done | bytes 131104 | tf_op jit(solution)/shard_map/outputs_home/ppermute | solution.py:410
  154.8 2.8 %collective-permute-done.21.refs_9_ = bf16[4,128,128]{2,1,0:T(8,128)(2,1)S(1)} collective-permute-done((bf16[4,128,128]{2,1,0:T(8,128)(2,1)S(1)}, bf16[4,128,128]{2,1,0:T(8,128)(2,1)S(1)}, u32[]{:S(2)}, u32[]{:S(2)}) %collective-permute-start.21) | collective-permute-done | bytes 131104 | tf_op jit(solution)/shard_map/outputs_home/ppermute | solution.py:410
  157.6 2.2 %gather.1 = (bf16[256,640]{1,0:T(8,128)(2,1)}, bf16[256,640]{1,0:T(8,128)(2,1)}, bf16[256,640]{1,0:T(8,128)(2,1)}, bf16[256,640]{1,0:T(8,128)(2,1)}) custom-call(s32[14]{0:T(128)S(1)} %dynamic-slice_bitcast_fusion.table, bf16[2,2,128,128]{3,2,1,0:T(8,128)(2,1)S(1)} %collective-permute-done.10.refs_0_, ...), custom_call_target="tpu_custom_call" | custom-call | tf_op jit(solution)/shard_map/settle/gather/pallas_call | solution.py:153
  (22 shorter events, 0.3 us)
Async XLA Ops:
  0.6 1.3 copy-start.1
  0.6 1.6 copy-start.2
  3.6 5.6 %copy-start = (bf16[256,640]{1,0:T(8,128)(2,1)S(1)}, bf16[256,640]{1,0:T(8,128)(2,1)}, u32[]{:S(2)}) copy-start(bf16[256,640]{1,0:T(8,128)(2,1)} %upstream.1) | copy-start | bytes 983044
  3.6 19.2 %all-to-all-start = ((bf16[8,3,5,32,128]{4,3,2,1,0:T(8,128)(2,1)}), bf16[8,3,5,32,128]{4,3,2,1,0:T(8,128)(2,1)S(1)}, u32[]{:S(2)}, u32[]{:S(2)}) async-start(bf16[8,3,5,32,128]{4,3,2,1,0:T(8,128)(2,1)} %pad_maximum_fusion), calls=%async_computation | async-start | bytes 1966080 | tf_op jit(solution)/shard_map/heads/all_to_all | solution.py:427
  10.1 13.9 %collective-permute-start = (bf16[2,128,128]{2,1,0:T(8,128)(2,1)S(1)}, bf16[2,128,128]{2,1,0:T(8,128)(2,1)S(1)}, u32[]{:S(2)}, u32[]{:S(2)}) collective-permute-start(bf16[2,128,128]{2,1,0:T(8,128)(2,1)S(1)} %get-tuple-element.42), channel_id=1, source_target_pairs={{0,0},{56,8},{8,16},{32,24},{16,32},{40,40},{24,48},{48,56},{64,64... | collective-permute-start | bytes 196616 | tf_op jit(solution)/shard_map/upstream_to_units/ppermute | solution.py:410
  13.9 10.1 %collective-permute-start.1 = (bf16[2,128,128]{2,1,0:T(8,128)(2,1)S(1)}, bf16[2,128,128]{2,1,0:T(8,128)(2,1)S(1)}, u32[]{:S(2)}, u32[]{:S(2)}) collective-permute-start(bf16[2,128,128]{2,1,0:T(8,128)(2,1)S(1)} %get-tuple-element.43), channel_id=1, source_target_pairs={{32,0},{24,8},{40,16},{0,24},{48,32},{8,40},{56,48},{16,56},{96,64... | collective-permute-start | bytes 196616 | tf_op jit(solution)/shard_map/upstream_to_units/ppermute | solution.py:410
  17.1 10.9 %collective-permute-start.2 = (bf16[2,128,128]{2,1,0:T(8,128)(2,1)S(1)}, bf16[2,128,128]{2,1,0:T(8,128)(2,1)S(1)}, u32[]{:S(2)}, u32[]{:S(2)}) collective-permute-start(bf16[2,128,128]{2,1,0:T(8,128)(2,1)S(1)} %get-tuple-element.44), channel_id=1, source_target_pairs={{8,0},{32,8},{16,16},{40,24},{24,32},{48,40},{0,48},{56,56},{72,64... | collective-permute-start | bytes 196616 | tf_op jit(solution)/shard_map/upstream_to_units/ppermute | solution.py:410
  28.0 38.4 %all-to-all-start.1 = ((bf16[32,19,8,128]{3,2,1,0:T(8,128)(2,1)}), bf16[32,19,8,128]{3,2,1,0:T(8,128)(2,1)S(1)}, u32[]{:S(2)}, u32[]{:S(2)}) async-start(bf16[32,19,8,128]{3,2,1,0:T(8,128)(2,1)} %deal.1), calls=%async_computation.1 | async-start | bytes 2490368 | tf_op jit(solution)/shard_map/tiles/all_to_all | solution.py:430
  33.8 34.5 %collective-permute-start.3 = (bf16[2,128,128]{2,1,0:T(8,128)(2,1)S(1)}, bf16[2,128,128]{2,1,0:T(8,128)(2,1)S(1)}, u32[]{:S(2)}, u32[]{:S(2)}) collective-permute-start(bf16[2,128,128]{2,1,0:T(8,128)(2,1)S(1)} %get-tuple-element.46), channel_id=1, source_target_pairs={{40,0},{0,8},{48,16},{8,24},{56,32},{16,40},{32,48},{24,56},{104,6... | collective-permute-start | bytes 196616 | tf_op jit(solution)/shard_map/upstream_to_units/ppermute | solution.py:410
  36.3 32.1 %collective-permute-start.4 = (bf16[128,128]{1,0:T(8,128)(2,1)S(1)}, bf16[128,128]{1,0:T(8,128)(2,1)S(1)}, u32[]{:S(2)}, u32[]{:S(2)}) collective-permute-start(bf16[128,128]{1,0:T(8,128)(2,1)S(1)} %get-tuple-element.47), channel_id=1, source_target_pairs={{16,0},{48,8},{24,16},{56,24},{0,32},{32,40},{8,48},{40,56},{80,64... | collective-permute-start | bytes 98312 | tf_op jit(solution)/shard_map/upstream_to_units/ppermute | solution.py:410
  39.8 28.5 %collective-permute-start.5 = (bf16[128,128]{1,0:T(8,128)(2,1)S(1)}, bf16[128,128]{1,0:T(8,128)(2,1)S(1)}, u32[]{:S(2)}, u32[]{:S(2)}) collective-permute-start(bf16[128,128]{1,0:T(8,128)(2,1)S(1)} %get-tuple-element.48), channel_id=1, source_target_pairs={{48,0},{16,8},{56,16},{24,24},{32,32},{0,40},{40,48},{8,56},{112,6... | collective-permute-start | bytes 98312 | tf_op jit(solution)/shard_map/upstream_to_units/ppermute | solution.py:410
  68.4 10.6 %collective-permute-start.7 = (bf16[14,128,128]{2,1,0:T(8,128)(2,1)S(1)}, bf16[14,128,128]{2,1,0:T(8,128)(2,1)S(1)}, u32[]{:S(2)}, u32[]{:S(2)}) collective-permute-start(bf16[14,128,128]{2,1,0:T(8,128)(2,1)S(1)} %get-tuple-element.80), channel_id=1, source_target_pairs={{64,0},{72,8},{80,16},{88,24},{96,32},{104,40},{112,48},{120,56},{... | collective-permute-start | bytes 1376264 | tf_op jit(solution)/shard_map/halos/ppermute | solution.py:410
  71.1 12.0 %collective-permute-start.6 = (bf16[14,128,128]{2,1,0:T(8,128)(2,1)S(1)}, bf16[14,128,128]{2,1,0:T(8,128)(2,1)S(1)}, u32[]{:S(2)}, u32[]{:S(2)}) collective-permute-start(bf16[14,128,128]{2,1,0:T(8,128)(2,1)S(1)} %get-tuple-element.81), channel_id=1, source_target_pairs={{0,64},{8,72},{16,80},{24,88},{32,96},{40,104},{48,112},{56,120},{... | collective-permute-start | bytes 1376264 | tf_op jit(solution)/shard_map/halos/ppermute | solution.py:410
  93.3 21.2 %collective-permute-start.8 = (bf16[2,7,128,128]{3,2,1,0:T(8,128)(2,1)S(1)}, bf16[2,7,128,128]{3,2,1,0:T(8,128)(2,1)S(1)}, u32[]{:S(2)}, u32[]{:S(2)}) collective-permute-start(bf16[2,7,128,128]{3,2,1,0:T(8,128)(2,1)S(1)} %get-tuple-element.56), channel_id=1, source_target_pairs={{0,64},{8,72},{16,80},{24,88},{32,96},{40,104},{48,112},{56,120},{... | collective-permute-start | bytes 1376264 | tf_op jit(solution)/shard_map/terms/ppermute | solution.py:410
  94.6 19.9 %collective-permute-start.9 = (bf16[2,7,128,128]{3,2,1,0:T(8,128)(2,1)S(1)}, bf16[2,7,128,128]{3,2,1,0:T(8,128)(2,1)S(1)}, u32[]{:S(2)}, u32[]{:S(2)}) collective-permute-start(bf16[2,7,128,128]{3,2,1,0:T(8,128)(2,1)S(1)} %get-tuple-element.57), channel_id=1, source_target_pairs={{64,0},{72,8},{80,16},{88,24},{96,32},{104,40},{112,48},{120,56},{... | collective-permute-start | bytes 1376264 | tf_op jit(solution)/shard_map/terms/ppermute | solution.py:410
  99.1 11.7 %collective-permute-start.10 = (bf16[2,2,128,128]{3,2,1,0:T(8,128)(2,1)S(1)}, bf16[2,2,128,128]{3,2,1,0:T(8,128)(2,1)S(1)}, u32[]{:S(2)}, u32[]{:S(2)}) collective-permute-start(bf16[2,2,128,128]{3,2,1,0:T(8,128)(2,1)S(1)} %get-tuple-element.58), channel_id=1, source_target_pairs={{0,0},{8,56},{16,8},{24,32},{32,16},{40,40},{48,24},{56,48},{64,64... | collective-permute-start | bytes 393224 | tf_op jit(solution)/shard_map/terms/ppermute | solution.py:410
  102.8 11.7 %collective-permute-start.11 = (bf16[2,2,128,128]{3,2,1,0:T(8,128)(2,1)S(1)}, bf16[2,2,128,128]{3,2,1,0:T(8,128)(2,1)S(1)}, u32[]{:S(2)}, u32[]{:S(2)}) collective-permute-start(bf16[2,2,128,128]{3,2,1,0:T(8,128)(2,1)S(1)} %get-tuple-element.59), channel_id=1, source_target_pairs={{0,32},{8,24},{16,40},{24,0},{32,48},{40,8},{48,56},{56,16},{64,96... | collective-permute-start | bytes 393224 | tf_op jit(solution)/shard_map/terms/ppermute | solution.py:410
  103.9 17.2 %collective-permute-start.14 = (bf16[2,2,128,128]{3,2,1,0:T(8,128)(2,1)S(1)}, bf16[2,2,128,128]{3,2,1,0:T(8,128)(2,1)S(1)}, u32[]{:S(2)}, u32[]{:S(2)}) collective-permute-start(bf16[2,2,128,128]{3,2,1,0:T(8,128)(2,1)S(1)} %get-tuple-element.67), channel_id=1, source_target_pairs={{0,8},{8,32},{16,16},{24,40},{32,24},{40,48},{48,0},{56,56},{64,72... | collective-permute-start | bytes 393224 | tf_op jit(solution)/shard_map/terms/ppermute | solution.py:410
  110.8 10.2 %collective-permute-start.15 = (bf16[2,2,128,128]{3,2,1,0:T(8,128)(2,1)S(1)}, bf16[2,2,128,128]{3,2,1,0:T(8,128)(2,1)S(1)}, u32[]{:S(2)}, u32[]{:S(2)}) collective-permute-start(bf16[2,2,128,128]{3,2,1,0:T(8,128)(2,1)S(1)} %get-tuple-element.68), channel_id=1, source_target_pairs={{0,40},{8,0},{16,48},{24,8},{32,56},{40,16},{48,32},{56,24},{64,10... | collective-permute-start | bytes 393224 | tf_op jit(solution)/shard_map/terms/ppermute | solution.py:410
  114.5 7.1 %collective-permute-start.12 = (bf16[2,2,128,128]{3,2,1,0:T(8,128)(2,1)S(1)}, bf16[2,2,128,128]{3,2,1,0:T(8,128)(2,1)S(1)}, u32[]{:S(2)}, u32[]{:S(2)}) collective-permute-start(bf16[2,2,128,128]{3,2,1,0:T(8,128)(2,1)S(1)} %get-tuple-element.65), channel_id=1, source_target_pairs={{0,8},{8,16},{16,24},{24,32},{32,40},{40,48},{48,56},{64,72},{72,8... | collective-permute-start | bytes 393224 | tf_op jit(solution)/shard_map/terms/ppermute | solution.py:410
  119.1 7.3 %collective-permute-start.13 = (bf16[2,2,128,128]{3,2,1,0:T(8,128)(2,1)S(1)}, bf16[2,2,128,128]{3,2,1,0:T(8,128)(2,1)S(1)}, u32[]{:S(2)}, u32[]{:S(2)}) collective-permute-start(bf16[2,2,128,128]{3,2,1,0:T(8,128)(2,1)S(1)} %get-tuple-element.66), channel_id=1, source_target_pairs={{8,0},{16,8},{24,16},{32,24},{40,32},{48,40},{56,48},{72,64},{80,7... | collective-permute-start | bytes 393224 | tf_op jit(solution)/shard_map/terms/ppermute | solution.py:410
  127.1 19.6 %collective-permute-start.16 = (bf16[2,2,128,128]{3,2,1,0:T(8,128)(2,1)S(1)}, bf16[2,2,128,128]{3,2,1,0:T(8,128)(2,1)S(1)}, u32[]{:S(2)}, u32[]{:S(2)}) collective-permute-start(bf16[2,2,128,128]{3,2,1,0:T(8,128)(2,1)S(1)} %get-tuple-element.74), channel_id=1, source_target_pairs={{0,0},{8,56},{16,8},{24,32},{32,16},{40,40},{48,24},{56,48},{64,64... | collective-permute-start | bytes 393224 | tf_op jit(solution)/shard_map/outputs_home/ppermute | solution.py:410
  130.9 19.8 %collective-permute-start.17 = (bf16[2,2,128,128]{3,2,1,0:T(8,128)(2,1)S(1)}, bf16[2,2,128,128]{3,2,1,0:T(8,128)(2,1)S(1)}, u32[]{:S(2)}, u32[]{:S(2)}) collective-permute-start(bf16[2,2,128,128]{3,2,1,0:T(8,128)(2,1)S(1)} %get-tuple-element.75), channel_id=1, source_target_pairs={{0,32},{8,24},{16,40},{24,0},{32,48},{40,8},{48,56},{56,16},{64,96... | collective-permute-start | bytes 393224 | tf_op jit(solution)/shard_map/outputs_home/ppermute | solution.py:410
  138.3 12.4 %collective-permute-start.18 = (bf16[2,2,128,128]{3,2,1,0:T(8,128)(2,1)S(1)}, bf16[2,2,128,128]{3,2,1,0:T(8,128)(2,1)S(1)}, u32[]{:S(2)}, u32[]{:S(2)}) collective-permute-start(bf16[2,2,128,128]{3,2,1,0:T(8,128)(2,1)S(1)} %get-tuple-element.76), channel_id=1, source_target_pairs={{0,8},{8,32},{16,16},{24,40},{32,24},{40,48},{48,0},{56,56},{64,72... | collective-permute-start | bytes 393224 | tf_op jit(solution)/shard_map/outputs_home/ppermute | solution.py:410
  145.2 6.1 %collective-permute-start.19 = (bf16[2,2,128,128]{3,2,1,0:T(8,128)(2,1)S(1)}, bf16[2,2,128,128]{3,2,1,0:T(8,128)(2,1)S(1)}, u32[]{:S(2)}, u32[]{:S(2)}) collective-permute-start(bf16[2,2,128,128]{3,2,1,0:T(8,128)(2,1)S(1)} %get-tuple-element.77), channel_id=1, source_target_pairs={{0,40},{8,0},{16,48},{24,8},{32,56},{40,16},{48,32},{56,24},{64,10... | collective-permute-start | bytes 393224 | tf_op jit(solution)/shard_map/outputs_home/ppermute | solution.py:410
  145.3 9.5 %collective-permute-start.20 = (bf16[4,128,128]{2,1,0:T(8,128)(2,1)S(1)}, bf16[4,128,128]{2,1,0:T(8,128)(2,1)S(1)}, u32[]{:S(2)}, u32[]{:S(2)}) collective-permute-start(bf16[4,128,128]{2,1,0:T(8,128)(2,1)S(1)} %get-tuple-element.78), channel_id=1, source_target_pairs={{0,16},{8,48},{16,24},{24,56},{32,0},{40,32},{48,8},{56,40},{64,80... | collective-permute-start | bytes 393224 | tf_op jit(solution)/shard_map/outputs_home/ppermute | solution.py:410
  146.7 10.8 %collective-permute-start.21 = (bf16[4,128,128]{2,1,0:T(8,128)(2,1)S(1)}, bf16[4,128,128]{2,1,0:T(8,128)(2,1)S(1)}, u32[]{:S(2)}, u32[]{:S(2)}) collective-permute-start(bf16[4,128,128]{2,1,0:T(8,128)(2,1)S(1)} %get-tuple-element.79), channel_id=1, source_target_pairs={{0,48},{8,16},{16,56},{24,24},{32,32},{40,0},{48,40},{56,8},{64,11... | collective-permute-start | bytes 393224 | tf_op jit(solution)/shard_map/outputs_home/ppermute | solution.py:410

commit v4 on v3

--- a/solution.py
+++ b/solution.py
@@ -37,13 +37,14 @@
     return route(step)
 
 
+def first_of(which, odd):
+    return (3 * odd, 2 - odd, 4 - 4 * odd)[which]
+
+
 def owner_of(which, turn):
     def step(strip, slot):
         odd = slot % 2
-        if which == 2:
-            unit = 5 * slot + (0 if odd else 4)
-        else:
-            unit = 5 * slot + odd + 2 * which
+        unit = 5 * slot + first_of(which, odd)
         return (strip, ((turn + odd) % 2) * 4 + (unit % 8) // 2)
 
     return route(step)
@@ -80,7 +81,7 @@
             if which == 2:
                 unit = 10 * ((pair + 2) % 4) + 4
             elif (row + turn) % 2:
-                unit = 10 * ((pair - 3 - which) % 4) + 6 + 2 * which
+                unit = 10 * ((pair - 3 * which) % 4) + 8 - 2 * which
             else:
                 unit = 10 * ((pair - which) % 4) + 2 * which
             heads.append(unit // 8)
@@ -131,7 +132,8 @@
 
 
 def gather_kernel(table, *refs):
-    firsts, seconds, singles, outs, single = refs[:4], refs[4:8], refs[8:10], refs[10:14], refs[14]
+    early, free, late, singles = refs[:2], refs[2:4], refs[4:6], refs[6:8]
+    outs, single = refs[8:12], refs[12]
     line = lax.broadcasted_iota(jnp.int32, (2 * TILE, 2 * TILE), 0)
     col = lax.broadcasted_iota(jnp.int32, (2 * TILE, 2 * TILE), 1)
     source = ((line >> 2) & 1) * TILE + (line >> 3) * 4 + (line & 3)
@@ -139,7 +141,8 @@
     for kind, out in enumerate(outs):
         for at in range(4):
             head = pl.multiple_of(table[at] * HEAD_DIM, HEAD_DIM)
-            tiles = (firsts, seconds)[kind // 2][at][kind % 2].reshape(2 * TILE, HEAD_DIM)
+            edge = (early, late)[kind // 2][at % 2].at[kind % 2]
+            tiles = (edge[...] if at < 2 else free[at % 2][kind]).reshape(2 * TILE, HEAD_DIM)
             out[:, pl.ds(head, HEAD_DIM)] = nn(order, tiles).astype(LOW)
         flip = table[6] == 1
         one, two = singles[0][kind], singles[1][kind]
@@ -149,16 +152,16 @@
         out[:, pl.ds(head, HEAD_DIM)] = nn(order, single[...]).astype(LOW)
 
 
-def gather(table, first, second):
+def gather(table, received):
     return pl.pallas_call(
         gather_kernel,
         out_shape=[jax.ShapeDtypeStruct((2 * TILE, HEADS_HERE * HEAD_DIM), LOW)] * 4,
-        in_specs=[pl.BlockSpec(memory_space=pltpu.SMEM)] + whole(10),
+        in_specs=[pl.BlockSpec(memory_space=pltpu.SMEM)] + whole(8),
         out_specs=whole(4),
         scratch_shapes=[pltpu.VMEM((2 * TILE, HEAD_DIM), LOW)],
         compiler_params=pltpu.CompilerParams(vmem_limit_bytes=16 << 20),
         name="gather",
-    )(table, *first, *second)
+    )(table, *received)
 
 
 def deal_kernel(swapped, out):
@@ -186,21 +189,13 @@
     )(swapped)
 
 
-def send_pairs(odd, held, outs):
-    for out, (which, turn) in zip(outs, OWNER_STEPS):
-        row = (turn + odd) % 2
-        for kind in range(2):
-            for part in range(2):
-                out[kind, part] = held[kind, row, odd + 2 * which + part]
-
-
-def pair_shapes():
-    return [jax.ShapeDtypeStruct((2, 2, TILE, HEAD_DIM), LOW)] * 4
+def pair_shapes(kinds, count):
+    return [jax.ShapeDtypeStruct((kinds, 2, TILE, HEAD_DIM), LOW)] * count
 
 
 def attend_kernel(table, own, above, below, *refs):
-    grads, firsts, rest, terms, edges = refs[:6], refs[6:10], refs[10], refs[11], refs[12:14]
-    pair, turned, grad, total, held = refs[14:]
+    grads, firsts, rest, terms, edges = refs[:6], refs[6:8], refs[8], refs[9], refs[10:12]
+    pair, turned, grad, total, held = refs[12:]
     strip, odd = table[7], table[8]
     scaling = HEAD_DIM**-0.5
     rate = scaling * math.log2(math.e)
@@ -217,11 +212,12 @@
                 turned[kind, at, row] = pair[kind, at, row].T
     for at, (which, turn) in enumerate(OWNER_STEPS):
         row = (turn + odd) % 2
+        first = first_of(which, odd)
         if which == 2:
-            grad[row, 4 - 4 * odd] = grads[at][...]
+            grad[row, first] = grads[at][...]
         else:
             for part in range(2):
-                grad[row, odd + 2 * which + part] = grads[at][part]
+                grad[row, first + part] = grads[at][part]
     total[...] = jnp.zeros_like(total)
 
     def one_unit(unit, carry):
@@ -314,10 +310,13 @@
         return carry
 
     lax.fori_loop(0, 5, one_unit, 0)
-    send_pairs(odd, held, firsts)
     for kind in range(2):
-        for row in range(2):
-            rest[kind, row] = held[kind, row, 4 - 4 * odd]
+        for turn in range(2):
+            row = (turn + odd) % 2
+            for part in range(2):
+                firsts[turn][kind, part] = held[kind, row, first_of(0, odd) + part]
+                rest[kind, turn, part] = held[kind, row, first_of(1, odd) + part]
+            rest[kind, turn, 2] = held[kind, row, first_of(2, odd)]
     for kind, factor in ((0, scaling), (1, 1.0)):
         for at in range(7):
             for row in range(2):
@@ -332,15 +331,15 @@
 def attend(table, own, halos, grads):
     return pl.pallas_call(
         attend_kernel,
-        out_shape=pair_shapes()
+        out_shape=pair_shapes(2, 2)
         + [
-            jax.ShapeDtypeStruct((2, 2, TILE, HEAD_DIM), LOW),
+            jax.ShapeDtypeStruct((2, 2, 3, TILE, HEAD_DIM), LOW),
             jax.ShapeDtypeStruct((2, 2, 7, TILE, HEAD_DIM), WIDE),
             jax.ShapeDtypeStruct((2, 7, TILE, HEAD_DIM), LOW),
             jax.ShapeDtypeStruct((2, 7, TILE, HEAD_DIM), LOW),
         ],
         in_specs=[pl.BlockSpec(memory_space=pltpu.SMEM)] + whole(9),
-        out_specs=whole(8),
+        out_specs=whole(6),
         scratch_shapes=[
             pltpu.VMEM((2, 7, 4, TILE, HEAD_DIM), LOW),
             pltpu.VMEM((2, 7, 4, HEAD_DIM, TILE), LOW),
@@ -356,51 +355,63 @@
     )(table, own, *halos, *grads)
 
 
-def rims_kernel(terms, above, below, right, left):
+def rims_kernel(table, rest, terms, above, below, right, left, *outs):
+    odd = table[8]
+    edges = (above, below)
     for kind in range(2):
-        for row, edge in enumerate((above, below)):
+        for row, edge in enumerate(edges):
             for out, at in ((right, 6), (left, 0)):
                 out[kind, row] = (terms[kind, row, at] + edge[kind, at].astype(WIDE)).astype(LOW)
-
-
-def rims(terms, edges):
+    for turn in range(2):
+        for part in range(2):
+            at = first_of(1, odd) + part + 1
+            for kind in range(2):
+                outs[turn][kind, part] = rest[kind, turn, part]
+                flip = (turn + odd) % 2 == 1
+                edge = jnp.where(flip, below[kind, at], above[kind, at])
+                value = terms[kind, (turn + odd) % 2, at] + edge.astype(WIDE)
+                outs[turn][2 + kind, part] = value.astype(LOW)
+
+
+def rims(table, rest, terms, edges):
     return pl.pallas_call(
         rims_kernel,
-        out_shape=column_shapes(),
-        in_specs=whole(3),
-        out_specs=whole(2),
+        out_shape=column_shapes() + pair_shapes(4, 2),
+        in_specs=[pl.BlockSpec(memory_space=pltpu.SMEM)] + whole(4),
+        out_specs=whole(4),
         compiler_params=pltpu.CompilerParams(vmem_limit_bytes=16 << 20),
         name="rims",
-    )(terms, *edges)
-
-
-def combine_kernel(table, rest, terms, *refs):
-    edges, columns, outs, held = refs[:2], refs[2:4], refs[4:10], refs[10]
+    )(table, rest, terms, *edges)
+
+
+def combine_kernel(table, rest, terms, above, below, before, after, *outs):
     odd = table[8]
-    for kind in range(2):
-        for row in range(2):
-            for at in range(5):
-                value = terms[kind, row, at + 1] + edges[row][kind, at + 1].astype(WIDE)
-                if at == 0:
-                    value = value + columns[0][kind, row].astype(WIDE)
-                if at == 4:
-                    value = value + columns[1][kind, row].astype(WIDE)
-                held[kind, row, at] = value.astype(LOW)
-    send_pairs(odd, held, outs[:4])
+    flipped = odd == 1
     for turn in range(2):
         row = (turn + odd) % 2
         for kind in range(2):
-            outs[4 + turn][kind] = rest[kind, row]
-            outs[4 + turn][2 + kind] = held[kind, row, 4 - 4 * odd]
+
+            def summed(at):
+                edge = jnp.where(row == 1, below[kind, at + 1], above[kind, at + 1])
+                return terms[kind, row, at + 1] + edge.astype(WIDE)
+
+            first = first_of(0, odd)
+            left = before[kind, row].astype(WIDE)
+            right = after[kind, row].astype(WIDE)
+            one, two = summed(first), summed(first + 1)
+            outs[turn][kind, 0] = jnp.where(flipped, one, one + left).astype(LOW)
+            outs[turn][kind, 1] = jnp.where(flipped, two + right, two).astype(LOW)
+            alone = summed(first_of(2, odd)) + jnp.where(flipped, left, right)
+            outs[2 + turn][kind] = rest[kind, turn, 2]
+            outs[2 + turn][2 + kind] = alone.astype(LOW)
 
 
 def combine(table, rest, terms, edges, columns):
     return pl.pallas_call(
         combine_kernel,
-        out_shape=pair_shapes() + [jax.ShapeDtypeStruct((4, TILE, HEAD_DIM), LOW)] * 2,
+        out_shape=pair_shapes(2, 2) + [jax.ShapeDtypeStruct((4, TILE, HEAD_DIM), LOW)] * 2,
         in_specs=[pl.BlockSpec(memory_space=pltpu.SMEM)] + whole(6),
-        out_specs=whole(6),
-        scratch_shapes=[pltpu.VMEM((2, 2, 5, TILE, HEAD_DIM), LOW)],
+        out_specs=whole(4),
         compiler_params=pltpu.CompilerParams(vmem_limit_bytes=16 << 20),
         name="combine",
     )(table, rest, terms, *edges, *columns)
@@ -434,18 +445,21 @@
     with jax.named_scope("halos"):
         halos = send_all([own[1, 5:], own[0, 5:]], row_routes)
     with jax.named_scope("attention"):
-        *first, rest, terms, above, below = attend(place, own, halos, early + late)
-    with jax.named_scope("terms"):
+        *edge_pairs, rest, terms, above, below = attend(place, own, halos, early + late)
+    with jax.named_scope("row_terms"):
         edges = send_all([above, below], row_routes)
-        early = send_all(first[:2], to_owner[:2])
+        early = send_all(edge_pairs, to_owner[:2])
         edges, early = lax.optimization_barrier((edges, early))
-        columns = send_all(rims(terms, edges), column_routes)
-        late = send_all(first[2:], to_owner[2:])
-        columns, late = lax.optimization_barrier((columns, late))
+    with jax.named_scope("column_terms"):
+        right, left, *free = rims(place, rest, terms, edges)
+        columns = send_all([right, left], column_routes)
+        free = send_all(free, to_owner[2:4])
     with jax.named_scope("outputs_home"):
-        second = send_all(combine(place, rest, terms, edges, columns), to_owner)
+        leaving = combine(place, rest, terms, edges, columns)
+        leaving, free = lax.optimization_barrier((leaving, free))
+        late = send_all(leaving, to_owner[:2] + to_owner[4:])
     with jax.named_scope("settle"):
-        return tuple(gather(place, early + late, second))
+        return tuple(gather(place, early + free + late))
 
 
 def solution(mesh):

time: 160 us -> 159 us (level)
  the two profiles are of different devices: /device:TPU:60 before, /device:TPU:40 now
where the time goes in v4:
time: 159 us
  starting transfers between devices  73.6 us (46%)
  waiting for transfers between devices  64 us (40%)
  Pallas kernels  15.8 us (10%)
  local copies, waits for them, and re-layouts  3.23 us (2%)
    ppermute x20, starting transfers between devices, send_all(): lax.ppermute(part, 'tile', path)  60.6 us
    ppermute x20, waiting for transfers between devices, send_all(): lax.ppermute(part, 'tile', path)  38.4 us
    all_to_all x1, waiting for transfers between devices, local(): got = lax.all_to_all(dealt, 'tile', 0, 0, tiled=True)  23.2 us
    pallas_call x1, Pallas kernels, attend(): pl.pallas_call(attend_kernel, out_shape=pair_shapes(2, 2) + [jax.ShapeDty...  10.1 us
    all_to_all x1, starting transfers between devices, local(): got = lax.all_to_all(dealt, 'tile', 0, 0, tiled=True)  8.62 us
    all_to_all x1, starting transfers between devices, local(): swapped = lax.all_to_all(jnp.stack(lines, axis=1), 'head', 0, 0, tiled=True)  4.43 us
  transfers between devices with their start and end apart: 22, of which 14 were waited for; matrix products, arithmetic and copies ran while one was open for 1% of the time, Pallas kernels for 2%

profile of v4, /device:TPU:40, one launch (start us, length us, event | category | flops | bytes accessed | tf_op | source)
XLA Modules:
  0.0 158.7 jit_solution(16388489153413036308)
XLA Ops:
  0.7 1.2 reshape.32
  1.8 0.1 copy.9
  2.0 0.1 reshape.34
  2.1 0.1 copy.10
  2.2 0.1 reshape.36
  2.4 0.1 copy.11
  2.5 1.1 pad_maximum_fusion
  3.6 4.4 %all-to-all-start = ((bf16[8,3,5,32,128]{4,3,2,1,0:T(8,128)(2,1)}), bf16[8,3,5,32,128]{4,3,2,1,0:T(8,128)(2,1)S(1)}, u32[]{:S(2)}, u32[]{:S(2)}) async-start(bf16[8,3,5,32,128]{4,3,2,1,0:T(8,128)(2,1)} %pad_maximum_fusion), calls=%async_computation | async-start | bytes 1966080 | tf_op jit(solution)/shard_map/heads/all_to_all | solution.py:438
  8.0 0.7 dynamic-slice_bitcast_fusion.table
  8.7 0.9 spread.1
  9.6 3.8 %collective-permute-start = (bf16[2,128,128]{2,1,0:T(8,128)(2,1)S(1)}, bf16[2,128,128]{2,1,0:T(8,128)(2,1)S(1)}, u32[]{:S(2)}, u32[]{:S(2)}) collective-permute-start(bf16[2,128,128]{2,1,0:T(8,128)(2,1)S(1)} %get-tuple-element.42), channel_id=1, source_target_pairs={{0,0},{32,8},{8,16},{40,24},{16,32},{48,40},{24,48},{56,56},{64,64... | collective-permute-start | bytes 196616 | tf_op jit(solution)/shard_map/upstream_to_units/ppermute | solution.py:421
  13.5 5.5 %collective-permute-start.1 = (bf16[2,128,128]{2,1,0:T(8,128)(2,1)S(1)}, bf16[2,128,128]{2,1,0:T(8,128)(2,1)S(1)}, u32[]{:S(2)}, u32[]{:S(2)}) collective-permute-start(bf16[2,128,128]{2,1,0:T(8,128)(2,1)S(1)} %get-tuple-element.43), channel_id=1, source_target_pairs={{32,0},{0,8},{40,16},{8,24},{48,32},{16,40},{56,48},{24,56},{96,64... | collective-permute-start | bytes 196616 | tf_op jit(solution)/shard_map/upstream_to_units/ppermute | solution.py:421
  18.9 1.9 %collective-permute-start.2 = (bf16[2,128,128]{2,1,0:T(8,128)(2,1)S(1)}, bf16[2,128,128]{2,1,0:T(8,128)(2,1)S(1)}, u32[]{:S(2)}, u32[]{:S(2)}) collective-permute-start(bf16[2,128,128]{2,1,0:T(8,128)(2,1)S(1)} %get-tuple-element.44), channel_id=1, source_target_pairs={{8,0},{56,8},{16,16},{32,24},{24,32},{40,40},{0,48},{48,56},{72,64... | collective-permute-start | bytes 196616 | tf_op jit(solution)/shard_map/upstream_to_units/ppermute | solution.py:421
  20.8 2.4 %all-to-all-done.swapped = bf16[8,3,5,32,128]{4,3,2,1,0:T(8,128)(2,1)S(1)} async-done(((bf16[8,3,5,32,128]{4,3,2,1,0:T(8,128)(2,1)}), bf16[8,3,5,32,128]{4,3,2,1,0:T(8,128)(2,1)S(1)}, u32[]{:S(2)}, u32[]{:S(2)}) %all-to-all-start) | async-done | bytes 983072 | tf_op jit(solution)/shard_map/heads/all_to_all | solution.py:438
  23.3 1.2 deal.1
  24.5 2.6 %collective-permute-done.2.refs_2_ = bf16[2,128,128]{2,1,0:T(8,128)(2,1)S(1)} collective-permute-done((bf16[2,128,128]{2,1,0:T(8,128)(2,1)S(1)}, bf16[2,128,128]{2,1,0:T(8,128)(2,1)S(1)}, u32[]{:S(2)}, u32[]{:S(2)}) %collective-permute-start.2) | collective-permute-done | bytes 65568 | tf_op jit(solution)/shard_map/upstream_to_units/ppermute | solution.py:421
  27.2 8.6 %all-to-all-start.1 = ((bf16[32,19,8,128]{3,2,1,0:T(8,128)(2,1)}), bf16[32,19,8,128]{3,2,1,0:T(8,128)(2,1)S(1)}, u32[]{:S(2)}, u32[]{:S(2)}) async-start(bf16[32,19,8,128]{3,2,1,0:T(8,128)(2,1)} %deal.1), calls=%async_computation.1 | async-start | bytes 2490368 | tf_op jit(solution)/shard_map/tiles/all_to_all | solution.py:441
  35.8 4.5 %collective-permute-start.3 = (bf16[2,128,128]{2,1,0:T(8,128)(2,1)S(1)}, bf16[2,128,128]{2,1,0:T(8,128)(2,1)S(1)}, u32[]{:S(2)}, u32[]{:S(2)}) collective-permute-start(bf16[2,128,128]{2,1,0:T(8,128)(2,1)S(1)} %get-tuple-element.46), channel_id=1, source_target_pairs={{40,0},{24,8},{48,16},{0,24},{56,32},{8,40},{32,48},{16,56},{104,6... | collective-permute-start | bytes 196616 | tf_op jit(solution)/shard_map/upstream_to_units/ppermute | solution.py:421
  40.4 1.5 collective-permute-start.4
  41.8 2.5 %collective-permute-start.5 = (bf16[128,128]{1,0:T(8,128)(2,1)S(1)}, bf16[128,128]{1,0:T(8,128)(2,1)S(1)}, u32[]{:S(2)}, u32[]{:S(2)}) collective-permute-start(bf16[128,128]{1,0:T(8,128)(2,1)S(1)} %get-tuple-element.48), channel_id=1, source_target_pairs={{48,0},{16,8},{56,16},{24,24},{32,32},{0,40},{40,48},{8,56},{112,6... | collective-permute-start | bytes 98312 | tf_op jit(solution)/shard_map/upstream_to_units/ppermute | solution.py:421
  44.3 23.2 %all-to-all-done.1 = bf16[32,19,8,128]{3,2,1,0:T(8,128)(2,1)S(1)} async-done(((bf16[32,19,8,128]{3,2,1,0:T(8,128)(2,1)}), bf16[32,19,8,128]{3,2,1,0:T(8,128)(2,1)S(1)}, u32[]{:S(2)}, u32[]{:S(2)}) %all-to-all-start.1) | async-done | bytes 1245216 | tf_op jit(solution)/shard_map/tiles/all_to_all | solution.py:441
  67.5 0.7 copy.12
  68.2 1.6 collective-permute-done.4.refs_4_
  69.8 3.1 %collective-permute-start.7 = (bf16[14,128,128]{2,1,0:T(8,128)(2,1)S(1)}, bf16[14,128,128]{2,1,0:T(8,128)(2,1)S(1)}, u32[]{:S(2)}, u32[]{:S(2)}) collective-permute-start(bf16[14,128,128]{2,1,0:T(8,128)(2,1)S(1)} %get-tuple-element.80), channel_id=1, source_target_pairs={{64,0},{72,8},{80,16},{88,24},{96,32},{104,40},{112,48},{120,56},{... | collective-permute-start | bytes 1376264 | tf_op jit(solution)/shard_map/halos/ppermute | solution.py:421
  73.0 2.7 %collective-permute-start.6 = (bf16[14,128,128]{2,1,0:T(8,128)(2,1)S(1)}, bf16[14,128,128]{2,1,0:T(8,128)(2,1)S(1)}, u32[]{:S(2)}, u32[]{:S(2)}) collective-permute-start(bf16[14,128,128]{2,1,0:T(8,128)(2,1)S(1)} %get-tuple-element.81), channel_id=1, source_target_pairs={{0,64},{8,72},{16,80},{24,88},{32,96},{40,104},{48,112},{56,120},{... | collective-permute-start | bytes 1376264 | tf_op jit(solution)/shard_map/halos/ppermute | solution.py:421
  75.7 6.3 %collective-permute-done.7.below = bf16[14,128,128]{2,1,0:T(8,128)(2,1)S(1)} collective-permute-done((bf16[14,128,128]{2,1,0:T(8,128)(2,1)S(1)}, bf16[14,128,128]{2,1,0:T(8,128)(2,1)S(1)}, u32[]{:S(2)}, u32[]{:S(2)}) %collective-permute-start.7) | collective-permute-done | bytes 458784 | tf_op jit(solution)/shard_map/halos/ppermute | solution.py:421
  82.0 2.2 %collective-permute-done.6.above = bf16[14,128,128]{2,1,0:T(8,128)(2,1)S(1)} collective-permute-done((bf16[14,128,128]{2,1,0:T(8,128)(2,1)S(1)}, bf16[14,128,128]{2,1,0:T(8,128)(2,1)S(1)}, u32[]{:S(2)}, u32[]{:S(2)}) %collective-permute-start.6) | collective-permute-done | bytes 458784 | tf_op jit(solution)/shard_map/halos/ppermute | solution.py:421
  84.2 10.1 %attend.1 = (bf16[2,2,128,128]{3,2,1,0:T(8,128)(2,1)S(1)}, bf16[2,2,128,128]{3,2,1,0:T(8,128)(2,1)S(1)}, bf16[2,2,3,128,128]{4,3,2,1,0:T(8,128)(2,1)S(1)}, f32[2...) custom-call(s32[14]{0:T(128)S(1)} %dynamic-slice_bitcast_fusion.table, ...), custom_call_target="tpu_custom_call" | custom-call | flops 3000000000 | bytes 8000000 | tf_op jit(solution)/shard_map/attention/attend/pallas_call | solution.py:332
  94.3 3.4 %collective-permute-start.8 = (bf16[2,7,128,128]{3,2,1,0:T(8,128)(2,1)S(1)}, bf16[2,7,128,128]{3,2,1,0:T(8,128)(2,1)S(1)}, u32[]{:S(2)}, u32[]{:S(2)}) collective-permute-start(bf16[2,7,128,128]{3,2,1,0:T(8,128)(2,1)S(1)} %get-tuple-element.56), channel_id=1, source_target_pairs={{0,64},{8,72},{16,80},{24,88},{32,96},{40,104},{48,112},{56,120},{... | collective-permute-start | bytes 1376264 | tf_op jit(solution)/shard_map/row_terms/ppermute | solution.py:421
  97.7 2.5 %collective-permute-start.9 = (bf16[2,7,128,128]{3,2,1,0:T(8,128)(2,1)S(1)}, bf16[2,7,128,128]{3,2,1,0:T(8,128)(2,1)S(1)}, u32[]{:S(2)}, u32[]{:S(2)}) collective-permute-start(bf16[2,7,128,128]{3,2,1,0:T(8,128)(2,1)S(1)} %get-tuple-element.57), channel_id=1, source_target_pairs={{64,0},{72,8},{80,16},{88,24},{96,32},{104,40},{112,48},{120,56},{... | collective-permute-start | bytes 1376264 | tf_op jit(solution)/shard_map/row_terms/ppermute | solution.py:421
  100.2 4.5 %collective-permute-start.10 = (bf16[2,2,128,128]{3,2,1,0:T(8,128)(2,1)S(1)}, bf16[2,2,128,128]{3,2,1,0:T(8,128)(2,1)S(1)}, u32[]{:S(2)}, u32[]{:S(2)}) collective-permute-start(bf16[2,2,128,128]{3,2,1,0:T(8,128)(2,1)S(1)} %get-tuple-element.58), channel_id=1, source_target_pairs={{0,0},{8,32},{16,8},{24,40},{32,16},{40,48},{48,24},{56,56},{64,64... | collective-permute-start | bytes 393224 | tf_op jit(solution)/shard_map/row_terms/ppermute | solution.py:421
  104.8 3.6 %collective-permute-done.10.refs_0_ = bf16[2,2,128,128]{3,2,1,0:T(8,128)(2,1)S(1)} collective-permute-done((bf16[2,2,128,128]{3,2,1,0:T(8,128)(2,1)S(1)}, bf16[2,2,128,128]{3,2,1,0:T(8,128)(2,1)S(1)}, u32[]{:S(2)}, u32[]{:S(2)}) %collective-permute-start.10) | collective-permute-done | bytes 131104 | tf_op jit(solution)/shard_map/row_terms/ppermute | solution.py:421
  108.4 2.3 %collective-permute-done.11.refs_1_ = bf16[2,2,128,128]{3,2,1,0:T(8,128)(2,1)S(1)} collective-permute-done((bf16[2,2,128,128]{3,2,1,0:T(8,128)(2,1)S(1)}, bf16[2,2,128,128]{3,2,1,0:T(8,128)(2,1)S(1)}, u32[]{:S(2)}, u32[]{:S(2)}) %collective-permute-start.11) | collective-permute-done | bytes 131104 | tf_op jit(solution)/shard_map/row_terms/ppermute | solution.py:421
  110.7 0.7 rims.1
  111.4 5.0 %collective-permute-start.14 = (bf16[4,2,128,128]{3,2,1,0:T(8,128)(2,1)S(1)}, bf16[4,2,128,128]{3,2,1,0:T(8,128)(2,1)S(1)}, u32[]{:S(2)}, u32[]{:S(2)}) collective-permute-start(bf16[4,2,128,128]{3,2,1,0:T(8,128)(2,1)S(1)} %get-tuple-element.72), channel_id=1, source_target_pairs={{0,8},{8,56},{16,16},{24,32},{32,24},{40,40},{48,0},{56,48},{64,72... | collective-permute-start | bytes 786440 | tf_op jit(solution)/shard_map/column_terms/ppermute | solution.py:421
  116.3 2.4 %collective-permute-start.15 = (bf16[4,2,128,128]{3,2,1,0:T(8,128)(2,1)S(1)}, bf16[4,2,128,128]{3,2,1,0:T(8,128)(2,1)S(1)}, u32[]{:S(2)}, u32[]{:S(2)}) collective-permute-start(bf16[4,2,128,128]{3,2,1,0:T(8,128)(2,1)S(1)} %get-tuple-element.73), channel_id=1, source_target_pairs={{0,40},{8,24},{16,48},{24,0},{32,56},{40,8},{48,32},{56,16},{64,10... | collective-permute-start | bytes 786440 | tf_op jit(solution)/shard_map/column_terms/ppermute | solution.py:421
  118.8 3.4 %collective-permute-start.12 = (bf16[2,2,128,128]{3,2,1,0:T(8,128)(2,1)S(1)}, bf16[2,2,128,128]{3,2,1,0:T(8,128)(2,1)S(1)}, u32[]{:S(2)}, u32[]{:S(2)}) collective-permute-start(bf16[2,2,128,128]{3,2,1,0:T(8,128)(2,1)S(1)} %get-tuple-element.66), channel_id=1, source_target_pairs={{0,8},{8,16},{16,24},{24,32},{32,40},{40,48},{48,56},{64,72},{72,8... | collective-permute-start | bytes 393224 | tf_op jit(solution)/shard_map/column_terms/ppermute | solution.py:421
  122.2 2.7 %collective-permute-start.13 = (bf16[2,2,128,128]{3,2,1,0:T(8,128)(2,1)S(1)}, bf16[2,2,128,128]{3,2,1,0:T(8,128)(2,1)S(1)}, u32[]{:S(2)}, u32[]{:S(2)}) collective-permute-start(bf16[2,2,128,128]{3,2,1,0:T(8,128)(2,1)S(1)} %get-tuple-element.67), channel_id=1, source_target_pairs={{8,0},{16,8},{24,16},{32,24},{40,32},{48,40},{56,48},{72,64},{80,7... | collective-permute-start | bytes 393224 | tf_op jit(solution)/shard_map/column_terms/ppermute | solution.py:421
  124.9 7.5 %collective-permute-done.12.before = bf16[2,2,128,128]{3,2,1,0:T(8,128)(2,1)S(1)} collective-permute-done((bf16[2,2,128,128]{3,2,1,0:T(8,128)(2,1)S(1)}, bf16[2,2,128,128]{3,2,1,0:T(8,128)(2,1)S(1)}, u32[]{:S(2)}, u32[]{:S(2)}) %collective-permute-start.12) | collective-permute-done | bytes 131104 | tf_op jit(solution)/shard_map/column_terms/ppermute | solution.py:421
  132.4 0.3 collective-permute-done.13.after
  132.7 0.7 combine.1
  133.5 5.6 %collective-permute-start.16 = (bf16[2,2,128,128]{3,2,1,0:T(8,128)(2,1)S(1)}, bf16[2,2,128,128]{3,2,1,0:T(8,128)(2,1)S(1)}, u32[]{:S(2)}, u32[]{:S(2)}) collective-permute-start(bf16[2,2,128,128]{3,2,1,0:T(8,128)(2,1)S(1)} %get-tuple-element.76), channel_id=1, source_target_pairs={{0,0},{8,32},{16,8},{24,40},{32,16},{40,48},{48,24},{56,56},{64,64... | collective-permute-start | bytes 393224 | tf_op jit(solution)/shard_map/outputs_home/ppermute | solution.py:421
  139.2 3.2 %collective-permute-start.18 = (bf16[4,128,128]{2,1,0:T(8,128)(2,1)S(1)}, bf16[4,128,128]{2,1,0:T(8,128)(2,1)S(1)}, u32[]{:S(2)}, u32[]{:S(2)}) collective-permute-start(bf16[4,128,128]{2,1,0:T(8,128)(2,1)S(1)} %get-tuple-element.78), channel_id=1, source_target_pairs={{0,16},{8,48},{16,24},{24,56},{32,0},{40,32},{48,8},{56,40},{64,80... | collective-permute-start | bytes 393224 | tf_op jit(solution)/shard_map/outputs_home/ppermute | solution.py:421
  142.4 2.1 %collective-permute-start.19 = (bf16[4,128,128]{2,1,0:T(8,128)(2,1)S(1)}, bf16[4,128,128]{2,1,0:T(8,128)(2,1)S(1)}, u32[]{:S(2)}, u32[]{:S(2)}) collective-permute-start(bf16[4,128,128]{2,1,0:T(8,128)(2,1)S(1)} %get-tuple-element.79), channel_id=1, source_target_pairs={{0,48},{8,16},{16,56},{24,24},{32,32},{40,0},{48,40},{56,8},{64,11... | collective-permute-start | bytes 393224 | tf_op jit(solution)/shard_map/outputs_home/ppermute | solution.py:421
  144.6 1.5 collective-permute-done.17.refs_5_
  146.1 2.9 %collective-permute-done.18.refs_6_ = bf16[4,128,128]{2,1,0:T(8,128)(2,1)S(1)} collective-permute-done((bf16[4,128,128]{2,1,0:T(8,128)(2,1)S(1)}, bf16[4,128,128]{2,1,0:T(8,128)(2,1)S(1)}, u32[]{:S(2)}, u32[]{:S(2)}) %collective-permute-start.18) | collective-permute-done | bytes 131104 | tf_op jit(solution)/shard_map/outputs_home/ppermute | solution.py:421
  149.0 7.5 %collective-permute-done.19.refs_7_ = bf16[4,128,128]{2,1,0:T(8,128)(2,1)S(1)} collective-permute-done((bf16[4,128,128]{2,1,0:T(8,128)(2,1)S(1)}, bf16[4,128,128]{2,1,0:T(8,128)(2,1)S(1)}, u32[]{:S(2)}, u32[]{:S(2)}) %collective-permute-start.19) | collective-permute-done | bytes 131104 | tf_op jit(solution)/shard_map/outputs_home/ppermute | solution.py:421
  156.5 2.2 %gather.1 = (bf16[256,640]{1,0:T(8,128)(2,1)}, bf16[256,640]{1,0:T(8,128)(2,1)}, bf16[256,640]{1,0:T(8,128)(2,1)}, bf16[256,640]{1,0:T(8,128)(2,1)}) custom-call(s32[14]{0:T(128)S(1)} %dynamic-slice_bitcast_fusion.table, bf16[2,2,128,128]{3,2,1,0:T(8,128)(2,1)S(1)} %collective-permute-done.10.refs_0_, ...), custom_call_target="tpu_custom_call" | custom-call | tf_op jit(solution)/shard_map/settle/gather/pallas_call | solution.py:156
  (18 shorter events, 0.4 us)
Async XLA Ops:
  0.6 1.3 copy-start.1
  0.6 1.6 %copy-start.2 = (bf16[1,8,4,5120]{3,2,1,0:T(4,128)(2,1)S(1)}, bf16[1,8,4,5120]{3,2,1,0:T(4,128)(2,1)}, u32[]{:S(2)}) copy-start(bf16[1,8,4,5120]{3,2,1,0:T(4,128)(2,1)} %param.7) | copy-start | bytes 983044
  3.6 5.1 %copy-start = (bf16[256,640]{1,0:T(8,128)(2,1)S(1)}, bf16[256,640]{1,0:T(8,128)(2,1)}, u32[]{:S(2)}) copy-start(bf16[256,640]{1,0:T(8,128)(2,1)} %upstream.1) | copy-start | bytes 983044
  3.6 19.7 %all-to-all-start = ((bf16[8,3,5,32,128]{4,3,2,1,0:T(8,128)(2,1)}), bf16[8,3,5,32,128]{4,3,2,1,0:T(8,128)(2,1)S(1)}, u32[]{:S(2)}, u32[]{:S(2)}) async-start(bf16[8,3,5,32,128]{4,3,2,1,0:T(8,128)(2,1)} %pad_maximum_fusion), calls=%async_computation | async-start | bytes 1966080 | tf_op jit(solution)/shard_map/heads/all_to_all | solution.py:438
  9.6 14.9 %collective-permute-start = (bf16[2,128,128]{2,1,0:T(8,128)(2,1)S(1)}, bf16[2,128,128]{2,1,0:T(8,128)(2,1)S(1)}, u32[]{:S(2)}, u32[]{:S(2)}) collective-permute-start(bf16[2,128,128]{2,1,0:T(8,128)(2,1)S(1)} %get-tuple-element.42), channel_id=1, source_target_pairs={{0,0},{32,8},{8,16},{40,24},{16,32},{48,40},{24,48},{56,56},{64,64... | collective-permute-start | bytes 196616 | tf_op jit(solution)/shard_map/upstream_to_units/ppermute | solution.py:421
  13.5 11.1 %collective-permute-start.1 = (bf16[2,128,128]{2,1,0:T(8,128)(2,1)S(1)}, bf16[2,128,128]{2,1,0:T(8,128)(2,1)S(1)}, u32[]{:S(2)}, u32[]{:S(2)}) collective-permute-start(bf16[2,128,128]{2,1,0:T(8,128)(2,1)S(1)} %get-tuple-element.43), channel_id=1, source_target_pairs={{32,0},{0,8},{40,16},{8,24},{48,32},{16,40},{56,48},{24,56},{96,64... | collective-permute-start | bytes 196616 | tf_op jit(solution)/shard_map/upstream_to_units/ppermute | solution.py:421
  18.9 8.3 %collective-permute-start.2 = (bf16[2,128,128]{2,1,0:T(8,128)(2,1)S(1)}, bf16[2,128,128]{2,1,0:T(8,128)(2,1)S(1)}, u32[]{:S(2)}, u32[]{:S(2)}) collective-permute-start(bf16[2,128,128]{2,1,0:T(8,128)(2,1)S(1)} %get-tuple-element.44), channel_id=1, source_target_pairs={{8,0},{56,8},{16,16},{32,24},{24,32},{40,40},{0,48},{48,56},{72,64... | collective-permute-start | bytes 196616 | tf_op jit(solution)/shard_map/upstream_to_units/ppermute | solution.py:421
  27.2 40.3 %all-to-all-start.1 = ((bf16[32,19,8,128]{3,2,1,0:T(8,128)(2,1)}), bf16[32,19,8,128]{3,2,1,0:T(8,128)(2,1)S(1)}, u32[]{:S(2)}, u32[]{:S(2)}) async-start(bf16[32,19,8,128]{3,2,1,0:T(8,128)(2,1)} %deal.1), calls=%async_computation.1 | async-start | bytes 2490368 | tf_op jit(solution)/shard_map/tiles/all_to_all | solution.py:441
  35.8 33.9 %collective-permute-start.3 = (bf16[2,128,128]{2,1,0:T(8,128)(2,1)S(1)}, bf16[2,128,128]{2,1,0:T(8,128)(2,1)S(1)}, u32[]{:S(2)}, u32[]{:S(2)}) collective-permute-start(bf16[2,128,128]{2,1,0:T(8,128)(2,1)S(1)} %get-tuple-element.46), channel_id=1, source_target_pairs={{40,0},{24,8},{48,16},{0,24},{56,32},{8,40},{32,48},{16,56},{104,6... | collective-permute-start | bytes 196616 | tf_op jit(solution)/shard_map/upstream_to_units/ppermute | solution.py:421
  40.4 29.4 %collective-permute-start.4 = (bf16[128,128]{1,0:T(8,128)(2,1)S(1)}, bf16[128,128]{1,0:T(8,128)(2,1)S(1)}, u32[]{:S(2)}, u32[]{:S(2)}) collective-permute-start(bf16[128,128]{1,0:T(8,128)(2,1)S(1)} %get-tuple-element.47), channel_id=1, source_target_pairs={{16,0},{48,8},{24,16},{56,24},{0,32},{32,40},{8,48},{40,56},{80,64... | collective-permute-start | bytes 98312 | tf_op jit(solution)/shard_map/upstream_to_units/ppermute | solution.py:421
  41.8 27.9 %collective-permute-start.5 = (bf16[128,128]{1,0:T(8,128)(2,1)S(1)}, bf16[128,128]{1,0:T(8,128)(2,1)S(1)}, u32[]{:S(2)}, u32[]{:S(2)}) collective-permute-start(bf16[128,128]{1,0:T(8,128)(2,1)S(1)} %get-tuple-element.48), channel_id=1, source_target_pairs={{48,0},{16,8},{56,16},{24,24},{32,32},{0,40},{40,48},{8,56},{112,6... | collective-permute-start | bytes 98312 | tf_op jit(solution)/shard_map/upstream_to_units/ppermute | solution.py:421
  69.8 12.2 %collective-permute-start.7 = (bf16[14,128,128]{2,1,0:T(8,128)(2,1)S(1)}, bf16[14,128,128]{2,1,0:T(8,128)(2,1)S(1)}, u32[]{:S(2)}, u32[]{:S(2)}) collective-permute-start(bf16[14,128,128]{2,1,0:T(8,128)(2,1)S(1)} %get-tuple-element.80), channel_id=1, source_target_pairs={{64,0},{72,8},{80,16},{88,24},{96,32},{104,40},{112,48},{120,56},{... | collective-permute-start | bytes 1376264 | tf_op jit(solution)/shard_map/halos/ppermute | solution.py:421
  73.0 11.3 %collective-permute-start.6 = (bf16[14,128,128]{2,1,0:T(8,128)(2,1)S(1)}, bf16[14,128,128]{2,1,0:T(8,128)(2,1)S(1)}, u32[]{:S(2)}, u32[]{:S(2)}) collective-permute-start(bf16[14,128,128]{2,1,0:T(8,128)(2,1)S(1)} %get-tuple-element.81), channel_id=1, source_target_pairs={{0,64},{8,72},{16,80},{24,88},{32,96},{40,104},{48,112},{56,120},{... | collective-permute-start | bytes 1376264 | tf_op jit(solution)/shard_map/halos/ppermute | solution.py:421
  94.3 16.4 %collective-permute-start.8 = (bf16[2,7,128,128]{3,2,1,0:T(8,128)(2,1)S(1)}, bf16[2,7,128,128]{3,2,1,0:T(8,128)(2,1)S(1)}, u32[]{:S(2)}, u32[]{:S(2)}) collective-permute-start(bf16[2,7,128,128]{3,2,1,0:T(8,128)(2,1)S(1)} %get-tuple-element.56), channel_id=1, source_target_pairs={{0,64},{8,72},{16,80},{24,88},{32,96},{40,104},{48,112},{56,120},{... | collective-permute-start | bytes 1376264 | tf_op jit(solution)/shard_map/row_terms/ppermute | solution.py:421
  97.7 13.0 %collective-permute-start.9 = (bf16[2,7,128,128]{3,2,1,0:T(8,128)(2,1)S(1)}, bf16[2,7,128,128]{3,2,1,0:T(8,128)(2,1)S(1)}, u32[]{:S(2)}, u32[]{:S(2)}) collective-permute-start(bf16[2,7,128,128]{3,2,1,0:T(8,128)(2,1)S(1)} %get-tuple-element.57), channel_id=1, source_target_pairs={{64,0},{72,8},{80,16},{88,24},{96,32},{104,40},{112,48},{120,56},{... | collective-permute-start | bytes 1376264 | tf_op jit(solution)/shard_map/row_terms/ppermute | solution.py:421
  100.2 8.2 %collective-permute-start.10 = (bf16[2,2,128,128]{3,2,1,0:T(8,128)(2,1)S(1)}, bf16[2,2,128,128]{3,2,1,0:T(8,128)(2,1)S(1)}, u32[]{:S(2)}, u32[]{:S(2)}) collective-permute-start(bf16[2,2,128,128]{3,2,1,0:T(8,128)(2,1)S(1)} %get-tuple-element.58), channel_id=1, source_target_pairs={{0,0},{8,32},{16,8},{24,40},{32,16},{40,48},{48,24},{56,56},{64,64... | collective-permute-start | bytes 393224 | tf_op jit(solution)/shard_map/row_terms/ppermute | solution.py:421
  104.7 6.0 %collective-permute-start.11 = (bf16[2,2,128,128]{3,2,1,0:T(8,128)(2,1)S(1)}, bf16[2,2,128,128]{3,2,1,0:T(8,128)(2,1)S(1)}, u32[]{:S(2)}, u32[]{:S(2)}) collective-permute-start(bf16[2,2,128,128]{3,2,1,0:T(8,128)(2,1)S(1)} %get-tuple-element.59), channel_id=1, source_target_pairs={{0,32},{8,0},{16,40},{24,8},{32,48},{40,16},{48,56},{56,24},{64,96... | collective-permute-start | bytes 393224 | tf_op jit(solution)/shard_map/row_terms/ppermute | solution.py:421
  111.4 22.0 %collective-permute-start.14 = (bf16[4,2,128,128]{3,2,1,0:T(8,128)(2,1)S(1)}, bf16[4,2,128,128]{3,2,1,0:T(8,128)(2,1)S(1)}, u32[]{:S(2)}, u32[]{:S(2)}) collective-permute-start(bf16[4,2,128,128]{3,2,1,0:T(8,128)(2,1)S(1)} %get-tuple-element.72), channel_id=1, source_target_pairs={{0,8},{8,56},{16,16},{24,32},{32,24},{40,40},{48,0},{56,48},{64,72... | collective-permute-start | bytes 786440 | tf_op jit(solution)/shard_map/column_terms/ppermute | solution.py:421
  116.3 17.1 %collective-permute-start.15 = (bf16[4,2,128,128]{3,2,1,0:T(8,128)(2,1)S(1)}, bf16[4,2,128,128]{3,2,1,0:T(8,128)(2,1)S(1)}, u32[]{:S(2)}, u32[]{:S(2)}) collective-permute-start(bf16[4,2,128,128]{3,2,1,0:T(8,128)(2,1)S(1)} %get-tuple-element.73), channel_id=1, source_target_pairs={{0,40},{8,24},{16,48},{24,0},{32,56},{40,8},{48,32},{56,16},{64,10... | collective-permute-start | bytes 786440 | tf_op jit(solution)/shard_map/column_terms/ppermute | solution.py:421
  118.8 13.6 %collective-permute-start.12 = (bf16[2,2,128,128]{3,2,1,0:T(8,128)(2,1)S(1)}, bf16[2,2,128,128]{3,2,1,0:T(8,128)(2,1)S(1)}, u32[]{:S(2)}, u32[]{:S(2)}) collective-permute-start(bf16[2,2,128,128]{3,2,1,0:T(8,128)(2,1)S(1)} %get-tuple-element.66), channel_id=1, source_target_pairs={{0,8},{8,16},{16,24},{24,32},{32,40},{40,48},{48,56},{64,72},{72,8... | collective-permute-start | bytes 393224 | tf_op jit(solution)/shard_map/column_terms/ppermute | solution.py:421
  122.2 10.5 %collective-permute-start.13 = (bf16[2,2,128,128]{3,2,1,0:T(8,128)(2,1)S(1)}, bf16[2,2,128,128]{3,2,1,0:T(8,128)(2,1)S(1)}, u32[]{:S(2)}, u32[]{:S(2)}) collective-permute-start(bf16[2,2,128,128]{3,2,1,0:T(8,128)(2,1)S(1)} %get-tuple-element.67), channel_id=1, source_target_pairs={{8,0},{16,8},{24,16},{32,24},{40,32},{48,40},{56,48},{72,64},{80,7... | collective-permute-start | bytes 393224 | tf_op jit(solution)/shard_map/column_terms/ppermute | solution.py:421
  133.5 11.1 %collective-permute-start.16 = (bf16[2,2,128,128]{3,2,1,0:T(8,128)(2,1)S(1)}, bf16[2,2,128,128]{3,2,1,0:T(8,128)(2,1)S(1)}, u32[]{:S(2)}, u32[]{:S(2)}) collective-permute-start(bf16[2,2,128,128]{3,2,1,0:T(8,128)(2,1)S(1)} %get-tuple-element.76), channel_id=1, source_target_pairs={{0,0},{8,32},{16,8},{24,40},{32,16},{40,48},{48,24},{56,56},{64,64... | collective-permute-start | bytes 393224 | tf_op jit(solution)/shard_map/outputs_home/ppermute | solution.py:421
  139.1 7.0 %collective-permute-start.17 = (bf16[2,2,128,128]{3,2,1,0:T(8,128)(2,1)S(1)}, bf16[2,2,128,128]{3,2,1,0:T(8,128)(2,1)S(1)}, u32[]{:S(2)}, u32[]{:S(2)}) collective-permute-start(bf16[2,2,128,128]{3,2,1,0:T(8,128)(2,1)S(1)} %get-tuple-element.77), channel_id=1, source_target_pairs={{0,32},{8,0},{16,40},{24,8},{32,48},{40,16},{48,56},{56,24},{64,96... | collective-permute-start | bytes 393224 | tf_op jit(solution)/shard_map/outputs_home/ppermute | solution.py:421
  139.2 9.8 %collective-permute-start.18 = (bf16[4,128,128]{2,1,0:T(8,128)(2,1)S(1)}, bf16[4,128,128]{2,1,0:T(8,128)(2,1)S(1)}, u32[]{:S(2)}, u32[]{:S(2)}) collective-permute-start(bf16[4,128,128]{2,1,0:T(8,128)(2,1)S(1)} %get-tuple-element.78), channel_id=1, source_target_pairs={{0,16},{8,48},{16,24},{24,56},{32,0},{40,32},{48,8},{56,40},{64,80... | collective-permute-start | bytes 393224 | tf_op jit(solution)/shard_map/outputs_home/ppermute | solution.py:421
  142.4 14.0 %collective-permute-start.19 = (bf16[4,128,128]{2,1,0:T(8,128)(2,1)S(1)}, bf16[4,128,128]{2,1,0:T(8,128)(2,1)S(1)}, u32[]{:S(2)}, u32[]{:S(2)}) collective-permute-start(bf16[4,128,128]{2,1,0:T(8,128)(2,1)S(1)} %get-tuple-element.79), channel_id=1, source_target_pairs={{0,48},{8,16},{16,56},{24,24},{32,32},{40,0},{48,40},{56,8},{64,11... | collective-permute-start | bytes 393224 | tf_op jit(solution)/shard_map/outputs_home/ppermute | solution.py:421

commit v5 on v4

--- a/solution.py
+++ b/solution.py
@@ -132,8 +132,8 @@
 
 
 def gather_kernel(table, *refs):
-    early, free, late, singles = refs[:2], refs[2:4], refs[4:6], refs[6:8]
-    outs, single = refs[8:12], refs[12]
+    free, late, singles = refs[:2], refs[2:4], refs[4:6]
+    outs, single = refs[6:10], refs[10]
     line = lax.broadcasted_iota(jnp.int32, (2 * TILE, 2 * TILE), 0)
     col = lax.broadcasted_iota(jnp.int32, (2 * TILE, 2 * TILE), 1)
     source = ((line >> 2) & 1) * TILE + (line >> 3) * 4 + (line & 3)
@@ -141,8 +141,7 @@
     for kind, out in enumerate(outs):
         for at in range(4):
             head = pl.multiple_of(table[at] * HEAD_DIM, HEAD_DIM)
-            edge = (early, late)[kind // 2][at % 2].at[kind % 2]
-            tiles = (edge[...] if at < 2 else free[at % 2][kind]).reshape(2 * TILE, HEAD_DIM)
+            tiles = (late, free)[at // 2][at % 2][kind].reshape(2 * TILE, HEAD_DIM)
             out[:, pl.ds(head, HEAD_DIM)] = nn(order, tiles).astype(LOW)
         flip = table[6] == 1
         one, two = singles[0][kind], singles[1][kind]
@@ -156,7 +155,7 @@
     return pl.pallas_call(
         gather_kernel,
         out_shape=[jax.ShapeDtypeStruct((2 * TILE, HEADS_HERE * HEAD_DIM), LOW)] * 4,
-        in_specs=[pl.BlockSpec(memory_space=pltpu.SMEM)] + whole(8),
+        in_specs=[pl.BlockSpec(memory_space=pltpu.SMEM)] + whole(6),
         out_specs=whole(4),
         scratch_shapes=[pltpu.VMEM((2 * TILE, HEAD_DIM), LOW)],
         compiler_params=pltpu.CompilerParams(vmem_limit_bytes=16 << 20),
@@ -194,8 +193,8 @@
 
 
 def attend_kernel(table, own, above, below, *refs):
-    grads, firsts, rest, terms, edges = refs[:6], refs[6:8], refs[8], refs[9], refs[10:12]
-    pair, turned, grad, total, held = refs[12:]
+    grads, rest, terms, edges = refs[:6], refs[6], refs[7], refs[8:10]
+    pair, turned, outer_turned, grad, total, held = refs[10:]
     strip, odd = table[7], table[8]
     scaling = HEAD_DIM**-0.5
     rate = scaling * math.log2(math.e)
@@ -208,8 +207,10 @@
             pair[kind, at, 3] = below[7 * kind + at]
     for kind in range(2):
         for at in range(7):
-            for row in range(4):
-                turned[kind, at, row] = pair[kind, at, row].T
+            for row in range(2):
+                lanes = pl.ds((2 * at + row) * TILE, TILE)
+                turned[kind, :, lanes] = pair[kind, at, row].T
+                outer_turned[kind, row, :, pl.ds(at * TILE, TILE)] = pair[kind, at, 2 + row].T
     for at, (which, turn) in enumerate(OWNER_STEPS):
         row = (turn + odd) % 2
         first = first_of(which, odd)
@@ -267,14 +268,18 @@
 
         def mix(kind, parts):
             near = sum(
-                nn(turned[kind, unit + step, row], parts[step][row * TILE : (row + 1) * TILE])
+                nn(
+                    turned[kind, :, pl.ds(pl.multiple_of((unit + step) * 256, 256), 256)],
+                    parts[step],
+                )
                 for step in range(3)
-                for row in range(2)
             )
             far = [
                 sum(
                     nn(
-                        turned[kind, unit + step, 2 + row],
+                        outer_turned[
+                            kind, row, :, pl.ds(pl.multiple_of((unit + step) * TILE, TILE), TILE)
+                        ],
                         parts[3 + step][:, row * TILE : (row + 1) * TILE],
                     )
                     for step in range(3)
@@ -309,14 +314,14 @@
         fold(0, slopes, queries, both)
         return carry
 
-    lax.fori_loop(0, 5, one_unit, 0)
+    lax.fori_loop(0, 5, one_unit, 0, unroll=True)
     for kind in range(2):
         for turn in range(2):
             row = (turn + odd) % 2
             for part in range(2):
-                firsts[turn][kind, part] = held[kind, row, first_of(0, odd) + part]
-                rest[kind, turn, part] = held[kind, row, first_of(1, odd) + part]
-            rest[kind, turn, 2] = held[kind, row, first_of(2, odd)]
+                rest[kind, turn, part] = held[kind, row, first_of(0, odd) + part]
+                rest[kind, turn, 2 + part] = held[kind, row, first_of(1, odd) + part]
+            rest[kind, turn, 4] = held[kind, row, first_of(2, odd)]
     for kind, factor in ((0, scaling), (1, 1.0)):
         for at in range(7):
             for row in range(2):
@@ -331,18 +336,18 @@
 def attend(table, own, halos, grads):
     return pl.pallas_call(
         attend_kernel,
-        out_shape=pair_shapes(2, 2)
-        + [
-            jax.ShapeDtypeStruct((2, 2, 3, TILE, HEAD_DIM), LOW),
+        out_shape=[
+            jax.ShapeDtypeStruct((2, 2, 5, TILE, HEAD_DIM), LOW),
             jax.ShapeDtypeStruct((2, 2, 7, TILE, HEAD_DIM), WIDE),
             jax.ShapeDtypeStruct((2, 7, TILE, HEAD_DIM), LOW),
             jax.ShapeDtypeStruct((2, 7, TILE, HEAD_DIM), LOW),
         ],
         in_specs=[pl.BlockSpec(memory_space=pltpu.SMEM)] + whole(9),
-        out_specs=whole(6),
+        out_specs=whole(4),
         scratch_shapes=[
             pltpu.VMEM((2, 7, 4, TILE, HEAD_DIM), LOW),
-            pltpu.VMEM((2, 7, 4, HEAD_DIM, TILE), LOW),
+            pltpu.VMEM((2, HEAD_DIM, 14 * TILE), LOW),
+            pltpu.VMEM((2, 2, HEAD_DIM, 7 * TILE), LOW),
             pltpu.VMEM((2, 5, TILE, HEAD_DIM), LOW),
             pltpu.VMEM((2, 7, 4, TILE, HEAD_DIM), WIDE),
             pltpu.VMEM((2, 2, 5, TILE, HEAD_DIM), LOW),
@@ -366,7 +371,7 @@
         for part in range(2):
             at = first_of(1, odd) + part + 1
             for kind in range(2):
-                outs[turn][kind, part] = rest[kind, turn, part]
+                outs[turn][kind, part] = rest[kind, turn, 2 + part]
                 flip = (turn + odd) % 2 == 1
                 edge = jnp.where(flip, below[kind, at], above[kind, at])
                 value = terms[kind, (turn + odd) % 2, at] + edge.astype(WIDE)
@@ -399,17 +404,19 @@
             left = before[kind, row].astype(WIDE)
             right = after[kind, row].astype(WIDE)
             one, two = summed(first), summed(first + 1)
-            outs[turn][kind, 0] = jnp.where(flipped, one, one + left).astype(LOW)
-            outs[turn][kind, 1] = jnp.where(flipped, two + right, two).astype(LOW)
+            for part in range(2):
+                outs[turn][kind, part] = rest[kind, turn, part]
+            outs[turn][2 + kind, 0] = jnp.where(flipped, one, one + left).astype(LOW)
+            outs[turn][2 + kind, 1] = jnp.where(flipped, two + right, two).astype(LOW)
             alone = summed(first_of(2, odd)) + jnp.where(flipped, left, right)
-            outs[2 + turn][kind] = rest[kind, turn, 2]
+            outs[2 + turn][kind] = rest[kind, turn, 4]
             outs[2 + turn][2 + kind] = alone.astype(LOW)
 
 
 def combine(table, rest, terms, edges, columns):
     return pl.pallas_call(
         combine_kernel,
-        out_shape=pair_shapes(2, 2) + [jax.ShapeDtypeStruct((4, TILE, HEAD_DIM), LOW)] * 2,
+        out_shape=pair_shapes(4, 2) + [jax.ShapeDtypeStruct((4, TILE, HEAD_DIM), LOW)] * 2,
         in_specs=[pl.BlockSpec(memory_space=pltpu.SMEM)] + whole(6),
         out_specs=whole(4),
         compiler_params=pltpu.CompilerParams(vmem_limit_bytes=16 << 20),
@@ -445,11 +452,9 @@
     with jax.named_scope("halos"):
         halos = send_all([own[1, 5:], own[0, 5:]], row_routes)
     with jax.named_scope("attention"):
-        *edge_pairs, rest, terms, above, below = attend(place, own, halos, early + late)
+        rest, terms, above, below = attend(place, own, halos, early + late)
     with jax.named_scope("row_terms"):
         edges = send_all([above, below], row_routes)
-        early = send_all(edge_pairs, to_owner[:2])
-        edges, early = lax.optimization_barrier((edges, early))
     with jax.named_scope("column_terms"):
         right, left, *free = rims(place, rest, terms, edges)
         columns = send_all([right, left], column_routes)
@@ -459,7 +464,7 @@
         leaving, free = lax.optimization_barrier((leaving, free))
         late = send_all(leaving, to_owner[:2] + to_owner[4:])
     with jax.named_scope("settle"):
-        return tuple(gather(place, early + free + late))
+        return tuple(gather(place, free + late))
 
 
 def solution(mesh):

time: 159 us -> 158 us (level)
  the two profiles are of different devices: /device:TPU:40 before, /device:TPU:73 now
where the time goes in v5:
time: 158 us
  waiting for transfers between devices  69.7 us (44%)
  starting transfers between devices  69.1 us (44%)
  Pallas kernels  13.8 us (9%)
  local copies, waits for them, and re-layouts  3.23 us (2%)
    ppermute x18, starting transfers between devices, send_all(): lax.ppermute(part, 'tile', path)  53.8 us
    ppermute x18, waiting for transfers between devices, send_all(): lax.ppermute(part, 'tile', path)  42.5 us
    all_to_all x1, waiting for transfers between devices, local(): got = lax.all_to_all(dealt, 'tile', 0, 0, tiled=True)  22 us
    all_to_all x1, starting transfers between devices, local(): got = lax.all_to_all(dealt, 'tile', 0, 0, tiled=True)  10.2 us
    pallas_call x1, Pallas kernels, attend(): pl.pallas_call(attend_kernel, out_shape=[jax.ShapeDtypeStruct((2, 2, 5, T...  8.12 us
    all_to_all x1, waiting for transfers between devices, local(): swapped = lax.all_to_all(jnp.stack(lines, axis=1), 'head', 0, 0, tiled=True)  5.2 us
    all_to_all x1, starting transfers between devices, local(): swapped = lax.all_to_all(jnp.stack(lines, axis=1), 'head', 0, 0, tiled=True)  5.1 us
  transfers between devices with their start and end apart: 20, of which 11 were waited for; matrix products, arithmetic and copies ran while one was open for 1% of the time, Pallas kernels for 2%

profile of v5, /device:TPU:73, one launch (start us, length us, event | category | flops | bytes accessed | tf_op | source)
XLA Modules:
  0.0 157.9 jit_solution(3721976181798036858)
XLA Ops:
  0.7 1.2 reshape.32
  1.8 0.1 copy.9
  2.0 0.1 reshape.34
  2.1 0.1 copy.10
  2.2 0.1 reshape.36
  2.4 0.1 copy.11
  2.5 1.1 pad_maximum_fusion
  3.6 5.1 %all-to-all-start = ((bf16[8,3,5,32,128]{4,3,2,1,0:T(8,128)(2,1)}), bf16[8,3,5,32,128]{4,3,2,1,0:T(8,128)(2,1)S(1)}, u32[]{:S(2)}, u32[]{:S(2)}) async-start(bf16[8,3,5,32,128]{4,3,2,1,0:T(8,128)(2,1)} %pad_maximum_fusion), calls=%async_computation | async-start | bytes 1966080 | tf_op jit(solution)/shard_map/heads/all_to_all | solution.py:445
  8.7 0.7 dynamic-slice_bitcast_fusion.table
  9.4 0.9 spread.1
  10.3 6.1 %collective-permute-start = (bf16[2,128,128]{2,1,0:T(8,128)(2,1)S(1)}, bf16[2,128,128]{2,1,0:T(8,128)(2,1)S(1)}, u32[]{:S(2)}, u32[]{:S(2)}) collective-permute-start(bf16[2,128,128]{2,1,0:T(8,128)(2,1)S(1)} %get-tuple-element.36), channel_id=1, source_target_pairs={{0,0},{32,8},{8,16},{40,24},{16,32},{48,40},{24,48},{56,56},{64,64... | collective-permute-start | bytes 196616 | tf_op jit(solution)/shard_map/upstream_to_units/ppermute | solution.py:428
  16.4 0.8 collective-permute-start.1
  17.2 0.7 collective-permute-start.2
  17.9 5.2 %all-to-all-done.swapped = bf16[8,3,5,32,128]{4,3,2,1,0:T(8,128)(2,1)S(1)} async-done(((bf16[8,3,5,32,128]{4,3,2,1,0:T(8,128)(2,1)}), bf16[8,3,5,32,128]{4,3,2,1,0:T(8,128)(2,1)S(1)}, u32[]{:S(2)}, u32[]{:S(2)}) %all-to-all-start) | async-done | bytes 983072 | tf_op jit(solution)/shard_map/heads/all_to_all | solution.py:445
  23.1 1.2 deal.1
  24.3 0.0 collective-permute-done.refs_0_
  24.3 10.2 %all-to-all-start.1 = ((bf16[32,19,8,128]{3,2,1,0:T(8,128)(2,1)}), bf16[32,19,8,128]{3,2,1,0:T(8,128)(2,1)S(1)}, u32[]{:S(2)}, u32[]{:S(2)}) async-start(bf16[32,19,8,128]{3,2,1,0:T(8,128)(2,1)} %deal.1), calls=%async_computation.1 | async-start | bytes 2490368 | tf_op jit(solution)/shard_map/tiles/all_to_all | solution.py:448
  34.6 2.5 %collective-permute-start.3 = (bf16[2,128,128]{2,1,0:T(8,128)(2,1)S(1)}, bf16[2,128,128]{2,1,0:T(8,128)(2,1)S(1)}, u32[]{:S(2)}, u32[]{:S(2)}) collective-permute-start(bf16[2,128,128]{2,1,0:T(8,128)(2,1)S(1)} %get-tuple-element.40), channel_id=1, source_target_pairs={{40,0},{24,8},{48,16},{0,24},{56,32},{8,40},{32,48},{16,56},{104,6... | collective-permute-start | bytes 196616 | tf_op jit(solution)/shard_map/upstream_to_units/ppermute | solution.py:428
  37.1 0.9 collective-permute-start.4
  37.9 4.3 %collective-permute-start.5 = (bf16[128,128]{1,0:T(8,128)(2,1)S(1)}, bf16[128,128]{1,0:T(8,128)(2,1)S(1)}, u32[]{:S(2)}, u32[]{:S(2)}) collective-permute-start(bf16[128,128]{1,0:T(8,128)(2,1)S(1)} %get-tuple-element.42), channel_id=1, source_target_pairs={{48,0},{16,8},{56,16},{24,24},{32,32},{0,40},{40,48},{8,56},{112,6... | collective-permute-start | bytes 98312 | tf_op jit(solution)/shard_map/upstream_to_units/ppermute | solution.py:428
  42.2 22.0 %all-to-all-done.1 = bf16[32,19,8,128]{3,2,1,0:T(8,128)(2,1)S(1)} async-done(((bf16[32,19,8,128]{3,2,1,0:T(8,128)(2,1)}), bf16[32,19,8,128]{3,2,1,0:T(8,128)(2,1)S(1)}, u32[]{:S(2)}, u32[]{:S(2)}) %all-to-all-start.1) | async-done | bytes 1245216 | tf_op jit(solution)/shard_map/tiles/all_to_all | solution.py:448
  64.2 0.7 copy.12
  64.9 0.1 collective-permute-done.5.refs_5_
  65.0 0.6 collective-permute-done.3.refs_3_
  65.6 0.1 slice_bitcast_fusion
  65.7 2.8 %collective-permute-start.7 = (bf16[14,128,128]{2,1,0:T(8,128)(2,1)S(1)}, bf16[14,128,128]{2,1,0:T(8,128)(2,1)S(1)}, u32[]{:S(2)}, u32[]{:S(2)}) collective-permute-start(bf16[14,128,128]{2,1,0:T(8,128)(2,1)S(1)} %get-tuple-element.68), channel_id=1, source_target_pairs={{64,0},{72,8},{80,16},{88,24},{96,32},{104,40},{112,48},{120,56},{... | collective-permute-start | bytes 1376264 | tf_op jit(solution)/shard_map/halos/ppermute | solution.py:428
  68.5 2.7 %collective-permute-start.6 = (bf16[14,128,128]{2,1,0:T(8,128)(2,1)S(1)}, bf16[14,128,128]{2,1,0:T(8,128)(2,1)S(1)}, u32[]{:S(2)}, u32[]{:S(2)}) collective-permute-start(bf16[14,128,128]{2,1,0:T(8,128)(2,1)S(1)} %get-tuple-element.69), channel_id=1, source_target_pairs={{0,64},{8,72},{16,80},{24,88},{32,96},{40,104},{48,112},{56,120},{... | collective-permute-start | bytes 1376264 | tf_op jit(solution)/shard_map/halos/ppermute | solution.py:428
  71.2 4.5 %collective-permute-done.7.below = bf16[14,128,128]{2,1,0:T(8,128)(2,1)S(1)} collective-permute-done((bf16[14,128,128]{2,1,0:T(8,128)(2,1)S(1)}, bf16[14,128,128]{2,1,0:T(8,128)(2,1)S(1)}, u32[]{:S(2)}, u32[]{:S(2)}) %collective-permute-start.7) | collective-permute-done | bytes 458784 | tf_op jit(solution)/shard_map/halos/ppermute | solution.py:428
  75.7 3.1 %collective-permute-done.6.above = bf16[14,128,128]{2,1,0:T(8,128)(2,1)S(1)} collective-permute-done((bf16[14,128,128]{2,1,0:T(8,128)(2,1)S(1)}, bf16[14,128,128]{2,1,0:T(8,128)(2,1)S(1)}, u32[]{:S(2)}, u32[]{:S(2)}) %collective-permute-start.6) | collective-permute-done | bytes 458784 | tf_op jit(solution)/shard_map/halos/ppermute | solution.py:428
  78.8 8.1 %attend.1 = (bf16[2,2,5,128,128]{4,3,2,1,0:T(8,128)(2,1)S(1)}, f32[2,2,7,128,128]{4,3,2,1,0:T(8,128)S(1)}, bf16[2,7,128,128]{3,2,1,0:T(8,128)(2,1)S(1)}, bf16[2,7,128,128]{3,2,1,0:T(8,128)(2,1)S(1)}) custom-call(s32[14]{0:T(128)S(1)} %dynamic-slice_bitcast_fusion.table, bf16[2,19,128,128]{3,2,1,0:T(8,128)(2,1)S(1)} %bitcast.20, ...), custom_call_target="tpu_custom_call" | custom-call | flops 3000000000 | bytes 8000000 | tf_op jit(solution)/shard_map/attention/attend/pallas_call | solution.py:337
  86.9 1.9 %collective-permute-start.8 = (bf16[2,7,128,128]{3,2,1,0:T(8,128)(2,1)S(1)}, bf16[2,7,128,128]{3,2,1,0:T(8,128)(2,1)S(1)}, u32[]{:S(2)}, u32[]{:S(2)}) collective-permute-start(bf16[2,7,128,128]{3,2,1,0:T(8,128)(2,1)S(1)} %get-tuple-element.52), channel_id=1, source_target_pairs={{0,64},{8,72},{16,80},{24,88},{32,96},{40,104},{48,112},{56,120},{... | collective-permute-start | bytes 1376264 | tf_op jit(solution)/shard_map/row_terms/ppermute | solution.py:428
  88.9 3.4 %collective-permute-start.9 = (bf16[2,7,128,128]{3,2,1,0:T(8,128)(2,1)S(1)}, bf16[2,7,128,128]{3,2,1,0:T(8,128)(2,1)S(1)}, u32[]{:S(2)}, u32[]{:S(2)}) collective-permute-start(bf16[2,7,128,128]{3,2,1,0:T(8,128)(2,1)S(1)} %get-tuple-element.53), channel_id=1, source_target_pairs={{64,0},{72,8},{80,16},{88,24},{96,32},{104,40},{112,48},{120,56},{... | collective-permute-start | bytes 1376264 | tf_op jit(solution)/shard_map/row_terms/ppermute | solution.py:428
  92.3 3.9 %collective-permute-done.8.above = bf16[2,7,128,128]{3,2,1,0:T(8,128)(2,1)S(1)} collective-permute-done((bf16[2,7,128,128]{3,2,1,0:T(8,128)(2,1)S(1)}, bf16[2,7,128,128]{3,2,1,0:T(8,128)(2,1)S(1)}, u32[]{:S(2)}, u32[]{:S(2)}) %collective-permute-start.8) | collective-permute-done | bytes 458784 | tf_op jit(solution)/shard_map/row_terms/ppermute | solution.py:428
  96.2 2.4 %collective-permute-done.9.below = bf16[2,7,128,128]{3,2,1,0:T(8,128)(2,1)S(1)} collective-permute-done((bf16[2,7,128,128]{3,2,1,0:T(8,128)(2,1)S(1)}, bf16[2,7,128,128]{3,2,1,0:T(8,128)(2,1)S(1)}, u32[]{:S(2)}, u32[]{:S(2)}) %collective-permute-start.9) | collective-permute-done | bytes 458784 | tf_op jit(solution)/shard_map/row_terms/ppermute | solution.py:428
  98.5 0.7 rims.1
  99.2 0.7 collective-permute-start.12
  99.9 9.6 %collective-permute-start.13 = (bf16[4,2,128,128]{3,2,1,0:T(8,128)(2,1)S(1)}, bf16[4,2,128,128]{3,2,1,0:T(8,128)(2,1)S(1)}, u32[]{:S(2)}, u32[]{:S(2)}) collective-permute-start(bf16[4,2,128,128]{3,2,1,0:T(8,128)(2,1)S(1)} %get-tuple-element.61), channel_id=1, source_target_pairs={{0,40},{8,24},{16,48},{24,0},{32,56},{40,8},{48,32},{56,16},{64,10... | collective-permute-start | bytes 786440 | tf_op jit(solution)/shard_map/column_terms/ppermute | solution.py:428
  109.5 4.5 %collective-permute-start.10 = (bf16[2,2,128,128]{3,2,1,0:T(8,128)(2,1)S(1)}, bf16[2,2,128,128]{3,2,1,0:T(8,128)(2,1)S(1)}, u32[]{:S(2)}, u32[]{:S(2)}) collective-permute-start(bf16[2,2,128,128]{3,2,1,0:T(8,128)(2,1)S(1)} %get-tuple-element.54), channel_id=1, source_target_pairs={{0,8},{8,16},{16,24},{24,32},{32,40},{40,48},{48,56},{64,72},{72,8... | collective-permute-start | bytes 393224 | tf_op jit(solution)/shard_map/column_terms/ppermute | solution.py:428
  113.9 3.1 %collective-permute-start.11 = (bf16[2,2,128,128]{3,2,1,0:T(8,128)(2,1)S(1)}, bf16[2,2,128,128]{3,2,1,0:T(8,128)(2,1)S(1)}, u32[]{:S(2)}, u32[]{:S(2)}) collective-permute-start(bf16[2,2,128,128]{3,2,1,0:T(8,128)(2,1)S(1)} %get-tuple-element.55), channel_id=1, source_target_pairs={{8,0},{16,8},{24,16},{32,24},{40,32},{48,40},{56,48},{72,64},{80,7... | collective-permute-start | bytes 393224 | tf_op jit(solution)/shard_map/column_terms/ppermute | solution.py:428
  117.0 8.9 %collective-permute-done.10.before = bf16[2,2,128,128]{3,2,1,0:T(8,128)(2,1)S(1)} collective-permute-done((bf16[2,2,128,128]{3,2,1,0:T(8,128)(2,1)S(1)}, bf16[2,2,128,128]{3,2,1,0:T(8,128)(2,1)S(1)}, u32[]{:S(2)}, u32[]{:S(2)}) %collective-permute-start.10) | collective-permute-done | bytes 131104 | tf_op jit(solution)/shard_map/column_terms/ppermute | solution.py:428
  125.9 0.7 combine.1
  126.7 2.3 %collective-permute-start.14 = (bf16[4,2,128,128]{3,2,1,0:T(8,128)(2,1)S(1)}, bf16[4,2,128,128]{3,2,1,0:T(8,128)(2,1)S(1)}, u32[]{:S(2)}, u32[]{:S(2)}) collective-permute-start(bf16[4,2,128,128]{3,2,1,0:T(8,128)(2,1)S(1)} %get-tuple-element.64), channel_id=1, source_target_pairs={{0,0},{8,32},{16,8},{24,40},{32,16},{40,48},{48,24},{56,56},{64,64... | collective-permute-start | bytes 786440 | tf_op jit(solution)/shard_map/outputs_home/ppermute | solution.py:428
  129.0 3.0 %collective-permute-start.15 = (bf16[4,2,128,128]{3,2,1,0:T(8,128)(2,1)S(1)}, bf16[4,2,128,128]{3,2,1,0:T(8,128)(2,1)S(1)}, u32[]{:S(2)}, u32[]{:S(2)}) collective-permute-start(bf16[4,2,128,128]{3,2,1,0:T(8,128)(2,1)S(1)} %get-tuple-element.65), channel_id=1, source_target_pairs={{0,32},{8,0},{16,40},{24,8},{32,48},{40,16},{48,56},{56,24},{64,96... | collective-permute-start | bytes 786440 | tf_op jit(solution)/shard_map/outputs_home/ppermute | solution.py:428
  132.1 1.2 collective-permute-start.16
  133.3 3.4 %collective-permute-start.17 = (bf16[4,128,128]{2,1,0:T(8,128)(2,1)S(1)}, bf16[4,128,128]{2,1,0:T(8,128)(2,1)S(1)}, u32[]{:S(2)}, u32[]{:S(2)}) collective-permute-start(bf16[4,128,128]{2,1,0:T(8,128)(2,1)S(1)} %get-tuple-element.67), channel_id=1, source_target_pairs={{0,48},{8,16},{16,56},{24,24},{32,32},{40,0},{48,40},{56,8},{64,11... | collective-permute-start | bytes 393224 | tf_op jit(solution)/shard_map/outputs_home/ppermute | solution.py:428
  136.7 15.2 %collective-permute-done.16.refs_4_ = bf16[4,128,128]{2,1,0:T(8,128)(2,1)S(1)} collective-permute-done((bf16[4,128,128]{2,1,0:T(8,128)(2,1)S(1)}, bf16[4,128,128]{2,1,0:T(8,128)(2,1)S(1)}, u32[]{:S(2)}, u32[]{:S(2)}) %collective-permute-start.16) | collective-permute-done | bytes 131104 | tf_op jit(solution)/shard_map/outputs_home/ppermute | solution.py:428
  151.8 3.8 %collective-permute-done.14.refs_2_ = bf16[4,2,128,128]{3,2,1,0:T(8,128)(2,1)S(1)} collective-permute-done((bf16[4,2,128,128]{3,2,1,0:T(8,128)(2,1)S(1)}, bf16[4,2,128,128]{3,2,1,0:T(8,128)(2,1)S(1)}, u32[]{:S(2)}, u32[]{:S(2)}) %collective-permute-start.14) | collective-permute-done | bytes 262176 | tf_op jit(solution)/shard_map/outputs_home/ppermute | solution.py:428
  155.7 2.2 %gather.1 = (bf16[256,640]{1,0:T(8,128)(2,1)}, bf16[256,640]{1,0:T(8,128)(2,1)}, bf16[256,640]{1,0:T(8,128)(2,1)}, bf16[256,640]{1,0:T(8,128)(2,1)}) custom-call(s32[14]{0:T(128)S(1)} %dynamic-slice_bitcast_fusion.table, bf16[4,2,128,128]{3,2,1,0:T(8,128)(2,1)S(1)} %collective-permute-done.12.refs_0_, ...), custom_call_target="tpu_custom_call" | custom-call | tf_op jit(solution)/shard_map/settle/gather/pallas_call | solution.py:155
  (14 shorter events, 0.0 us)
Async XLA Ops:
  0.6 1.3 copy-start.1
  0.6 1.6 %copy-start.2 = (bf16[1,8,4,5120]{3,2,1,0:T(4,128)(2,1)S(1)}, bf16[1,8,4,5120]{3,2,1,0:T(4,128)(2,1)}, u32[]{:S(2)}) copy-start(bf16[1,8,4,5120]{3,2,1,0:T(4,128)(2,1)} %param.7) | copy-start | bytes 983044
  3.6 5.8 %copy-start = (bf16[256,640]{1,0:T(8,128)(2,1)S(1)}, bf16[256,640]{1,0:T(8,128)(2,1)}, u32[]{:S(2)}) copy-start(bf16[256,640]{1,0:T(8,128)(2,1)} %upstream.1) | copy-start | bytes 983044
  3.6 19.5 %all-to-all-start = ((bf16[8,3,5,32,128]{4,3,2,1,0:T(8,128)(2,1)}), bf16[8,3,5,32,128]{4,3,2,1,0:T(8,128)(2,1)S(1)}, u32[]{:S(2)}, u32[]{:S(2)}) async-start(bf16[8,3,5,32,128]{4,3,2,1,0:T(8,128)(2,1)} %pad_maximum_fusion), calls=%async_computation | async-start | bytes 1966080 | tf_op jit(solution)/shard_map/heads/all_to_all | solution.py:445
  10.3 14.0 %collective-permute-start = (bf16[2,128,128]{2,1,0:T(8,128)(2,1)S(1)}, bf16[2,128,128]{2,1,0:T(8,128)(2,1)S(1)}, u32[]{:S(2)}, u32[]{:S(2)}) collective-permute-start(bf16[2,128,128]{2,1,0:T(8,128)(2,1)S(1)} %get-tuple-element.36), channel_id=1, source_target_pairs={{0,0},{32,8},{8,16},{40,24},{16,32},{48,40},{24,48},{56,56},{64,64... | collective-permute-start | bytes 196616 | tf_op jit(solution)/shard_map/upstream_to_units/ppermute | solution.py:428
  16.4 7.9 %collective-permute-start.1 = (bf16[2,128,128]{2,1,0:T(8,128)(2,1)S(1)}, bf16[2,128,128]{2,1,0:T(8,128)(2,1)S(1)}, u32[]{:S(2)}, u32[]{:S(2)}) collective-permute-start(bf16[2,128,128]{2,1,0:T(8,128)(2,1)S(1)} %get-tuple-element.37), channel_id=1, source_target_pairs={{32,0},{0,8},{40,16},{8,24},{48,32},{16,40},{56,48},{24,56},{96,64... | collective-permute-start | bytes 196616 | tf_op jit(solution)/shard_map/upstream_to_units/ppermute | solution.py:428
  17.2 7.1 %collective-permute-start.2 = (bf16[2,128,128]{2,1,0:T(8,128)(2,1)S(1)}, bf16[2,128,128]{2,1,0:T(8,128)(2,1)S(1)}, u32[]{:S(2)}, u32[]{:S(2)}) collective-permute-start(bf16[2,128,128]{2,1,0:T(8,128)(2,1)S(1)} %get-tuple-element.38), channel_id=1, source_target_pairs={{8,0},{56,8},{16,16},{32,24},{24,32},{40,40},{0,48},{48,56},{72,64... | collective-permute-start | bytes 196616 | tf_op jit(solution)/shard_map/upstream_to_units/ppermute | solution.py:428
  24.3 39.9 %all-to-all-start.1 = ((bf16[32,19,8,128]{3,2,1,0:T(8,128)(2,1)}), bf16[32,19,8,128]{3,2,1,0:T(8,128)(2,1)S(1)}, u32[]{:S(2)}, u32[]{:S(2)}) async-start(bf16[32,19,8,128]{3,2,1,0:T(8,128)(2,1)} %deal.1), calls=%async_computation.1 | async-start | bytes 2490368 | tf_op jit(solution)/shard_map/tiles/all_to_all | solution.py:448
  34.6 31.0 %collective-permute-start.3 = (bf16[2,128,128]{2,1,0:T(8,128)(2,1)S(1)}, bf16[2,128,128]{2,1,0:T(8,128)(2,1)S(1)}, u32[]{:S(2)}, u32[]{:S(2)}) collective-permute-start(bf16[2,128,128]{2,1,0:T(8,128)(2,1)S(1)} %get-tuple-element.40), channel_id=1, source_target_pairs={{40,0},{24,8},{48,16},{0,24},{56,32},{8,40},{32,48},{16,56},{104,6... | collective-permute-start | bytes 196616 | tf_op jit(solution)/shard_map/upstream_to_units/ppermute | solution.py:428
  37.1 27.8 %collective-permute-start.4 = (bf16[128,128]{1,0:T(8,128)(2,1)S(1)}, bf16[128,128]{1,0:T(8,128)(2,1)S(1)}, u32[]{:S(2)}, u32[]{:S(2)}) collective-permute-start(bf16[128,128]{1,0:T(8,128)(2,1)S(1)} %get-tuple-element.41), channel_id=1, source_target_pairs={{16,0},{48,8},{24,16},{56,24},{0,32},{32,40},{8,48},{40,56},{80,64... | collective-permute-start | bytes 98312 | tf_op jit(solution)/shard_map/upstream_to_units/ppermute | solution.py:428
  37.9 27.0 %collective-permute-start.5 = (bf16[128,128]{1,0:T(8,128)(2,1)S(1)}, bf16[128,128]{1,0:T(8,128)(2,1)S(1)}, u32[]{:S(2)}, u32[]{:S(2)}) collective-permute-start(bf16[128,128]{1,0:T(8,128)(2,1)S(1)} %get-tuple-element.42), channel_id=1, source_target_pairs={{48,0},{16,8},{56,16},{24,24},{32,32},{0,40},{40,48},{8,56},{112,6... | collective-permute-start | bytes 98312 | tf_op jit(solution)/shard_map/upstream_to_units/ppermute | solution.py:428
  65.7 10.0 %collective-permute-start.7 = (bf16[14,128,128]{2,1,0:T(8,128)(2,1)S(1)}, bf16[14,128,128]{2,1,0:T(8,128)(2,1)S(1)}, u32[]{:S(2)}, u32[]{:S(2)}) collective-permute-start(bf16[14,128,128]{2,1,0:T(8,128)(2,1)S(1)} %get-tuple-element.68), channel_id=1, source_target_pairs={{64,0},{72,8},{80,16},{88,24},{96,32},{104,40},{112,48},{120,56},{... | collective-permute-start | bytes 1376264 | tf_op jit(solution)/shard_map/halos/ppermute | solution.py:428
  68.5 10.3 %collective-permute-start.6 = (bf16[14,128,128]{2,1,0:T(8,128)(2,1)S(1)}, bf16[14,128,128]{2,1,0:T(8,128)(2,1)S(1)}, u32[]{:S(2)}, u32[]{:S(2)}) collective-permute-start(bf16[14,128,128]{2,1,0:T(8,128)(2,1)S(1)} %get-tuple-element.69), channel_id=1, source_target_pairs={{0,64},{8,72},{16,80},{24,88},{32,96},{40,104},{48,112},{56,120},{... | collective-permute-start | bytes 1376264 | tf_op jit(solution)/shard_map/halos/ppermute | solution.py:428
  86.9 9.2 %collective-permute-start.8 = (bf16[2,7,128,128]{3,2,1,0:T(8,128)(2,1)S(1)}, bf16[2,7,128,128]{3,2,1,0:T(8,128)(2,1)S(1)}, u32[]{:S(2)}, u32[]{:S(2)}) collective-permute-start(bf16[2,7,128,128]{3,2,1,0:T(8,128)(2,1)S(1)} %get-tuple-element.52), channel_id=1, source_target_pairs={{0,64},{8,72},{16,80},{24,88},{32,96},{40,104},{48,112},{56,120},{... | collective-permute-start | bytes 1376264 | tf_op jit(solution)/shard_map/row_terms/ppermute | solution.py:428
  88.9 9.7 %collective-permute-start.9 = (bf16[2,7,128,128]{3,2,1,0:T(8,128)(2,1)S(1)}, bf16[2,7,128,128]{3,2,1,0:T(8,128)(2,1)S(1)}, u32[]{:S(2)}, u32[]{:S(2)}) collective-permute-start(bf16[2,7,128,128]{3,2,1,0:T(8,128)(2,1)S(1)} %get-tuple-element.53), channel_id=1, source_target_pairs={{64,0},{72,8},{80,16},{88,24},{96,32},{104,40},{112,48},{120,56},{... | collective-permute-start | bytes 1376264 | tf_op jit(solution)/shard_map/row_terms/ppermute | solution.py:428
  99.2 27.5 %collective-permute-start.12 = (bf16[4,2,128,128]{3,2,1,0:T(8,128)(2,1)S(1)}, bf16[4,2,128,128]{3,2,1,0:T(8,128)(2,1)S(1)}, u32[]{:S(2)}, u32[]{:S(2)}) collective-permute-start(bf16[4,2,128,128]{3,2,1,0:T(8,128)(2,1)S(1)} %get-tuple-element.60), channel_id=1, source_target_pairs={{0,8},{8,56},{16,16},{24,32},{32,24},{40,40},{48,0},{56,48},{64,72... | collective-permute-start | bytes 786440 | tf_op jit(solution)/shard_map/column_terms/ppermute | solution.py:428
  99.9 26.8 %collective-permute-start.13 = (bf16[4,2,128,128]{3,2,1,0:T(8,128)(2,1)S(1)}, bf16[4,2,128,128]{3,2,1,0:T(8,128)(2,1)S(1)}, u32[]{:S(2)}, u32[]{:S(2)}) collective-permute-start(bf16[4,2,128,128]{3,2,1,0:T(8,128)(2,1)S(1)} %get-tuple-element.61), channel_id=1, source_target_pairs={{0,40},{8,24},{16,48},{24,0},{32,56},{40,8},{48,32},{56,16},{64,10... | collective-permute-start | bytes 786440 | tf_op jit(solution)/shard_map/column_terms/ppermute | solution.py:428
  109.5 16.5 %collective-permute-start.10 = (bf16[2,2,128,128]{3,2,1,0:T(8,128)(2,1)S(1)}, bf16[2,2,128,128]{3,2,1,0:T(8,128)(2,1)S(1)}, u32[]{:S(2)}, u32[]{:S(2)}) collective-permute-start(bf16[2,2,128,128]{3,2,1,0:T(8,128)(2,1)S(1)} %get-tuple-element.54), channel_id=1, source_target_pairs={{0,8},{8,16},{16,24},{24,32},{32,40},{40,48},{48,56},{64,72},{72,8... | collective-permute-start | bytes 393224 | tf_op jit(solution)/shard_map/column_terms/ppermute | solution.py:428
  113.9 12.0 %collective-permute-start.11 = (bf16[2,2,128,128]{3,2,1,0:T(8,128)(2,1)S(1)}, bf16[2,2,128,128]{3,2,1,0:T(8,128)(2,1)S(1)}, u32[]{:S(2)}, u32[]{:S(2)}) collective-permute-start(bf16[2,2,128,128]{3,2,1,0:T(8,128)(2,1)S(1)} %get-tuple-element.55), channel_id=1, source_target_pairs={{8,0},{16,8},{24,16},{32,24},{40,32},{48,40},{56,48},{72,64},{80,7... | collective-permute-start | bytes 393224 | tf_op jit(solution)/shard_map/column_terms/ppermute | solution.py:428
  126.7 29.0 %collective-permute-start.14 = (bf16[4,2,128,128]{3,2,1,0:T(8,128)(2,1)S(1)}, bf16[4,2,128,128]{3,2,1,0:T(8,128)(2,1)S(1)}, u32[]{:S(2)}, u32[]{:S(2)}) collective-permute-start(bf16[4,2,128,128]{3,2,1,0:T(8,128)(2,1)S(1)} %get-tuple-element.64), channel_id=1, source_target_pairs={{0,0},{8,32},{16,8},{24,40},{32,16},{40,48},{48,24},{56,56},{64,64... | collective-permute-start | bytes 786440 | tf_op jit(solution)/shard_map/outputs_home/ppermute | solution.py:428
  129.0 26.6 %collective-permute-start.15 = (bf16[4,2,128,128]{3,2,1,0:T(8,128)(2,1)S(1)}, bf16[4,2,128,128]{3,2,1,0:T(8,128)(2,1)S(1)}, u32[]{:S(2)}, u32[]{:S(2)}) collective-permute-start(bf16[4,2,128,128]{3,2,1,0:T(8,128)(2,1)S(1)} %get-tuple-element.65), channel_id=1, source_target_pairs={{0,32},{8,0},{16,40},{24,8},{32,48},{40,16},{48,56},{56,24},{64,96... | collective-permute-start | bytes 786440 | tf_op jit(solution)/shard_map/outputs_home/ppermute | solution.py:428
  132.1 19.8 %collective-permute-start.16 = (bf16[4,128,128]{2,1,0:T(8,128)(2,1)S(1)}, bf16[4,128,128]{2,1,0:T(8,128)(2,1)S(1)}, u32[]{:S(2)}, u32[]{:S(2)}) collective-permute-start(bf16[4,128,128]{2,1,0:T(8,128)(2,1)S(1)} %get-tuple-element.66), channel_id=1, source_target_pairs={{0,16},{8,48},{16,24},{24,56},{32,0},{40,32},{48,8},{56,40},{64,80... | collective-permute-start | bytes 393224 | tf_op jit(solution)/shard_map/outputs_home/ppermute | solution.py:428
  133.3 18.6 %collective-permute-start.17 = (bf16[4,128,128]{2,1,0:T(8,128)(2,1)S(1)}, bf16[4,128,128]{2,1,0:T(8,128)(2,1)S(1)}, u32[]{:S(2)}, u32[]{:S(2)}) collective-permute-start(bf16[4,128,128]{2,1,0:T(8,128)(2,1)S(1)} %get-tuple-element.67), channel_id=1, source_target_pairs={{0,48},{8,16},{16,56},{24,24},{32,32},{40,0},{48,40},{56,8},{64,11... | collective-permute-start | bytes 393224 | tf_op jit(solution)/shard_map/outputs_home/ppermute | solution.py:428

commit v6 on v5

--- a/solution.py
+++ b/solution.py
@@ -29,10 +29,16 @@
     return pairs
 
 
+def run_at(slot):
+    return (5 - slot) % SLOTS
+
+
 def shifted(rows, columns):
     def step(strip, slot):
-        there = (strip + rows, slot + columns)
-        return there if 0 <= there[0] < STRIPS and 0 <= there[1] < SLOTS else None
+        there = (strip + rows, run_at(slot) + columns)
+        if 0 <= there[0] < STRIPS and 0 <= there[1] < SLOTS:
+            return there[0], run_at(there[1])
+        return None
 
     return route(step)
 
@@ -43,8 +49,9 @@
 
 def owner_of(which, turn):
     def step(strip, slot):
-        odd = slot % 2
-        unit = 5 * slot + first_of(which, odd)
+        run = run_at(slot)
+        odd = run % 2
+        unit = 5 * run + first_of(which, odd)
         return (strip, ((turn + odd) % 2) * 4 + (unit % 8) // 2)
 
     return route(step)
@@ -92,7 +99,9 @@
 def place_table():
     owners = owner_rows()
     rows = [
-        owners[slot] + [strip, slot % 2] + [(5 * slot + at) % 8 for at in range(5)]
+        owners[slot]
+        + [strip, run_at(slot) % 2]
+        + [(5 * run_at(slot) + at) % 8 for at in range(5)]
         for strip in range(STRIPS)
         for slot in range(SLOTS)
     ]
@@ -133,22 +142,25 @@
 
 def gather_kernel(table, *refs):
     free, late, singles = refs[:2], refs[2:4], refs[4:6]
-    outs, single = refs[6:10], refs[10]
+    outs = refs[6:10]
     line = lax.broadcasted_iota(jnp.int32, (2 * TILE, 2 * TILE), 0)
     col = lax.broadcasted_iota(jnp.int32, (2 * TILE, 2 * TILE), 1)
     source = ((line >> 2) & 1) * TILE + (line >> 3) * 4 + (line & 3)
     order = (col == source).astype(LOW)
-    for kind, out in enumerate(outs):
-        for at in range(4):
-            head = pl.multiple_of(table[at] * HEAD_DIM, HEAD_DIM)
-            tiles = (late, free)[at // 2][at % 2][kind].reshape(2 * TILE, HEAD_DIM)
-            out[:, pl.ds(head, HEAD_DIM)] = nn(order, tiles).astype(LOW)
-        flip = table[6] == 1
-        one, two = singles[0][kind], singles[1][kind]
-        single[:TILE] = jnp.where(flip, two, one)
-        single[TILE:] = jnp.where(flip, one, two)
-        head = pl.multiple_of(table[4] * HEAD_DIM, HEAD_DIM)
-        out[:, pl.ds(head, HEAD_DIM)] = nn(order, single[...]).astype(LOW)
+    flip = table[6] == 1
+
+    def place(at, tiles):
+        head = pl.multiple_of(table[at] * HEAD_DIM, HEAD_DIM)
+        ordered = nn(order, jnp.concatenate(tiles, axis=1)).astype(LOW)
+        for kind, out in enumerate(outs):
+            out[:, pl.ds(head, HEAD_DIM)] = ordered[:, kind * HEAD_DIM : (kind + 1) * HEAD_DIM]
+
+    for at in range(4):
+        received = (late, free)[at // 2][at % 2]
+        place(at, [received[kind].reshape(2 * TILE, HEAD_DIM) for kind in range(4)])
+    one, two = singles[0][...], singles[1][...]
+    tops, lows = jnp.where(flip, two, one), jnp.where(flip, one, two)
+    place(4, [jnp.concatenate([tops[kind], lows[kind]], axis=0) for kind in range(4)])
 
 
 def gather(table, received):
@@ -157,16 +169,35 @@
         out_shape=[jax.ShapeDtypeStruct((2 * TILE, HEADS_HERE * HEAD_DIM), LOW)] * 4,
         in_specs=[pl.BlockSpec(memory_space=pltpu.SMEM)] + whole(6),
         out_specs=whole(4),
-        scratch_shapes=[pltpu.VMEM((2 * TILE, HEAD_DIM), LOW)],
         compiler_params=pltpu.CompilerParams(vmem_limit_bytes=16 << 20),
         name="gather",
     )(table, *received)
 
 
+def pack_kernel(query, key, value, out):
+    for kind, slab in enumerate((query, key, value)):
+        for group in range(8):
+            for head in range(HEADS_HERE):
+                at = (group * HEADS_HERE + head) * HEAD_DIM
+                lines = slab[0, :, :, at : at + HEAD_DIM]
+                out[group, kind, head] = lines.reshape(32, HEAD_DIM)
+
+
+def pack(query, key, value):
+    return pl.pallas_call(
+        pack_kernel,
+        out_shape=jax.ShapeDtypeStruct((8, 3, HEADS_HERE, 32, HEAD_DIM), LOW),
+        in_specs=whole(3),
+        out_specs=whole(1)[0],
+        compiler_params=pltpu.CompilerParams(vmem_limit_bytes=16 << 20),
+        name="pack",
+    )(query, key, value)
+
+
 def deal_kernel(swapped, out):
     for slot in range(SLOTS):
         for at in range(7):
-            unit = min(max(5 * slot + at - 1, 0), 39)
+            unit = min(max(5 * run_at(slot) + at - 1, 0), 39)
             head, column = unit // 8, unit % 8
             for kind in range(3):
                 if kind == 0 and not 1 <= at <= 5:
@@ -438,11 +469,8 @@
         grads = send_all(spread(place, upstream), [flipped(path) for path in to_owner])
 
     with jax.named_scope("heads"):
-        lines = [
-            slab.reshape(8, 4, 40, 128).transpose(2, 0, 1, 3).reshape(8, 5, 32, 128)
-            for slab in (query_slab, key_slab, value_slab)
-        ]
-        swapped = lax.all_to_all(jnp.stack(lines, axis=1), "head", 0, 0, tiled=True)
+        lines = pack(query_slab, key_slab, value_slab)
+        swapped = lax.all_to_all(lines, "head", 0, 0, tiled=True)
     with jax.named_scope("tiles"):
         dealt, early = lax.optimization_barrier((deal(swapped), grads[:EARLY]))
         got = lax.all_to_all(dealt, "tile", 0, 0, tiled=True)

time: 158 us -> 159 us (level)
  the two profiles are of different devices: /device:TPU:73 before, /device:TPU:40 now
where the time goes in v6:
time: 159 us; the launch traced here: 157 us
  starting transfers between devices  86.9 us (55%)
  waiting for transfers between devices  50 us (31%)
  Pallas kernels  15.2 us (10%)
  local copies, waits for them, and re-layouts  4.34 us (3%)
    ppermute x18, starting transfers between devices, send_all(): lax.ppermute(part, 'tile', path)  71.7 us
    ppermute x18, waiting for transfers between devices, send_all(): lax.ppermute(part, 'tile', path)  29.3 us
    all_to_all x1, waiting for transfers between devices, local(): got = lax.all_to_all(dealt, 'tile', 0, 0, tiled=True)  20.6 us
    all_to_all x1, starting transfers between devices, local(): got = lax.all_to_all(dealt, 'tile', 0, 0, tiled=True)  10.8 us
    pallas_call x1, Pallas kernels, attend(): pl.pallas_call(attend_kernel, out_shape=[jax.ShapeDtypeStruct((2, 2, 5, T...  8.13 us
    all_to_all x1, starting transfers between devices, local(): swapped = lax.all_to_all(lines, 'head', 0, 0, tiled=True)  4.43 us
  transfers between devices with their start and end apart: 20, of which 9 were waited for; matrix products, arithmetic and copies ran while one was open for 1% of the time, Pallas kernels for 2%

profile of v6, /device:TPU:40, one launch (start us, length us, event | category | flops | bytes accessed | tf_op | source)
XLA Modules:
  0.0 157.3 jit_solution(9136775372692594256)
XLA Ops:
  0.6 1.0 copy-done.1
  1.6 1.0 copy-done.2
  2.6 1.0 copy-done.3
  3.6 1.4 pack.1
  4.9 4.4 %all-to-all-start = ((bf16[8,3,5,32,128]{4,3,2,1,0:T(8,128)(2,1)}), bf16[8,3,5,32,128]{4,3,2,1,0:T(8,128)(2,1)S(1)}, u32[]{:S(2)}, u32[]{:S(2)}) async-start(bf16[8,3,5,32,128]{4,3,2,1,0:T(8,128)(2,1)} %pack.1), calls=%async_computation | async-start | bytes 1966080 | tf_op jit(solution)/shard_map/heads/all_to_all | solution.py:473
  9.4 0.7 dynamic-slice_bitcast_fusion.table
  10.0 0.9 spread.1
  11.0 5.2 %collective-permute-start = (bf16[2,128,128]{2,1,0:T(8,128)(2,1)S(1)}, bf16[2,128,128]{2,1,0:T(8,128)(2,1)S(1)}, u32[]{:S(2)}, u32[]{:S(2)}) collective-permute-start(bf16[2,128,128]{2,1,0:T(8,128)(2,1)S(1)} %get-tuple-element.36), channel_id=1, source_target_pairs={{48,0},{16,8},{40,16},{8,24},{32,32},{0,40},{56,48},{24,56},{112,6... | collective-permute-start | bytes 196616 | tf_op jit(solution)/shard_map/upstream_to_units/ppermute | solution.py:459
  16.1 1.9 %collective-permute-start.1 = (bf16[2,128,128]{2,1,0:T(8,128)(2,1)S(1)}, bf16[2,128,128]{2,1,0:T(8,128)(2,1)S(1)}, u32[]{:S(2)}, u32[]{:S(2)}) collective-permute-start(bf16[2,128,128]{2,1,0:T(8,128)(2,1)S(1)} %get-tuple-element.37), channel_id=1, source_target_pairs={{16,0},{48,8},{8,16},{40,24},{0,32},{32,40},{24,48},{56,56},{80,64... | collective-permute-start | bytes 196616 | tf_op jit(solution)/shard_map/upstream_to_units/ppermute | solution.py:459
  18.1 10.0 %collective-permute-start.2 = (bf16[2,128,128]{2,1,0:T(8,128)(2,1)S(1)}, bf16[2,128,128]{2,1,0:T(8,128)(2,1)S(1)}, u32[]{:S(2)}, u32[]{:S(2)}) collective-permute-start(bf16[2,128,128]{2,1,0:T(8,128)(2,1)S(1)} %get-tuple-element.38), channel_id=1, source_target_pairs={{40,0},{24,8},{32,16},{16,24},{56,32},{8,40},{48,48},{0,56},{104,6... | collective-permute-start | bytes 196616 | tf_op jit(solution)/shard_map/upstream_to_units/ppermute | solution.py:459
  28.0 0.0 all-to-all-done.swapped
  28.0 1.3 deal.1
  29.3 0.0 collective-permute-done.refs_0_
  29.3 0.0 collective-permute-done.1.refs_1_
  29.3 0.6 collective-permute-done.2.refs_2_
  29.9 10.8 %all-to-all-start.1 = ((bf16[32,19,8,128]{3,2,1,0:T(8,128)(2,1)}), bf16[32,19,8,128]{3,2,1,0:T(8,128)(2,1)S(1)}, u32[]{:S(2)}, u32[]{:S(2)}) async-start(bf16[32,19,8,128]{3,2,1,0:T(8,128)(2,1)} %deal.1), calls=%async_computation.1 | async-start | bytes 2490368 | tf_op jit(solution)/shard_map/tiles/all_to_all | solution.py:476
  40.7 2.5 %collective-permute-start.3 = (bf16[2,128,128]{2,1,0:T(8,128)(2,1)S(1)}, bf16[2,128,128]{2,1,0:T(8,128)(2,1)S(1)}, u32[]{:S(2)}, u32[]{:S(2)}) collective-permute-start(bf16[2,128,128]{2,1,0:T(8,128)(2,1)S(1)} %get-tuple-element.40), channel_id=1, source_target_pairs={{8,0},{56,8},{0,16},{48,24},{24,32},{40,40},{16,48},{32,56},{72,64... | collective-permute-start | bytes 196616 | tf_op jit(solution)/shard_map/upstream_to_units/ppermute | solution.py:459
  43.2 5.5 %collective-permute-start.4 = (bf16[128,128]{1,0:T(8,128)(2,1)S(1)}, bf16[128,128]{1,0:T(8,128)(2,1)S(1)}, u32[]{:S(2)}, u32[]{:S(2)}) collective-permute-start(bf16[128,128]{1,0:T(8,128)(2,1)S(1)} %get-tuple-element.41), channel_id=1, source_target_pairs={{32,0},{0,8},{56,16},{24,24},{48,32},{16,40},{40,48},{8,56},{96,64... | collective-permute-start | bytes 98312 | tf_op jit(solution)/shard_map/upstream_to_units/ppermute | solution.py:459
  48.7 4.3 %collective-permute-start.5 = (bf16[128,128]{1,0:T(8,128)(2,1)S(1)}, bf16[128,128]{1,0:T(8,128)(2,1)S(1)}, u32[]{:S(2)}, u32[]{:S(2)}) collective-permute-start(bf16[128,128]{1,0:T(8,128)(2,1)S(1)} %get-tuple-element.42), channel_id=1, source_target_pairs={{0,0},{32,8},{24,16},{56,24},{16,32},{48,40},{8,48},{40,56},{64,64... | collective-permute-start | bytes 98312 | tf_op jit(solution)/shard_map/upstream_to_units/ppermute | solution.py:459
  53.0 20.6 %all-to-all-done.1 = bf16[32,19,8,128]{3,2,1,0:T(8,128)(2,1)S(1)} async-done(((bf16[32,19,8,128]{3,2,1,0:T(8,128)(2,1)}), bf16[32,19,8,128]{3,2,1,0:T(8,128)(2,1)S(1)}, u32[]{:S(2)}, u32[]{:S(2)}) %all-to-all-start.1) | async-done | bytes 1245216 | tf_op jit(solution)/shard_map/tiles/all_to_all | solution.py:476
  73.6 0.7 copy.9
  74.3 0.0 collective-permute-done.4.refs_4_
  74.3 0.0 collective-permute-done.3.refs_3_
  74.3 0.1 slice_bitcast_fusion
  74.4 2.5 %collective-permute-start.7 = (bf16[14,128,128]{2,1,0:T(8,128)(2,1)S(1)}, bf16[14,128,128]{2,1,0:T(8,128)(2,1)S(1)}, u32[]{:S(2)}, u32[]{:S(2)}) collective-permute-start(bf16[14,128,128]{2,1,0:T(8,128)(2,1)S(1)} %get-tuple-element.68), channel_id=1, source_target_pairs={{64,0},{72,8},{80,16},{88,24},{96,32},{104,40},{112,48},{120,56},{... | collective-permute-start | bytes 1376264 | tf_op jit(solution)/shard_map/halos/ppermute | solution.py:459
  76.9 3.4 %collective-permute-start.6 = (bf16[14,128,128]{2,1,0:T(8,128)(2,1)S(1)}, bf16[14,128,128]{2,1,0:T(8,128)(2,1)S(1)}, u32[]{:S(2)}, u32[]{:S(2)}) collective-permute-start(bf16[14,128,128]{2,1,0:T(8,128)(2,1)S(1)} %get-tuple-element.69), channel_id=1, source_target_pairs={{0,64},{8,72},{16,80},{24,88},{32,96},{40,104},{48,112},{56,120},{... | collective-permute-start | bytes 1376264 | tf_op jit(solution)/shard_map/halos/ppermute | solution.py:459
  80.2 4.5 %collective-permute-done.7.below = bf16[14,128,128]{2,1,0:T(8,128)(2,1)S(1)} collective-permute-done((bf16[14,128,128]{2,1,0:T(8,128)(2,1)S(1)}, bf16[14,128,128]{2,1,0:T(8,128)(2,1)S(1)}, u32[]{:S(2)}, u32[]{:S(2)}) %collective-permute-start.7) | collective-permute-done | bytes 458784 | tf_op jit(solution)/shard_map/halos/ppermute | solution.py:459
  84.8 2.5 %collective-permute-done.6.above = bf16[14,128,128]{2,1,0:T(8,128)(2,1)S(1)} collective-permute-done((bf16[14,128,128]{2,1,0:T(8,128)(2,1)S(1)}, bf16[14,128,128]{2,1,0:T(8,128)(2,1)S(1)}, u32[]{:S(2)}, u32[]{:S(2)}) %collective-permute-start.6) | collective-permute-done | bytes 458784 | tf_op jit(solution)/shard_map/halos/ppermute | solution.py:459
  87.2 8.1 %attend.1 = (bf16[2,2,5,128,128]{4,3,2,1,0:T(8,128)(2,1)S(1)}, f32[2,2,7,128,128]{4,3,2,1,0:T(8,128)S(1)}, bf16[2,7,128,128]{3,2,1,0:T(8,128)(2,1)S(1)}, bf16[2,7,128,128]{3,2,1,0:T(8,128)(2,1)S(1)}) custom-call(s32[14]{0:T(128)S(1)} %dynamic-slice_bitcast_fusion.table, bf16[2,19,128,128]{3,2,1,0:T(8,128)(2,1)S(1)} %bitcast.11, ...), custom_call_target="tpu_custom_call" | custom-call | flops 3000000000 | bytes 8000000 | tf_op jit(solution)/shard_map/attention/attend/pallas_call | solution.py:368
  95.4 3.4 %collective-permute-start.8 = (bf16[2,7,128,128]{3,2,1,0:T(8,128)(2,1)S(1)}, bf16[2,7,128,128]{3,2,1,0:T(8,128)(2,1)S(1)}, u32[]{:S(2)}, u32[]{:S(2)}) collective-permute-start(bf16[2,7,128,128]{3,2,1,0:T(8,128)(2,1)S(1)} %get-tuple-element.52), channel_id=1, source_target_pairs={{0,64},{8,72},{16,80},{24,88},{32,96},{40,104},{48,112},{56,120},{... | collective-permute-start | bytes 1376264 | tf_op jit(solution)/shard_map/row_terms/ppermute | solution.py:459
  98.8 2.5 %collective-permute-start.9 = (bf16[2,7,128,128]{3,2,1,0:T(8,128)(2,1)S(1)}, bf16[2,7,128,128]{3,2,1,0:T(8,128)(2,1)S(1)}, u32[]{:S(2)}, u32[]{:S(2)}) collective-permute-start(bf16[2,7,128,128]{3,2,1,0:T(8,128)(2,1)S(1)} %get-tuple-element.53), channel_id=1, source_target_pairs={{64,0},{72,8},{80,16},{88,24},{96,32},{104,40},{112,48},{120,56},{... | collective-permute-start | bytes 1376264 | tf_op jit(solution)/shard_map/row_terms/ppermute | solution.py:459
  101.2 4.5 %collective-permute-done.8.above = bf16[2,7,128,128]{3,2,1,0:T(8,128)(2,1)S(1)} collective-permute-done((bf16[2,7,128,128]{3,2,1,0:T(8,128)(2,1)S(1)}, bf16[2,7,128,128]{3,2,1,0:T(8,128)(2,1)S(1)}, u32[]{:S(2)}, u32[]{:S(2)}) %collective-permute-start.8) | collective-permute-done | bytes 458784 | tf_op jit(solution)/shard_map/row_terms/ppermute | solution.py:459
  105.7 3.4 %collective-permute-done.9.below = bf16[2,7,128,128]{3,2,1,0:T(8,128)(2,1)S(1)} collective-permute-done((bf16[2,7,128,128]{3,2,1,0:T(8,128)(2,1)S(1)}, bf16[2,7,128,128]{3,2,1,0:T(8,128)(2,1)S(1)}, u32[]{:S(2)}, u32[]{:S(2)}) %collective-permute-start.9) | collective-permute-done | bytes 458784 | tf_op jit(solution)/shard_map/row_terms/ppermute | solution.py:459
  109.1 0.7 rims.1
  109.8 4.2 %collective-permute-start.12 = (bf16[4,2,128,128]{3,2,1,0:T(8,128)(2,1)S(1)}, bf16[4,2,128,128]{3,2,1,0:T(8,128)(2,1)S(1)}, u32[]{:S(2)}, u32[]{:S(2)}) collective-permute-start(bf16[4,2,128,128]{3,2,1,0:T(8,128)(2,1)S(1)} %get-tuple-element.60), channel_id=1, source_target_pairs={{0,40},{8,24},{16,32},{24,16},{32,56},{40,8},{48,48},{56,0},{64,10... | collective-permute-start | bytes 786440 | tf_op jit(solution)/shard_map/column_terms/ppermute | solution.py:459
  114.0 5.1 %collective-permute-start.13 = (bf16[4,2,128,128]{3,2,1,0:T(8,128)(2,1)S(1)}, bf16[4,2,128,128]{3,2,1,0:T(8,128)(2,1)S(1)}, u32[]{:S(2)}, u32[]{:S(2)}) collective-permute-start(bf16[4,2,128,128]{3,2,1,0:T(8,128)(2,1)S(1)} %get-tuple-element.61), channel_id=1, source_target_pairs={{0,8},{8,56},{16,0},{24,48},{32,24},{40,40},{48,16},{56,32},{64,72... | collective-permute-start | bytes 786440 | tf_op jit(solution)/shard_map/column_terms/ppermute | solution.py:459
  119.1 1.9 %collective-permute-start.10 = (bf16[2,2,128,128]{3,2,1,0:T(8,128)(2,1)S(1)}, bf16[2,2,128,128]{3,2,1,0:T(8,128)(2,1)S(1)}, u32[]{:S(2)}, u32[]{:S(2)}) collective-permute-start(bf16[2,2,128,128]{3,2,1,0:T(8,128)(2,1)S(1)} %get-tuple-element.54), channel_id=1, source_target_pairs={{0,56},{8,0},{16,8},{24,16},{32,24},{40,32},{56,48},{64,120},{72,6... | collective-permute-start | bytes 393224 | tf_op jit(solution)/shard_map/column_terms/ppermute | solution.py:459
  121.0 3.9 %collective-permute-start.11 = (bf16[2,2,128,128]{3,2,1,0:T(8,128)(2,1)S(1)}, bf16[2,2,128,128]{3,2,1,0:T(8,128)(2,1)S(1)}, u32[]{:S(2)}, u32[]{:S(2)}) collective-permute-start(bf16[2,2,128,128]{3,2,1,0:T(8,128)(2,1)S(1)} %get-tuple-element.55), channel_id=1, source_target_pairs={{0,8},{8,16},{16,24},{24,32},{32,40},{48,56},{56,0},{64,72},{72,80... | collective-permute-start | bytes 393224 | tf_op jit(solution)/shard_map/column_terms/ppermute | solution.py:459
  124.9 3.3 %collective-permute-done.10.before = bf16[2,2,128,128]{3,2,1,0:T(8,128)(2,1)S(1)} collective-permute-done((bf16[2,2,128,128]{3,2,1,0:T(8,128)(2,1)S(1)}, bf16[2,2,128,128]{3,2,1,0:T(8,128)(2,1)S(1)}, u32[]{:S(2)}, u32[]{:S(2)}) %collective-permute-start.10) | collective-permute-done | bytes 131104 | tf_op jit(solution)/shard_map/column_terms/ppermute | solution.py:459
  128.3 2.5 %collective-permute-done.11.after = bf16[2,2,128,128]{3,2,1,0:T(8,128)(2,1)S(1)} collective-permute-done((bf16[2,2,128,128]{3,2,1,0:T(8,128)(2,1)S(1)}, bf16[2,2,128,128]{3,2,1,0:T(8,128)(2,1)S(1)}, u32[]{:S(2)}, u32[]{:S(2)}) %collective-permute-start.11) | collective-permute-done | bytes 131104 | tf_op jit(solution)/shard_map/column_terms/ppermute | solution.py:459
  130.8 0.7 combine.1
  131.5 0.0 collective-permute-done.12.refs_0_
  131.5 2.4 %collective-permute-start.14 = (bf16[4,2,128,128]{3,2,1,0:T(8,128)(2,1)S(1)}, bf16[4,2,128,128]{3,2,1,0:T(8,128)(2,1)S(1)}, u32[]{:S(2)}, u32[]{:S(2)}) collective-permute-start(bf16[4,2,128,128]{3,2,1,0:T(8,128)(2,1)S(1)} %get-tuple-element.64), channel_id=1, source_target_pairs={{0,48},{8,16},{16,40},{24,8},{32,32},{40,0},{48,56},{56,24},{64,11... | collective-permute-start | bytes 786440 | tf_op jit(solution)/shard_map/outputs_home/ppermute | solution.py:459
  134.0 5.1 %collective-permute-start.15 = (bf16[4,2,128,128]{3,2,1,0:T(8,128)(2,1)S(1)}, bf16[4,2,128,128]{3,2,1,0:T(8,128)(2,1)S(1)}, u32[]{:S(2)}, u32[]{:S(2)}) collective-permute-start(bf16[4,2,128,128]{3,2,1,0:T(8,128)(2,1)S(1)} %get-tuple-element.65), channel_id=1, source_target_pairs={{0,16},{8,48},{16,8},{24,40},{32,0},{40,32},{48,24},{56,56},{64,80... | collective-permute-start | bytes 786440 | tf_op jit(solution)/shard_map/outputs_home/ppermute | solution.py:459
  139.1 1.9 %collective-permute-start.16 = (bf16[4,128,128]{2,1,0:T(8,128)(2,1)S(1)}, bf16[4,128,128]{2,1,0:T(8,128)(2,1)S(1)}, u32[]{:S(2)}, u32[]{:S(2)}) collective-permute-start(bf16[4,128,128]{2,1,0:T(8,128)(2,1)S(1)} %get-tuple-element.66), channel_id=1, source_target_pairs={{0,32},{8,0},{16,56},{24,24},{32,48},{40,16},{48,40},{56,8},{64,96... | collective-permute-start | bytes 393224 | tf_op jit(solution)/shard_map/outputs_home/ppermute | solution.py:459
  141.0 6.1 %collective-permute-start.17 = (bf16[4,128,128]{2,1,0:T(8,128)(2,1)S(1)}, bf16[4,128,128]{2,1,0:T(8,128)(2,1)S(1)}, u32[]{:S(2)}, u32[]{:S(2)}) collective-permute-start(bf16[4,128,128]{2,1,0:T(8,128)(2,1)S(1)} %get-tuple-element.67), channel_id=1, source_target_pairs={{0,0},{8,32},{16,24},{24,56},{32,16},{40,48},{48,8},{56,40},{64,64... | collective-permute-start | bytes 393224 | tf_op jit(solution)/shard_map/outputs_home/ppermute | solution.py:459
  147.2 8.0 %collective-permute-done.16.refs_4_ = bf16[4,128,128]{2,1,0:T(8,128)(2,1)S(1)} collective-permute-done((bf16[4,128,128]{2,1,0:T(8,128)(2,1)S(1)}, bf16[4,128,128]{2,1,0:T(8,128)(2,1)S(1)}, u32[]{:S(2)}, u32[]{:S(2)}) %collective-permute-start.16) | collective-permute-done | bytes 131104 | tf_op jit(solution)/shard_map/outputs_home/ppermute | solution.py:459
  155.2 2.1 %gather.1 = (bf16[256,640]{1,0:T(8,128)(2,1)}, bf16[256,640]{1,0:T(8,128)(2,1)}, bf16[256,640]{1,0:T(8,128)(2,1)}, bf16[256,640]{1,0:T(8,128)(2,1)}) custom-call(s32[14]{0:T(128)S(1)} %dynamic-slice_bitcast_fusion.table, bf16[4,2,128,128]{3,2,1,0:T(8,128)(2,1)S(1)} %collective-permute-done.12.refs_0_, ...), custom_call_target="tpu_custom_call" | custom-call | tf_op jit(solution)/shard_map/settle/gather/pallas_call | solution.py:167
  (10 shorter events, 0.0 us)
Async XLA Ops:
  0.6 1.0 copy-start.1
  1.6 1.0 copy-start.2
  2.6 1.0 copy-start.3
  4.9 5.1 %copy-start = (bf16[256,640]{1,0:T(8,128)(2,1)S(1)}, bf16[256,640]{1,0:T(8,128)(2,1)}, u32[]{:S(2)}) copy-start(bf16[256,640]{1,0:T(8,128)(2,1)} %upstream.1) | copy-start | bytes 983044
  4.9 23.1 %all-to-all-start = ((bf16[8,3,5,32,128]{4,3,2,1,0:T(8,128)(2,1)}), bf16[8,3,5,32,128]{4,3,2,1,0:T(8,128)(2,1)S(1)}, u32[]{:S(2)}, u32[]{:S(2)}) async-start(bf16[8,3,5,32,128]{4,3,2,1,0:T(8,128)(2,1)} %pack.1), calls=%async_computation | async-start | bytes 1966080 | tf_op jit(solution)/shard_map/heads/all_to_all | solution.py:473
  11.0 18.4 %collective-permute-start = (bf16[2,128,128]{2,1,0:T(8,128)(2,1)S(1)}, bf16[2,128,128]{2,1,0:T(8,128)(2,1)S(1)}, u32[]{:S(2)}, u32[]{:S(2)}) collective-permute-start(bf16[2,128,128]{2,1,0:T(8,128)(2,1)S(1)} %get-tuple-element.36), channel_id=1, source_target_pairs={{48,0},{16,8},{40,16},{8,24},{32,32},{0,40},{56,48},{24,56},{112,6... | collective-permute-start | bytes 196616 | tf_op jit(solution)/shard_map/upstream_to_units/ppermute | solution.py:459
  16.1 13.2 %collective-permute-start.1 = (bf16[2,128,128]{2,1,0:T(8,128)(2,1)S(1)}, bf16[2,128,128]{2,1,0:T(8,128)(2,1)S(1)}, u32[]{:S(2)}, u32[]{:S(2)}) collective-permute-start(bf16[2,128,128]{2,1,0:T(8,128)(2,1)S(1)} %get-tuple-element.37), channel_id=1, source_target_pairs={{16,0},{48,8},{8,16},{40,24},{0,32},{32,40},{24,48},{56,56},{80,64... | collective-permute-start | bytes 196616 | tf_op jit(solution)/shard_map/upstream_to_units/ppermute | solution.py:459
  18.1 11.9 %collective-permute-start.2 = (bf16[2,128,128]{2,1,0:T(8,128)(2,1)S(1)}, bf16[2,128,128]{2,1,0:T(8,128)(2,1)S(1)}, u32[]{:S(2)}, u32[]{:S(2)}) collective-permute-start(bf16[2,128,128]{2,1,0:T(8,128)(2,1)S(1)} %get-tuple-element.38), channel_id=1, source_target_pairs={{40,0},{24,8},{32,16},{16,24},{56,32},{8,40},{48,48},{0,56},{104,6... | collective-permute-start | bytes 196616 | tf_op jit(solution)/shard_map/upstream_to_units/ppermute | solution.py:459
  29.9 43.7 %all-to-all-start.1 = ((bf16[32,19,8,128]{3,2,1,0:T(8,128)(2,1)}), bf16[32,19,8,128]{3,2,1,0:T(8,128)(2,1)S(1)}, u32[]{:S(2)}, u32[]{:S(2)}) async-start(bf16[32,19,8,128]{3,2,1,0:T(8,128)(2,1)} %deal.1), calls=%async_computation.1 | async-start | bytes 2490368 | tf_op jit(solution)/shard_map/tiles/all_to_all | solution.py:476
  40.7 33.6 %collective-permute-start.3 = (bf16[2,128,128]{2,1,0:T(8,128)(2,1)S(1)}, bf16[2,128,128]{2,1,0:T(8,128)(2,1)S(1)}, u32[]{:S(2)}, u32[]{:S(2)}) collective-permute-start(bf16[2,128,128]{2,1,0:T(8,128)(2,1)S(1)} %get-tuple-element.40), channel_id=1, source_target_pairs={{8,0},{56,8},{0,16},{48,24},{24,32},{40,40},{16,48},{32,56},{72,64... | collective-permute-start | bytes 196616 | tf_op jit(solution)/shard_map/upstream_to_units/ppermute | solution.py:459
  43.2 31.1 %collective-permute-start.4 = (bf16[128,128]{1,0:T(8,128)(2,1)S(1)}, bf16[128,128]{1,0:T(8,128)(2,1)S(1)}, u32[]{:S(2)}, u32[]{:S(2)}) collective-permute-start(bf16[128,128]{1,0:T(8,128)(2,1)S(1)} %get-tuple-element.41), channel_id=1, source_target_pairs={{32,0},{0,8},{56,16},{24,24},{48,32},{16,40},{40,48},{8,56},{96,64... | collective-permute-start | bytes 98312 | tf_op jit(solution)/shard_map/upstream_to_units/ppermute | solution.py:459
  48.7 25.6 %collective-permute-start.5 = (bf16[128,128]{1,0:T(8,128)(2,1)S(1)}, bf16[128,128]{1,0:T(8,128)(2,1)S(1)}, u32[]{:S(2)}, u32[]{:S(2)}) collective-permute-start(bf16[128,128]{1,0:T(8,128)(2,1)S(1)} %get-tuple-element.42), channel_id=1, source_target_pairs={{0,0},{32,8},{24,16},{56,24},{16,32},{48,40},{8,48},{40,56},{64,64... | collective-permute-start | bytes 98312 | tf_op jit(solution)/shard_map/upstream_to_units/ppermute | solution.py:459
  74.4 10.4 %collective-permute-start.7 = (bf16[14,128,128]{2,1,0:T(8,128)(2,1)S(1)}, bf16[14,128,128]{2,1,0:T(8,128)(2,1)S(1)}, u32[]{:S(2)}, u32[]{:S(2)}) collective-permute-start(bf16[14,128,128]{2,1,0:T(8,128)(2,1)S(1)} %get-tuple-element.68), channel_id=1, source_target_pairs={{64,0},{72,8},{80,16},{88,24},{96,32},{104,40},{112,48},{120,56},{... | collective-permute-start | bytes 1376264 | tf_op jit(solution)/shard_map/halos/ppermute | solution.py:459
  76.9 10.4 %collective-permute-start.6 = (bf16[14,128,128]{2,1,0:T(8,128)(2,1)S(1)}, bf16[14,128,128]{2,1,0:T(8,128)(2,1)S(1)}, u32[]{:S(2)}, u32[]{:S(2)}) collective-permute-start(bf16[14,128,128]{2,1,0:T(8,128)(2,1)S(1)} %get-tuple-element.69), channel_id=1, source_target_pairs={{0,64},{8,72},{16,80},{24,88},{32,96},{40,104},{48,112},{56,120},{... | collective-permute-start | bytes 1376264 | tf_op jit(solution)/shard_map/halos/ppermute | solution.py:459
  95.4 10.4 %collective-permute-start.8 = (bf16[2,7,128,128]{3,2,1,0:T(8,128)(2,1)S(1)}, bf16[2,7,128,128]{3,2,1,0:T(8,128)(2,1)S(1)}, u32[]{:S(2)}, u32[]{:S(2)}) collective-permute-start(bf16[2,7,128,128]{3,2,1,0:T(8,128)(2,1)S(1)} %get-tuple-element.52), channel_id=1, source_target_pairs={{0,64},{8,72},{16,80},{24,88},{32,96},{40,104},{48,112},{56,120},{... | collective-permute-start | bytes 1376264 | tf_op jit(solution)/shard_map/row_terms/ppermute | solution.py:459
  98.8 10.4 %collective-permute-start.9 = (bf16[2,7,128,128]{3,2,1,0:T(8,128)(2,1)S(1)}, bf16[2,7,128,128]{3,2,1,0:T(8,128)(2,1)S(1)}, u32[]{:S(2)}, u32[]{:S(2)}) collective-permute-start(bf16[2,7,128,128]{3,2,1,0:T(8,128)(2,1)S(1)} %get-tuple-element.53), channel_id=1, source_target_pairs={{64,0},{72,8},{80,16},{88,24},{96,32},{104,40},{112,48},{120,56},{... | collective-permute-start | bytes 1376264 | tf_op jit(solution)/shard_map/row_terms/ppermute | solution.py:459
  109.8 21.7 %collective-permute-start.12 = (bf16[4,2,128,128]{3,2,1,0:T(8,128)(2,1)S(1)}, bf16[4,2,128,128]{3,2,1,0:T(8,128)(2,1)S(1)}, u32[]{:S(2)}, u32[]{:S(2)}) collective-permute-start(bf16[4,2,128,128]{3,2,1,0:T(8,128)(2,1)S(1)} %get-tuple-element.60), channel_id=1, source_target_pairs={{0,40},{8,24},{16,32},{24,16},{32,56},{40,8},{48,48},{56,0},{64,10... | collective-permute-start | bytes 786440 | tf_op jit(solution)/shard_map/column_terms/ppermute | solution.py:459
  114.0 17.5 %collective-permute-start.13 = (bf16[4,2,128,128]{3,2,1,0:T(8,128)(2,1)S(1)}, bf16[4,2,128,128]{3,2,1,0:T(8,128)(2,1)S(1)}, u32[]{:S(2)}, u32[]{:S(2)}) collective-permute-start(bf16[4,2,128,128]{3,2,1,0:T(8,128)(2,1)S(1)} %get-tuple-element.61), channel_id=1, source_target_pairs={{0,8},{8,56},{16,0},{24,48},{32,24},{40,40},{48,16},{56,32},{64,72... | collective-permute-start | bytes 786440 | tf_op jit(solution)/shard_map/column_terms/ppermute | solution.py:459
  119.1 9.2 %collective-permute-start.10 = (bf16[2,2,128,128]{3,2,1,0:T(8,128)(2,1)S(1)}, bf16[2,2,128,128]{3,2,1,0:T(8,128)(2,1)S(1)}, u32[]{:S(2)}, u32[]{:S(2)}) collective-permute-start(bf16[2,2,128,128]{3,2,1,0:T(8,128)(2,1)S(1)} %get-tuple-element.54), channel_id=1, source_target_pairs={{0,56},{8,0},{16,8},{24,16},{32,24},{40,32},{56,48},{64,120},{72,6... | collective-permute-start | bytes 393224 | tf_op jit(solution)/shard_map/column_terms/ppermute | solution.py:459
  121.0 9.8 %collective-permute-start.11 = (bf16[2,2,128,128]{3,2,1,0:T(8,128)(2,1)S(1)}, bf16[2,2,128,128]{3,2,1,0:T(8,128)(2,1)S(1)}, u32[]{:S(2)}, u32[]{:S(2)}) collective-permute-start(bf16[2,2,128,128]{3,2,1,0:T(8,128)(2,1)S(1)} %get-tuple-element.55), channel_id=1, source_target_pairs={{0,8},{8,16},{16,24},{24,32},{32,40},{48,56},{56,0},{64,72},{72,80... | collective-permute-start | bytes 393224 | tf_op jit(solution)/shard_map/column_terms/ppermute | solution.py:459
  131.5 23.6 %collective-permute-start.14 = (bf16[4,2,128,128]{3,2,1,0:T(8,128)(2,1)S(1)}, bf16[4,2,128,128]{3,2,1,0:T(8,128)(2,1)S(1)}, u32[]{:S(2)}, u32[]{:S(2)}) collective-permute-start(bf16[4,2,128,128]{3,2,1,0:T(8,128)(2,1)S(1)} %get-tuple-element.64), channel_id=1, source_target_pairs={{0,48},{8,16},{16,40},{24,8},{32,32},{40,0},{48,56},{56,24},{64,11... | collective-permute-start | bytes 786440 | tf_op jit(solution)/shard_map/outputs_home/ppermute | solution.py:459
  134.0 21.2 %collective-permute-start.15 = (bf16[4,2,128,128]{3,2,1,0:T(8,128)(2,1)S(1)}, bf16[4,2,128,128]{3,2,1,0:T(8,128)(2,1)S(1)}, u32[]{:S(2)}, u32[]{:S(2)}) collective-permute-start(bf16[4,2,128,128]{3,2,1,0:T(8,128)(2,1)S(1)} %get-tuple-element.65), channel_id=1, source_target_pairs={{0,16},{8,48},{16,8},{24,40},{32,0},{40,32},{48,24},{56,56},{64,80... | collective-permute-start | bytes 786440 | tf_op jit(solution)/shard_map/outputs_home/ppermute | solution.py:459
  139.1 16.0 %collective-permute-start.16 = (bf16[4,128,128]{2,1,0:T(8,128)(2,1)S(1)}, bf16[4,128,128]{2,1,0:T(8,128)(2,1)S(1)}, u32[]{:S(2)}, u32[]{:S(2)}) collective-permute-start(bf16[4,128,128]{2,1,0:T(8,128)(2,1)S(1)} %get-tuple-element.66), channel_id=1, source_target_pairs={{0,32},{8,0},{16,56},{24,24},{32,48},{40,16},{48,40},{56,8},{64,96... | collective-permute-start | bytes 393224 | tf_op jit(solution)/shard_map/outputs_home/ppermute | solution.py:459
  141.0 14.1 %collective-permute-start.17 = (bf16[4,128,128]{2,1,0:T(8,128)(2,1)S(1)}, bf16[4,128,128]{2,1,0:T(8,128)(2,1)S(1)}, u32[]{:S(2)}, u32[]{:S(2)}) collective-permute-start(bf16[4,128,128]{2,1,0:T(8,128)(2,1)S(1)} %get-tuple-element.67), channel_id=1, source_target_pairs={{0,0},{8,32},{16,24},{24,56},{32,16},{40,48},{48,8},{56,40},{64,64... | collective-permute-start | bytes 393224 | tf_op jit(solution)/shard_map/outputs_home/ppermute | solution.py:459

commit v7 on v6

--- a/solution.py
+++ b/solution.py
@@ -174,44 +174,23 @@
     )(table, *received)
 
 
-def pack_kernel(query, key, value, out):
-    for kind, slab in enumerate((query, key, value)):
-        for group in range(8):
-            for head in range(HEADS_HERE):
-                at = (group * HEADS_HERE + head) * HEAD_DIM
-                lines = slab[0, :, :, at : at + HEAD_DIM]
-                out[group, kind, head] = lines.reshape(32, HEAD_DIM)
-
-
-def pack(query, key, value):
-    return pl.pallas_call(
-        pack_kernel,
-        out_shape=jax.ShapeDtypeStruct((8, 3, HEADS_HERE, 32, HEAD_DIM), LOW),
-        in_specs=whole(3),
-        out_specs=whole(1)[0],
-        compiler_params=pltpu.CompilerParams(vmem_limit_bytes=16 << 20),
-        name="pack",
-    )(query, key, value)
-
-
-def deal_kernel(swapped, out):
+def deal_kernel(kinds, halo, swapped, out):
+    count = 5 + 2 * halo
     for slot in range(SLOTS):
-        for at in range(7):
-            unit = min(max(5 * run_at(slot) + at - 1, 0), 39)
+        for at in range(count):
+            unit = min(max(5 * run_at(slot) + at - halo, 0), 39)
             head, column = unit // 8, unit % 8
-            for kind in range(3):
-                if kind == 0 and not 1 <= at <= 5:
-                    continue
-                place = at - 1 if kind == 0 else 7 * kind - 2 + at
+            for place, kind in enumerate(kinds):
                 lines = swapped[column, kind, head].reshape(STRIPS, 8, HEAD_DIM)
                 for strip in range(STRIPS):
-                    out[strip * SLOTS + slot, place] = lines[strip]
-
-
-def deal(swapped):
-    return pl.pallas_call(
-        deal_kernel,
-        out_shape=jax.ShapeDtypeStruct((STRIPS * SLOTS, 19, 8, HEAD_DIM), LOW),
+                    out[strip * SLOTS + slot, place * count + at] = lines[strip]
+
+
+def deal(swapped, kinds, halo):
+    tiles = len(kinds) * (5 + 2 * halo)
+    return pl.pallas_call(
+        functools.partial(deal_kernel, kinds, halo),
+        out_shape=jax.ShapeDtypeStruct((STRIPS * SLOTS, tiles, 8, HEAD_DIM), LOW),
         in_specs=whole(1),
         out_specs=whole(1)[0],
         compiler_params=pltpu.CompilerParams(vmem_limit_bytes=16 << 20),
@@ -223,7 +202,7 @@
     return [jax.ShapeDtypeStruct((kinds, 2, TILE, HEAD_DIM), LOW)] * count
 
 
-def attend_kernel(table, own, above, below, *refs):
+def attend_kernel(table, own, beside, above, below, *refs):
     grads, rest, terms, edges = refs[:6], refs[6], refs[7], refs[8:10]
     pair, turned, outer_turned, grad, total, held = refs[10:]
     strip, odd = table[7], table[8]
@@ -233,7 +212,7 @@
     for kind in range(2):
         for at in range(7):
             for row in range(2):
-                pair[kind, at, row] = own[row, 5 + 7 * kind + at]
+                pair[kind, at, row] = beside[row, 7 * kind + at]
             pair[kind, at, 2] = above[7 * kind + at]
             pair[kind, at, 3] = below[7 * kind + at]
     for kind in range(2):
@@ -364,7 +343,7 @@
     return [jax.ShapeDtypeStruct((2, 2, TILE, HEAD_DIM), LOW)] * 2
 
 
-def attend(table, own, halos, grads):
+def attend(table, own, pair, halos, grads):
     return pl.pallas_call(
         attend_kernel,
         out_shape=[
@@ -373,7 +352,7 @@
             jax.ShapeDtypeStruct((2, 7, TILE, HEAD_DIM), LOW),
             jax.ShapeDtypeStruct((2, 7, TILE, HEAD_DIM), LOW),
         ],
-        in_specs=[pl.BlockSpec(memory_space=pltpu.SMEM)] + whole(9),
+        in_specs=[pl.BlockSpec(memory_space=pltpu.SMEM)] + whole(10),
         out_specs=whole(4),
         scratch_shapes=[
             pltpu.VMEM((2, 7, 4, TILE, HEAD_DIM), LOW),
@@ -388,7 +367,7 @@
             flops=3_000_000_000, bytes_accessed=8_000_000, transcendentals=1_500_000
         ),
         name="attend",
-    )(table, own, *halos, *grads)
+    )(table, own, pair, *halos, *grads)
 
 
 def rims_kernel(table, rest, terms, above, below, right, left, *outs):
@@ -469,18 +448,29 @@
         grads = send_all(spread(place, upstream), [flipped(path) for path in to_owner])
 
     with jax.named_scope("heads"):
-        lines = pack(query_slab, key_slab, value_slab)
-        swapped = lax.all_to_all(lines, "head", 0, 0, tiled=True)
-    with jax.named_scope("tiles"):
-        dealt, early = lax.optimization_barrier((deal(swapped), grads[:EARLY]))
+        lines = [
+            slab.reshape(8, 4, 40, 128).transpose(2, 0, 1, 3).reshape(8, 5, 32, 128)
+            for slab in (query_slab, key_slab, value_slab)
+        ]
+        swapped = lax.all_to_all(jnp.stack(lines, axis=1), "head", 0, 0, tiled=True)
+
+    def by_tile(dealt):
         got = lax.all_to_all(dealt, "tile", 0, 0, tiled=True)
-        own = got.reshape(32, 19, 2, 4, 128).transpose(2, 1, 0, 3, 4)
-        own = own.reshape(2, 19, TILE, HEAD_DIM)
-        own, late = lax.optimization_barrier((own, grads[EARLY:]))
+        tiles = got.reshape(32, -1, 2, 4, 128).transpose(2, 1, 0, 3, 4)
+        return tiles.reshape(2, -1, TILE, HEAD_DIM)
+
+    with jax.named_scope("key_value_tiles"):
+        dealt, early = lax.optimization_barrier((deal(swapped, (1, 2), 1), grads[:EARLY]))
+        pair = by_tile(dealt)
+    with jax.named_scope("query_tiles"):
+        pair, late, dealt = lax.optimization_barrier(
+            (pair, grads[EARLY:], deal(swapped, (0,), 0))
+        )
+        own = by_tile(dealt)
     with jax.named_scope("halos"):
-        halos = send_all([own[1, 5:], own[0, 5:]], row_routes)
+        halos = send_all([pair[1], pair[0]], row_routes)
     with jax.named_scope("attention"):
-        rest, terms, above, below = attend(place, own, halos, early + late)
+        rest, terms, above, below = attend(place, own, pair, halos, early + late)
     with jax.named_scope("row_terms"):
         edges = send_all([above, below], row_routes)
     with jax.named_scope("column_terms"):

time: 159 us -> 164 us (1.031)
  starting transfers between devices: 86.9 us -> 92.6 us
  waiting for transfers between devices: 50 us -> 48.1 us
    all_to_all x2 -> x3, starting transfers between devices: 15.2 us -> 22.2 us  [the longest x2 17.9 us: by_tile(): got = lax.all_to_all(dealt, 'tile', 0, 0, tiled=True)]
    unnamed x8 -> x4, local copies, waits for them, and re-layouts: 2.91 us -> 0.01 us
    reshape x1 -> x8, local copies, waits for them, and re-layouts: 0.65 us -> 3.34 us  [the longest x6 2.75 us: local(): slab.reshape(8, 4, 40, 128).transpose(2, 0, 1, 3).reshape(8, 5, 32, 128)]
    all_to_all x2 -> x3, waiting for transfers between devices: 20.6 us -> 18.8 us  [the longest x2 18.8 us: by_tile(): got = lax.all_to_all(dealt, 'tile', 0, 0, tiled=True)]
  transfers between devices with their start and end apart: 20 -> 21, of which waited for: 9 -> 10; matrix products, arithmetic and copies ran while one was open for 1% -> 1% of each run, Pallas kernels for 2% -> 2%
where the time goes in v7:
time: 164 us; the launch traced here: 161 us
  starting transfers between devices  92.6 us (56%)
  waiting for transfers between devices  48.1 us (29%)
  Pallas kernels  14.4 us (9%)
  local copies, waits for them, and re-layouts  4.13 us (3%)
    ppermute x18, starting transfers between devices, send_all(): lax.ppermute(part, 'tile', path)  70.4 us
    ppermute x18, waiting for transfers between devices, send_all(): lax.ppermute(part, 'tile', path)  29.3 us
    all_to_all x2, waiting for transfers between devices, by_tile(): got = lax.all_to_all(dealt, 'tile', 0, 0, tiled=True)  18.8 us
    all_to_all x2, starting transfers between devices, by_tile(): got = lax.all_to_all(dealt, 'tile', 0, 0, tiled=True)  17.9 us
    pallas_call x1, Pallas kernels, attend(): pl.pallas_call(attend_kernel, out_shape=[jax.ShapeDtypeStruct((2, 2, 5, T...  8.14 us
    all_to_all x1, starting transfers between devices, local(): swapped = lax.all_to_all(jnp.stack(lines, axis=1), 'head', 0, 0, tiled=True)  4.3 us
  transfers between devices with their start and end apart: 21, of which 10 were waited for; matrix products, arithmetic and copies ran while one was open for 1% of the time, Pallas kernels for 2%

profile of v7, /device:TPU:40, one launch (start us, length us, event | category | flops | bytes accessed | tf_op | source)
XLA Modules:
  0.0 161.4 jit_solution(710314902639088561)
XLA Ops:
  0.6 1.1 reshape.38
  1.8 0.1 copy.9
  1.9 1.1 reshape.40
  3.0 0.1 copy.10
  3.2 0.1 reshape.42
  3.3 0.1 copy.11
  3.4 1.1 pad_maximum_fusion
  4.5 4.3 %all-to-all-start = ((bf16[8,3,5,32,128]{4,3,2,1,0:T(8,128)(2,1)}), bf16[8,3,5,32,128]{4,3,2,1,0:T(8,128)(2,1)S(1)}, u32[]{:S(2)}, u32[]{:S(2)}) async-start(bf16[8,3,5,32,128]{4,3,2,1,0:T(8,128)(2,1)} %pad_maximum_fusion), calls=%async_computation | async-start | bytes 1966080 | tf_op jit(solution)/shard_map/heads/all_to_all | solution.py:455
  8.8 0.7 dynamic-slice_bitcast_fusion.table
  9.5 0.9 spread.1
  10.4 5.2 %collective-permute-start = (bf16[2,128,128]{2,1,0:T(8,128)(2,1)S(1)}, bf16[2,128,128]{2,1,0:T(8,128)(2,1)S(1)}, u32[]{:S(2)}, u32[]{:S(2)}) collective-permute-start(bf16[2,128,128]{2,1,0:T(8,128)(2,1)S(1)} %get-tuple-element.37), channel_id=1, source_target_pairs={{48,0},{16,8},{40,16},{8,24},{32,32},{0,40},{56,48},{24,56},{112,6... | collective-permute-start | bytes 196616 | tf_op jit(solution)/shard_map/upstream_to_units/ppermute | solution.py:438
  15.6 1.9 %collective-permute-start.1 = (bf16[2,128,128]{2,1,0:T(8,128)(2,1)S(1)}, bf16[2,128,128]{2,1,0:T(8,128)(2,1)S(1)}, u32[]{:S(2)}, u32[]{:S(2)}) collective-permute-start(bf16[2,128,128]{2,1,0:T(8,128)(2,1)S(1)} %get-tuple-element.38), channel_id=1, source_target_pairs={{16,0},{48,8},{8,16},{40,24},{0,32},{32,40},{24,48},{56,56},{80,64... | collective-permute-start | bytes 196616 | tf_op jit(solution)/shard_map/upstream_to_units/ppermute | solution.py:438
  17.6 10.0 %collective-permute-start.2 = (bf16[2,128,128]{2,1,0:T(8,128)(2,1)S(1)}, bf16[2,128,128]{2,1,0:T(8,128)(2,1)S(1)}, u32[]{:S(2)}, u32[]{:S(2)}) collective-permute-start(bf16[2,128,128]{2,1,0:T(8,128)(2,1)S(1)} %get-tuple-element.39), channel_id=1, source_target_pairs={{40,0},{24,8},{32,16},{16,24},{56,32},{8,40},{48,48},{0,56},{104,6... | collective-permute-start | bytes 196616 | tf_op jit(solution)/shard_map/upstream_to_units/ppermute | solution.py:438
  27.5 1.1 deal.2
  28.6 0.8 collective-permute-done.2.refs_2_
  29.4 10.8 %all-to-all-start.1 = ((bf16[32,14,8,128]{3,2,1,0:T(8,128)(2,1)}), bf16[32,14,8,128]{3,2,1,0:T(8,128)(2,1)S(1)}, u32[]{:S(2)}, u32[]{:S(2)}) async-start(bf16[32,14,8,128]{3,2,1,0:T(8,128)(2,1)} %deal.2), calls=%async_computation.1 | async-start | bytes 1835008 | tf_op jit(solution)/shard_map/key_value_tiles/all_to_all | solution.py:458
  40.2 2.5 %collective-permute-start.3 = (bf16[2,128,128]{2,1,0:T(8,128)(2,1)S(1)}, bf16[2,128,128]{2,1,0:T(8,128)(2,1)S(1)}, u32[]{:S(2)}, u32[]{:S(2)}) collective-permute-start(bf16[2,128,128]{2,1,0:T(8,128)(2,1)S(1)} %get-tuple-element.41), channel_id=1, source_target_pairs={{8,0},{56,8},{0,16},{48,24},{24,32},{40,40},{16,48},{32,56},{72,64... | collective-permute-start | bytes 196616 | tf_op jit(solution)/shard_map/upstream_to_units/ppermute | solution.py:438
  42.7 5.5 %collective-permute-start.4 = (bf16[128,128]{1,0:T(8,128)(2,1)S(1)}, bf16[128,128]{1,0:T(8,128)(2,1)S(1)}, u32[]{:S(2)}, u32[]{:S(2)}) collective-permute-start(bf16[128,128]{1,0:T(8,128)(2,1)S(1)} %get-tuple-element.42), channel_id=1, source_target_pairs={{32,0},{0,8},{56,16},{24,24},{48,32},{16,40},{40,48},{8,56},{96,64... | collective-permute-start | bytes 98312 | tf_op jit(solution)/shard_map/upstream_to_units/ppermute | solution.py:438
  48.2 4.3 %collective-permute-start.5 = (bf16[128,128]{1,0:T(8,128)(2,1)S(1)}, bf16[128,128]{1,0:T(8,128)(2,1)S(1)}, u32[]{:S(2)}, u32[]{:S(2)}) collective-permute-start(bf16[128,128]{1,0:T(8,128)(2,1)S(1)} %get-tuple-element.43), channel_id=1, source_target_pairs={{0,0},{32,8},{24,16},{56,24},{16,32},{48,40},{8,48},{40,56},{64,64... | collective-permute-start | bytes 98312 | tf_op jit(solution)/shard_map/upstream_to_units/ppermute | solution.py:438
  52.5 0.8 deal.3
  53.2 12.9 %all-to-all-done.1 = bf16[32,14,8,128]{3,2,1,0:T(8,128)(2,1)S(1)} async-done(((bf16[32,14,8,128]{3,2,1,0:T(8,128)(2,1)}), bf16[32,14,8,128]{3,2,1,0:T(8,128)(2,1)S(1)}, u32[]{:S(2)}, u32[]{:S(2)}) %all-to-all-start.1) | async-done | bytes 917536 | tf_op jit(solution)/shard_map/key_value_tiles/all_to_all | solution.py:458
  66.2 0.5 copy.12
  66.7 7.1 %all-to-all-start.2 = ((bf16[32,5,8,128]{3,2,1,0:T(8,128)(2,1)}), bf16[32,5,8,128]{3,2,1,0:T(8,128)(2,1)S(1)}, u32[]{:S(2)}, u32[]{:S(2)}) async-start(bf16[32,5,8,128]{3,2,1,0:T(8,128)(2,1)} %deal.3), calls=%async_computation.2 | async-start | bytes 655360 | tf_op jit(solution)/shard_map/query_tiles/all_to_all | solution.py:458
  73.8 2.5 %collective-permute-start.7 = (bf16[14,128,128]{2,1,0:T(8,128)(2,1)S(1)}, bf16[14,128,128]{2,1,0:T(8,128)(2,1)S(1)}, u32[]{:S(2)}, u32[]{:S(2)}) collective-permute-start(bf16[14,128,128]{2,1,0:T(8,128)(2,1)S(1)} %get-tuple-element.70), channel_id=1, source_target_pairs={{64,0},{72,8},{80,16},{88,24},{96,32},{104,40},{112,48},{120,56},{... | collective-permute-start | bytes 1376264 | tf_op jit(solution)/shard_map/halos/ppermute | solution.py:438
  76.3 3.4 %collective-permute-start.6 = (bf16[14,128,128]{2,1,0:T(8,128)(2,1)S(1)}, bf16[14,128,128]{2,1,0:T(8,128)(2,1)S(1)}, u32[]{:S(2)}, u32[]{:S(2)}) collective-permute-start(bf16[14,128,128]{2,1,0:T(8,128)(2,1)S(1)} %get-tuple-element.71), channel_id=1, source_target_pairs={{0,64},{8,72},{16,80},{24,88},{32,96},{40,104},{48,112},{56,120},{... | collective-permute-start | bytes 1376264 | tf_op jit(solution)/shard_map/halos/ppermute | solution.py:438
  79.7 5.9 %all-to-all-done.2 = bf16[32,5,8,128]{3,2,1,0:T(8,128)(2,1)S(1)} async-done(((bf16[32,5,8,128]{3,2,1,0:T(8,128)(2,1)}), bf16[32,5,8,128]{3,2,1,0:T(8,128)(2,1)S(1)}, u32[]{:S(2)}, u32[]{:S(2)}) %all-to-all-start.2) | async-done | bytes 327712 | tf_op jit(solution)/shard_map/query_tiles/all_to_all | solution.py:458
  85.6 0.1 copy.13
  85.7 3.7 %collective-permute-done.7.below = bf16[14,128,128]{2,1,0:T(8,128)(2,1)S(1)} collective-permute-done((bf16[14,128,128]{2,1,0:T(8,128)(2,1)S(1)}, bf16[14,128,128]{2,1,0:T(8,128)(2,1)S(1)}, u32[]{:S(2)}, u32[]{:S(2)}) %collective-permute-start.7) | collective-permute-done | bytes 458784 | tf_op jit(solution)/shard_map/halos/ppermute | solution.py:438
  89.4 0.5 collective-permute-done.6.above
  89.9 8.1 %attend.1 = (bf16[2,2,5,128,128]{4,3,2,1,0:T(8,128)(2,1)S(1)}, f32[2,2,7,128,128]{4,3,2,1,0:T(8,128)S(1)}, bf16[2,7,128,128]{3,2,1,0:T(8,128)(2,1)S(1)}, bf16[2,7,128,128]{3,2,1,0:T(8,128)(2,1)S(1)}) custom-call(s32[14]{0:T(128)S(1)} %dynamic-slice_bitcast_fusion.table, bf16[2,5,128,128]{3,2,1,0:T(8,128)(2,1)S(1)} %bitcast.25, ...), custom_call_target="tpu_custom_call" | custom-call | flops 3000000000 | bytes 8000000 | tf_op jit(solution)/shard_map/attention/attend/pallas_call | solution.py:347
  98.1 3.4 %collective-permute-start.8 = (bf16[2,7,128,128]{3,2,1,0:T(8,128)(2,1)S(1)}, bf16[2,7,128,128]{3,2,1,0:T(8,128)(2,1)S(1)}, u32[]{:S(2)}, u32[]{:S(2)}) collective-permute-start(bf16[2,7,128,128]{3,2,1,0:T(8,128)(2,1)S(1)} %get-tuple-element.54), channel_id=1, source_target_pairs={{0,64},{8,72},{16,80},{24,88},{32,96},{40,104},{48,112},{56,120},{... | collective-permute-start | bytes 1376264 | tf_op jit(solution)/shard_map/row_terms/ppermute | solution.py:438
  101.5 2.5 %collective-permute-start.9 = (bf16[2,7,128,128]{3,2,1,0:T(8,128)(2,1)S(1)}, bf16[2,7,128,128]{3,2,1,0:T(8,128)(2,1)S(1)}, u32[]{:S(2)}, u32[]{:S(2)}) collective-permute-start(bf16[2,7,128,128]{3,2,1,0:T(8,128)(2,1)S(1)} %get-tuple-element.55), channel_id=1, source_target_pairs={{64,0},{72,8},{80,16},{88,24},{96,32},{104,40},{112,48},{120,56},{... | collective-permute-start | bytes 1376264 | tf_op jit(solution)/shard_map/row_terms/ppermute | solution.py:438
  104.0 6.3 %collective-permute-done.8.above = bf16[2,7,128,128]{3,2,1,0:T(8,128)(2,1)S(1)} collective-permute-done((bf16[2,7,128,128]{3,2,1,0:T(8,128)(2,1)S(1)}, bf16[2,7,128,128]{3,2,1,0:T(8,128)(2,1)S(1)}, u32[]{:S(2)}, u32[]{:S(2)}) %collective-permute-start.8) | collective-permute-done | bytes 458784 | tf_op jit(solution)/shard_map/row_terms/ppermute | solution.py:438
  110.3 3.0 %collective-permute-done.9.below = bf16[2,7,128,128]{3,2,1,0:T(8,128)(2,1)S(1)} collective-permute-done((bf16[2,7,128,128]{3,2,1,0:T(8,128)(2,1)S(1)}, bf16[2,7,128,128]{3,2,1,0:T(8,128)(2,1)S(1)}, u32[]{:S(2)}, u32[]{:S(2)}) %collective-permute-start.9) | collective-permute-done | bytes 458784 | tf_op jit(solution)/shard_map/row_terms/ppermute | solution.py:438
  113.3 0.7 rims.1
  114.0 4.4 %collective-permute-start.12 = (bf16[4,2,128,128]{3,2,1,0:T(8,128)(2,1)S(1)}, bf16[4,2,128,128]{3,2,1,0:T(8,128)(2,1)S(1)}, u32[]{:S(2)}, u32[]{:S(2)}) collective-permute-start(bf16[4,2,128,128]{3,2,1,0:T(8,128)(2,1)S(1)} %get-tuple-element.62), channel_id=1, source_target_pairs={{0,40},{8,24},{16,32},{24,16},{32,56},{40,8},{48,48},{56,0},{64,10... | collective-permute-start | bytes 786440 | tf_op jit(solution)/shard_map/column_terms/ppermute | solution.py:438
  118.5 3.2 %collective-permute-start.13 = (bf16[4,2,128,128]{3,2,1,0:T(8,128)(2,1)S(1)}, bf16[4,2,128,128]{3,2,1,0:T(8,128)(2,1)S(1)}, u32[]{:S(2)}, u32[]{:S(2)}) collective-permute-start(bf16[4,2,128,128]{3,2,1,0:T(8,128)(2,1)S(1)} %get-tuple-element.63), channel_id=1, source_target_pairs={{0,8},{8,56},{16,0},{24,48},{32,24},{40,40},{48,16},{56,32},{64,72... | collective-permute-start | bytes 786440 | tf_op jit(solution)/shard_map/column_terms/ppermute | solution.py:438
  121.6 2.9 %collective-permute-start.10 = (bf16[2,2,128,128]{3,2,1,0:T(8,128)(2,1)S(1)}, bf16[2,2,128,128]{3,2,1,0:T(8,128)(2,1)S(1)}, u32[]{:S(2)}, u32[]{:S(2)}) collective-permute-start(bf16[2,2,128,128]{3,2,1,0:T(8,128)(2,1)S(1)} %get-tuple-element.56), channel_id=1, source_target_pairs={{0,56},{8,0},{16,8},{24,16},{32,24},{40,32},{56,48},{64,120},{72,6... | collective-permute-start | bytes 393224 | tf_op jit(solution)/shard_map/column_terms/ppermute | solution.py:438
  124.5 3.4 %collective-permute-start.11 = (bf16[2,2,128,128]{3,2,1,0:T(8,128)(2,1)S(1)}, bf16[2,2,128,128]{3,2,1,0:T(8,128)(2,1)S(1)}, u32[]{:S(2)}, u32[]{:S(2)}) collective-permute-start(bf16[2,2,128,128]{3,2,1,0:T(8,128)(2,1)S(1)} %get-tuple-element.57), channel_id=1, source_target_pairs={{0,8},{8,16},{16,24},{24,32},{32,40},{48,56},{56,0},{64,72},{72,80... | collective-permute-start | bytes 393224 | tf_op jit(solution)/shard_map/column_terms/ppermute | solution.py:438
  127.9 5.3 %collective-permute-done.10.before = bf16[2,2,128,128]{3,2,1,0:T(8,128)(2,1)S(1)} collective-permute-done((bf16[2,2,128,128]{3,2,1,0:T(8,128)(2,1)S(1)}, bf16[2,2,128,128]{3,2,1,0:T(8,128)(2,1)S(1)}, u32[]{:S(2)}, u32[]{:S(2)}) %collective-permute-start.10) | collective-permute-done | bytes 131104 | tf_op jit(solution)/shard_map/column_terms/ppermute | solution.py:438
  133.2 1.8 %collective-permute-done.11.after = bf16[2,2,128,128]{3,2,1,0:T(8,128)(2,1)S(1)} collective-permute-done((bf16[2,2,128,128]{3,2,1,0:T(8,128)(2,1)S(1)}, bf16[2,2,128,128]{3,2,1,0:T(8,128)(2,1)S(1)}, u32[]{:S(2)}, u32[]{:S(2)}) %collective-permute-start.11) | collective-permute-done | bytes 131104 | tf_op jit(solution)/shard_map/column_terms/ppermute | solution.py:438
  135.0 0.7 combine.1
  135.8 2.4 %collective-permute-start.14 = (bf16[4,2,128,128]{3,2,1,0:T(8,128)(2,1)S(1)}, bf16[4,2,128,128]{3,2,1,0:T(8,128)(2,1)S(1)}, u32[]{:S(2)}, u32[]{:S(2)}) collective-permute-start(bf16[4,2,128,128]{3,2,1,0:T(8,128)(2,1)S(1)} %get-tuple-element.66), channel_id=1, source_target_pairs={{0,48},{8,16},{16,40},{24,8},{32,32},{40,0},{48,56},{56,24},{64,11... | collective-permute-start | bytes 786440 | tf_op jit(solution)/shard_map/outputs_home/ppermute | solution.py:438
  138.2 4.5 %collective-permute-start.15 = (bf16[4,2,128,128]{3,2,1,0:T(8,128)(2,1)S(1)}, bf16[4,2,128,128]{3,2,1,0:T(8,128)(2,1)S(1)}, u32[]{:S(2)}, u32[]{:S(2)}) collective-permute-start(bf16[4,2,128,128]{3,2,1,0:T(8,128)(2,1)S(1)} %get-tuple-element.67), channel_id=1, source_target_pairs={{0,16},{8,48},{16,8},{24,40},{32,0},{40,32},{48,24},{56,56},{64,80... | collective-permute-start | bytes 786440 | tf_op jit(solution)/shard_map/outputs_home/ppermute | solution.py:438
  142.7 1.9 %collective-permute-start.16 = (bf16[4,128,128]{2,1,0:T(8,128)(2,1)S(1)}, bf16[4,128,128]{2,1,0:T(8,128)(2,1)S(1)}, u32[]{:S(2)}, u32[]{:S(2)}) collective-permute-start(bf16[4,128,128]{2,1,0:T(8,128)(2,1)S(1)} %get-tuple-element.68), channel_id=1, source_target_pairs={{0,32},{8,0},{16,56},{24,24},{32,48},{40,16},{48,40},{56,8},{64,96... | collective-permute-start | bytes 393224 | tf_op jit(solution)/shard_map/outputs_home/ppermute | solution.py:438
  144.6 6.7 %collective-permute-start.17 = (bf16[4,128,128]{2,1,0:T(8,128)(2,1)S(1)}, bf16[4,128,128]{2,1,0:T(8,128)(2,1)S(1)}, u32[]{:S(2)}, u32[]{:S(2)}) collective-permute-start(bf16[4,128,128]{2,1,0:T(8,128)(2,1)S(1)} %get-tuple-element.69), channel_id=1, source_target_pairs={{0,0},{8,32},{16,24},{24,56},{32,16},{40,48},{48,8},{56,40},{64,64... | collective-permute-start | bytes 393224 | tf_op jit(solution)/shard_map/outputs_home/ppermute | solution.py:438
  151.4 7.8 %collective-permute-done.16.refs_4_ = bf16[4,128,128]{2,1,0:T(8,128)(2,1)S(1)} collective-permute-done((bf16[4,128,128]{2,1,0:T(8,128)(2,1)S(1)}, bf16[4,128,128]{2,1,0:T(8,128)(2,1)S(1)}, u32[]{:S(2)}, u32[]{:S(2)}) %collective-permute-start.16) | collective-permute-done | bytes 131104 | tf_op jit(solution)/shard_map/outputs_home/ppermute | solution.py:438
  159.2 2.1 %gather.1 = (bf16[256,640]{1,0:T(8,128)(2,1)}, bf16[256,640]{1,0:T(8,128)(2,1)}, bf16[256,640]{1,0:T(8,128)(2,1)}, bf16[256,640]{1,0:T(8,128)(2,1)}) custom-call(s32[14]{0:T(128)S(1)} %dynamic-slice_bitcast_fusion.table, bf16[4,2,128,128]{3,2,1,0:T(8,128)(2,1)S(1)} %collective-permute-done.12.refs_0_, ...), custom_call_target="tpu_custom_call" | custom-call | tf_op jit(solution)/shard_map/settle/gather/pallas_call | solution.py:167
  (16 shorter events, 0.1 us)
Async XLA Ops:
  0.6 2.5 %copy-start.1 = (bf16[1,8,4,5120]{3,2,1,0:T(4,128)(2,1)S(1)}, bf16[1,8,4,5120]{3,2,1,0:T(4,128)(2,1)}, u32[]{:S(2)}) copy-start(bf16[1,8,4,5120]{3,2,1,0:T(4,128)(2,1)} %param.7) | copy-start | bytes 983044
  3.4 6.1 %copy-start = (bf16[256,640]{1,0:T(8,128)(2,1)S(1)}, bf16[256,640]{1,0:T(8,128)(2,1)}, u32[]{:S(2)}) copy-start(bf16[256,640]{1,0:T(8,128)(2,1)} %upstream.1) | copy-start | bytes 983044
  4.5 23.0 %all-to-all-start = ((bf16[8,3,5,32,128]{4,3,2,1,0:T(8,128)(2,1)}), bf16[8,3,5,32,128]{4,3,2,1,0:T(8,128)(2,1)S(1)}, u32[]{:S(2)}, u32[]{:S(2)}) async-start(bf16[8,3,5,32,128]{4,3,2,1,0:T(8,128)(2,1)} %pad_maximum_fusion), calls=%async_computation | async-start | bytes 1966080 | tf_op jit(solution)/shard_map/heads/all_to_all | solution.py:455
  10.4 18.2 %collective-permute-start = (bf16[2,128,128]{2,1,0:T(8,128)(2,1)S(1)}, bf16[2,128,128]{2,1,0:T(8,128)(2,1)S(1)}, u32[]{:S(2)}, u32[]{:S(2)}) collective-permute-start(bf16[2,128,128]{2,1,0:T(8,128)(2,1)S(1)} %get-tuple-element.37), channel_id=1, source_target_pairs={{48,0},{16,8},{40,16},{8,24},{32,32},{0,40},{56,48},{24,56},{112,6... | collective-permute-start | bytes 196616 | tf_op jit(solution)/shard_map/upstream_to_units/ppermute | solution.py:438
  15.6 13.0 %collective-permute-start.1 = (bf16[2,128,128]{2,1,0:T(8,128)(2,1)S(1)}, bf16[2,128,128]{2,1,0:T(8,128)(2,1)S(1)}, u32[]{:S(2)}, u32[]{:S(2)}) collective-permute-start(bf16[2,128,128]{2,1,0:T(8,128)(2,1)S(1)} %get-tuple-element.38), channel_id=1, source_target_pairs={{16,0},{48,8},{8,16},{40,24},{0,32},{32,40},{24,48},{56,56},{80,64... | collective-permute-start | bytes 196616 | tf_op jit(solution)/shard_map/upstream_to_units/ppermute | solution.py:438
  17.6 11.9 %collective-permute-start.2 = (bf16[2,128,128]{2,1,0:T(8,128)(2,1)S(1)}, bf16[2,128,128]{2,1,0:T(8,128)(2,1)S(1)}, u32[]{:S(2)}, u32[]{:S(2)}) collective-permute-start(bf16[2,128,128]{2,1,0:T(8,128)(2,1)S(1)} %get-tuple-element.39), channel_id=1, source_target_pairs={{40,0},{24,8},{32,16},{16,24},{56,32},{8,40},{48,48},{0,56},{104,6... | collective-permute-start | bytes 196616 | tf_op jit(solution)/shard_map/upstream_to_units/ppermute | solution.py:438
  29.4 36.7 %all-to-all-start.1 = ((bf16[32,14,8,128]{3,2,1,0:T(8,128)(2,1)}), bf16[32,14,8,128]{3,2,1,0:T(8,128)(2,1)S(1)}, u32[]{:S(2)}, u32[]{:S(2)}) async-start(bf16[32,14,8,128]{3,2,1,0:T(8,128)(2,1)} %deal.2), calls=%async_computation.1 | async-start | bytes 1835008 | tf_op jit(solution)/shard_map/key_value_tiles/all_to_all | solution.py:458
  40.2 26.5 %collective-permute-start.3 = (bf16[2,128,128]{2,1,0:T(8,128)(2,1)S(1)}, bf16[2,128,128]{2,1,0:T(8,128)(2,1)S(1)}, u32[]{:S(2)}, u32[]{:S(2)}) collective-permute-start(bf16[2,128,128]{2,1,0:T(8,128)(2,1)S(1)} %get-tuple-element.41), channel_id=1, source_target_pairs={{8,0},{56,8},{0,16},{48,24},{24,32},{40,40},{16,48},{32,56},{72,64... | collective-permute-start | bytes 196616 | tf_op jit(solution)/shard_map/upstream_to_units/ppermute | solution.py:438
  42.7 24.0 %collective-permute-start.4 = (bf16[128,128]{1,0:T(8,128)(2,1)S(1)}, bf16[128,128]{1,0:T(8,128)(2,1)S(1)}, u32[]{:S(2)}, u32[]{:S(2)}) collective-permute-start(bf16[128,128]{1,0:T(8,128)(2,1)S(1)} %get-tuple-element.42), channel_id=1, source_target_pairs={{32,0},{0,8},{56,16},{24,24},{48,32},{16,40},{40,48},{8,56},{96,64... | collective-permute-start | bytes 98312 | tf_op jit(solution)/shard_map/upstream_to_units/ppermute | solution.py:438
  48.2 18.5 %collective-permute-start.5 = (bf16[128,128]{1,0:T(8,128)(2,1)S(1)}, bf16[128,128]{1,0:T(8,128)(2,1)S(1)}, u32[]{:S(2)}, u32[]{:S(2)}) collective-permute-start(bf16[128,128]{1,0:T(8,128)(2,1)S(1)} %get-tuple-element.43), channel_id=1, source_target_pairs={{0,0},{32,8},{24,16},{56,24},{16,32},{48,40},{8,48},{40,56},{64,64... | collective-permute-start | bytes 98312 | tf_op jit(solution)/shard_map/upstream_to_units/ppermute | solution.py:438
  66.7 18.9 %all-to-all-start.2 = ((bf16[32,5,8,128]{3,2,1,0:T(8,128)(2,1)}), bf16[32,5,8,128]{3,2,1,0:T(8,128)(2,1)S(1)}, u32[]{:S(2)}, u32[]{:S(2)}) async-start(bf16[32,5,8,128]{3,2,1,0:T(8,128)(2,1)} %deal.3), calls=%async_computation.2 | async-start | bytes 655360 | tf_op jit(solution)/shard_map/query_tiles/all_to_all | solution.py:458
  73.8 15.6 %collective-permute-start.7 = (bf16[14,128,128]{2,1,0:T(8,128)(2,1)S(1)}, bf16[14,128,128]{2,1,0:T(8,128)(2,1)S(1)}, u32[]{:S(2)}, u32[]{:S(2)}) collective-permute-start(bf16[14,128,128]{2,1,0:T(8,128)(2,1)S(1)} %get-tuple-element.70), channel_id=1, source_target_pairs={{64,0},{72,8},{80,16},{88,24},{96,32},{104,40},{112,48},{120,56},{... | collective-permute-start | bytes 1376264 | tf_op jit(solution)/shard_map/halos/ppermute | solution.py:438
  76.3 13.6 %collective-permute-start.6 = (bf16[14,128,128]{2,1,0:T(8,128)(2,1)S(1)}, bf16[14,128,128]{2,1,0:T(8,128)(2,1)S(1)}, u32[]{:S(2)}, u32[]{:S(2)}) collective-permute-start(bf16[14,128,128]{2,1,0:T(8,128)(2,1)S(1)} %get-tuple-element.71), channel_id=1, source_target_pairs={{0,64},{8,72},{16,80},{24,88},{32,96},{40,104},{48,112},{56,120},{... | collective-permute-start | bytes 1376264 | tf_op jit(solution)/shard_map/halos/ppermute | solution.py:438
  98.1 12.2 %collective-permute-start.8 = (bf16[2,7,128,128]{3,2,1,0:T(8,128)(2,1)S(1)}, bf16[2,7,128,128]{3,2,1,0:T(8,128)(2,1)S(1)}, u32[]{:S(2)}, u32[]{:S(2)}) collective-permute-start(bf16[2,7,128,128]{3,2,1,0:T(8,128)(2,1)S(1)} %get-tuple-element.54), channel_id=1, source_target_pairs={{0,64},{8,72},{16,80},{24,88},{32,96},{40,104},{48,112},{56,120},{... | collective-permute-start | bytes 1376264 | tf_op jit(solution)/shard_map/row_terms/ppermute | solution.py:438
  101.5 11.9 %collective-permute-start.9 = (bf16[2,7,128,128]{3,2,1,0:T(8,128)(2,1)S(1)}, bf16[2,7,128,128]{3,2,1,0:T(8,128)(2,1)S(1)}, u32[]{:S(2)}, u32[]{:S(2)}) collective-permute-start(bf16[2,7,128,128]{3,2,1,0:T(8,128)(2,1)S(1)} %get-tuple-element.55), channel_id=1, source_target_pairs={{64,0},{72,8},{80,16},{88,24},{96,32},{104,40},{112,48},{120,56},{... | collective-permute-start | bytes 1376264 | tf_op jit(solution)/shard_map/row_terms/ppermute | solution.py:438
  114.0 21.7 %collective-permute-start.12 = (bf16[4,2,128,128]{3,2,1,0:T(8,128)(2,1)S(1)}, bf16[4,2,128,128]{3,2,1,0:T(8,128)(2,1)S(1)}, u32[]{:S(2)}, u32[]{:S(2)}) collective-permute-start(bf16[4,2,128,128]{3,2,1,0:T(8,128)(2,1)S(1)} %get-tuple-element.62), channel_id=1, source_target_pairs={{0,40},{8,24},{16,32},{24,16},{32,56},{40,8},{48,48},{56,0},{64,10... | collective-permute-start | bytes 786440 | tf_op jit(solution)/shard_map/column_terms/ppermute | solution.py:438
  118.5 17.3 %collective-permute-start.13 = (bf16[4,2,128,128]{3,2,1,0:T(8,128)(2,1)S(1)}, bf16[4,2,128,128]{3,2,1,0:T(8,128)(2,1)S(1)}, u32[]{:S(2)}, u32[]{:S(2)}) collective-permute-start(bf16[4,2,128,128]{3,2,1,0:T(8,128)(2,1)S(1)} %get-tuple-element.63), channel_id=1, source_target_pairs={{0,8},{8,56},{16,0},{24,48},{32,24},{40,40},{48,16},{56,32},{64,72... | collective-permute-start | bytes 786440 | tf_op jit(solution)/shard_map/column_terms/ppermute | solution.py:438
  121.6 11.6 %collective-permute-start.10 = (bf16[2,2,128,128]{3,2,1,0:T(8,128)(2,1)S(1)}, bf16[2,2,128,128]{3,2,1,0:T(8,128)(2,1)S(1)}, u32[]{:S(2)}, u32[]{:S(2)}) collective-permute-start(bf16[2,2,128,128]{3,2,1,0:T(8,128)(2,1)S(1)} %get-tuple-element.56), channel_id=1, source_target_pairs={{0,56},{8,0},{16,8},{24,16},{32,24},{40,32},{56,48},{64,120},{72,6... | collective-permute-start | bytes 393224 | tf_op jit(solution)/shard_map/column_terms/ppermute | solution.py:438
  124.5 10.5 %collective-permute-start.11 = (bf16[2,2,128,128]{3,2,1,0:T(8,128)(2,1)S(1)}, bf16[2,2,128,128]{3,2,1,0:T(8,128)(2,1)S(1)}, u32[]{:S(2)}, u32[]{:S(2)}) collective-permute-start(bf16[2,2,128,128]{3,2,1,0:T(8,128)(2,1)S(1)} %get-tuple-element.57), channel_id=1, source_target_pairs={{0,8},{8,16},{16,24},{24,32},{32,40},{48,56},{56,0},{64,72},{72,80... | collective-permute-start | bytes 393224 | tf_op jit(solution)/shard_map/column_terms/ppermute | solution.py:438
  135.8 23.5 %collective-permute-start.14 = (bf16[4,2,128,128]{3,2,1,0:T(8,128)(2,1)S(1)}, bf16[4,2,128,128]{3,2,1,0:T(8,128)(2,1)S(1)}, u32[]{:S(2)}, u32[]{:S(2)}) collective-permute-start(bf16[4,2,128,128]{3,2,1,0:T(8,128)(2,1)S(1)} %get-tuple-element.66), channel_id=1, source_target_pairs={{0,48},{8,16},{16,40},{24,8},{32,32},{40,0},{48,56},{56,24},{64,11... | collective-permute-start | bytes 786440 | tf_op jit(solution)/shard_map/outputs_home/ppermute | solution.py:438
  138.2 21.0 %collective-permute-start.15 = (bf16[4,2,128,128]{3,2,1,0:T(8,128)(2,1)S(1)}, bf16[4,2,128,128]{3,2,1,0:T(8,128)(2,1)S(1)}, u32[]{:S(2)}, u32[]{:S(2)}) collective-permute-start(bf16[4,2,128,128]{3,2,1,0:T(8,128)(2,1)S(1)} %get-tuple-element.67), channel_id=1, source_target_pairs={{0,16},{8,48},{16,8},{24,40},{32,0},{40,32},{48,24},{56,56},{64,80... | collective-permute-start | bytes 786440 | tf_op jit(solution)/shard_map/outputs_home/ppermute | solution.py:438
  142.7 16.5 %collective-permute-start.16 = (bf16[4,128,128]{2,1,0:T(8,128)(2,1)S(1)}, bf16[4,128,128]{2,1,0:T(8,128)(2,1)S(1)}, u32[]{:S(2)}, u32[]{:S(2)}) collective-permute-start(bf16[4,128,128]{2,1,0:T(8,128)(2,1)S(1)} %get-tuple-element.68), channel_id=1, source_target_pairs={{0,32},{8,0},{16,56},{24,24},{32,48},{40,16},{48,40},{56,8},{64,96... | collective-permute-start | bytes 393224 | tf_op jit(solution)/shard_map/outputs_home/ppermute | solution.py:438
  144.6 14.6 %collective-permute-start.17 = (bf16[4,128,128]{2,1,0:T(8,128)(2,1)S(1)}, bf16[4,128,128]{2,1,0:T(8,128)(2,1)S(1)}, u32[]{:S(2)}, u32[]{:S(2)}) collective-permute-start(bf16[4,128,128]{2,1,0:T(8,128)(2,1)S(1)} %get-tuple-element.69), channel_id=1, source_target_pairs={{0,0},{8,32},{16,24},{24,56},{32,16},{40,48},{48,8},{56,40},{64,64... | collective-permute-start | bytes 393224 | tf_op jit(solution)/shard_map/outputs_home/ppermute | solution.py:438

commit v8 on v6

--- a/solution.py
+++ b/solution.py
@@ -141,8 +141,7 @@
 
 
 def gather_kernel(table, *refs):
-    free, late, singles = refs[:2], refs[2:4], refs[4:6]
-    outs = refs[6:10]
+    firsts, seconds, singles, outs = refs[:4], refs[4:8], refs[8:10], refs[10:14]
     line = lax.broadcasted_iota(jnp.int32, (2 * TILE, 2 * TILE), 0)
     col = lax.broadcasted_iota(jnp.int32, (2 * TILE, 2 * TILE), 1)
     source = ((line >> 2) & 1) * TILE + (line >> 3) * 4 + (line & 3)
@@ -156,8 +155,13 @@
             out[:, pl.ds(head, HEAD_DIM)] = ordered[:, kind * HEAD_DIM : (kind + 1) * HEAD_DIM]
 
     for at in range(4):
-        received = (late, free)[at // 2][at % 2]
-        place(at, [received[kind].reshape(2 * TILE, HEAD_DIM) for kind in range(4)])
+        place(
+            at,
+            [
+                (firsts, seconds)[kind // 2][at][kind % 2].reshape(2 * TILE, HEAD_DIM)
+                for kind in range(4)
+            ],
+        )
     one, two = singles[0][...], singles[1][...]
     tops, lows = jnp.where(flip, two, one), jnp.where(flip, one, two)
     place(4, [jnp.concatenate([tops[kind], lows[kind]], axis=0) for kind in range(4)])
@@ -167,31 +171,11 @@
     return pl.pallas_call(
         gather_kernel,
         out_shape=[jax.ShapeDtypeStruct((2 * TILE, HEADS_HERE * HEAD_DIM), LOW)] * 4,
-        in_specs=[pl.BlockSpec(memory_space=pltpu.SMEM)] + whole(6),
+        in_specs=[pl.BlockSpec(memory_space=pltpu.SMEM)] + whole(10),
         out_specs=whole(4),
         compiler_params=pltpu.CompilerParams(vmem_limit_bytes=16 << 20),
         name="gather",
     )(table, *received)
-
-
-def pack_kernel(query, key, value, out):
-    for kind, slab in enumerate((query, key, value)):
-        for group in range(8):
-            for head in range(HEADS_HERE):
-                at = (group * HEADS_HERE + head) * HEAD_DIM
-                lines = slab[0, :, :, at : at + HEAD_DIM]
-                out[group, kind, head] = lines.reshape(32, HEAD_DIM)
-
-
-def pack(query, key, value):
-    return pl.pallas_call(
-        pack_kernel,
-        out_shape=jax.ShapeDtypeStruct((8, 3, HEADS_HERE, 32, HEAD_DIM), LOW),
-        in_specs=whole(3),
-        out_specs=whole(1)[0],
-        compiler_params=pltpu.CompilerParams(vmem_limit_bytes=16 << 20),
-        name="pack",
-    )(query, key, value)
 
 
 def deal_kernel(swapped, out):
@@ -224,8 +208,8 @@
 
 
 def attend_kernel(table, own, above, below, *refs):
-    grads, rest, terms, edges = refs[:6], refs[6], refs[7], refs[8:10]
-    pair, turned, outer_turned, grad, total, held = refs[10:]
+    grads, firsts, rest, terms, edges = refs[:6], refs[6:10], refs[10], refs[11], refs[12:14]
+    pair, turned, outer_turned, grad, total, held = refs[14:]
     strip, odd = table[7], table[8]
     scaling = HEAD_DIM**-0.5
     rate = scaling * math.log2(math.e)
@@ -349,10 +333,11 @@
     for kind in range(2):
         for turn in range(2):
             row = (turn + odd) % 2
-            for part in range(2):
-                rest[kind, turn, part] = held[kind, row, first_of(0, odd) + part]
-                rest[kind, turn, 2 + part] = held[kind, row, first_of(1, odd) + part]
-            rest[kind, turn, 4] = held[kind, row, first_of(2, odd)]
+            for which in range(2):
+                for part in range(2):
+                    tile = held[kind, row, first_of(which, odd) + part]
+                    firsts[2 * which + turn][kind, part] = tile
+            rest[kind, turn] = held[kind, row, first_of(2, odd)]
     for kind, factor in ((0, scaling), (1, 1.0)):
         for at in range(7):
             for row in range(2):
@@ -367,14 +352,15 @@
 def attend(table, own, halos, grads):
     return pl.pallas_call(
         attend_kernel,
-        out_shape=[
-            jax.ShapeDtypeStruct((2, 2, 5, TILE, HEAD_DIM), LOW),
+        out_shape=pair_shapes(2, 4)
+        + [
+            jax.ShapeDtypeStruct((2, 2, TILE, HEAD_DIM), LOW),
             jax.ShapeDtypeStruct((2, 2, 7, TILE, HEAD_DIM), WIDE),
             jax.ShapeDtypeStruct((2, 7, TILE, HEAD_DIM), LOW),
             jax.ShapeDtypeStruct((2, 7, TILE, HEAD_DIM), LOW),
         ],
         in_specs=[pl.BlockSpec(memory_space=pltpu.SMEM)] + whole(9),
-        out_specs=whole(4),
+        out_specs=whole(8),
         scratch_shapes=[
             pltpu.VMEM((2, 7, 4, TILE, HEAD_DIM), LOW),
             pltpu.VMEM((2, HEAD_DIM, 14 * TILE), LOW),
@@ -391,7 +377,7 @@
     )(table, own, *halos, *grads)
 
 
-def rims_kernel(table, rest, terms, above, below, right, left, *outs):
+def rims_kernel(table, terms, above, below, right, left, *outs):
     odd = table[8]
     edges = (above, below)
     for kind in range(2):
@@ -402,22 +388,21 @@
         for part in range(2):
             at = first_of(1, odd) + part + 1
             for kind in range(2):
-                outs[turn][kind, part] = rest[kind, turn, 2 + part]
                 flip = (turn + odd) % 2 == 1
                 edge = jnp.where(flip, below[kind, at], above[kind, at])
                 value = terms[kind, (turn + odd) % 2, at] + edge.astype(WIDE)
-                outs[turn][2 + kind, part] = value.astype(LOW)
-
-
-def rims(table, rest, terms, edges):
+                outs[turn][kind, part] = value.astype(LOW)
+
+
+def rims(table, terms, edges):
     return pl.pallas_call(
         rims_kernel,
-        out_shape=column_shapes() + pair_shapes(4, 2),
-        in_specs=[pl.BlockSpec(memory_space=pltpu.SMEM)] + whole(4),
+        out_shape=column_shapes() + pair_shapes(2, 2),
+        in_specs=[pl.BlockSpec(memory_space=pltpu.SMEM)] + whole(3),
         out_specs=whole(4),
         compiler_params=pltpu.CompilerParams(vmem_limit_bytes=16 << 20),
         name="rims",
-    )(table, rest, terms, *edges)
+    )(table, terms, *edges)
 
 
 def combine_kernel(table, rest, terms, above, below, before, after, *outs):
@@ -435,19 +420,17 @@
             left = before[kind, row].astype(WIDE)
             right = after[kind, row].astype(WIDE)
             one, two = summed(first), summed(first + 1)
-            for part in range(2):
-                outs[turn][kind, part] = rest[kind, turn, part]
-            outs[turn][2 + kind, 0] = jnp.where(flipped, one, one + left).astype(LOW)
-            outs[turn][2 + kind, 1] = jnp.where(flipped, two + right, two).astype(LOW)
+            outs[turn][kind, 0] = jnp.where(flipped, one, one + left).astype(LOW)
+            outs[turn][kind, 1] = jnp.where(flipped, two + right, two).astype(LOW)
             alone = summed(first_of(2, odd)) + jnp.where(flipped, left, right)
-            outs[2 + turn][kind] = rest[kind, turn, 4]
+            outs[2 + turn][kind] = rest[kind, turn]
             outs[2 + turn][2 + kind] = alone.astype(LOW)
 
 
 def combine(table, rest, terms, edges, columns):
     return pl.pallas_call(
         combine_kernel,
-        out_shape=pair_shapes(4, 2) + [jax.ShapeDtypeStruct((4, TILE, HEAD_DIM), LOW)] * 2,
+        out_shape=pair_shapes(2, 2) + [jax.ShapeDtypeStruct((4, TILE, HEAD_DIM), LOW)] * 2,
         in_specs=[pl.BlockSpec(memory_space=pltpu.SMEM)] + whole(6),
         out_specs=whole(4),
         compiler_params=pltpu.CompilerParams(vmem_limit_bytes=16 << 20),
@@ -469,8 +452,11 @@
         grads = send_all(spread(place, upstream), [flipped(path) for path in to_owner])
 
     with jax.named_scope("heads"):
-        lines = pack(query_slab, key_slab, value_slab)
-        swapped = lax.all_to_all(lines, "head", 0, 0, tiled=True)
+        lines = [
+            slab.reshape(8, 4, 40, 128).transpose(2, 0, 1, 3).reshape(8, 5, 32, 128)
+            for slab in (query_slab, key_slab, value_slab)
+        ]
+        swapped = lax.all_to_all(jnp.stack(lines, axis=1), "head", 0, 0, tiled=True)
     with jax.named_scope("tiles"):
         dealt, early = lax.optimization_barrier((deal(swapped), grads[:EARLY]))
         got = lax.all_to_all(dealt, "tile", 0, 0, tiled=True)
@@ -480,19 +466,22 @@
     with jax.named_scope("halos"):
         halos = send_all([own[1, 5:], own[0, 5:]], row_routes)
     with jax.named_scope("attention"):
-        rest, terms, above, below = attend(place, own, halos, early + late)
+        *first, rest, terms, above, below = attend(place, own, halos, early + late)
     with jax.named_scope("row_terms"):
         edges = send_all([above, below], row_routes)
+        first = send_all(first, to_owner[:4])
+        edges, first[:2] = lax.optimization_barrier((edges, first[:2]))
     with jax.named_scope("column_terms"):
-        right, left, *free = rims(place, rest, terms, edges)
+        right, left, *free = rims(place, terms, edges)
         columns = send_all([right, left], column_routes)
         free = send_all(free, to_owner[2:4])
+        columns, first[2:] = lax.optimization_barrier((columns, first[2:]))
     with jax.named_scope("outputs_home"):
         leaving = combine(place, rest, terms, edges, columns)
         leaving, free = lax.optimization_barrier((leaving, free))
         late = send_all(leaving, to_owner[:2] + to_owner[4:])
     with jax.named_scope("settle"):
-        return tuple(gather(place, free + late))
+        return tuple(gather(place, first + late[:2] + free + late[2:]))
 
 
 def solution(mesh):

time: 159 us -> 164 us (1.031)
  starting transfers between devices: 86.9 us -> 104 us
  waiting for transfers between devices: 50 us -> 37.4 us
    ppermute x18 -> x22, starting transfers between devices: 71.7 us -> 89.3 us  [send_all(): lax.ppermute(part, 'tile', path)]
    ppermute x18 -> x22, waiting for transfers between devices: 29.3 us -> 16.7 us  [send_all(): lax.ppermute(part, 'tile', path)]
    unnamed x8 -> x6, local copies, waits for them, and re-layouts: 2.91 us -> 0.01 us
    reshape x0 -> x6, local copies, waits for them, and re-layouts: none -> 1.79 us  [local(): slab.reshape(8, 4, 40, 128).transpose(2, 0, 1, 3).reshape(8, 5, 32, 128)]
    pallas_call x4 -> x3, Pallas kernels: 10.9 us -> 9.52 us  [the longest x1 8.13 us: attend(): pl.pallas_call(attend_kernel, out_shape=pair_shapes(2, 4) + [jax.ShapeDty...]
  transfers between devices with their start and end apart: 20 -> 24, of which waited for: 9 -> 8; matrix products, arithmetic and copies ran while one was open for 1% -> 1% of each run, Pallas kernels for 2% -> 2%
where the time goes in v8:
time: 164 us; the launch traced here: 161 us
  starting transfers between devices  104 us (63%)
  waiting for transfers between devices  37.4 us (23%)
  Pallas kernels  13.8 us (8%)
  local copies, waits for them, and re-layouts  3.23 us (2%)
    ppermute x22, starting transfers between devices, send_all(): lax.ppermute(part, 'tile', path)  89.3 us
    all_to_all x1, waiting for transfers between devices, local(): got = lax.all_to_all(dealt, 'tile', 0, 0, tiled=True)  20.6 us
    ppermute x22, waiting for transfers between devices, send_all(): lax.ppermute(part, 'tile', path)  16.7 us
    all_to_all x1, starting transfers between devices, local(): got = lax.all_to_all(dealt, 'tile', 0, 0, tiled=True)  10.8 us
    pallas_call x1, Pallas kernels, attend(): pl.pallas_call(attend_kernel, out_shape=pair_shapes(2, 4) + [jax.ShapeDty...  8.13 us
    all_to_all x1, starting transfers between devices, local(): swapped = lax.all_to_all(jnp.stack(lines, axis=1), 'head', 0, 0, tiled=True)  4.43 us
  transfers between devices with their start and end apart: 24, of which 8 were waited for; matrix products, arithmetic and copies ran while one was open for 1% of the time, Pallas kernels for 2%

profile of v8, /device:TPU:40, one launch (start us, length us, event | category | flops | bytes accessed | tf_op | source)
XLA Modules:
  0.0 161.0 jit_solution(8671792798667247301)
XLA Ops:
  0.7 1.2 reshape.32
  1.8 0.1 copy.9
  2.0 0.1 reshape.34
  2.1 0.1 copy.10
  2.2 0.1 reshape.36
  2.4 0.1 copy.11
  2.5 1.1 pad_maximum_fusion
  3.6 4.4 %all-to-all-start = ((bf16[8,3,5,32,128]{4,3,2,1,0:T(8,128)(2,1)}), bf16[8,3,5,32,128]{4,3,2,1,0:T(8,128)(2,1)S(1)}, u32[]{:S(2)}, u32[]{:S(2)}) async-start(bf16[8,3,5,32,128]{4,3,2,1,0:T(8,128)(2,1)} %pad_maximum_fusion), calls=%async_computation | async-start | bytes 1966080 | tf_op jit(solution)/shard_map/heads/all_to_all | solution.py:459
  8.0 0.7 dynamic-slice_bitcast_fusion.table
  8.7 0.9 spread.1
  9.6 5.2 %collective-permute-start = (bf16[2,128,128]{2,1,0:T(8,128)(2,1)S(1)}, bf16[2,128,128]{2,1,0:T(8,128)(2,1)S(1)}, u32[]{:S(2)}, u32[]{:S(2)}) collective-permute-start(bf16[2,128,128]{2,1,0:T(8,128)(2,1)S(1)} %get-tuple-element.48), channel_id=1, source_target_pairs={{48,0},{16,8},{40,16},{8,24},{32,32},{0,40},{56,48},{24,56},{112,6... | collective-permute-start | bytes 196616 | tf_op jit(solution)/shard_map/upstream_to_units/ppermute | solution.py:442
  14.8 1.9 %collective-permute-start.1 = (bf16[2,128,128]{2,1,0:T(8,128)(2,1)S(1)}, bf16[2,128,128]{2,1,0:T(8,128)(2,1)S(1)}, u32[]{:S(2)}, u32[]{:S(2)}) collective-permute-start(bf16[2,128,128]{2,1,0:T(8,128)(2,1)S(1)} %get-tuple-element.49), channel_id=1, source_target_pairs={{16,0},{48,8},{8,16},{40,24},{0,32},{32,40},{24,48},{56,56},{80,64... | collective-permute-start | bytes 196616 | tf_op jit(solution)/shard_map/upstream_to_units/ppermute | solution.py:442
  16.7 10.0 %collective-permute-start.2 = (bf16[2,128,128]{2,1,0:T(8,128)(2,1)S(1)}, bf16[2,128,128]{2,1,0:T(8,128)(2,1)S(1)}, u32[]{:S(2)}, u32[]{:S(2)}) collective-permute-start(bf16[2,128,128]{2,1,0:T(8,128)(2,1)S(1)} %get-tuple-element.50), channel_id=1, source_target_pairs={{40,0},{24,8},{32,16},{16,24},{56,32},{8,40},{48,48},{0,56},{104,6... | collective-permute-start | bytes 196616 | tf_op jit(solution)/shard_map/upstream_to_units/ppermute | solution.py:442
  26.7 1.3 deal.1
  28.0 0.6 collective-permute-done.2.refs_2_
  28.6 10.8 %all-to-all-start.1 = ((bf16[32,19,8,128]{3,2,1,0:T(8,128)(2,1)}), bf16[32,19,8,128]{3,2,1,0:T(8,128)(2,1)S(1)}, u32[]{:S(2)}, u32[]{:S(2)}) async-start(bf16[32,19,8,128]{3,2,1,0:T(8,128)(2,1)} %deal.1), calls=%async_computation.1 | async-start | bytes 2490368 | tf_op jit(solution)/shard_map/tiles/all_to_all | solution.py:462
  39.4 2.5 %collective-permute-start.3 = (bf16[2,128,128]{2,1,0:T(8,128)(2,1)S(1)}, bf16[2,128,128]{2,1,0:T(8,128)(2,1)S(1)}, u32[]{:S(2)}, u32[]{:S(2)}) collective-permute-start(bf16[2,128,128]{2,1,0:T(8,128)(2,1)S(1)} %get-tuple-element.52), channel_id=1, source_target_pairs={{8,0},{56,8},{0,16},{48,24},{24,32},{40,40},{16,48},{32,56},{72,64... | collective-permute-start | bytes 196616 | tf_op jit(solution)/shard_map/upstream_to_units/ppermute | solution.py:442
  41.8 5.5 %collective-permute-start.4 = (bf16[128,128]{1,0:T(8,128)(2,1)S(1)}, bf16[128,128]{1,0:T(8,128)(2,1)S(1)}, u32[]{:S(2)}, u32[]{:S(2)}) collective-permute-start(bf16[128,128]{1,0:T(8,128)(2,1)S(1)} %get-tuple-element.53), channel_id=1, source_target_pairs={{32,0},{0,8},{56,16},{24,24},{48,32},{16,40},{40,48},{8,56},{96,64... | collective-permute-start | bytes 98312 | tf_op jit(solution)/shard_map/upstream_to_units/ppermute | solution.py:442
  47.3 4.3 %collective-permute-start.5 = (bf16[128,128]{1,0:T(8,128)(2,1)S(1)}, bf16[128,128]{1,0:T(8,128)(2,1)S(1)}, u32[]{:S(2)}, u32[]{:S(2)}) collective-permute-start(bf16[128,128]{1,0:T(8,128)(2,1)S(1)} %get-tuple-element.54), channel_id=1, source_target_pairs={{0,0},{32,8},{24,16},{56,24},{16,32},{48,40},{8,48},{40,56},{64,64... | collective-permute-start | bytes 98312 | tf_op jit(solution)/shard_map/upstream_to_units/ppermute | solution.py:442
  51.6 20.6 %all-to-all-done.1 = bf16[32,19,8,128]{3,2,1,0:T(8,128)(2,1)S(1)} async-done(((bf16[32,19,8,128]{3,2,1,0:T(8,128)(2,1)}), bf16[32,19,8,128]{3,2,1,0:T(8,128)(2,1)S(1)}, u32[]{:S(2)}, u32[]{:S(2)}) %all-to-all-start.1) | async-done | bytes 1245216 | tf_op jit(solution)/shard_map/tiles/all_to_all | solution.py:462
  72.2 0.7 copy.12
  72.9 0.1 slice_bitcast_fusion
  73.0 2.5 %collective-permute-start.7 = (bf16[14,128,128]{2,1,0:T(8,128)(2,1)S(1)}, bf16[14,128,128]{2,1,0:T(8,128)(2,1)S(1)}, u32[]{:S(2)}, u32[]{:S(2)}) collective-permute-start(bf16[14,128,128]{2,1,0:T(8,128)(2,1)S(1)} %get-tuple-element.92), channel_id=1, source_target_pairs={{64,0},{72,8},{80,16},{88,24},{96,32},{104,40},{112,48},{120,56},{... | collective-permute-start | bytes 1376264 | tf_op jit(solution)/shard_map/halos/ppermute | solution.py:442
  75.5 3.4 %collective-permute-start.6 = (bf16[14,128,128]{2,1,0:T(8,128)(2,1)S(1)}, bf16[14,128,128]{2,1,0:T(8,128)(2,1)S(1)}, u32[]{:S(2)}, u32[]{:S(2)}) collective-permute-start(bf16[14,128,128]{2,1,0:T(8,128)(2,1)S(1)} %get-tuple-element.93), channel_id=1, source_target_pairs={{0,64},{8,72},{16,80},{24,88},{32,96},{40,104},{48,112},{56,120},{... | collective-permute-start | bytes 1376264 | tf_op jit(solution)/shard_map/halos/ppermute | solution.py:442
  78.9 4.5 %collective-permute-done.7.below = bf16[14,128,128]{2,1,0:T(8,128)(2,1)S(1)} collective-permute-done((bf16[14,128,128]{2,1,0:T(8,128)(2,1)S(1)}, bf16[14,128,128]{2,1,0:T(8,128)(2,1)S(1)}, u32[]{:S(2)}, u32[]{:S(2)}) %collective-permute-start.7) | collective-permute-done | bytes 458784 | tf_op jit(solution)/shard_map/halos/ppermute | solution.py:442
  83.4 2.5 %collective-permute-done.6.above = bf16[14,128,128]{2,1,0:T(8,128)(2,1)S(1)} collective-permute-done((bf16[14,128,128]{2,1,0:T(8,128)(2,1)S(1)}, bf16[14,128,128]{2,1,0:T(8,128)(2,1)S(1)}, u32[]{:S(2)}, u32[]{:S(2)}) %collective-permute-start.6) | collective-permute-done | bytes 458784 | tf_op jit(solution)/shard_map/halos/ppermute | solution.py:442
  85.9 8.1 %attend.1 = (bf16[2,2,128,128]{3,2,1,0:T(8,128)(2,1)S(1)}, bf16[2,2,128,128]{3,2,1,0:T(8,128)(2,1)S(1)}, bf16[2,2,128,128]{3,2,1,0:T(8,128)(2,1)S(1)}, bf16[2,2,...) custom-call(s32[14]{0:T(128)S(1)} %dynamic-slice_bitcast_fusion.tabl, ...), custom_call_target="tpu_custom_call" | custom-call | flops 3000000000 | bytes 8000000 | tf_op jit(solution)/shard_map/attention/attend/pallas_call | solution.py:353
  94.0 3.4 %collective-permute-start.8 = (bf16[2,7,128,128]{3,2,1,0:T(8,128)(2,1)S(1)}, bf16[2,7,128,128]{3,2,1,0:T(8,128)(2,1)S(1)}, u32[]{:S(2)}, u32[]{:S(2)}) collective-permute-start(bf16[2,7,128,128]{3,2,1,0:T(8,128)(2,1)S(1)} %get-tuple-element.62), channel_id=1, source_target_pairs={{0,64},{8,72},{16,80},{24,88},{32,96},{40,104},{48,112},{56,120},{... | collective-permute-start | bytes 1376264 | tf_op jit(solution)/shard_map/row_terms/ppermute | solution.py:442
  97.4 2.5 %collective-permute-start.9 = (bf16[2,7,128,128]{3,2,1,0:T(8,128)(2,1)S(1)}, bf16[2,7,128,128]{3,2,1,0:T(8,128)(2,1)S(1)}, u32[]{:S(2)}, u32[]{:S(2)}) collective-permute-start(bf16[2,7,128,128]{3,2,1,0:T(8,128)(2,1)S(1)} %get-tuple-element.63), channel_id=1, source_target_pairs={{64,0},{72,8},{80,16},{88,24},{96,32},{104,40},{112,48},{120,56},{... | collective-permute-start | bytes 1376264 | tf_op jit(solution)/shard_map/row_terms/ppermute | solution.py:442
  99.9 2.7 %collective-permute-start.10 = (bf16[2,2,128,128]{3,2,1,0:T(8,128)(2,1)S(1)}, bf16[2,2,128,128]{3,2,1,0:T(8,128)(2,1)S(1)}, u32[]{:S(2)}, u32[]{:S(2)}) collective-permute-start(bf16[2,2,128,128]{3,2,1,0:T(8,128)(2,1)S(1)} %get-tuple-element.64), channel_id=1, source_target_pairs={{0,48},{8,16},{16,40},{24,8},{32,32},{40,0},{48,56},{56,24},{64,11... | collective-permute-start | bytes 393224 | tf_op jit(solution)/shard_map/row_terms/ppermute | solution.py:442
  102.6 4.7 %collective-permute-start.11 = (bf16[2,2,128,128]{3,2,1,0:T(8,128)(2,1)S(1)}, bf16[2,2,128,128]{3,2,1,0:T(8,128)(2,1)S(1)}, u32[]{:S(2)}, u32[]{:S(2)}) collective-permute-start(bf16[2,2,128,128]{3,2,1,0:T(8,128)(2,1)S(1)} %get-tuple-element.65), channel_id=1, source_target_pairs={{0,16},{8,48},{16,8},{24,40},{32,0},{40,32},{48,24},{56,56},{64,80... | collective-permute-start | bytes 393224 | tf_op jit(solution)/shard_map/row_terms/ppermute | solution.py:442
  107.3 7.2 %collective-permute-start.14 = (bf16[2,2,128,128]{3,2,1,0:T(8,128)(2,1)S(1)}, bf16[2,2,128,128]{3,2,1,0:T(8,128)(2,1)S(1)}, u32[]{:S(2)}, u32[]{:S(2)}) collective-permute-start(bf16[2,2,128,128]{3,2,1,0:T(8,128)(2,1)S(1)} %get-tuple-element.73), channel_id=1, source_target_pairs={{0,40},{8,24},{16,32},{24,16},{32,56},{40,8},{48,48},{56,0},{64,10... | collective-permute-start | bytes 393224 | tf_op jit(solution)/shard_map/row_terms/ppermute | solution.py:442
  114.5 1.9 %collective-permute-start.15 = (bf16[2,2,128,128]{3,2,1,0:T(8,128)(2,1)S(1)}, bf16[2,2,128,128]{3,2,1,0:T(8,128)(2,1)S(1)}, u32[]{:S(2)}, u32[]{:S(2)}) collective-permute-start(bf16[2,2,128,128]{3,2,1,0:T(8,128)(2,1)S(1)} %get-tuple-element.74), channel_id=1, source_target_pairs={{0,8},{8,56},{16,0},{24,48},{32,24},{40,40},{48,16},{56,32},{64,72... | collective-permute-start | bytes 393224 | tf_op jit(solution)/shard_map/row_terms/ppermute | solution.py:442
  116.4 0.7 rims.1
  117.1 5.8 %collective-permute-start.12 = (bf16[2,2,128,128]{3,2,1,0:T(8,128)(2,1)S(1)}, bf16[2,2,128,128]{3,2,1,0:T(8,128)(2,1)S(1)}, u32[]{:S(2)}, u32[]{:S(2)}) collective-permute-start(bf16[2,2,128,128]{3,2,1,0:T(8,128)(2,1)S(1)} %get-tuple-element.71), channel_id=1, source_target_pairs={{0,56},{8,0},{16,8},{24,16},{32,24},{40,32},{56,48},{64,120},{72,6... | collective-permute-start | bytes 393224 | tf_op jit(solution)/shard_map/column_terms/ppermute | solution.py:442
  122.9 1.9 %collective-permute-start.13 = (bf16[2,2,128,128]{3,2,1,0:T(8,128)(2,1)S(1)}, bf16[2,2,128,128]{3,2,1,0:T(8,128)(2,1)S(1)}, u32[]{:S(2)}, u32[]{:S(2)}) collective-permute-start(bf16[2,2,128,128]{3,2,1,0:T(8,128)(2,1)S(1)} %get-tuple-element.72), channel_id=1, source_target_pairs={{0,8},{8,16},{16,24},{24,32},{32,40},{48,56},{56,0},{64,72},{72,80... | collective-permute-start | bytes 393224 | tf_op jit(solution)/shard_map/column_terms/ppermute | solution.py:442
  124.8 1.9 %collective-permute-start.16 = (bf16[2,2,128,128]{3,2,1,0:T(8,128)(2,1)S(1)}, bf16[2,2,128,128]{3,2,1,0:T(8,128)(2,1)S(1)}, u32[]{:S(2)}, u32[]{:S(2)}) collective-permute-start(bf16[2,2,128,128]{3,2,1,0:T(8,128)(2,1)S(1)} %get-tuple-element.84), channel_id=1, source_target_pairs={{0,40},{8,24},{16,32},{24,16},{32,56},{40,8},{48,48},{56,0},{64,10... | collective-permute-start | bytes 393224 | tf_op jit(solution)/shard_map/column_terms/ppermute | solution.py:442
  126.8 6.6 %collective-permute-start.17 = (bf16[2,2,128,128]{3,2,1,0:T(8,128)(2,1)S(1)}, bf16[2,2,128,128]{3,2,1,0:T(8,128)(2,1)S(1)}, u32[]{:S(2)}, u32[]{:S(2)}) collective-permute-start(bf16[2,2,128,128]{3,2,1,0:T(8,128)(2,1)S(1)} %get-tuple-element.85), channel_id=1, source_target_pairs={{0,8},{8,56},{16,0},{24,48},{32,24},{40,40},{48,16},{56,32},{64,72... | collective-permute-start | bytes 393224 | tf_op jit(solution)/shard_map/column_terms/ppermute | solution.py:442
  133.4 0.7 combine.1
  134.1 1.7 %collective-permute-done.16.refs_6_ = bf16[2,2,128,128]{3,2,1,0:T(8,128)(2,1)S(1)} collective-permute-done((bf16[2,2,128,128]{3,2,1,0:T(8,128)(2,1)S(1)}, bf16[2,2,128,128]{3,2,1,0:T(8,128)(2,1)S(1)}, u32[]{:S(2)}, u32[]{:S(2)}) %collective-permute-start.16) | collective-permute-done | bytes 131104 | tf_op jit(solution)/shard_map/column_terms/ppermute | solution.py:442
  135.8 1.4 collective-permute-done.17.refs_7_
  137.2 6.0 %collective-permute-start.18 = (bf16[2,2,128,128]{3,2,1,0:T(8,128)(2,1)S(1)}, bf16[2,2,128,128]{3,2,1,0:T(8,128)(2,1)S(1)}, u32[]{:S(2)}, u32[]{:S(2)}) collective-permute-start(bf16[2,2,128,128]{3,2,1,0:T(8,128)(2,1)S(1)} %get-tuple-element.86), channel_id=1, source_target_pairs={{0,48},{8,16},{16,40},{24,8},{32,32},{40,0},{48,56},{56,24},{64,11... | collective-permute-start | bytes 393224 | tf_op jit(solution)/shard_map/outputs_home/ppermute | solution.py:442
  143.2 3.8 %collective-permute-start.19 = (bf16[2,2,128,128]{3,2,1,0:T(8,128)(2,1)S(1)}, bf16[2,2,128,128]{3,2,1,0:T(8,128)(2,1)S(1)}, u32[]{:S(2)}, u32[]{:S(2)}) collective-permute-start(bf16[2,2,128,128]{3,2,1,0:T(8,128)(2,1)S(1)} %get-tuple-element.87), channel_id=1, source_target_pairs={{0,16},{8,48},{16,8},{24,40},{32,0},{40,32},{48,24},{56,56},{64,80... | collective-permute-start | bytes 393224 | tf_op jit(solution)/shard_map/outputs_home/ppermute | solution.py:442
  147.0 1.9 %collective-permute-start.20 = (bf16[4,128,128]{2,1,0:T(8,128)(2,1)S(1)}, bf16[4,128,128]{2,1,0:T(8,128)(2,1)S(1)}, u32[]{:S(2)}, u32[]{:S(2)}) collective-permute-start(bf16[4,128,128]{2,1,0:T(8,128)(2,1)S(1)} %get-tuple-element.90), channel_id=1, source_target_pairs={{0,32},{8,0},{16,56},{24,24},{32,48},{40,16},{48,40},{56,8},{64,96... | collective-permute-start | bytes 393224 | tf_op jit(solution)/shard_map/outputs_home/ppermute | solution.py:442
  149.0 3.8 %collective-permute-start.21 = (bf16[4,128,128]{2,1,0:T(8,128)(2,1)S(1)}, bf16[4,128,128]{2,1,0:T(8,128)(2,1)S(1)}, u32[]{:S(2)}, u32[]{:S(2)}) collective-permute-start(bf16[4,128,128]{2,1,0:T(8,128)(2,1)S(1)} %get-tuple-element.91), channel_id=1, source_target_pairs={{0,0},{8,32},{16,24},{24,56},{32,16},{40,48},{48,8},{56,40},{64,64... | collective-permute-start | bytes 393224 | tf_op jit(solution)/shard_map/outputs_home/ppermute | solution.py:442
  152.8 3.2 %collective-permute-done.20.refs_8_ = bf16[4,128,128]{2,1,0:T(8,128)(2,1)S(1)} collective-permute-done((bf16[4,128,128]{2,1,0:T(8,128)(2,1)S(1)}, bf16[4,128,128]{2,1,0:T(8,128)(2,1)S(1)}, u32[]{:S(2)}, u32[]{:S(2)}) %collective-permute-start.20) | collective-permute-done | bytes 131104 | tf_op jit(solution)/shard_map/outputs_home/ppermute | solution.py:442
  156.0 2.8 %collective-permute-done.21.refs_9_ = bf16[4,128,128]{2,1,0:T(8,128)(2,1)S(1)} collective-permute-done((bf16[4,128,128]{2,1,0:T(8,128)(2,1)S(1)}, bf16[4,128,128]{2,1,0:T(8,128)(2,1)S(1)}, u32[]{:S(2)}, u32[]{:S(2)}) %collective-permute-start.21) | collective-permute-done | bytes 131104 | tf_op jit(solution)/shard_map/outputs_home/ppermute | solution.py:442
  158.8 2.1 %gather.1 = (bf16[256,640]{1,0:T(8,128)(2,1)}, bf16[256,640]{1,0:T(8,128)(2,1)}, bf16[256,640]{1,0:T(8,128)(2,1)}, bf16[256,640]{1,0:T(8,128)(2,1)}) custom-call(s32[14]{0:T(128)S(1)} %dynamic-slice_bitcast_fusion.table, bf16[2,2,128,128]{3,2,1,0:T(8,128)(2,1)S(1)} %collective-permute-done.10.refs_0_, ...), custom_call_target="tpu_custom_call" | custom-call | tf_op jit(solution)/shard_map/settle/gather/pallas_call | solution.py:171
  (22 shorter events, 0.1 us)
Async XLA Ops:
  0.6 1.3 copy-start.1
  0.6 1.6 copy-start.2
  3.6 5.1 %copy-start = (bf16[256,640]{1,0:T(8,128)(2,1)S(1)}, bf16[256,640]{1,0:T(8,128)(2,1)}, u32[]{:S(2)}) copy-start(bf16[256,640]{1,0:T(8,128)(2,1)} %upstream.1) | copy-start | bytes 983044
  3.6 23.1 %all-to-all-start = ((bf16[8,3,5,32,128]{4,3,2,1,0:T(8,128)(2,1)}), bf16[8,3,5,32,128]{4,3,2,1,0:T(8,128)(2,1)S(1)}, u32[]{:S(2)}, u32[]{:S(2)}) async-start(bf16[8,3,5,32,128]{4,3,2,1,0:T(8,128)(2,1)} %pad_maximum_fusion), calls=%async_computation | async-start | bytes 1966080 | tf_op jit(solution)/shard_map/heads/all_to_all | solution.py:459
  9.6 18.4 %collective-permute-start = (bf16[2,128,128]{2,1,0:T(8,128)(2,1)S(1)}, bf16[2,128,128]{2,1,0:T(8,128)(2,1)S(1)}, u32[]{:S(2)}, u32[]{:S(2)}) collective-permute-start(bf16[2,128,128]{2,1,0:T(8,128)(2,1)S(1)} %get-tuple-element.48), channel_id=1, source_target_pairs={{48,0},{16,8},{40,16},{8,24},{32,32},{0,40},{56,48},{24,56},{112,6... | collective-permute-start | bytes 196616 | tf_op jit(solution)/shard_map/upstream_to_units/ppermute | solution.py:442
  14.8 13.2 %collective-permute-start.1 = (bf16[2,128,128]{2,1,0:T(8,128)(2,1)S(1)}, bf16[2,128,128]{2,1,0:T(8,128)(2,1)S(1)}, u32[]{:S(2)}, u32[]{:S(2)}) collective-permute-start(bf16[2,128,128]{2,1,0:T(8,128)(2,1)S(1)} %get-tuple-element.49), channel_id=1, source_target_pairs={{16,0},{48,8},{8,16},{40,24},{0,32},{32,40},{24,48},{56,56},{80,64... | collective-permute-start | bytes 196616 | tf_op jit(solution)/shard_map/upstream_to_units/ppermute | solution.py:442
  16.7 11.9 %collective-permute-start.2 = (bf16[2,128,128]{2,1,0:T(8,128)(2,1)S(1)}, bf16[2,128,128]{2,1,0:T(8,128)(2,1)S(1)}, u32[]{:S(2)}, u32[]{:S(2)}) collective-permute-start(bf16[2,128,128]{2,1,0:T(8,128)(2,1)S(1)} %get-tuple-element.50), channel_id=1, source_target_pairs={{40,0},{24,8},{32,16},{16,24},{56,32},{8,40},{48,48},{0,56},{104,6... | collective-permute-start | bytes 196616 | tf_op jit(solution)/shard_map/upstream_to_units/ppermute | solution.py:442
  28.6 43.7 %all-to-all-start.1 = ((bf16[32,19,8,128]{3,2,1,0:T(8,128)(2,1)}), bf16[32,19,8,128]{3,2,1,0:T(8,128)(2,1)S(1)}, u32[]{:S(2)}, u32[]{:S(2)}) async-start(bf16[32,19,8,128]{3,2,1,0:T(8,128)(2,1)} %deal.1), calls=%async_computation.1 | async-start | bytes 2490368 | tf_op jit(solution)/shard_map/tiles/all_to_all | solution.py:462
  39.4 33.6 %collective-permute-start.3 = (bf16[2,128,128]{2,1,0:T(8,128)(2,1)S(1)}, bf16[2,128,128]{2,1,0:T(8,128)(2,1)S(1)}, u32[]{:S(2)}, u32[]{:S(2)}) collective-permute-start(bf16[2,128,128]{2,1,0:T(8,128)(2,1)S(1)} %get-tuple-element.52), channel_id=1, source_target_pairs={{8,0},{56,8},{0,16},{48,24},{24,32},{40,40},{16,48},{32,56},{72,64... | collective-permute-start | bytes 196616 | tf_op jit(solution)/shard_map/upstream_to_units/ppermute | solution.py:442
  41.8 31.1 %collective-permute-start.4 = (bf16[128,128]{1,0:T(8,128)(2,1)S(1)}, bf16[128,128]{1,0:T(8,128)(2,1)S(1)}, u32[]{:S(2)}, u32[]{:S(2)}) collective-permute-start(bf16[128,128]{1,0:T(8,128)(2,1)S(1)} %get-tuple-element.53), channel_id=1, source_target_pairs={{32,0},{0,8},{56,16},{24,24},{48,32},{16,40},{40,48},{8,56},{96,64... | collective-permute-start | bytes 98312 | tf_op jit(solution)/shard_map/upstream_to_units/ppermute | solution.py:442
  47.3 25.6 %collective-permute-start.5 = (bf16[128,128]{1,0:T(8,128)(2,1)S(1)}, bf16[128,128]{1,0:T(8,128)(2,1)S(1)}, u32[]{:S(2)}, u32[]{:S(2)}) collective-permute-start(bf16[128,128]{1,0:T(8,128)(2,1)S(1)} %get-tuple-element.54), channel_id=1, source_target_pairs={{0,0},{32,8},{24,16},{56,24},{16,32},{48,40},{8,48},{40,56},{64,64... | collective-permute-start | bytes 98312 | tf_op jit(solution)/shard_map/upstream_to_units/ppermute | solution.py:442
  73.0 10.4 %collective-permute-start.7 = (bf16[14,128,128]{2,1,0:T(8,128)(2,1)S(1)}, bf16[14,128,128]{2,1,0:T(8,128)(2,1)S(1)}, u32[]{:S(2)}, u32[]{:S(2)}) collective-permute-start(bf16[14,128,128]{2,1,0:T(8,128)(2,1)S(1)} %get-tuple-element.92), channel_id=1, source_target_pairs={{64,0},{72,8},{80,16},{88,24},{96,32},{104,40},{112,48},{120,56},{... | collective-permute-start | bytes 1376264 | tf_op jit(solution)/shard_map/halos/ppermute | solution.py:442
  75.5 10.4 %collective-permute-start.6 = (bf16[14,128,128]{2,1,0:T(8,128)(2,1)S(1)}, bf16[14,128,128]{2,1,0:T(8,128)(2,1)S(1)}, u32[]{:S(2)}, u32[]{:S(2)}) collective-permute-start(bf16[14,128,128]{2,1,0:T(8,128)(2,1)S(1)} %get-tuple-element.93), channel_id=1, source_target_pairs={{0,64},{8,72},{16,80},{24,88},{32,96},{40,104},{48,112},{56,120},{... | collective-permute-start | bytes 1376264 | tf_op jit(solution)/shard_map/halos/ppermute | solution.py:442
  94.0 22.4 %collective-permute-start.8 = (bf16[2,7,128,128]{3,2,1,0:T(8,128)(2,1)S(1)}, bf16[2,7,128,128]{3,2,1,0:T(8,128)(2,1)S(1)}, u32[]{:S(2)}, u32[]{:S(2)}) collective-permute-start(bf16[2,7,128,128]{3,2,1,0:T(8,128)(2,1)S(1)} %get-tuple-element.62), channel_id=1, source_target_pairs={{0,64},{8,72},{16,80},{24,88},{32,96},{40,104},{48,112},{56,120},{... | collective-permute-start | bytes 1376264 | tf_op jit(solution)/shard_map/row_terms/ppermute | solution.py:442
  97.4 19.0 %collective-permute-start.9 = (bf16[2,7,128,128]{3,2,1,0:T(8,128)(2,1)S(1)}, bf16[2,7,128,128]{3,2,1,0:T(8,128)(2,1)S(1)}, u32[]{:S(2)}, u32[]{:S(2)}) collective-permute-start(bf16[2,7,128,128]{3,2,1,0:T(8,128)(2,1)S(1)} %get-tuple-element.63), channel_id=1, source_target_pairs={{64,0},{72,8},{80,16},{88,24},{96,32},{104,40},{112,48},{120,56},{... | collective-permute-start | bytes 1376264 | tf_op jit(solution)/shard_map/row_terms/ppermute | solution.py:442
  99.9 14.6 %collective-permute-start.10 = (bf16[2,2,128,128]{3,2,1,0:T(8,128)(2,1)S(1)}, bf16[2,2,128,128]{3,2,1,0:T(8,128)(2,1)S(1)}, u32[]{:S(2)}, u32[]{:S(2)}) collective-permute-start(bf16[2,2,128,128]{3,2,1,0:T(8,128)(2,1)S(1)} %get-tuple-element.64), channel_id=1, source_target_pairs={{0,48},{8,16},{16,40},{24,8},{32,32},{40,0},{48,56},{56,24},{64,11... | collective-permute-start | bytes 393224 | tf_op jit(solution)/shard_map/row_terms/ppermute | solution.py:442
  102.6 13.8 %collective-permute-start.11 = (bf16[2,2,128,128]{3,2,1,0:T(8,128)(2,1)S(1)}, bf16[2,2,128,128]{3,2,1,0:T(8,128)(2,1)S(1)}, u32[]{:S(2)}, u32[]{:S(2)}) collective-permute-start(bf16[2,2,128,128]{3,2,1,0:T(8,128)(2,1)S(1)} %get-tuple-element.65), channel_id=1, source_target_pairs={{0,16},{8,48},{16,8},{24,40},{32,0},{40,32},{48,24},{56,56},{64,80... | collective-permute-start | bytes 393224 | tf_op jit(solution)/shard_map/row_terms/ppermute | solution.py:442
  107.3 19.5 %collective-permute-start.14 = (bf16[2,2,128,128]{3,2,1,0:T(8,128)(2,1)S(1)}, bf16[2,2,128,128]{3,2,1,0:T(8,128)(2,1)S(1)}, u32[]{:S(2)}, u32[]{:S(2)}) collective-permute-start(bf16[2,2,128,128]{3,2,1,0:T(8,128)(2,1)S(1)} %get-tuple-element.73), channel_id=1, source_target_pairs={{0,40},{8,24},{16,32},{24,16},{32,56},{40,8},{48,48},{56,0},{64,10... | collective-permute-start | bytes 393224 | tf_op jit(solution)/shard_map/row_terms/ppermute | solution.py:442
  114.5 18.9 %collective-permute-start.15 = (bf16[2,2,128,128]{3,2,1,0:T(8,128)(2,1)S(1)}, bf16[2,2,128,128]{3,2,1,0:T(8,128)(2,1)S(1)}, u32[]{:S(2)}, u32[]{:S(2)}) collective-permute-start(bf16[2,2,128,128]{3,2,1,0:T(8,128)(2,1)S(1)} %get-tuple-element.74), channel_id=1, source_target_pairs={{0,8},{8,56},{16,0},{24,48},{32,24},{40,40},{48,16},{56,32},{64,72... | collective-permute-start | bytes 393224 | tf_op jit(solution)/shard_map/row_terms/ppermute | solution.py:442
  117.1 16.3 %collective-permute-start.12 = (bf16[2,2,128,128]{3,2,1,0:T(8,128)(2,1)S(1)}, bf16[2,2,128,128]{3,2,1,0:T(8,128)(2,1)S(1)}, u32[]{:S(2)}, u32[]{:S(2)}) collective-permute-start(bf16[2,2,128,128]{3,2,1,0:T(8,128)(2,1)S(1)} %get-tuple-element.71), channel_id=1, source_target_pairs={{0,56},{8,0},{16,8},{24,16},{32,24},{40,32},{56,48},{64,120},{72,6... | collective-permute-start | bytes 393224 | tf_op jit(solution)/shard_map/column_terms/ppermute | solution.py:442
  122.9 10.5 %collective-permute-start.13 = (bf16[2,2,128,128]{3,2,1,0:T(8,128)(2,1)S(1)}, bf16[2,2,128,128]{3,2,1,0:T(8,128)(2,1)S(1)}, u32[]{:S(2)}, u32[]{:S(2)}) collective-permute-start(bf16[2,2,128,128]{3,2,1,0:T(8,128)(2,1)S(1)} %get-tuple-element.72), channel_id=1, source_target_pairs={{0,8},{8,16},{16,24},{24,32},{32,40},{48,56},{56,0},{64,72},{72,80... | collective-permute-start | bytes 393224 | tf_op jit(solution)/shard_map/column_terms/ppermute | solution.py:442
  124.8 11.0 %collective-permute-start.16 = (bf16[2,2,128,128]{3,2,1,0:T(8,128)(2,1)S(1)}, bf16[2,2,128,128]{3,2,1,0:T(8,128)(2,1)S(1)}, u32[]{:S(2)}, u32[]{:S(2)}) collective-permute-start(bf16[2,2,128,128]{3,2,1,0:T(8,128)(2,1)S(1)} %get-tuple-element.84), channel_id=1, source_target_pairs={{0,40},{8,24},{16,32},{24,16},{32,56},{40,8},{48,48},{56,0},{64,10... | collective-permute-start | bytes 393224 | tf_op jit(solution)/shard_map/column_terms/ppermute | solution.py:442
  126.8 10.4 %collective-permute-start.17 = (bf16[2,2,128,128]{3,2,1,0:T(8,128)(2,1)S(1)}, bf16[2,2,128,128]{3,2,1,0:T(8,128)(2,1)S(1)}, u32[]{:S(2)}, u32[]{:S(2)}) collective-permute-start(bf16[2,2,128,128]{3,2,1,0:T(8,128)(2,1)S(1)} %get-tuple-element.85), channel_id=1, source_target_pairs={{0,8},{8,56},{16,0},{24,48},{32,24},{40,40},{48,16},{56,32},{64,72... | collective-permute-start | bytes 393224 | tf_op jit(solution)/shard_map/column_terms/ppermute | solution.py:442
  137.2 15.6 %collective-permute-start.18 = (bf16[2,2,128,128]{3,2,1,0:T(8,128)(2,1)S(1)}, bf16[2,2,128,128]{3,2,1,0:T(8,128)(2,1)S(1)}, u32[]{:S(2)}, u32[]{:S(2)}) collective-permute-start(bf16[2,2,128,128]{3,2,1,0:T(8,128)(2,1)S(1)} %get-tuple-element.86), channel_id=1, source_target_pairs={{0,48},{8,16},{16,40},{24,8},{32,32},{40,0},{48,56},{56,24},{64,11... | collective-permute-start | bytes 393224 | tf_op jit(solution)/shard_map/outputs_home/ppermute | solution.py:442
  143.2 9.6 %collective-permute-start.19 = (bf16[2,2,128,128]{3,2,1,0:T(8,128)(2,1)S(1)}, bf16[2,2,128,128]{3,2,1,0:T(8,128)(2,1)S(1)}, u32[]{:S(2)}, u32[]{:S(2)}) collective-permute-start(bf16[2,2,128,128]{3,2,1,0:T(8,128)(2,1)S(1)} %get-tuple-element.87), channel_id=1, source_target_pairs={{0,16},{8,48},{16,8},{24,40},{32,0},{40,32},{48,24},{56,56},{64,80... | collective-permute-start | bytes 393224 | tf_op jit(solution)/shard_map/outputs_home/ppermute | solution.py:442
  147.0 9.0 %collective-permute-start.20 = (bf16[4,128,128]{2,1,0:T(8,128)(2,1)S(1)}, bf16[4,128,128]{2,1,0:T(8,128)(2,1)S(1)}, u32[]{:S(2)}, u32[]{:S(2)}) collective-permute-start(bf16[4,128,128]{2,1,0:T(8,128)(2,1)S(1)} %get-tuple-element.90), channel_id=1, source_target_pairs={{0,32},{8,0},{16,56},{24,24},{32,48},{40,16},{48,40},{56,8},{64,96... | collective-permute-start | bytes 393224 | tf_op jit(solution)/shard_map/outputs_home/ppermute | solution.py:442
  149.0 9.9 %collective-permute-start.21 = (bf16[4,128,128]{2,1,0:T(8,128)(2,1)S(1)}, bf16[4,128,128]{2,1,0:T(8,128)(2,1)S(1)}, u32[]{:S(2)}, u32[]{:S(2)}) collective-permute-start(bf16[4,128,128]{2,1,0:T(8,128)(2,1)S(1)} %get-tuple-element.91), channel_id=1, source_target_pairs={{0,0},{8,32},{16,24},{24,56},{32,16},{40,48},{48,8},{56,40},{64,64... | collective-permute-start | bytes 393224 | tf_op jit(solution)/shard_map/outputs_home/ppermute | solution.py:442

commit v9 on v6

--- a/solution.py
+++ b/solution.py
@@ -57,6 +57,14 @@
     return route(step)
 
 
+def on_cores(which, turn):
+    pairs = []
+    for group in range(8):
+        for source, target in owner_of(which, (turn + group) % 2):
+            pairs.append((source * 8 + group, target * 8 + group))
+    return pairs
+
+
 def flipped(pairs):
     return [(target, source) for source, target in pairs]
 
@@ -64,6 +72,7 @@
 ROW_STEPS = ((1, 0), (-1, 0))
 COLUMN_STEPS = ((0, 1), (0, -1))
 EARLY = 3
+BOTH = ("tile", "head")
 OWNER_STEPS = tuple((which, turn) for which in range(3) for turn in range(2))
 
 
@@ -79,7 +88,7 @@
     return [pl.BlockSpec(memory_space=pltpu.VMEM)] * count
 
 
-def owner_rows():
+def owner_rows(core):
     rows = []
     for slot in range(SLOTS):
         row, pair = slot // 4, slot % 4
@@ -87,26 +96,27 @@
         for which, turn in OWNER_STEPS:
             if which == 2:
                 unit = 10 * ((pair + 2) % 4) + 4
-            elif (row + turn) % 2:
+            elif (row + turn + core) % 2:
                 unit = 10 * ((pair - 3 * which) % 4) + 8 - 2 * which
             else:
                 unit = 10 * ((pair - which) % 4) + 2 * which
             heads.append(unit // 8)
-        rows.append(heads + [row])
+        rows.append(heads + [(row + core) % 2])
     return rows
 
 
 def place_table():
-    owners = owner_rows()
-    rows = [
-        owners[slot]
-        + [strip, run_at(slot) % 2]
-        + [(5 * run_at(slot) + at) % 8 for at in range(5)]
-        for strip in range(STRIPS)
-        for slot in range(SLOTS)
-    ]
+    rows = []
+    for strip in range(STRIPS):
+        for slot in range(SLOTS):
+            run = run_at(slot)
+            for core in range(2):
+                columns = [(5 * run + at) % 8 for at in range(5)]
+                swap = (run + core) % 2
+                rows.append(owner_rows(core)[slot] + [strip, run % 2] + columns + [swap])
     every = jnp.asarray(np.array(rows, np.int32))
-    return lax.dynamic_index_in_dim(every, lax.axis_index("tile"), 0, keepdims=False)
+    at = lax.axis_index("tile") * 2 + lax.axis_index("head") % 2
+    return lax.dynamic_index_in_dim(every, at, 0, keepdims=False)
 
 
 def spread_kernel(table, upstream, *outs):
@@ -174,26 +184,6 @@
     )(table, *received)
 
 
-def pack_kernel(query, key, value, out):
-    for kind, slab in enumerate((query, key, value)):
-        for group in range(8):
-            for head in range(HEADS_HERE):
-                at = (group * HEADS_HERE + head) * HEAD_DIM
-                lines = slab[0, :, :, at : at + HEAD_DIM]
-                out[group, kind, head] = lines.reshape(32, HEAD_DIM)
-
-
-def pack(query, key, value):
-    return pl.pallas_call(
-        pack_kernel,
-        out_shape=jax.ShapeDtypeStruct((8, 3, HEADS_HERE, 32, HEAD_DIM), LOW),
-        in_specs=whole(3),
-        out_specs=whole(1)[0],
-        compiler_params=pltpu.CompilerParams(vmem_limit_bytes=16 << 20),
-        name="pack",
-    )(query, key, value)
-
-
 def deal_kernel(swapped, out):
     for slot in range(SLOTS):
         for at in range(7):
@@ -226,7 +216,7 @@
 def attend_kernel(table, own, above, below, *refs):
     grads, rest, terms, edges = refs[:6], refs[6], refs[7], refs[8:10]
     pair, turned, outer_turned, grad, total, held = refs[10:]
-    strip, odd = table[7], table[8]
+    strip, odd, swap = table[7], table[8], table[14]
     scaling = HEAD_DIM**-0.5
     rate = scaling * math.log2(math.e)
 
@@ -243,7 +233,7 @@
                 turned[kind, :, lanes] = pair[kind, at, row].T
                 outer_turned[kind, row, :, pl.ds(at * TILE, TILE)] = pair[kind, at, 2 + row].T
     for at, (which, turn) in enumerate(OWNER_STEPS):
-        row = (turn + odd) % 2
+        row = (turn + swap) % 2
         first = first_of(which, odd)
         if which == 2:
             grad[row, first] = grads[at][...]
@@ -348,7 +338,7 @@
     lax.fori_loop(0, 5, one_unit, 0, unroll=True)
     for kind in range(2):
         for turn in range(2):
-            row = (turn + odd) % 2
+            row = (turn + swap) % 2
             for part in range(2):
                 rest[kind, turn, part] = held[kind, row, first_of(0, odd) + part]
                 rest[kind, turn, 2 + part] = held[kind, row, first_of(1, odd) + part]
@@ -392,7 +382,7 @@
 
 
 def rims_kernel(table, rest, terms, above, below, right, left, *outs):
-    odd = table[8]
+    odd, swap = table[8], table[14]
     edges = (above, below)
     for kind in range(2):
         for row, edge in enumerate(edges):
@@ -403,9 +393,9 @@
             at = first_of(1, odd) + part + 1
             for kind in range(2):
                 outs[turn][kind, part] = rest[kind, turn, 2 + part]
-                flip = (turn + odd) % 2 == 1
+                flip = (turn + swap) % 2 == 1
                 edge = jnp.where(flip, below[kind, at], above[kind, at])
-                value = terms[kind, (turn + odd) % 2, at] + edge.astype(WIDE)
+                value = terms[kind, (turn + swap) % 2, at] + edge.astype(WIDE)
                 outs[turn][2 + kind, part] = value.astype(LOW)
 
 
@@ -421,10 +411,10 @@
 
 
 def combine_kernel(table, rest, terms, above, below, before, after, *outs):
-    odd = table[8]
+    odd, swap = table[8], table[14]
     flipped = odd == 1
     for turn in range(2):
-        row = (turn + odd) % 2
+        row = (turn + swap) % 2
         for kind in range(2):
 
             def summed(at):
@@ -455,22 +445,25 @@
     )(table, rest, terms, *edges, *columns)
 
 
-def send_all(parts, routes):
-    return [lax.ppermute(part, "tile", path) for part, path in zip(parts, routes)]
+def send_all(parts, routes, axis="tile"):
+    return [lax.ppermute(part, axis, path) for part, path in zip(parts, routes)]
 
 
 def local(query_slab, key_slab, value_slab, upstream):
     place = place_table()
-    to_owner = [owner_of(which, turn) for which, turn in OWNER_STEPS]
+    to_owner = [on_cores(which, turn) for which, turn in OWNER_STEPS]
     row_routes = [shifted(*step) for step in ROW_STEPS]
     column_routes = [shifted(*step) for step in COLUMN_STEPS]
 
     with jax.named_scope("upstream_to_units"):
-        grads = send_all(spread(place, upstream), [flipped(path) for path in to_owner])
+        grads = send_all(spread(place, upstream), [flipped(path) for path in to_owner], BOTH)
 
     with jax.named_scope("heads"):
-        lines = pack(query_slab, key_slab, value_slab)
-        swapped = lax.all_to_all(lines, "head", 0, 0, tiled=True)
+        lines = [
+            slab.reshape(8, 4, 40, 128).transpose(2, 0, 1, 3).reshape(8, 5, 32, 128)
+            for slab in (query_slab, key_slab, value_slab)
+        ]
+        swapped = lax.all_to_all(jnp.stack(lines, axis=1), "head", 0, 0, tiled=True)
     with jax.named_scope("tiles"):
         dealt, early = lax.optimization_barrier((deal(swapped), grads[:EARLY]))
         got = lax.all_to_all(dealt, "tile", 0, 0, tiled=True)
@@ -486,11 +479,11 @@
     with jax.named_scope("column_terms"):
         right, left, *free = rims(place, rest, terms, edges)
         columns = send_all([right, left], column_routes)
-        free = send_all(free, to_owner[2:4])
+        free = send_all(free, to_owner[2:4], BOTH)
     with jax.named_scope("outputs_home"):
         leaving = combine(place, rest, terms, edges, columns)
         leaving, free = lax.optimization_barrier((leaving, free))
-        late = send_all(leaving, to_owner[:2] + to_owner[4:])
+        late = send_all(leaving, to_owner[:2] + to_owner[4:], BOTH)
     with jax.named_scope("settle"):
         return tuple(gather(place, free + late))
 

time: 159 us -> 158 us (level)
  waiting for transfers between devices: 50 us -> 51.8 us
    ppermute x18, waiting for transfers between devices: 29.3 us -> 32.7 us  [send_all(): return [lax.ppermute(part, axis, path) for part, path in zip(parts, routes)]]
    unnamed x8 -> x6, local copies, waits for them, and re-layouts: 2.91 us -> 0.01 us
    reshape x0 -> x6, local copies, waits for them, and re-layouts: none -> 1.79 us  [local(): slab.reshape(8, 4, 40, 128).transpose(2, 0, 1, 3).reshape(8, 5, 32, 128)]
where the time goes in v9:
time: 158 us; the launch traced here: 156 us
  starting transfers between devices  85.4 us (54%)
  waiting for transfers between devices  51.8 us (33%)
  Pallas kernels  13.8 us (9%)
  local copies, waits for them, and re-layouts  3.23 us (2%)
    ppermute x18, starting transfers between devices, send_all(): return [lax.ppermute(part, axis, path) for part, path in zip(parts, routes)]  70.2 us
    ppermute x18, waiting for transfers between devices, send_all(): return [lax.ppermute(part, axis, path) for part, path in zip(parts, routes)]  32.7 us
    all_to_all x1, waiting for transfers between devices, local(): got = lax.all_to_all(dealt, 'tile', 0, 0, tiled=True)  19.1 us
    all_to_all x1, starting transfers between devices, local(): got = lax.all_to_all(dealt, 'tile', 0, 0, tiled=True)  10.8 us
    pallas_call x1, Pallas kernels, attend(): pl.pallas_call(attend_kernel, out_shape=[jax.ShapeDtypeStruct((2, 2, 5, T...  8.12 us
    all_to_all x1, starting transfers between devices, local(): swapped = lax.all_to_all(jnp.stack(lines, axis=1), 'head', 0, 0, tiled=True)  4.43 us
  transfers between devices with their start and end apart: 20, of which 9 were waited for; matrix products, arithmetic and copies ran while one was open for 1% of the time, Pallas kernels for 2%

profile of v9, /device:TPU:40, one launch (start us, length us, event | category | flops | bytes accessed | tf_op | source)
XLA Modules:
  0.0 156.2 jit_solution(5254901800520062400)
XLA Ops:
  0.7 1.2 reshape.32
  1.8 0.1 copy.9
  2.0 0.1 reshape.34
  2.1 0.1 copy.10
  2.2 0.1 reshape.36
  2.4 0.1 copy.11
  2.5 1.1 pad_maximum_fusion
  3.6 4.4 %all-to-all-start = ((bf16[8,3,5,32,128]{4,3,2,1,0:T(8,128)(2,1)}), bf16[8,3,5,32,128]{4,3,2,1,0:T(8,128)(2,1)S(1)}, u32[]{:S(2)}, u32[]{:S(2)}) async-start(bf16[8,3,5,32,128]{4,3,2,1,0:T(8,128)(2,1)} %pad_maximum_fusion), calls=%async_computation | async-start | bytes 1966080 | tf_op jit(solution)/shard_map/heads/all_to_all | solution.py:466
  8.0 0.7 dynamic-slice_bitcast_fusion.table
  8.7 0.9 spread.1
  9.6 5.2 %collective-permute-start = (bf16[2,128,128]{2,1,0:T(8,128)(2,1)S(1)}, bf16[2,128,128]{2,1,0:T(8,128)(2,1)S(1)}, u32[]{:S(2)}, u32[]{:S(2)}) collective-permute-start(bf16[2,128,128]{2,1,0:T(8,128)(2,1)S(1)} %get-tuple-element.36), channel_id=1, source_target_pairs={{48,0},{16,8},{40,16},{8,24},{32,32},{0,40},{56,48},{24,56},{112,6... | collective-permute-start | bytes 196616 | tf_op jit(solution)/shard_map/upstream_to_units/ppermute | solution.py:449
  14.8 1.9 %collective-permute-start.1 = (bf16[2,128,128]{2,1,0:T(8,128)(2,1)S(1)}, bf16[2,128,128]{2,1,0:T(8,128)(2,1)S(1)}, u32[]{:S(2)}, u32[]{:S(2)}) collective-permute-start(bf16[2,128,128]{2,1,0:T(8,128)(2,1)S(1)} %get-tuple-element.37), channel_id=1, source_target_pairs={{16,0},{48,8},{8,16},{40,24},{0,32},{32,40},{24,48},{56,56},{80,64... | collective-permute-start | bytes 196616 | tf_op jit(solution)/shard_map/upstream_to_units/ppermute | solution.py:449
  16.7 10.0 %collective-permute-start.2 = (bf16[2,128,128]{2,1,0:T(8,128)(2,1)S(1)}, bf16[2,128,128]{2,1,0:T(8,128)(2,1)S(1)}, u32[]{:S(2)}, u32[]{:S(2)}) collective-permute-start(bf16[2,128,128]{2,1,0:T(8,128)(2,1)S(1)} %get-tuple-element.38), channel_id=1, source_target_pairs={{40,0},{24,8},{32,16},{16,24},{56,32},{8,40},{48,48},{0,56},{104,6... | collective-permute-start | bytes 196616 | tf_op jit(solution)/shard_map/upstream_to_units/ppermute | solution.py:449
  26.7 0.0 all-to-all-done.swapped
  26.7 1.2 deal.1
  28.0 0.0 collective-permute-done.refs_0_
  28.0 0.0 collective-permute-done.1.refs_1_
  28.0 0.6 collective-permute-done.2.refs_2_
  28.6 10.8 %all-to-all-start.1 = ((bf16[32,19,8,128]{3,2,1,0:T(8,128)(2,1)}), bf16[32,19,8,128]{3,2,1,0:T(8,128)(2,1)S(1)}, u32[]{:S(2)}, u32[]{:S(2)}) async-start(bf16[32,19,8,128]{3,2,1,0:T(8,128)(2,1)} %deal.1), calls=%async_computation.1 | async-start | bytes 2490368 | tf_op jit(solution)/shard_map/tiles/all_to_all | solution.py:469
  39.4 2.5 %collective-permute-start.3 = (bf16[2,128,128]{2,1,0:T(8,128)(2,1)S(1)}, bf16[2,128,128]{2,1,0:T(8,128)(2,1)S(1)}, u32[]{:S(2)}, u32[]{:S(2)}) collective-permute-start(bf16[2,128,128]{2,1,0:T(8,128)(2,1)S(1)} %get-tuple-element.40), channel_id=1, source_target_pairs={{8,0},{56,8},{0,16},{48,24},{24,32},{40,40},{16,48},{32,56},{72,64... | collective-permute-start | bytes 196616 | tf_op jit(solution)/shard_map/upstream_to_units/ppermute | solution.py:449
  41.9 5.5 %collective-permute-start.4 = (bf16[128,128]{1,0:T(8,128)(2,1)S(1)}, bf16[128,128]{1,0:T(8,128)(2,1)S(1)}, u32[]{:S(2)}, u32[]{:S(2)}) collective-permute-start(bf16[128,128]{1,0:T(8,128)(2,1)S(1)} %get-tuple-element.41), channel_id=1, source_target_pairs={{32,0},{0,8},{56,16},{24,24},{48,32},{16,40},{40,48},{8,56},{96,64... | collective-permute-start | bytes 98312 | tf_op jit(solution)/shard_map/upstream_to_units/ppermute | solution.py:449
  47.3 4.3 %collective-permute-start.5 = (bf16[128,128]{1,0:T(8,128)(2,1)S(1)}, bf16[128,128]{1,0:T(8,128)(2,1)S(1)}, u32[]{:S(2)}, u32[]{:S(2)}) collective-permute-start(bf16[128,128]{1,0:T(8,128)(2,1)S(1)} %get-tuple-element.42), channel_id=1, source_target_pairs={{0,0},{32,8},{24,16},{56,24},{16,32},{48,40},{8,48},{40,56},{64,64... | collective-permute-start | bytes 98312 | tf_op jit(solution)/shard_map/upstream_to_units/ppermute | solution.py:449
  51.6 19.1 %all-to-all-done.1 = bf16[32,19,8,128]{3,2,1,0:T(8,128)(2,1)S(1)} async-done(((bf16[32,19,8,128]{3,2,1,0:T(8,128)(2,1)}), bf16[32,19,8,128]{3,2,1,0:T(8,128)(2,1)S(1)}, u32[]{:S(2)}, u32[]{:S(2)}) %all-to-all-start.1) | async-done | bytes 1245216 | tf_op jit(solution)/shard_map/tiles/all_to_all | solution.py:469
  70.7 0.7 copy.12
  71.4 0.1 slice_bitcast_fusion
  71.5 3.2 %collective-permute-start.7 = (bf16[14,128,128]{2,1,0:T(8,128)(2,1)S(1)}, bf16[14,128,128]{2,1,0:T(8,128)(2,1)S(1)}, u32[]{:S(2)}, u32[]{:S(2)}) collective-permute-start(bf16[14,128,128]{2,1,0:T(8,128)(2,1)S(1)} %get-tuple-element.68), channel_id=1, source_target_pairs={{64,0},{72,8},{80,16},{88,24},{96,32},{104,40},{112,48},{120,56},{... | collective-permute-start | bytes 1376264 | tf_op jit(solution)/shard_map/halos/ppermute | solution.py:449
  74.8 2.6 %collective-permute-start.6 = (bf16[14,128,128]{2,1,0:T(8,128)(2,1)S(1)}, bf16[14,128,128]{2,1,0:T(8,128)(2,1)S(1)}, u32[]{:S(2)}, u32[]{:S(2)}) collective-permute-start(bf16[14,128,128]{2,1,0:T(8,128)(2,1)S(1)} %get-tuple-element.69), channel_id=1, source_target_pairs={{0,64},{8,72},{16,80},{24,88},{32,96},{40,104},{48,112},{56,120},{... | collective-permute-start | bytes 1376264 | tf_op jit(solution)/shard_map/halos/ppermute | solution.py:449
  77.4 6.5 %collective-permute-done.7.below = bf16[14,128,128]{2,1,0:T(8,128)(2,1)S(1)} collective-permute-done((bf16[14,128,128]{2,1,0:T(8,128)(2,1)S(1)}, bf16[14,128,128]{2,1,0:T(8,128)(2,1)S(1)}, u32[]{:S(2)}, u32[]{:S(2)}) %collective-permute-start.7) | collective-permute-done | bytes 458784 | tf_op jit(solution)/shard_map/halos/ppermute | solution.py:449
  83.9 1.9 %collective-permute-done.6.above = bf16[14,128,128]{2,1,0:T(8,128)(2,1)S(1)} collective-permute-done((bf16[14,128,128]{2,1,0:T(8,128)(2,1)S(1)}, bf16[14,128,128]{2,1,0:T(8,128)(2,1)S(1)}, u32[]{:S(2)}, u32[]{:S(2)}) %collective-permute-start.6) | collective-permute-done | bytes 458784 | tf_op jit(solution)/shard_map/halos/ppermute | solution.py:449
  85.8 8.1 %attend.1 = (bf16[2,2,5,128,128]{4,3,2,1,0:T(8,128)(2,1)S(1)}, f32[2,2,7,128,128]{4,3,2,1,0:T(8,128)S(1)}, bf16[2,7,128,128]{3,2,1,0:T(8,128)(2,1)S(1)}, bf16[2,7,128,128]{3,2,1,0:T(8,128)(2,1)S(1)}) custom-call(s32[15]{0:T(128)S(1)} %dynamic-slice_bitcast_fusion.table, bf16[2,19,128,128]{3,2,1,0:T(8,128)(2,1)S(1)} %bitcast.20, ...), custom_call_target="tpu_custom_call" | custom-call | flops 3000000000 | bytes 8000000 | tf_op jit(solution)/shard_map/attention/attend/pallas_call | solution.py:358
  94.0 3.7 %collective-permute-start.8 = (bf16[2,7,128,128]{3,2,1,0:T(8,128)(2,1)S(1)}, bf16[2,7,128,128]{3,2,1,0:T(8,128)(2,1)S(1)}, u32[]{:S(2)}, u32[]{:S(2)}) collective-permute-start(bf16[2,7,128,128]{3,2,1,0:T(8,128)(2,1)S(1)} %get-tuple-element.52), channel_id=1, source_target_pairs={{0,64},{8,72},{16,80},{24,88},{32,96},{40,104},{48,112},{56,120},{... | collective-permute-start | bytes 1376264 | tf_op jit(solution)/shard_map/row_terms/ppermute | solution.py:449
  97.6 2.2 %collective-permute-start.9 = (bf16[2,7,128,128]{3,2,1,0:T(8,128)(2,1)S(1)}, bf16[2,7,128,128]{3,2,1,0:T(8,128)(2,1)S(1)}, u32[]{:S(2)}, u32[]{:S(2)}) collective-permute-start(bf16[2,7,128,128]{3,2,1,0:T(8,128)(2,1)S(1)} %get-tuple-element.53), channel_id=1, source_target_pairs={{64,0},{72,8},{80,16},{88,24},{96,32},{104,40},{112,48},{120,56},{... | collective-permute-start | bytes 1376264 | tf_op jit(solution)/shard_map/row_terms/ppermute | solution.py:449
  99.8 4.6 %collective-permute-done.8.above = bf16[2,7,128,128]{3,2,1,0:T(8,128)(2,1)S(1)} collective-permute-done((bf16[2,7,128,128]{3,2,1,0:T(8,128)(2,1)S(1)}, bf16[2,7,128,128]{3,2,1,0:T(8,128)(2,1)S(1)}, u32[]{:S(2)}, u32[]{:S(2)}) %collective-permute-start.8) | collective-permute-done | bytes 458784 | tf_op jit(solution)/shard_map/row_terms/ppermute | solution.py:449
  104.4 4.1 %collective-permute-done.9.below = bf16[2,7,128,128]{3,2,1,0:T(8,128)(2,1)S(1)} collective-permute-done((bf16[2,7,128,128]{3,2,1,0:T(8,128)(2,1)S(1)}, bf16[2,7,128,128]{3,2,1,0:T(8,128)(2,1)S(1)}, u32[]{:S(2)}, u32[]{:S(2)}) %collective-permute-start.9) | collective-permute-done | bytes 458784 | tf_op jit(solution)/shard_map/row_terms/ppermute | solution.py:449
  108.5 0.7 rims.1
  109.2 2.7 %collective-permute-start.12 = (bf16[4,2,128,128]{3,2,1,0:T(8,128)(2,1)S(1)}, bf16[4,2,128,128]{3,2,1,0:T(8,128)(2,1)S(1)}, u32[]{:S(2)}, u32[]{:S(2)}) collective-permute-start(bf16[4,2,128,128]{3,2,1,0:T(8,128)(2,1)S(1)} %get-tuple-element.60), channel_id=1, source_target_pairs={{0,40},{8,24},{16,32},{24,16},{32,56},{40,8},{48,48},{56,0},{64,10... | collective-permute-start | bytes 786440 | tf_op jit(solution)/shard_map/column_terms/ppermute | solution.py:449
  111.9 4.5 %collective-permute-start.13 = (bf16[4,2,128,128]{3,2,1,0:T(8,128)(2,1)S(1)}, bf16[4,2,128,128]{3,2,1,0:T(8,128)(2,1)S(1)}, u32[]{:S(2)}, u32[]{:S(2)}) collective-permute-start(bf16[4,2,128,128]{3,2,1,0:T(8,128)(2,1)S(1)} %get-tuple-element.61), channel_id=1, source_target_pairs={{0,8},{8,56},{16,0},{24,48},{32,24},{40,40},{48,16},{56,32},{64,72... | collective-permute-start | bytes 786440 | tf_op jit(solution)/shard_map/column_terms/ppermute | solution.py:449
  116.4 3.0 %collective-permute-start.10 = (bf16[2,2,128,128]{3,2,1,0:T(8,128)(2,1)S(1)}, bf16[2,2,128,128]{3,2,1,0:T(8,128)(2,1)S(1)}, u32[]{:S(2)}, u32[]{:S(2)}) collective-permute-start(bf16[2,2,128,128]{3,2,1,0:T(8,128)(2,1)S(1)} %get-tuple-element.54), channel_id=1, source_target_pairs={{0,56},{8,0},{16,8},{24,16},{32,24},{40,32},{56,48},{64,120},{72,6... | collective-permute-start | bytes 393224 | tf_op jit(solution)/shard_map/column_terms/ppermute | solution.py:449
  119.4 3.4 %collective-permute-start.11 = (bf16[2,2,128,128]{3,2,1,0:T(8,128)(2,1)S(1)}, bf16[2,2,128,128]{3,2,1,0:T(8,128)(2,1)S(1)}, u32[]{:S(2)}, u32[]{:S(2)}) collective-permute-start(bf16[2,2,128,128]{3,2,1,0:T(8,128)(2,1)S(1)} %get-tuple-element.55), channel_id=1, source_target_pairs={{0,8},{8,16},{16,24},{24,32},{32,40},{48,56},{56,0},{64,72},{72,80... | collective-permute-start | bytes 393224 | tf_op jit(solution)/shard_map/column_terms/ppermute | solution.py:449
  122.8 5.2 %collective-permute-done.10.before = bf16[2,2,128,128]{3,2,1,0:T(8,128)(2,1)S(1)} collective-permute-done((bf16[2,2,128,128]{3,2,1,0:T(8,128)(2,1)S(1)}, bf16[2,2,128,128]{3,2,1,0:T(8,128)(2,1)S(1)}, u32[]{:S(2)}, u32[]{:S(2)}) %collective-permute-start.10) | collective-permute-done | bytes 131104 | tf_op jit(solution)/shard_map/column_terms/ppermute | solution.py:449
  128.0 2.2 %collective-permute-done.11.after = bf16[2,2,128,128]{3,2,1,0:T(8,128)(2,1)S(1)} collective-permute-done((bf16[2,2,128,128]{3,2,1,0:T(8,128)(2,1)S(1)}, bf16[2,2,128,128]{3,2,1,0:T(8,128)(2,1)S(1)}, u32[]{:S(2)}, u32[]{:S(2)}) %collective-permute-start.11) | collective-permute-done | bytes 131104 | tf_op jit(solution)/shard_map/column_terms/ppermute | solution.py:449
  130.2 0.7 combine.1
  130.9 2.2 %collective-permute-start.14 = (bf16[4,2,128,128]{3,2,1,0:T(8,128)(2,1)S(1)}, bf16[4,2,128,128]{3,2,1,0:T(8,128)(2,1)S(1)}, u32[]{:S(2)}, u32[]{:S(2)}) collective-permute-start(bf16[4,2,128,128]{3,2,1,0:T(8,128)(2,1)S(1)} %get-tuple-element.64), channel_id=1, source_target_pairs={{0,48},{8,16},{16,40},{24,8},{32,32},{40,0},{48,56},{56,24},{64,11... | collective-permute-start | bytes 786440 | tf_op jit(solution)/shard_map/outputs_home/ppermute | solution.py:449
  133.1 2.0 %collective-permute-start.15 = (bf16[4,2,128,128]{3,2,1,0:T(8,128)(2,1)S(1)}, bf16[4,2,128,128]{3,2,1,0:T(8,128)(2,1)S(1)}, u32[]{:S(2)}, u32[]{:S(2)}) collective-permute-start(bf16[4,2,128,128]{3,2,1,0:T(8,128)(2,1)S(1)} %get-tuple-element.65), channel_id=1, source_target_pairs={{0,16},{8,48},{16,8},{24,40},{32,0},{40,32},{48,24},{56,56},{64,80... | collective-permute-start | bytes 786440 | tf_op jit(solution)/shard_map/outputs_home/ppermute | solution.py:449
  135.1 3.3 %collective-permute-start.16 = (bf16[4,128,128]{2,1,0:T(8,128)(2,1)S(1)}, bf16[4,128,128]{2,1,0:T(8,128)(2,1)S(1)}, u32[]{:S(2)}, u32[]{:S(2)}) collective-permute-start(bf16[4,128,128]{2,1,0:T(8,128)(2,1)S(1)} %get-tuple-element.66), channel_id=1, source_target_pairs={{0,32},{8,0},{16,56},{24,24},{32,48},{40,16},{48,40},{56,8},{64,96... | collective-permute-start | bytes 393224 | tf_op jit(solution)/shard_map/outputs_home/ppermute | solution.py:449
  138.4 8.1 %collective-permute-start.17 = (bf16[4,128,128]{2,1,0:T(8,128)(2,1)S(1)}, bf16[4,128,128]{2,1,0:T(8,128)(2,1)S(1)}, u32[]{:S(2)}, u32[]{:S(2)}) collective-permute-start(bf16[4,128,128]{2,1,0:T(8,128)(2,1)S(1)} %get-tuple-element.67), channel_id=1, source_target_pairs={{0,0},{8,32},{16,24},{24,56},{32,16},{40,48},{48,8},{56,40},{64,64... | collective-permute-start | bytes 393224 | tf_op jit(solution)/shard_map/outputs_home/ppermute | solution.py:449
  146.5 7.5 %collective-permute-done.17.refs_5_ = bf16[4,128,128]{2,1,0:T(8,128)(2,1)S(1)} collective-permute-done((bf16[4,128,128]{2,1,0:T(8,128)(2,1)S(1)}, bf16[4,128,128]{2,1,0:T(8,128)(2,1)S(1)}, u32[]{:S(2)}, u32[]{:S(2)}) %collective-permute-start.17) | collective-permute-done | bytes 131104 | tf_op jit(solution)/shard_map/outputs_home/ppermute | solution.py:449
  154.1 2.1 %gather.1 = (bf16[256,640]{1,0:T(8,128)(2,1)}, bf16[256,640]{1,0:T(8,128)(2,1)}, bf16[256,640]{1,0:T(8,128)(2,1)}, bf16[256,640]{1,0:T(8,128)(2,1)}) custom-call(s32[15]{0:T(128)S(1)} %dynamic-slice_bitcast_fusion.table, bf16[4,2,128,128]{3,2,1,0:T(8,128)(2,1)S(1)} %collective-permute-done.12.refs_0_, ...), custom_call_target="tpu_custom_call" | custom-call | tf_op jit(solution)/shard_map/settle/gather/pallas_call | solution.py:177
  (14 shorter events, 0.0 us)
Async XLA Ops:
  0.6 1.3 copy-start.1
  0.6 1.6 %copy-start.2 = (bf16[1,8,4,5120]{3,2,1,0:T(4,128)(2,1)S(1)}, bf16[1,8,4,5120]{3,2,1,0:T(4,128)(2,1)}, u32[]{:S(2)}) copy-start(bf16[1,8,4,5120]{3,2,1,0:T(4,128)(2,1)} %param.7) | copy-start | bytes 983044
  3.6 5.1 %copy-start = (bf16[256,640]{1,0:T(8,128)(2,1)S(1)}, bf16[256,640]{1,0:T(8,128)(2,1)}, u32[]{:S(2)}) copy-start(bf16[256,640]{1,0:T(8,128)(2,1)} %upstream.1) | copy-start | bytes 983044
  3.6 23.1 %all-to-all-start = ((bf16[8,3,5,32,128]{4,3,2,1,0:T(8,128)(2,1)}), bf16[8,3,5,32,128]{4,3,2,1,0:T(8,128)(2,1)S(1)}, u32[]{:S(2)}, u32[]{:S(2)}) async-start(bf16[8,3,5,32,128]{4,3,2,1,0:T(8,128)(2,1)} %pad_maximum_fusion), calls=%async_computation | async-start | bytes 1966080 | tf_op jit(solution)/shard_map/heads/all_to_all | solution.py:466
  9.6 18.3 %collective-permute-start = (bf16[2,128,128]{2,1,0:T(8,128)(2,1)S(1)}, bf16[2,128,128]{2,1,0:T(8,128)(2,1)S(1)}, u32[]{:S(2)}, u32[]{:S(2)}) collective-permute-start(bf16[2,128,128]{2,1,0:T(8,128)(2,1)S(1)} %get-tuple-element.36), channel_id=1, source_target_pairs={{48,0},{16,8},{40,16},{8,24},{32,32},{0,40},{56,48},{24,56},{112,6... | collective-permute-start | bytes 196616 | tf_op jit(solution)/shard_map/upstream_to_units/ppermute | solution.py:449
  14.8 13.2 %collective-permute-start.1 = (bf16[2,128,128]{2,1,0:T(8,128)(2,1)S(1)}, bf16[2,128,128]{2,1,0:T(8,128)(2,1)S(1)}, u32[]{:S(2)}, u32[]{:S(2)}) collective-permute-start(bf16[2,128,128]{2,1,0:T(8,128)(2,1)S(1)} %get-tuple-element.37), channel_id=1, source_target_pairs={{16,0},{48,8},{8,16},{40,24},{0,32},{32,40},{24,48},{56,56},{80,64... | collective-permute-start | bytes 196616 | tf_op jit(solution)/shard_map/upstream_to_units/ppermute | solution.py:449
  16.7 11.9 %collective-permute-start.2 = (bf16[2,128,128]{2,1,0:T(8,128)(2,1)S(1)}, bf16[2,128,128]{2,1,0:T(8,128)(2,1)S(1)}, u32[]{:S(2)}, u32[]{:S(2)}) collective-permute-start(bf16[2,128,128]{2,1,0:T(8,128)(2,1)S(1)} %get-tuple-element.38), channel_id=1, source_target_pairs={{40,0},{24,8},{32,16},{16,24},{56,32},{8,40},{48,48},{0,56},{104,6... | collective-permute-start | bytes 196616 | tf_op jit(solution)/shard_map/upstream_to_units/ppermute | solution.py:449
  28.6 42.1 %all-to-all-start.1 = ((bf16[32,19,8,128]{3,2,1,0:T(8,128)(2,1)}), bf16[32,19,8,128]{3,2,1,0:T(8,128)(2,1)S(1)}, u32[]{:S(2)}, u32[]{:S(2)}) async-start(bf16[32,19,8,128]{3,2,1,0:T(8,128)(2,1)} %deal.1), calls=%async_computation.1 | async-start | bytes 2490368 | tf_op jit(solution)/shard_map/tiles/all_to_all | solution.py:469
  39.4 32.0 %collective-permute-start.3 = (bf16[2,128,128]{2,1,0:T(8,128)(2,1)S(1)}, bf16[2,128,128]{2,1,0:T(8,128)(2,1)S(1)}, u32[]{:S(2)}, u32[]{:S(2)}) collective-permute-start(bf16[2,128,128]{2,1,0:T(8,128)(2,1)S(1)} %get-tuple-element.40), channel_id=1, source_target_pairs={{8,0},{56,8},{0,16},{48,24},{24,32},{40,40},{16,48},{32,56},{72,64... | collective-permute-start | bytes 196616 | tf_op jit(solution)/shard_map/upstream_to_units/ppermute | solution.py:449
  41.9 29.5 %collective-permute-start.4 = (bf16[128,128]{1,0:T(8,128)(2,1)S(1)}, bf16[128,128]{1,0:T(8,128)(2,1)S(1)}, u32[]{:S(2)}, u32[]{:S(2)}) collective-permute-start(bf16[128,128]{1,0:T(8,128)(2,1)S(1)} %get-tuple-element.41), channel_id=1, source_target_pairs={{32,0},{0,8},{56,16},{24,24},{48,32},{16,40},{40,48},{8,56},{96,64... | collective-permute-start | bytes 98312 | tf_op jit(solution)/shard_map/upstream_to_units/ppermute | solution.py:449
  47.3 24.1 %collective-permute-start.5 = (bf16[128,128]{1,0:T(8,128)(2,1)S(1)}, bf16[128,128]{1,0:T(8,128)(2,1)S(1)}, u32[]{:S(2)}, u32[]{:S(2)}) collective-permute-start(bf16[128,128]{1,0:T(8,128)(2,1)S(1)} %get-tuple-element.42), channel_id=1, source_target_pairs={{0,0},{32,8},{24,16},{56,24},{16,32},{48,40},{8,48},{40,56},{64,64... | collective-permute-start | bytes 98312 | tf_op jit(solution)/shard_map/upstream_to_units/ppermute | solution.py:449
  71.5 12.4 %collective-permute-start.7 = (bf16[14,128,128]{2,1,0:T(8,128)(2,1)S(1)}, bf16[14,128,128]{2,1,0:T(8,128)(2,1)S(1)}, u32[]{:S(2)}, u32[]{:S(2)}) collective-permute-start(bf16[14,128,128]{2,1,0:T(8,128)(2,1)S(1)} %get-tuple-element.68), channel_id=1, source_target_pairs={{64,0},{72,8},{80,16},{88,24},{96,32},{104,40},{112,48},{120,56},{... | collective-permute-start | bytes 1376264 | tf_op jit(solution)/shard_map/halos/ppermute | solution.py:449
  74.8 11.1 %collective-permute-start.6 = (bf16[14,128,128]{2,1,0:T(8,128)(2,1)S(1)}, bf16[14,128,128]{2,1,0:T(8,128)(2,1)S(1)}, u32[]{:S(2)}, u32[]{:S(2)}) collective-permute-start(bf16[14,128,128]{2,1,0:T(8,128)(2,1)S(1)} %get-tuple-element.69), channel_id=1, source_target_pairs={{0,64},{8,72},{16,80},{24,88},{32,96},{40,104},{48,112},{56,120},{... | collective-permute-start | bytes 1376264 | tf_op jit(solution)/shard_map/halos/ppermute | solution.py:449
  94.0 10.5 %collective-permute-start.8 = (bf16[2,7,128,128]{3,2,1,0:T(8,128)(2,1)S(1)}, bf16[2,7,128,128]{3,2,1,0:T(8,128)(2,1)S(1)}, u32[]{:S(2)}, u32[]{:S(2)}) collective-permute-start(bf16[2,7,128,128]{3,2,1,0:T(8,128)(2,1)S(1)} %get-tuple-element.52), channel_id=1, source_target_pairs={{0,64},{8,72},{16,80},{24,88},{32,96},{40,104},{48,112},{56,120},{... | collective-permute-start | bytes 1376264 | tf_op jit(solution)/shard_map/row_terms/ppermute | solution.py:449
  97.6 10.9 %collective-permute-start.9 = (bf16[2,7,128,128]{3,2,1,0:T(8,128)(2,1)S(1)}, bf16[2,7,128,128]{3,2,1,0:T(8,128)(2,1)S(1)}, u32[]{:S(2)}, u32[]{:S(2)}) collective-permute-start(bf16[2,7,128,128]{3,2,1,0:T(8,128)(2,1)S(1)} %get-tuple-element.53), channel_id=1, source_target_pairs={{64,0},{72,8},{80,16},{88,24},{96,32},{104,40},{112,48},{120,56},{... | collective-permute-start | bytes 1376264 | tf_op jit(solution)/shard_map/row_terms/ppermute | solution.py:449
  109.2 21.7 %collective-permute-start.12 = (bf16[4,2,128,128]{3,2,1,0:T(8,128)(2,1)S(1)}, bf16[4,2,128,128]{3,2,1,0:T(8,128)(2,1)S(1)}, u32[]{:S(2)}, u32[]{:S(2)}) collective-permute-start(bf16[4,2,128,128]{3,2,1,0:T(8,128)(2,1)S(1)} %get-tuple-element.60), channel_id=1, source_target_pairs={{0,40},{8,24},{16,32},{24,16},{32,56},{40,8},{48,48},{56,0},{64,10... | collective-permute-start | bytes 786440 | tf_op jit(solution)/shard_map/column_terms/ppermute | solution.py:449
  111.9 19.0 %collective-permute-start.13 = (bf16[4,2,128,128]{3,2,1,0:T(8,128)(2,1)S(1)}, bf16[4,2,128,128]{3,2,1,0:T(8,128)(2,1)S(1)}, u32[]{:S(2)}, u32[]{:S(2)}) collective-permute-start(bf16[4,2,128,128]{3,2,1,0:T(8,128)(2,1)S(1)} %get-tuple-element.61), channel_id=1, source_target_pairs={{0,8},{8,56},{16,0},{24,48},{32,24},{40,40},{48,16},{56,32},{64,72... | collective-permute-start | bytes 786440 | tf_op jit(solution)/shard_map/column_terms/ppermute | solution.py:449
  116.4 11.6 %collective-permute-start.10 = (bf16[2,2,128,128]{3,2,1,0:T(8,128)(2,1)S(1)}, bf16[2,2,128,128]{3,2,1,0:T(8,128)(2,1)S(1)}, u32[]{:S(2)}, u32[]{:S(2)}) collective-permute-start(bf16[2,2,128,128]{3,2,1,0:T(8,128)(2,1)S(1)} %get-tuple-element.54), channel_id=1, source_target_pairs={{0,56},{8,0},{16,8},{24,16},{32,24},{40,32},{56,48},{64,120},{72,6... | collective-permute-start | bytes 393224 | tf_op jit(solution)/shard_map/column_terms/ppermute | solution.py:449
  119.4 10.7 %collective-permute-start.11 = (bf16[2,2,128,128]{3,2,1,0:T(8,128)(2,1)S(1)}, bf16[2,2,128,128]{3,2,1,0:T(8,128)(2,1)S(1)}, u32[]{:S(2)}, u32[]{:S(2)}) collective-permute-start(bf16[2,2,128,128]{3,2,1,0:T(8,128)(2,1)S(1)} %get-tuple-element.55), channel_id=1, source_target_pairs={{0,8},{8,16},{16,24},{24,32},{32,40},{48,56},{56,0},{64,72},{72,80... | collective-permute-start | bytes 393224 | tf_op jit(solution)/shard_map/column_terms/ppermute | solution.py:449
  130.9 23.2 %collective-permute-start.14 = (bf16[4,2,128,128]{3,2,1,0:T(8,128)(2,1)S(1)}, bf16[4,2,128,128]{3,2,1,0:T(8,128)(2,1)S(1)}, u32[]{:S(2)}, u32[]{:S(2)}) collective-permute-start(bf16[4,2,128,128]{3,2,1,0:T(8,128)(2,1)S(1)} %get-tuple-element.64), channel_id=1, source_target_pairs={{0,48},{8,16},{16,40},{24,8},{32,32},{40,0},{48,56},{56,24},{64,11... | collective-permute-start | bytes 786440 | tf_op jit(solution)/shard_map/outputs_home/ppermute | solution.py:449
  133.1 20.9 %collective-permute-start.15 = (bf16[4,2,128,128]{3,2,1,0:T(8,128)(2,1)S(1)}, bf16[4,2,128,128]{3,2,1,0:T(8,128)(2,1)S(1)}, u32[]{:S(2)}, u32[]{:S(2)}) collective-permute-start(bf16[4,2,128,128]{3,2,1,0:T(8,128)(2,1)S(1)} %get-tuple-element.65), channel_id=1, source_target_pairs={{0,16},{8,48},{16,8},{24,40},{32,0},{40,32},{48,24},{56,56},{64,80... | collective-permute-start | bytes 786440 | tf_op jit(solution)/shard_map/outputs_home/ppermute | solution.py:449
  135.1 11.4 %collective-permute-start.16 = (bf16[4,128,128]{2,1,0:T(8,128)(2,1)S(1)}, bf16[4,128,128]{2,1,0:T(8,128)(2,1)S(1)}, u32[]{:S(2)}, u32[]{:S(2)}) collective-permute-start(bf16[4,128,128]{2,1,0:T(8,128)(2,1)S(1)} %get-tuple-element.66), channel_id=1, source_target_pairs={{0,32},{8,0},{16,56},{24,24},{32,48},{40,16},{48,40},{56,8},{64,96... | collective-permute-start | bytes 393224 | tf_op jit(solution)/shard_map/outputs_home/ppermute | solution.py:449
  138.4 15.6 %collective-permute-start.17 = (bf16[4,128,128]{2,1,0:T(8,128)(2,1)S(1)}, bf16[4,128,128]{2,1,0:T(8,128)(2,1)S(1)}, u32[]{:S(2)}, u32[]{:S(2)}) collective-permute-start(bf16[4,128,128]{2,1,0:T(8,128)(2,1)S(1)} %get-tuple-element.67), channel_id=1, source_target_pairs={{0,0},{8,32},{16,24},{24,56},{32,16},{40,48},{48,8},{56,40},{64,64... | collective-permute-start | bytes 393224 | tf_op jit(solution)/shard_map/outputs_home/ppermute | solution.py:449

commit v10 on v9

--- a/solution.py
+++ b/solution.py
@@ -65,11 +65,18 @@
     return pairs
 
 
+def rows_on_cores(first):
+    pairs = []
+    for group in range(8):
+        for source, target in shifted(first if group % 2 == 0 else -first, 0):
+            pairs.append((source * 8 + group, target * 8 + group))
+    return pairs
+
+
 def flipped(pairs):
     return [(target, source) for source, target in pairs]
 
 
-ROW_STEPS = ((1, 0), (-1, 0))
 COLUMN_STEPS = ((0, 1), (0, -1))
 EARLY = 3
 BOTH = ("tile", "head")
@@ -113,7 +120,7 @@
             for core in range(2):
                 columns = [(5 * run + at) % 8 for at in range(5)]
                 swap = (run + core) % 2
-                rows.append(owner_rows(core)[slot] + [strip, run % 2] + columns + [swap])
+                rows.append(owner_rows(core)[slot] + [strip, run % 2] + columns + [swap, core])
     every = jnp.asarray(np.array(rows, np.int32))
     at = lax.axis_index("tile") * 2 + lax.axis_index("head") % 2
     return lax.dynamic_index_in_dim(every, at, 0, keepdims=False)
@@ -213,10 +220,10 @@
     return [jax.ShapeDtypeStruct((kinds, 2, TILE, HEAD_DIM), LOW)] * count
 
 
-def attend_kernel(table, own, above, below, *refs):
+def attend_kernel(table, own, one, two, *refs):
     grads, rest, terms, edges = refs[:6], refs[6], refs[7], refs[8:10]
     pair, turned, outer_turned, grad, total, held = refs[10:]
-    strip, odd, swap = table[7], table[8], table[14]
+    strip, odd, swap, core = table[7], table[8], table[14], table[15]
     scaling = HEAD_DIM**-0.5
     rate = scaling * math.log2(math.e)
 
@@ -224,8 +231,8 @@
         for at in range(7):
             for row in range(2):
                 pair[kind, at, row] = own[row, 5 + 7 * kind + at]
-            pair[kind, at, 2] = above[7 * kind + at]
-            pair[kind, at, 3] = below[7 * kind + at]
+            pair[kind, at, 2 + core] = one[7 * kind + at]
+            pair[kind, at, 3 - core] = two[7 * kind + at]
     for kind in range(2):
         for at in range(7):
             for row in range(2):
@@ -347,7 +354,8 @@
         for at in range(7):
             for row in range(2):
                 terms[kind, row, at] = total[kind, at, row] * factor
-                edges[row][kind, at] = (total[kind, at, 3 - row] * factor).astype(LOW)
+            edges[0][kind, at] = (total[kind, at, 3 - core] * factor).astype(LOW)
+            edges[1][kind, at] = (total[kind, at, 2 + core] * factor).astype(LOW)
 
 
 def column_shapes():
@@ -381,20 +389,20 @@
     )(table, own, *halos, *grads)
 
 
-def rims_kernel(table, rest, terms, above, below, right, left, *outs):
-    odd, swap = table[8], table[14]
-    edges = (above, below)
+def rims_kernel(table, rest, terms, first, second, right, left, *outs):
+    odd, swap, core = table[8], table[14], table[15]
     for kind in range(2):
-        for row, edge in enumerate(edges):
+        for row in range(2):
             for out, at in ((right, 6), (left, 0)):
-                out[kind, row] = (terms[kind, row, at] + edge[kind, at].astype(WIDE)).astype(LOW)
+                edge = jnp.where(core == row, first[kind, at], second[kind, at])
+                out[kind, row] = (terms[kind, row, at] + edge.astype(WIDE)).astype(LOW)
     for turn in range(2):
         for part in range(2):
             at = first_of(1, odd) + part + 1
             for kind in range(2):
                 outs[turn][kind, part] = rest[kind, turn, 2 + part]
-                flip = (turn + swap) % 2 == 1
-                edge = jnp.where(flip, below[kind, at], above[kind, at])
+                same = (turn + swap) % 2 == core
+                edge = jnp.where(same, first[kind, at], second[kind, at])
                 value = terms[kind, (turn + swap) % 2, at] + edge.astype(WIDE)
                 outs[turn][2 + kind, part] = value.astype(LOW)
 
@@ -410,15 +418,15 @@
     )(table, rest, terms, *edges)
 
 
-def combine_kernel(table, rest, terms, above, below, before, after, *outs):
-    odd, swap = table[8], table[14]
+def combine_kernel(table, rest, terms, upper, lower, before, after, *outs):
+    odd, swap, core = table[8], table[14], table[15]
     flipped = odd == 1
     for turn in range(2):
         row = (turn + swap) % 2
         for kind in range(2):
 
             def summed(at):
-                edge = jnp.where(row == 1, below[kind, at + 1], above[kind, at + 1])
+                edge = jnp.where(row == core, upper[kind, at + 1], lower[kind, at + 1])
                 return terms[kind, row, at + 1] + edge.astype(WIDE)
 
             first = first_of(0, odd)
@@ -452,7 +460,8 @@
 def local(query_slab, key_slab, value_slab, upstream):
     place = place_table()
     to_owner = [on_cores(which, turn) for which, turn in OWNER_STEPS]
-    row_routes = [shifted(*step) for step in ROW_STEPS]
+    row_routes = [rows_on_cores(first) for first in (1, -1)]
+    core = lax.axis_index("head") % 2
     column_routes = [shifted(*step) for step in COLUMN_STEPS]
 
     with jax.named_scope("upstream_to_units"):
@@ -471,11 +480,13 @@
         own = own.reshape(2, 19, TILE, HEAD_DIM)
         own, late = lax.optimization_barrier((own, grads[EARLY:]))
     with jax.named_scope("halos"):
-        halos = send_all([own[1, 5:], own[0, 5:]], row_routes)
+        pair = own[:, 5:]
+        leaving = [lax.dynamic_index_in_dim(pair, at, 0, keepdims=False) for at in (1 - core, core)]
+        halos = send_all(leaving, row_routes, BOTH)
     with jax.named_scope("attention"):
-        rest, terms, above, below = attend(place, own, halos, early + late)
+        rest, terms, *edges = attend(place, own, halos, early + late)
     with jax.named_scope("row_terms"):
-        edges = send_all([above, below], row_routes)
+        edges = send_all(edges, row_routes, BOTH)
     with jax.named_scope("column_terms"):
         right, left, *free = rims(place, rest, terms, edges)
         columns = send_all([right, left], column_routes)

time: 158 us -> 162 us (1.025)
  waiting for transfers between devices: 51.8 us -> 57.1 us
    ppermute x18, waiting for transfers between devices: 32.7 us -> 38 us  [send_all(): return [lax.ppermute(part, axis, path) for part, path in zip(parts, routes)]]
  transfers between devices with their start and end apart: 20 -> 20, of which waited for: 9 -> 8; matrix products, arithmetic and copies ran while one was open for 1% -> 1% of each run, Pallas kernels for 2% -> 2%
where the time goes in v10:
time: 162 us; the launch traced here: 161 us
  starting transfers between devices  84.2 us (52%)
  waiting for transfers between devices  57.1 us (35%)
  Pallas kernels  13.9 us (9%)
  local copies, waits for them, and re-layouts  3.32 us (2%)
    ppermute x18, starting transfers between devices, send_all(): return [lax.ppermute(part, axis, path) for part, path in zip(parts, routes)]  69 us
    ppermute x18, waiting for transfers between devices, send_all(): return [lax.ppermute(part, axis, path) for part, path in zip(parts, routes)]  38 us
    all_to_all x1, waiting for transfers between devices, local(): got = lax.all_to_all(dealt, 'tile', 0, 0, tiled=True)  19.1 us
    all_to_all x1, starting transfers between devices, local(): got = lax.all_to_all(dealt, 'tile', 0, 0, tiled=True)  10.8 us
    pallas_call x1, Pallas kernels, attend(): pl.pallas_call(attend_kernel, out_shape=[jax.ShapeDtypeStruct((2, 2, 5, T...  8.22 us
    all_to_all x1, starting transfers between devices, local(): swapped = lax.all_to_all(jnp.stack(lines, axis=1), 'head', 0, 0, tiled=True)  4.43 us
  transfers between devices with their start and end apart: 20, of which 8 were waited for; matrix products, arithmetic and copies ran while one was open for 1% of the time, Pallas kernels for 2%

profile of v10, /device:TPU:40, one launch (start us, length us, event | category | flops | bytes accessed | tf_op | source)
XLA Modules:
  0.0 160.6 jit_solution(16495202453554351396)
XLA Ops:
  0.7 1.2 reshape.32
  1.8 0.1 copy.9
  2.0 0.1 reshape.34
  2.1 0.1 copy.10
  2.2 0.1 reshape.36
  2.4 0.1 copy.11
  2.5 1.1 pad_maximum_fusion
  3.6 4.4 %all-to-all-start = ((bf16[8,3,5,32,128]{4,3,2,1,0:T(8,128)(2,1)}), bf16[8,3,5,32,128]{4,3,2,1,0:T(8,128)(2,1)S(1)}, u32[]{:S(2)}, u32[]{:S(2)}) async-start(bf16[8,3,5,32,128]{4,3,2,1,0:T(8,128)(2,1)} %pad_maximum_fusion), calls=%async_computation | async-start | bytes 1966080 | tf_op jit(solution)/shard_map/heads/all_to_all | solution.py:475
  8.0 0.7 fusion.table
  8.7 0.9 spread.1
  9.6 5.2 %collective-permute-start = (bf16[2,128,128]{2,1,0:T(8,128)(2,1)S(1)}, bf16[2,128,128]{2,1,0:T(8,128)(2,1)S(1)}, u32[]{:S(2)}, u32[]{:S(2)}) collective-permute-start(bf16[2,128,128]{2,1,0:T(8,128)(2,1)S(1)} %get-tuple-element.36), channel_id=1, source_target_pairs={{48,0},{16,8},{40,16},{8,24},{32,32},{0,40},{56,48},{24,56},{112,6... | collective-permute-start | bytes 196616 | tf_op jit(solution)/shard_map/upstream_to_units/ppermute | solution.py:457
  14.8 1.9 %collective-permute-start.1 = (bf16[2,128,128]{2,1,0:T(8,128)(2,1)S(1)}, bf16[2,128,128]{2,1,0:T(8,128)(2,1)S(1)}, u32[]{:S(2)}, u32[]{:S(2)}) collective-permute-start(bf16[2,128,128]{2,1,0:T(8,128)(2,1)S(1)} %get-tuple-element.37), channel_id=1, source_target_pairs={{16,0},{48,8},{8,16},{40,24},{0,32},{32,40},{24,48},{56,56},{80,64... | collective-permute-start | bytes 196616 | tf_op jit(solution)/shard_map/upstream_to_units/ppermute | solution.py:457
  16.7 10.0 %collective-permute-start.2 = (bf16[2,128,128]{2,1,0:T(8,128)(2,1)S(1)}, bf16[2,128,128]{2,1,0:T(8,128)(2,1)S(1)}, u32[]{:S(2)}, u32[]{:S(2)}) collective-permute-start(bf16[2,128,128]{2,1,0:T(8,128)(2,1)S(1)} %get-tuple-element.38), channel_id=1, source_target_pairs={{40,0},{24,8},{32,16},{16,24},{56,32},{8,40},{48,48},{0,56},{104,6... | collective-permute-start | bytes 196616 | tf_op jit(solution)/shard_map/upstream_to_units/ppermute | solution.py:457
  26.7 0.0 all-to-all-done.swapped
  26.7 1.2 deal.1
  28.0 0.0 collective-permute-done.refs_0_
  28.0 0.0 collective-permute-done.1.refs_1_
  28.0 0.6 collective-permute-done.2.refs_2_
  28.6 10.8 %all-to-all-start.1 = ((bf16[32,19,8,128]{3,2,1,0:T(8,128)(2,1)}), bf16[32,19,8,128]{3,2,1,0:T(8,128)(2,1)S(1)}, u32[]{:S(2)}, u32[]{:S(2)}) async-start(bf16[32,19,8,128]{3,2,1,0:T(8,128)(2,1)} %deal.1), calls=%async_computation.1 | async-start | bytes 2490368 | tf_op jit(solution)/shard_map/tiles/all_to_all | solution.py:478
  39.4 2.5 %collective-permute-start.3 = (bf16[2,128,128]{2,1,0:T(8,128)(2,1)S(1)}, bf16[2,128,128]{2,1,0:T(8,128)(2,1)S(1)}, u32[]{:S(2)}, u32[]{:S(2)}) collective-permute-start(bf16[2,128,128]{2,1,0:T(8,128)(2,1)S(1)} %get-tuple-element.40), channel_id=1, source_target_pairs={{8,0},{56,8},{0,16},{48,24},{24,32},{40,40},{16,48},{32,56},{72,64... | collective-permute-start | bytes 196616 | tf_op jit(solution)/shard_map/upstream_to_units/ppermute | solution.py:457
  41.9 5.5 %collective-permute-start.4 = (bf16[128,128]{1,0:T(8,128)(2,1)S(1)}, bf16[128,128]{1,0:T(8,128)(2,1)S(1)}, u32[]{:S(2)}, u32[]{:S(2)}) collective-permute-start(bf16[128,128]{1,0:T(8,128)(2,1)S(1)} %get-tuple-element.41), channel_id=1, source_target_pairs={{32,0},{0,8},{56,16},{24,24},{48,32},{16,40},{40,48},{8,56},{96,64... | collective-permute-start | bytes 98312 | tf_op jit(solution)/shard_map/upstream_to_units/ppermute | solution.py:457
  47.3 4.3 %collective-permute-start.5 = (bf16[128,128]{1,0:T(8,128)(2,1)S(1)}, bf16[128,128]{1,0:T(8,128)(2,1)S(1)}, u32[]{:S(2)}, u32[]{:S(2)}) collective-permute-start(bf16[128,128]{1,0:T(8,128)(2,1)S(1)} %get-tuple-element.42), channel_id=1, source_target_pairs={{0,0},{32,8},{24,16},{56,24},{16,32},{48,40},{8,48},{40,56},{64,64... | collective-permute-start | bytes 98312 | tf_op jit(solution)/shard_map/upstream_to_units/ppermute | solution.py:457
  51.6 19.1 %all-to-all-done.1 = bf16[32,19,8,128]{3,2,1,0:T(8,128)(2,1)S(1)} async-done(((bf16[32,19,8,128]{3,2,1,0:T(8,128)(2,1)}), bf16[32,19,8,128]{3,2,1,0:T(8,128)(2,1)S(1)}, u32[]{:S(2)}, u32[]{:S(2)}) %all-to-all-start.1) | async-done | bytes 1245216 | tf_op jit(solution)/shard_map/tiles/all_to_all | solution.py:478
  70.7 0.7 copy.12
  71.4 0.1 slice.3
  71.5 0.1 dynamic-slice_bitcast_fusion
  71.6 3.2 %collective-permute-start.7 = (bf16[14,128,128]{2,1,0:T(8,128)(2,1)S(1)}, bf16[14,128,128]{2,1,0:T(8,128)(2,1)S(1)}, u32[]{:S(2)}, u32[]{:S(2)}) collective-permute-start(bf16[14,128,128]{2,1,0:T(8,128)(2,1)S(1)} %get-tuple-element.68), channel_id=1, source_target_pairs={{64,0},{72,8},{80,16},{88,24},{96,32},{104,40},{112,48},{120,56},{... | collective-permute-start | bytes 1376264 | tf_op jit(solution)/shard_map/halos/ppermute | solution.py:457
  74.9 2.6 %collective-permute-start.6 = (bf16[14,128,128]{2,1,0:T(8,128)(2,1)S(1)}, bf16[14,128,128]{2,1,0:T(8,128)(2,1)S(1)}, u32[]{:S(2)}, u32[]{:S(2)}) collective-permute-start(bf16[14,128,128]{2,1,0:T(8,128)(2,1)S(1)} %get-tuple-element.69), channel_id=1, source_target_pairs={{0,64},{8,72},{16,80},{24,88},{32,96},{40,104},{48,112},{56,120},{... | collective-permute-start | bytes 1376264 | tf_op jit(solution)/shard_map/halos/ppermute | solution.py:457
  77.5 9.4 %collective-permute-done.7.two = bf16[14,128,128]{2,1,0:T(8,128)(2,1)S(1)} collective-permute-done((bf16[14,128,128]{2,1,0:T(8,128)(2,1)S(1)}, bf16[14,128,128]{2,1,0:T(8,128)(2,1)S(1)}, u32[]{:S(2)}, u32[]{:S(2)}) %collective-permute-start.7) | collective-permute-done | bytes 458784 | tf_op jit(solution)/shard_map/halos/ppermute | solution.py:457
  86.9 8.2 %attend.1 = (bf16[2,2,5,128,128]{4,3,2,1,0:T(8,128)(2,1)S(1)}, f32[2,2,7,128,128]{4,3,2,1,0:T(8,128)S(1)}, bf16[2,7,128,128]{3,2,1,0:T(8,128)(2,1)S(1)}, bf16[2,7,128,128]{3,2,1,0:T(8,128)(2,1)S(1)}) custom-call(s32[16]{0:T(128)S(1)} %fusion.table, bf16[2,19,128,128]{3,2,1,0:T(8,128)(2,1)S(1)} %bitcast.20, ...), custom_call_target="tpu_custom_call" | custom-call | flops 3000000000 | bytes 8000000 | tf_op jit(solution)/shard_map/attention/attend/pallas_call | solution.py:366
  95.1 2.8 %collective-permute-start.8 = (bf16[2,7,128,128]{3,2,1,0:T(8,128)(2,1)S(1)}, bf16[2,7,128,128]{3,2,1,0:T(8,128)(2,1)S(1)}, u32[]{:S(2)}, u32[]{:S(2)}) collective-permute-start(bf16[2,7,128,128]{3,2,1,0:T(8,128)(2,1)S(1)} %get-tuple-element.52), channel_id=1, source_target_pairs={{0,64},{8,72},{16,80},{24,88},{32,96},{40,104},{48,112},{56,120},{... | collective-permute-start | bytes 1376264 | tf_op jit(solution)/shard_map/row_terms/ppermute | solution.py:457
  97.9 3.1 %collective-permute-start.9 = (bf16[2,7,128,128]{3,2,1,0:T(8,128)(2,1)S(1)}, bf16[2,7,128,128]{3,2,1,0:T(8,128)(2,1)S(1)}, u32[]{:S(2)}, u32[]{:S(2)}) collective-permute-start(bf16[2,7,128,128]{3,2,1,0:T(8,128)(2,1)S(1)} %get-tuple-element.53), channel_id=1, source_target_pairs={{64,0},{72,8},{80,16},{88,24},{96,32},{104,40},{112,48},{120,56},{... | collective-permute-start | bytes 1376264 | tf_op jit(solution)/shard_map/row_terms/ppermute | solution.py:457
  101.0 8.2 %collective-permute-done.8.first.upper = bf16[2,7,128,128]{3,2,1,0:T(8,128)(2,1)S(1)} collective-permute-done((bf16[2,7,128,128]{3,2,1,0:T(8,128)(2,1)S(1)}, bf16[2,7,128,128]{3,2,1,0:T(8,128)(2,1)S(1)}, u32[]{:S(2)}, u32[]{:S(2)}) %collective-permute-start.8) | collective-permute-done | bytes 458784 | tf_op jit(solution)/shard_map/row_terms/ppermute | solution.py:457
  109.2 0.3 collective-permute-done.9.second.lower
  109.5 0.7 rims.1
  110.2 4.6 %collective-permute-start.12 = (bf16[4,2,128,128]{3,2,1,0:T(8,128)(2,1)S(1)}, bf16[4,2,128,128]{3,2,1,0:T(8,128)(2,1)S(1)}, u32[]{:S(2)}, u32[]{:S(2)}) collective-permute-start(bf16[4,2,128,128]{3,2,1,0:T(8,128)(2,1)S(1)} %get-tuple-element.60), channel_id=1, source_target_pairs={{0,40},{8,24},{16,32},{24,16},{32,56},{40,8},{48,48},{56,0},{64,10... | collective-permute-start | bytes 786440 | tf_op jit(solution)/shard_map/column_terms/ppermute | solution.py:457
  114.8 1.9 %collective-permute-start.13 = (bf16[4,2,128,128]{3,2,1,0:T(8,128)(2,1)S(1)}, bf16[4,2,128,128]{3,2,1,0:T(8,128)(2,1)S(1)}, u32[]{:S(2)}, u32[]{:S(2)}) collective-permute-start(bf16[4,2,128,128]{3,2,1,0:T(8,128)(2,1)S(1)} %get-tuple-element.61), channel_id=1, source_target_pairs={{0,8},{8,56},{16,0},{24,48},{32,24},{40,40},{48,16},{56,32},{64,72... | collective-permute-start | bytes 786440 | tf_op jit(solution)/shard_map/column_terms/ppermute | solution.py:457
  116.7 3.9 %collective-permute-start.10 = (bf16[2,2,128,128]{3,2,1,0:T(8,128)(2,1)S(1)}, bf16[2,2,128,128]{3,2,1,0:T(8,128)(2,1)S(1)}, u32[]{:S(2)}, u32[]{:S(2)}) collective-permute-start(bf16[2,2,128,128]{3,2,1,0:T(8,128)(2,1)S(1)} %get-tuple-element.54), channel_id=1, source_target_pairs={{0,56},{8,0},{16,8},{24,16},{32,24},{40,32},{56,48},{64,120},{72,6... | collective-permute-start | bytes 393224 | tf_op jit(solution)/shard_map/column_terms/ppermute | solution.py:457
  120.7 1.9 %collective-permute-start.11 = (bf16[2,2,128,128]{3,2,1,0:T(8,128)(2,1)S(1)}, bf16[2,2,128,128]{3,2,1,0:T(8,128)(2,1)S(1)}, u32[]{:S(2)}, u32[]{:S(2)}) collective-permute-start(bf16[2,2,128,128]{3,2,1,0:T(8,128)(2,1)S(1)} %get-tuple-element.55), channel_id=1, source_target_pairs={{0,8},{8,16},{16,24},{24,32},{32,40},{48,56},{56,0},{64,72},{72,80... | collective-permute-start | bytes 393224 | tf_op jit(solution)/shard_map/column_terms/ppermute | solution.py:457
  122.6 8.7 %collective-permute-done.10.before = bf16[2,2,128,128]{3,2,1,0:T(8,128)(2,1)S(1)} collective-permute-done((bf16[2,2,128,128]{3,2,1,0:T(8,128)(2,1)S(1)}, bf16[2,2,128,128]{3,2,1,0:T(8,128)(2,1)S(1)}, u32[]{:S(2)}, u32[]{:S(2)}) %collective-permute-start.10) | collective-permute-done | bytes 131104 | tf_op jit(solution)/shard_map/column_terms/ppermute | solution.py:457
  131.3 0.7 combine.1
  132.0 2.6 %collective-permute-start.14 = (bf16[4,2,128,128]{3,2,1,0:T(8,128)(2,1)S(1)}, bf16[4,2,128,128]{3,2,1,0:T(8,128)(2,1)S(1)}, u32[]{:S(2)}, u32[]{:S(2)}) collective-permute-start(bf16[4,2,128,128]{3,2,1,0:T(8,128)(2,1)S(1)} %get-tuple-element.64), channel_id=1, source_target_pairs={{0,48},{8,16},{16,40},{24,8},{32,32},{40,0},{48,56},{56,24},{64,11... | collective-permute-start | bytes 786440 | tf_op jit(solution)/shard_map/outputs_home/ppermute | solution.py:457
  134.7 4.7 %collective-permute-start.15 = (bf16[4,2,128,128]{3,2,1,0:T(8,128)(2,1)S(1)}, bf16[4,2,128,128]{3,2,1,0:T(8,128)(2,1)S(1)}, u32[]{:S(2)}, u32[]{:S(2)}) collective-permute-start(bf16[4,2,128,128]{3,2,1,0:T(8,128)(2,1)S(1)} %get-tuple-element.65), channel_id=1, source_target_pairs={{0,16},{8,48},{16,8},{24,40},{32,0},{40,32},{48,24},{56,56},{64,80... | collective-permute-start | bytes 786440 | tf_op jit(solution)/shard_map/outputs_home/ppermute | solution.py:457
  139.4 1.9 %collective-permute-start.16 = (bf16[4,128,128]{2,1,0:T(8,128)(2,1)S(1)}, bf16[4,128,128]{2,1,0:T(8,128)(2,1)S(1)}, u32[]{:S(2)}, u32[]{:S(2)}) collective-permute-start(bf16[4,128,128]{2,1,0:T(8,128)(2,1)S(1)} %get-tuple-element.66), channel_id=1, source_target_pairs={{0,32},{8,0},{16,56},{24,24},{32,48},{40,16},{48,40},{56,8},{64,96... | collective-permute-start | bytes 393224 | tf_op jit(solution)/shard_map/outputs_home/ppermute | solution.py:457
  141.3 6.4 %collective-permute-start.17 = (bf16[4,128,128]{2,1,0:T(8,128)(2,1)S(1)}, bf16[4,128,128]{2,1,0:T(8,128)(2,1)S(1)}, u32[]{:S(2)}, u32[]{:S(2)}) collective-permute-start(bf16[4,128,128]{2,1,0:T(8,128)(2,1)S(1)} %get-tuple-element.67), channel_id=1, source_target_pairs={{0,0},{8,32},{16,24},{24,56},{32,16},{40,48},{48,8},{56,40},{64,64... | collective-permute-start | bytes 393224 | tf_op jit(solution)/shard_map/outputs_home/ppermute | solution.py:457
  147.7 1.9 %collective-permute-done.16.refs_4_ = bf16[4,128,128]{2,1,0:T(8,128)(2,1)S(1)} collective-permute-done((bf16[4,128,128]{2,1,0:T(8,128)(2,1)S(1)}, bf16[4,128,128]{2,1,0:T(8,128)(2,1)S(1)}, u32[]{:S(2)}, u32[]{:S(2)}) %collective-permute-start.16) | collective-permute-done | bytes 131104 | tf_op jit(solution)/shard_map/outputs_home/ppermute | solution.py:457
  149.6 8.9 %collective-permute-done.17.refs_5_ = bf16[4,128,128]{2,1,0:T(8,128)(2,1)S(1)} collective-permute-done((bf16[4,128,128]{2,1,0:T(8,128)(2,1)S(1)}, bf16[4,128,128]{2,1,0:T(8,128)(2,1)S(1)}, u32[]{:S(2)}, u32[]{:S(2)}) %collective-permute-start.17) | collective-permute-done | bytes 131104 | tf_op jit(solution)/shard_map/outputs_home/ppermute | solution.py:457
  158.5 2.1 %gather.1 = (bf16[256,640]{1,0:T(8,128)(2,1)}, bf16[256,640]{1,0:T(8,128)(2,1)}, bf16[256,640]{1,0:T(8,128)(2,1)}, bf16[256,640]{1,0:T(8,128)(2,1)}) custom-call(s32[16]{0:T(128)S(1)} %fusion.table, bf16[4,2,128,128]{3,2,1,0:T(8,128)(2,1)S(1)} %collective-permute-done.12.refs_0_, bf16[4,2,128,128]{3,2,1,0:T(8,128)(2,1)S(1)} %collective-permute-done.13.refs_1_, ...), custom_call_target="tpu_custom_call" | custom-call | tf_op jit(solution)/shard_map/settle/gather/pallas_call | solution.py:184
  (15 shorter events, 0.0 us)
Async XLA Ops:
  0.6 1.3 copy-start.1
  0.6 1.6 copy-start.2
  3.6 5.1 %copy-start = (bf16[256,640]{1,0:T(8,128)(2,1)S(1)}, bf16[256,640]{1,0:T(8,128)(2,1)}, u32[]{:S(2)}) copy-start(bf16[256,640]{1,0:T(8,128)(2,1)} %upstream.1) | copy-start | bytes 983044
  3.6 23.1 %all-to-all-start = ((bf16[8,3,5,32,128]{4,3,2,1,0:T(8,128)(2,1)}), bf16[8,3,5,32,128]{4,3,2,1,0:T(8,128)(2,1)S(1)}, u32[]{:S(2)}, u32[]{:S(2)}) async-start(bf16[8,3,5,32,128]{4,3,2,1,0:T(8,128)(2,1)} %pad_maximum_fusion), calls=%async_computation | async-start | bytes 1966080 | tf_op jit(solution)/shard_map/heads/all_to_all | solution.py:475
  9.6 18.3 %collective-permute-start = (bf16[2,128,128]{2,1,0:T(8,128)(2,1)S(1)}, bf16[2,128,128]{2,1,0:T(8,128)(2,1)S(1)}, u32[]{:S(2)}, u32[]{:S(2)}) collective-permute-start(bf16[2,128,128]{2,1,0:T(8,128)(2,1)S(1)} %get-tuple-element.36), channel_id=1, source_target_pairs={{48,0},{16,8},{40,16},{8,24},{32,32},{0,40},{56,48},{24,56},{112,6... | collective-permute-start | bytes 196616 | tf_op jit(solution)/shard_map/upstream_to_units/ppermute | solution.py:457
  14.8 13.2 %collective-permute-start.1 = (bf16[2,128,128]{2,1,0:T(8,128)(2,1)S(1)}, bf16[2,128,128]{2,1,0:T(8,128)(2,1)S(1)}, u32[]{:S(2)}, u32[]{:S(2)}) collective-permute-start(bf16[2,128,128]{2,1,0:T(8,128)(2,1)S(1)} %get-tuple-element.37), channel_id=1, source_target_pairs={{16,0},{48,8},{8,16},{40,24},{0,32},{32,40},{24,48},{56,56},{80,64... | collective-permute-start | bytes 196616 | tf_op jit(solution)/shard_map/upstream_to_units/ppermute | solution.py:457
  16.7 11.9 %collective-permute-start.2 = (bf16[2,128,128]{2,1,0:T(8,128)(2,1)S(1)}, bf16[2,128,128]{2,1,0:T(8,128)(2,1)S(1)}, u32[]{:S(2)}, u32[]{:S(2)}) collective-permute-start(bf16[2,128,128]{2,1,0:T(8,128)(2,1)S(1)} %get-tuple-element.38), channel_id=1, source_target_pairs={{40,0},{24,8},{32,16},{16,24},{56,32},{8,40},{48,48},{0,56},{104,6... | collective-permute-start | bytes 196616 | tf_op jit(solution)/shard_map/upstream_to_units/ppermute | solution.py:457
  28.6 42.1 %all-to-all-start.1 = ((bf16[32,19,8,128]{3,2,1,0:T(8,128)(2,1)}), bf16[32,19,8,128]{3,2,1,0:T(8,128)(2,1)S(1)}, u32[]{:S(2)}, u32[]{:S(2)}) async-start(bf16[32,19,8,128]{3,2,1,0:T(8,128)(2,1)} %deal.1), calls=%async_computation.1 | async-start | bytes 2490368 | tf_op jit(solution)/shard_map/tiles/all_to_all | solution.py:478
  39.4 32.0 %collective-permute-start.3 = (bf16[2,128,128]{2,1,0:T(8,128)(2,1)S(1)}, bf16[2,128,128]{2,1,0:T(8,128)(2,1)S(1)}, u32[]{:S(2)}, u32[]{:S(2)}) collective-permute-start(bf16[2,128,128]{2,1,0:T(8,128)(2,1)S(1)} %get-tuple-element.40), channel_id=1, source_target_pairs={{8,0},{56,8},{0,16},{48,24},{24,32},{40,40},{16,48},{32,56},{72,64... | collective-permute-start | bytes 196616 | tf_op jit(solution)/shard_map/upstream_to_units/ppermute | solution.py:457
  41.9 29.5 %collective-permute-start.4 = (bf16[128,128]{1,0:T(8,128)(2,1)S(1)}, bf16[128,128]{1,0:T(8,128)(2,1)S(1)}, u32[]{:S(2)}, u32[]{:S(2)}) collective-permute-start(bf16[128,128]{1,0:T(8,128)(2,1)S(1)} %get-tuple-element.41), channel_id=1, source_target_pairs={{32,0},{0,8},{56,16},{24,24},{48,32},{16,40},{40,48},{8,56},{96,64... | collective-permute-start | bytes 98312 | tf_op jit(solution)/shard_map/upstream_to_units/ppermute | solution.py:457
  47.3 24.1 %collective-permute-start.5 = (bf16[128,128]{1,0:T(8,128)(2,1)S(1)}, bf16[128,128]{1,0:T(8,128)(2,1)S(1)}, u32[]{:S(2)}, u32[]{:S(2)}) collective-permute-start(bf16[128,128]{1,0:T(8,128)(2,1)S(1)} %get-tuple-element.42), channel_id=1, source_target_pairs={{0,0},{32,8},{24,16},{56,24},{16,32},{48,40},{8,48},{40,56},{64,64... | collective-permute-start | bytes 98312 | tf_op jit(solution)/shard_map/upstream_to_units/ppermute | solution.py:457
  71.6 15.3 %collective-permute-start.7 = (bf16[14,128,128]{2,1,0:T(8,128)(2,1)S(1)}, bf16[14,128,128]{2,1,0:T(8,128)(2,1)S(1)}, u32[]{:S(2)}, u32[]{:S(2)}) collective-permute-start(bf16[14,128,128]{2,1,0:T(8,128)(2,1)S(1)} %get-tuple-element.68), channel_id=1, source_target_pairs={{64,0},{72,8},{80,16},{88,24},{96,32},{104,40},{112,48},{120,56},{... | collective-permute-start | bytes 1376264 | tf_op jit(solution)/shard_map/halos/ppermute | solution.py:457
  74.9 12.0 %collective-permute-start.6 = (bf16[14,128,128]{2,1,0:T(8,128)(2,1)S(1)}, bf16[14,128,128]{2,1,0:T(8,128)(2,1)S(1)}, u32[]{:S(2)}, u32[]{:S(2)}) collective-permute-start(bf16[14,128,128]{2,1,0:T(8,128)(2,1)S(1)} %get-tuple-element.69), channel_id=1, source_target_pairs={{0,64},{8,72},{16,80},{24,88},{32,96},{40,104},{48,112},{56,120},{... | collective-permute-start | bytes 1376264 | tf_op jit(solution)/shard_map/halos/ppermute | solution.py:457
  95.1 14.1 %collective-permute-start.8 = (bf16[2,7,128,128]{3,2,1,0:T(8,128)(2,1)S(1)}, bf16[2,7,128,128]{3,2,1,0:T(8,128)(2,1)S(1)}, u32[]{:S(2)}, u32[]{:S(2)}) collective-permute-start(bf16[2,7,128,128]{3,2,1,0:T(8,128)(2,1)S(1)} %get-tuple-element.52), channel_id=1, source_target_pairs={{0,64},{8,72},{16,80},{24,88},{32,96},{40,104},{48,112},{56,120},{... | collective-permute-start | bytes 1376264 | tf_op jit(solution)/shard_map/row_terms/ppermute | solution.py:457
  97.9 11.6 %collective-permute-start.9 = (bf16[2,7,128,128]{3,2,1,0:T(8,128)(2,1)S(1)}, bf16[2,7,128,128]{3,2,1,0:T(8,128)(2,1)S(1)}, u32[]{:S(2)}, u32[]{:S(2)}) collective-permute-start(bf16[2,7,128,128]{3,2,1,0:T(8,128)(2,1)S(1)} %get-tuple-element.53), channel_id=1, source_target_pairs={{64,0},{72,8},{80,16},{88,24},{96,32},{104,40},{112,48},{120,56},{... | collective-permute-start | bytes 1376264 | tf_op jit(solution)/shard_map/row_terms/ppermute | solution.py:457
  110.2 21.8 %collective-permute-start.12 = (bf16[4,2,128,128]{3,2,1,0:T(8,128)(2,1)S(1)}, bf16[4,2,128,128]{3,2,1,0:T(8,128)(2,1)S(1)}, u32[]{:S(2)}, u32[]{:S(2)}) collective-permute-start(bf16[4,2,128,128]{3,2,1,0:T(8,128)(2,1)S(1)} %get-tuple-element.60), channel_id=1, source_target_pairs={{0,40},{8,24},{16,32},{24,16},{32,56},{40,8},{48,48},{56,0},{64,10... | collective-permute-start | bytes 786440 | tf_op jit(solution)/shard_map/column_terms/ppermute | solution.py:457
  114.8 17.2 %collective-permute-start.13 = (bf16[4,2,128,128]{3,2,1,0:T(8,128)(2,1)S(1)}, bf16[4,2,128,128]{3,2,1,0:T(8,128)(2,1)S(1)}, u32[]{:S(2)}, u32[]{:S(2)}) collective-permute-start(bf16[4,2,128,128]{3,2,1,0:T(8,128)(2,1)S(1)} %get-tuple-element.61), channel_id=1, source_target_pairs={{0,8},{8,56},{16,0},{24,48},{32,24},{40,40},{48,16},{56,32},{64,72... | collective-permute-start | bytes 786440 | tf_op jit(solution)/shard_map/column_terms/ppermute | solution.py:457
  116.7 14.5 %collective-permute-start.10 = (bf16[2,2,128,128]{3,2,1,0:T(8,128)(2,1)S(1)}, bf16[2,2,128,128]{3,2,1,0:T(8,128)(2,1)S(1)}, u32[]{:S(2)}, u32[]{:S(2)}) collective-permute-start(bf16[2,2,128,128]{3,2,1,0:T(8,128)(2,1)S(1)} %get-tuple-element.54), channel_id=1, source_target_pairs={{0,56},{8,0},{16,8},{24,16},{32,24},{40,32},{56,48},{64,120},{72,6... | collective-permute-start | bytes 393224 | tf_op jit(solution)/shard_map/column_terms/ppermute | solution.py:457
  120.7 10.6 %collective-permute-start.11 = (bf16[2,2,128,128]{3,2,1,0:T(8,128)(2,1)S(1)}, bf16[2,2,128,128]{3,2,1,0:T(8,128)(2,1)S(1)}, u32[]{:S(2)}, u32[]{:S(2)}) collective-permute-start(bf16[2,2,128,128]{3,2,1,0:T(8,128)(2,1)S(1)} %get-tuple-element.55), channel_id=1, source_target_pairs={{0,8},{8,16},{16,24},{24,32},{32,40},{48,56},{56,0},{64,72},{72,80... | collective-permute-start | bytes 393224 | tf_op jit(solution)/shard_map/column_terms/ppermute | solution.py:457
  132.0 26.5 %collective-permute-start.14 = (bf16[4,2,128,128]{3,2,1,0:T(8,128)(2,1)S(1)}, bf16[4,2,128,128]{3,2,1,0:T(8,128)(2,1)S(1)}, u32[]{:S(2)}, u32[]{:S(2)}) collective-permute-start(bf16[4,2,128,128]{3,2,1,0:T(8,128)(2,1)S(1)} %get-tuple-element.64), channel_id=1, source_target_pairs={{0,48},{8,16},{16,40},{24,8},{32,32},{40,0},{48,56},{56,24},{64,11... | collective-permute-start | bytes 786440 | tf_op jit(solution)/shard_map/outputs_home/ppermute | solution.py:457
  134.7 23.8 %collective-permute-start.15 = (bf16[4,2,128,128]{3,2,1,0:T(8,128)(2,1)S(1)}, bf16[4,2,128,128]{3,2,1,0:T(8,128)(2,1)S(1)}, u32[]{:S(2)}, u32[]{:S(2)}) collective-permute-start(bf16[4,2,128,128]{3,2,1,0:T(8,128)(2,1)S(1)} %get-tuple-element.65), channel_id=1, source_target_pairs={{0,16},{8,48},{16,8},{24,40},{32,0},{40,32},{48,24},{56,56},{64,80... | collective-permute-start | bytes 786440 | tf_op jit(solution)/shard_map/outputs_home/ppermute | solution.py:457
  139.4 10.2 %collective-permute-start.16 = (bf16[4,128,128]{2,1,0:T(8,128)(2,1)S(1)}, bf16[4,128,128]{2,1,0:T(8,128)(2,1)S(1)}, u32[]{:S(2)}, u32[]{:S(2)}) collective-permute-start(bf16[4,128,128]{2,1,0:T(8,128)(2,1)S(1)} %get-tuple-element.66), channel_id=1, source_target_pairs={{0,32},{8,0},{16,56},{24,24},{32,48},{40,16},{48,40},{56,8},{64,96... | collective-permute-start | bytes 393224 | tf_op jit(solution)/shard_map/outputs_home/ppermute | solution.py:457
  141.3 17.2 %collective-permute-start.17 = (bf16[4,128,128]{2,1,0:T(8,128)(2,1)S(1)}, bf16[4,128,128]{2,1,0:T(8,128)(2,1)S(1)}, u32[]{:S(2)}, u32[]{:S(2)}) collective-permute-start(bf16[4,128,128]{2,1,0:T(8,128)(2,1)S(1)} %get-tuple-element.67), channel_id=1, source_target_pairs={{0,0},{8,32},{16,24},{24,56},{32,16},{40,48},{48,8},{56,40},{64,64... | collective-permute-start | bytes 393224 | tf_op jit(solution)/shard_map/outputs_home/ppermute | solution.py:457

commit v11 on v9

--- a/solution.py
+++ b/solution.py
@@ -30,7 +30,7 @@
 
 
 def run_at(slot):
-    return (5 - slot) % SLOTS
+    return slot
 
 
 def shifted(rows, columns):

time: 158 us -> 168 us (1.063)
  the two profiles are of different devices: /device:TPU:40 before, /device:TPU:19 now
where the time goes in v11:
time: 168 us; the launch traced here: 167 us
  waiting for transfers between devices  74.3 us (44%)
  starting transfers between devices  74 us (44%)
  Pallas kernels  13.8 us (8%)
  local copies, waits for them, and re-layouts  3.23 us (2%)
    ppermute x18, starting transfers between devices, send_all(): return [lax.ppermute(part, axis, path) for part, path in zip(parts, routes)]  59.9 us
    ppermute x18, waiting for transfers between devices, send_all(): return [lax.ppermute(part, axis, path) for part, path in zip(parts, routes)]  51.9 us
    all_to_all x1, waiting for transfers between devices, local(): got = lax.all_to_all(dealt, 'tile', 0, 0, tiled=True)  22.3 us
    all_to_all x1, starting transfers between devices, local(): got = lax.all_to_all(dealt, 'tile', 0, 0, tiled=True)  8.78 us
    pallas_call x1, Pallas kernels, attend(): pl.pallas_call(attend_kernel, out_shape=[jax.ShapeDtypeStruct((2, 2, 5, T...  8.11 us
    all_to_all x1, starting transfers between devices, local(): swapped = lax.all_to_all(jnp.stack(lines, axis=1), 'head', 0, 0, tiled=True)  5.28 us
  transfers between devices with their start and end apart: 20, of which 11 were waited for; matrix products, arithmetic and copies ran while one was open for 1% of the time, Pallas kernels for 2%

profile of v11, /device:TPU:19, one launch (start us, length us, event | category | flops | bytes accessed | tf_op | source)
XLA Modules:
  0.0 167.3 jit_solution(5743379369690072159)
XLA Ops:
  0.7 1.2 reshape.32
  1.8 0.1 copy.9
  2.0 0.1 reshape.34
  2.1 0.1 copy.10
  2.2 0.1 reshape.36
  2.4 0.1 copy.11
  2.5 1.1 pad_maximum_fusion
  3.6 5.3 %all-to-all-start = ((bf16[8,3,5,32,128]{4,3,2,1,0:T(8,128)(2,1)}), bf16[8,3,5,32,128]{4,3,2,1,0:T(8,128)(2,1)S(1)}, u32[]{:S(2)}, u32[]{:S(2)}) async-start(bf16[8,3,5,32,128]{4,3,2,1,0:T(8,128)(2,1)} %pad_maximum_fusion), calls=%async_computation | async-start | bytes 1966080 | tf_op jit(solution)/shard_map/heads/all_to_all | solution.py:466
  8.9 0.7 dynamic-slice_bitcast_fusion.table
  9.6 0.9 spread.1
  10.5 3.5 %collective-permute-start = (bf16[2,128,128]{2,1,0:T(8,128)(2,1)S(1)}, bf16[2,128,128]{2,1,0:T(8,128)(2,1)S(1)}, u32[]{:S(2)}, u32[]{:S(2)}) collective-permute-start(bf16[2,128,128]{2,1,0:T(8,128)(2,1)S(1)} %get-tuple-element.36), channel_id=1, source_target_pairs={{0,0},{32,8},{8,16},{40,24},{16,32},{48,40},{24,48},{56,56},{64,64... | collective-permute-start | bytes 196616 | tf_op jit(solution)/shard_map/upstream_to_units/ppermute | solution.py:449
  14.0 0.7 collective-permute-start.1
  14.7 10.8 %collective-permute-start.2 = (bf16[2,128,128]{2,1,0:T(8,128)(2,1)S(1)}, bf16[2,128,128]{2,1,0:T(8,128)(2,1)S(1)}, u32[]{:S(2)}, u32[]{:S(2)}) collective-permute-start(bf16[2,128,128]{2,1,0:T(8,128)(2,1)S(1)} %get-tuple-element.38), channel_id=1, source_target_pairs={{8,0},{56,8},{16,16},{32,24},{24,32},{40,40},{0,48},{48,56},{72,64... | collective-permute-start | bytes 196616 | tf_op jit(solution)/shard_map/upstream_to_units/ppermute | solution.py:449
  25.5 1.2 deal.1
  26.7 0.0 collective-permute-done.refs_0_
  26.7 2.8 %collective-permute-done.2.refs_2_ = bf16[2,128,128]{2,1,0:T(8,128)(2,1)S(1)} collective-permute-done((bf16[2,128,128]{2,1,0:T(8,128)(2,1)S(1)}, bf16[2,128,128]{2,1,0:T(8,128)(2,1)S(1)}, u32[]{:S(2)}, u32[]{:S(2)}) %collective-permute-start.2) | collective-permute-done | bytes 65568 | tf_op jit(solution)/shard_map/upstream_to_units/ppermute | solution.py:449
  29.5 8.8 %all-to-all-start.1 = ((bf16[32,19,8,128]{3,2,1,0:T(8,128)(2,1)}), bf16[32,19,8,128]{3,2,1,0:T(8,128)(2,1)S(1)}, u32[]{:S(2)}, u32[]{:S(2)}) async-start(bf16[32,19,8,128]{3,2,1,0:T(8,128)(2,1)} %deal.1), calls=%async_computation.1 | async-start | bytes 2490368 | tf_op jit(solution)/shard_map/tiles/all_to_all | solution.py:469
  38.3 5.2 %collective-permute-start.3 = (bf16[2,128,128]{2,1,0:T(8,128)(2,1)S(1)}, bf16[2,128,128]{2,1,0:T(8,128)(2,1)S(1)}, u32[]{:S(2)}, u32[]{:S(2)}) collective-permute-start(bf16[2,128,128]{2,1,0:T(8,128)(2,1)S(1)} %get-tuple-element.40), channel_id=1, source_target_pairs={{40,0},{24,8},{48,16},{0,24},{56,32},{8,40},{32,48},{16,56},{104,6... | collective-permute-start | bytes 196616 | tf_op jit(solution)/shard_map/upstream_to_units/ppermute | solution.py:449
  43.5 1.9 %collective-permute-start.4 = (bf16[128,128]{1,0:T(8,128)(2,1)S(1)}, bf16[128,128]{1,0:T(8,128)(2,1)S(1)}, u32[]{:S(2)}, u32[]{:S(2)}) collective-permute-start(bf16[128,128]{1,0:T(8,128)(2,1)S(1)} %get-tuple-element.41), channel_id=1, source_target_pairs={{16,0},{48,8},{24,16},{56,24},{0,32},{32,40},{8,48},{40,56},{80,64... | collective-permute-start | bytes 98312 | tf_op jit(solution)/shard_map/upstream_to_units/ppermute | solution.py:449
  45.5 2.7 %collective-permute-start.5 = (bf16[128,128]{1,0:T(8,128)(2,1)S(1)}, bf16[128,128]{1,0:T(8,128)(2,1)S(1)}, u32[]{:S(2)}, u32[]{:S(2)}) collective-permute-start(bf16[128,128]{1,0:T(8,128)(2,1)S(1)} %get-tuple-element.42), channel_id=1, source_target_pairs={{48,0},{16,8},{56,16},{24,24},{32,32},{0,40},{40,48},{8,56},{112,6... | collective-permute-start | bytes 98312 | tf_op jit(solution)/shard_map/upstream_to_units/ppermute | solution.py:449
  48.2 22.3 %all-to-all-done.1 = bf16[32,19,8,128]{3,2,1,0:T(8,128)(2,1)S(1)} async-done(((bf16[32,19,8,128]{3,2,1,0:T(8,128)(2,1)}), bf16[32,19,8,128]{3,2,1,0:T(8,128)(2,1)S(1)}, u32[]{:S(2)}, u32[]{:S(2)}) %all-to-all-start.1) | async-done | bytes 1245216 | tf_op jit(solution)/shard_map/tiles/all_to_all | solution.py:469
  70.5 0.7 copy.12
  71.2 0.7 collective-permute-done.4.refs_4_
  71.9 0.1 slice_bitcast_fusion
  71.9 2.2 %collective-permute-start.7 = (bf16[14,128,128]{2,1,0:T(8,128)(2,1)S(1)}, bf16[14,128,128]{2,1,0:T(8,128)(2,1)S(1)}, u32[]{:S(2)}, u32[]{:S(2)}) collective-permute-start(bf16[14,128,128]{2,1,0:T(8,128)(2,1)S(1)} %get-tuple-element.68), channel_id=1, source_target_pairs={{64,0},{72,8},{80,16},{88,24},{96,32},{104,40},{112,48},{120,56},{... | collective-permute-start | bytes 1376264 | tf_op jit(solution)/shard_map/halos/ppermute | solution.py:449
  74.1 3.1 %collective-permute-start.6 = (bf16[14,128,128]{2,1,0:T(8,128)(2,1)S(1)}, bf16[14,128,128]{2,1,0:T(8,128)(2,1)S(1)}, u32[]{:S(2)}, u32[]{:S(2)}) collective-permute-start(bf16[14,128,128]{2,1,0:T(8,128)(2,1)S(1)} %get-tuple-element.69), channel_id=1, source_target_pairs={{0,64},{8,72},{16,80},{24,88},{32,96},{40,104},{48,112},{56,120},{... | collective-permute-start | bytes 1376264 | tf_op jit(solution)/shard_map/halos/ppermute | solution.py:449
  77.3 9.0 %collective-permute-done.7.below = bf16[14,128,128]{2,1,0:T(8,128)(2,1)S(1)} collective-permute-done((bf16[14,128,128]{2,1,0:T(8,128)(2,1)S(1)}, bf16[14,128,128]{2,1,0:T(8,128)(2,1)S(1)}, u32[]{:S(2)}, u32[]{:S(2)}) %collective-permute-start.7) | collective-permute-done | bytes 458784 | tf_op jit(solution)/shard_map/halos/ppermute | solution.py:449
  86.3 2.6 %collective-permute-done.6.above = bf16[14,128,128]{2,1,0:T(8,128)(2,1)S(1)} collective-permute-done((bf16[14,128,128]{2,1,0:T(8,128)(2,1)S(1)}, bf16[14,128,128]{2,1,0:T(8,128)(2,1)S(1)}, u32[]{:S(2)}, u32[]{:S(2)}) %collective-permute-start.6) | collective-permute-done | bytes 458784 | tf_op jit(solution)/shard_map/halos/ppermute | solution.py:449
  88.9 8.1 %attend.1 = (bf16[2,2,5,128,128]{4,3,2,1,0:T(8,128)(2,1)S(1)}, f32[2,2,7,128,128]{4,3,2,1,0:T(8,128)S(1)}, bf16[2,7,128,128]{3,2,1,0:T(8,128)(2,1)S(1)}, bf16[2,7,128,128]{3,2,1,0:T(8,128)(2,1)S(1)}) custom-call(s32[15]{0:T(128)S(1)} %dynamic-slice_bitcast_fusion.table, bf16[2,19,128,128]{3,2,1,0:T(8,128)(2,1)S(1)} %bitcast.20, ...), custom_call_target="tpu_custom_call" | custom-call | flops 3000000000 | bytes 8000000 | tf_op jit(solution)/shard_map/attention/attend/pallas_call | solution.py:358
  97.0 2.5 %collective-permute-start.8 = (bf16[2,7,128,128]{3,2,1,0:T(8,128)(2,1)S(1)}, bf16[2,7,128,128]{3,2,1,0:T(8,128)(2,1)S(1)}, u32[]{:S(2)}, u32[]{:S(2)}) collective-permute-start(bf16[2,7,128,128]{3,2,1,0:T(8,128)(2,1)S(1)} %get-tuple-element.52), channel_id=1, source_target_pairs={{0,64},{8,72},{16,80},{24,88},{32,96},{40,104},{48,112},{56,120},{... | collective-permute-start | bytes 1376264 | tf_op jit(solution)/shard_map/row_terms/ppermute | solution.py:449
  99.5 2.8 %collective-permute-start.9 = (bf16[2,7,128,128]{3,2,1,0:T(8,128)(2,1)S(1)}, bf16[2,7,128,128]{3,2,1,0:T(8,128)(2,1)S(1)}, u32[]{:S(2)}, u32[]{:S(2)}) collective-permute-start(bf16[2,7,128,128]{3,2,1,0:T(8,128)(2,1)S(1)} %get-tuple-element.53), channel_id=1, source_target_pairs={{64,0},{72,8},{80,16},{88,24},{96,32},{104,40},{112,48},{120,56},{... | collective-permute-start | bytes 1376264 | tf_op jit(solution)/shard_map/row_terms/ppermute | solution.py:449
  102.3 8.3 %collective-permute-done.8.above = bf16[2,7,128,128]{3,2,1,0:T(8,128)(2,1)S(1)} collective-permute-done((bf16[2,7,128,128]{3,2,1,0:T(8,128)(2,1)S(1)}, bf16[2,7,128,128]{3,2,1,0:T(8,128)(2,1)S(1)}, u32[]{:S(2)}, u32[]{:S(2)}) %collective-permute-start.8) | collective-permute-done | bytes 458784 | tf_op jit(solution)/shard_map/row_terms/ppermute | solution.py:449
  110.6 1.8 %collective-permute-done.9.below = bf16[2,7,128,128]{3,2,1,0:T(8,128)(2,1)S(1)} collective-permute-done((bf16[2,7,128,128]{3,2,1,0:T(8,128)(2,1)S(1)}, bf16[2,7,128,128]{3,2,1,0:T(8,128)(2,1)S(1)}, u32[]{:S(2)}, u32[]{:S(2)}) %collective-permute-start.9) | collective-permute-done | bytes 458784 | tf_op jit(solution)/shard_map/row_terms/ppermute | solution.py:449
  112.5 0.7 rims.1
  113.1 2.2 %collective-permute-start.12 = (bf16[4,2,128,128]{3,2,1,0:T(8,128)(2,1)S(1)}, bf16[4,2,128,128]{3,2,1,0:T(8,128)(2,1)S(1)}, u32[]{:S(2)}, u32[]{:S(2)}) collective-permute-start(bf16[4,2,128,128]{3,2,1,0:T(8,128)(2,1)S(1)} %get-tuple-element.60), channel_id=1, source_target_pairs={{0,8},{8,56},{16,16},{24,32},{32,24},{40,40},{48,0},{56,48},{64,72... | collective-permute-start | bytes 786440 | tf_op jit(solution)/shard_map/column_terms/ppermute | solution.py:449
  115.4 3.2 %collective-permute-start.13 = (bf16[4,2,128,128]{3,2,1,0:T(8,128)(2,1)S(1)}, bf16[4,2,128,128]{3,2,1,0:T(8,128)(2,1)S(1)}, u32[]{:S(2)}, u32[]{:S(2)}) collective-permute-start(bf16[4,2,128,128]{3,2,1,0:T(8,128)(2,1)S(1)} %get-tuple-element.61), channel_id=1, source_target_pairs={{0,40},{8,24},{16,48},{24,0},{32,56},{40,8},{48,32},{56,16},{64,10... | collective-permute-start | bytes 786440 | tf_op jit(solution)/shard_map/column_terms/ppermute | solution.py:449
  118.6 4.7 %collective-permute-start.10 = (bf16[2,2,128,128]{3,2,1,0:T(8,128)(2,1)S(1)}, bf16[2,2,128,128]{3,2,1,0:T(8,128)(2,1)S(1)}, u32[]{:S(2)}, u32[]{:S(2)}) collective-permute-start(bf16[2,2,128,128]{3,2,1,0:T(8,128)(2,1)S(1)} %get-tuple-element.54), channel_id=1, source_target_pairs={{0,8},{8,16},{16,24},{24,32},{32,40},{40,48},{48,56},{64,72},{72,8... | collective-permute-start | bytes 393224 | tf_op jit(solution)/shard_map/column_terms/ppermute | solution.py:449
  123.3 1.3 collective-permute-start.11
  124.6 7.6 %collective-permute-done.10.before = bf16[2,2,128,128]{3,2,1,0:T(8,128)(2,1)S(1)} collective-permute-done((bf16[2,2,128,128]{3,2,1,0:T(8,128)(2,1)S(1)}, bf16[2,2,128,128]{3,2,1,0:T(8,128)(2,1)S(1)}, u32[]{:S(2)}, u32[]{:S(2)}) %collective-permute-start.10) | collective-permute-done | bytes 131104 | tf_op jit(solution)/shard_map/column_terms/ppermute | solution.py:449
  132.2 1.3 collective-permute-done.11.after
  133.5 0.7 combine.1
  134.2 3.3 %collective-permute-start.14 = (bf16[4,2,128,128]{3,2,1,0:T(8,128)(2,1)S(1)}, bf16[4,2,128,128]{3,2,1,0:T(8,128)(2,1)S(1)}, u32[]{:S(2)}, u32[]{:S(2)}) collective-permute-start(bf16[4,2,128,128]{3,2,1,0:T(8,128)(2,1)S(1)} %get-tuple-element.64), channel_id=1, source_target_pairs={{0,0},{8,32},{16,8},{24,40},{32,16},{40,48},{48,24},{56,56},{64,64... | collective-permute-start | bytes 786440 | tf_op jit(solution)/shard_map/outputs_home/ppermute | solution.py:449
  137.6 0.7 collective-permute-start.15
  138.3 7.2 %collective-permute-start.16 = (bf16[4,128,128]{2,1,0:T(8,128)(2,1)S(1)}, bf16[4,128,128]{2,1,0:T(8,128)(2,1)S(1)}, u32[]{:S(2)}, u32[]{:S(2)}) collective-permute-start(bf16[4,128,128]{2,1,0:T(8,128)(2,1)S(1)} %get-tuple-element.66), channel_id=1, source_target_pairs={{0,16},{8,48},{16,24},{24,56},{32,0},{40,32},{48,8},{56,40},{64,80... | collective-permute-start | bytes 393224 | tf_op jit(solution)/shard_map/outputs_home/ppermute | solution.py:449
  145.4 1.9 %collective-permute-start.17 = (bf16[4,128,128]{2,1,0:T(8,128)(2,1)S(1)}, bf16[4,128,128]{2,1,0:T(8,128)(2,1)S(1)}, u32[]{:S(2)}, u32[]{:S(2)}) collective-permute-start(bf16[4,128,128]{2,1,0:T(8,128)(2,1)S(1)} %get-tuple-element.67), channel_id=1, source_target_pairs={{0,48},{8,16},{16,56},{24,24},{32,32},{40,0},{48,40},{56,8},{64,11... | collective-permute-start | bytes 393224 | tf_op jit(solution)/shard_map/outputs_home/ppermute | solution.py:449
  147.3 9.2 %collective-permute-done.16.refs_4_ = bf16[4,128,128]{2,1,0:T(8,128)(2,1)S(1)} collective-permute-done((bf16[4,128,128]{2,1,0:T(8,128)(2,1)S(1)}, bf16[4,128,128]{2,1,0:T(8,128)(2,1)S(1)}, u32[]{:S(2)}, u32[]{:S(2)}) %collective-permute-start.16) | collective-permute-done | bytes 131104 | tf_op jit(solution)/shard_map/outputs_home/ppermute | solution.py:449
  156.6 8.6 %collective-permute-done.17.refs_5_ = bf16[4,128,128]{2,1,0:T(8,128)(2,1)S(1)} collective-permute-done((bf16[4,128,128]{2,1,0:T(8,128)(2,1)S(1)}, bf16[4,128,128]{2,1,0:T(8,128)(2,1)S(1)}, u32[]{:S(2)}, u32[]{:S(2)}) %collective-permute-start.17) | collective-permute-done | bytes 131104 | tf_op jit(solution)/shard_map/outputs_home/ppermute | solution.py:449
  165.2 2.1 %gather.1 = (bf16[256,640]{1,0:T(8,128)(2,1)}, bf16[256,640]{1,0:T(8,128)(2,1)}, bf16[256,640]{1,0:T(8,128)(2,1)}, bf16[256,640]{1,0:T(8,128)(2,1)}) custom-call(s32[15]{0:T(128)S(1)} %dynamic-slice_bitcast_fusion.table, bf16[4,2,128,128]{3,2,1,0:T(8,128)(2,1)S(1)} %collective-permute-done.12.refs_0_, ...), custom_call_target="tpu_custom_call" | custom-call | tf_op jit(solution)/shard_map/settle/gather/pallas_call | solution.py:177
  (14 shorter events, 0.0 us)
Async XLA Ops:
  0.6 1.3 copy-start.1
  0.6 1.6 copy-start.2
  3.6 6.0 %copy-start = (bf16[256,640]{1,0:T(8,128)(2,1)S(1)}, bf16[256,640]{1,0:T(8,128)(2,1)}, u32[]{:S(2)}) copy-start(bf16[256,640]{1,0:T(8,128)(2,1)} %upstream.1) | copy-start | bytes 983044
  3.6 21.9 %all-to-all-start = ((bf16[8,3,5,32,128]{4,3,2,1,0:T(8,128)(2,1)}), bf16[8,3,5,32,128]{4,3,2,1,0:T(8,128)(2,1)S(1)}, u32[]{:S(2)}, u32[]{:S(2)}) async-start(bf16[8,3,5,32,128]{4,3,2,1,0:T(8,128)(2,1)} %pad_maximum_fusion), calls=%async_computation | async-start | bytes 1966080 | tf_op jit(solution)/shard_map/heads/all_to_all | solution.py:466
  10.5 16.3 %collective-permute-start = (bf16[2,128,128]{2,1,0:T(8,128)(2,1)S(1)}, bf16[2,128,128]{2,1,0:T(8,128)(2,1)S(1)}, u32[]{:S(2)}, u32[]{:S(2)}) collective-permute-start(bf16[2,128,128]{2,1,0:T(8,128)(2,1)S(1)} %get-tuple-element.36), channel_id=1, source_target_pairs={{0,0},{32,8},{8,16},{40,24},{16,32},{48,40},{24,48},{56,56},{64,64... | collective-permute-start | bytes 196616 | tf_op jit(solution)/shard_map/upstream_to_units/ppermute | solution.py:449
  14.0 12.7 %collective-permute-start.1 = (bf16[2,128,128]{2,1,0:T(8,128)(2,1)S(1)}, bf16[2,128,128]{2,1,0:T(8,128)(2,1)S(1)}, u32[]{:S(2)}, u32[]{:S(2)}) collective-permute-start(bf16[2,128,128]{2,1,0:T(8,128)(2,1)S(1)} %get-tuple-element.37), channel_id=1, source_target_pairs={{32,0},{0,8},{40,16},{8,24},{48,32},{16,40},{56,48},{24,56},{96,64... | collective-permute-start | bytes 196616 | tf_op jit(solution)/shard_map/upstream_to_units/ppermute | solution.py:449
  14.7 14.8 %collective-permute-start.2 = (bf16[2,128,128]{2,1,0:T(8,128)(2,1)S(1)}, bf16[2,128,128]{2,1,0:T(8,128)(2,1)S(1)}, u32[]{:S(2)}, u32[]{:S(2)}) collective-permute-start(bf16[2,128,128]{2,1,0:T(8,128)(2,1)S(1)} %get-tuple-element.38), channel_id=1, source_target_pairs={{8,0},{56,8},{16,16},{32,24},{24,32},{40,40},{0,48},{48,56},{72,64... | collective-permute-start | bytes 196616 | tf_op jit(solution)/shard_map/upstream_to_units/ppermute | solution.py:449
  29.5 41.0 %all-to-all-start.1 = ((bf16[32,19,8,128]{3,2,1,0:T(8,128)(2,1)}), bf16[32,19,8,128]{3,2,1,0:T(8,128)(2,1)S(1)}, u32[]{:S(2)}, u32[]{:S(2)}) async-start(bf16[32,19,8,128]{3,2,1,0:T(8,128)(2,1)} %deal.1), calls=%async_computation.1 | async-start | bytes 2490368 | tf_op jit(solution)/shard_map/tiles/all_to_all | solution.py:469
  38.3 33.6 %collective-permute-start.3 = (bf16[2,128,128]{2,1,0:T(8,128)(2,1)S(1)}, bf16[2,128,128]{2,1,0:T(8,128)(2,1)S(1)}, u32[]{:S(2)}, u32[]{:S(2)}) collective-permute-start(bf16[2,128,128]{2,1,0:T(8,128)(2,1)S(1)} %get-tuple-element.40), channel_id=1, source_target_pairs={{40,0},{24,8},{48,16},{0,24},{56,32},{8,40},{32,48},{16,56},{104,6... | collective-permute-start | bytes 196616 | tf_op jit(solution)/shard_map/upstream_to_units/ppermute | solution.py:449
  43.5 28.3 %collective-permute-start.4 = (bf16[128,128]{1,0:T(8,128)(2,1)S(1)}, bf16[128,128]{1,0:T(8,128)(2,1)S(1)}, u32[]{:S(2)}, u32[]{:S(2)}) collective-permute-start(bf16[128,128]{1,0:T(8,128)(2,1)S(1)} %get-tuple-element.41), channel_id=1, source_target_pairs={{16,0},{48,8},{24,16},{56,24},{0,32},{32,40},{8,48},{40,56},{80,64... | collective-permute-start | bytes 98312 | tf_op jit(solution)/shard_map/upstream_to_units/ppermute | solution.py:449
  45.5 26.4 %collective-permute-start.5 = (bf16[128,128]{1,0:T(8,128)(2,1)S(1)}, bf16[128,128]{1,0:T(8,128)(2,1)S(1)}, u32[]{:S(2)}, u32[]{:S(2)}) collective-permute-start(bf16[128,128]{1,0:T(8,128)(2,1)S(1)} %get-tuple-element.42), channel_id=1, source_target_pairs={{48,0},{16,8},{56,16},{24,24},{32,32},{0,40},{40,48},{8,56},{112,6... | collective-permute-start | bytes 98312 | tf_op jit(solution)/shard_map/upstream_to_units/ppermute | solution.py:449
  71.9 14.3 %collective-permute-start.7 = (bf16[14,128,128]{2,1,0:T(8,128)(2,1)S(1)}, bf16[14,128,128]{2,1,0:T(8,128)(2,1)S(1)}, u32[]{:S(2)}, u32[]{:S(2)}) collective-permute-start(bf16[14,128,128]{2,1,0:T(8,128)(2,1)S(1)} %get-tuple-element.68), channel_id=1, source_target_pairs={{64,0},{72,8},{80,16},{88,24},{96,32},{104,40},{112,48},{120,56},{... | collective-permute-start | bytes 1376264 | tf_op jit(solution)/shard_map/halos/ppermute | solution.py:449
  74.1 14.8 %collective-permute-start.6 = (bf16[14,128,128]{2,1,0:T(8,128)(2,1)S(1)}, bf16[14,128,128]{2,1,0:T(8,128)(2,1)S(1)}, u32[]{:S(2)}, u32[]{:S(2)}) collective-permute-start(bf16[14,128,128]{2,1,0:T(8,128)(2,1)S(1)} %get-tuple-element.69), channel_id=1, source_target_pairs={{0,64},{8,72},{16,80},{24,88},{32,96},{40,104},{48,112},{56,120},{... | collective-permute-start | bytes 1376264 | tf_op jit(solution)/shard_map/halos/ppermute | solution.py:449
  97.0 13.6 %collective-permute-start.8 = (bf16[2,7,128,128]{3,2,1,0:T(8,128)(2,1)S(1)}, bf16[2,7,128,128]{3,2,1,0:T(8,128)(2,1)S(1)}, u32[]{:S(2)}, u32[]{:S(2)}) collective-permute-start(bf16[2,7,128,128]{3,2,1,0:T(8,128)(2,1)S(1)} %get-tuple-element.52), channel_id=1, source_target_pairs={{0,64},{8,72},{16,80},{24,88},{32,96},{40,104},{48,112},{56,120},{... | collective-permute-start | bytes 1376264 | tf_op jit(solution)/shard_map/row_terms/ppermute | solution.py:449
  99.5 12.9 %collective-permute-start.9 = (bf16[2,7,128,128]{3,2,1,0:T(8,128)(2,1)S(1)}, bf16[2,7,128,128]{3,2,1,0:T(8,128)(2,1)S(1)}, u32[]{:S(2)}, u32[]{:S(2)}) collective-permute-start(bf16[2,7,128,128]{3,2,1,0:T(8,128)(2,1)S(1)} %get-tuple-element.53), channel_id=1, source_target_pairs={{64,0},{72,8},{80,16},{88,24},{96,32},{104,40},{112,48},{120,56},{... | collective-permute-start | bytes 1376264 | tf_op jit(solution)/shard_map/row_terms/ppermute | solution.py:449
  113.1 21.1 %collective-permute-start.12 = (bf16[4,2,128,128]{3,2,1,0:T(8,128)(2,1)S(1)}, bf16[4,2,128,128]{3,2,1,0:T(8,128)(2,1)S(1)}, u32[]{:S(2)}, u32[]{:S(2)}) collective-permute-start(bf16[4,2,128,128]{3,2,1,0:T(8,128)(2,1)S(1)} %get-tuple-element.60), channel_id=1, source_target_pairs={{0,8},{8,56},{16,16},{24,32},{32,24},{40,40},{48,0},{56,48},{64,72... | collective-permute-start | bytes 786440 | tf_op jit(solution)/shard_map/column_terms/ppermute | solution.py:449
  115.4 18.9 %collective-permute-start.13 = (bf16[4,2,128,128]{3,2,1,0:T(8,128)(2,1)S(1)}, bf16[4,2,128,128]{3,2,1,0:T(8,128)(2,1)S(1)}, u32[]{:S(2)}, u32[]{:S(2)}) collective-permute-start(bf16[4,2,128,128]{3,2,1,0:T(8,128)(2,1)S(1)} %get-tuple-element.61), channel_id=1, source_target_pairs={{0,40},{8,24},{16,48},{24,0},{32,56},{40,8},{48,32},{56,16},{64,10... | collective-permute-start | bytes 786440 | tf_op jit(solution)/shard_map/column_terms/ppermute | solution.py:449
  118.6 13.6 %collective-permute-start.10 = (bf16[2,2,128,128]{3,2,1,0:T(8,128)(2,1)S(1)}, bf16[2,2,128,128]{3,2,1,0:T(8,128)(2,1)S(1)}, u32[]{:S(2)}, u32[]{:S(2)}) collective-permute-start(bf16[2,2,128,128]{3,2,1,0:T(8,128)(2,1)S(1)} %get-tuple-element.54), channel_id=1, source_target_pairs={{0,8},{8,16},{16,24},{24,32},{32,40},{40,48},{48,56},{64,72},{72,8... | collective-permute-start | bytes 393224 | tf_op jit(solution)/shard_map/column_terms/ppermute | solution.py:449
  123.3 10.2 %collective-permute-start.11 = (bf16[2,2,128,128]{3,2,1,0:T(8,128)(2,1)S(1)}, bf16[2,2,128,128]{3,2,1,0:T(8,128)(2,1)S(1)}, u32[]{:S(2)}, u32[]{:S(2)}) collective-permute-start(bf16[2,2,128,128]{3,2,1,0:T(8,128)(2,1)S(1)} %get-tuple-element.55), channel_id=1, source_target_pairs={{8,0},{16,8},{24,16},{32,24},{40,32},{48,40},{56,48},{72,64},{80,7... | collective-permute-start | bytes 393224 | tf_op jit(solution)/shard_map/column_terms/ppermute | solution.py:449
  134.2 30.9 %collective-permute-start.14 = (bf16[4,2,128,128]{3,2,1,0:T(8,128)(2,1)S(1)}, bf16[4,2,128,128]{3,2,1,0:T(8,128)(2,1)S(1)}, u32[]{:S(2)}, u32[]{:S(2)}) collective-permute-start(bf16[4,2,128,128]{3,2,1,0:T(8,128)(2,1)S(1)} %get-tuple-element.64), channel_id=1, source_target_pairs={{0,0},{8,32},{16,8},{24,40},{32,16},{40,48},{48,24},{56,56},{64,64... | collective-permute-start | bytes 786440 | tf_op jit(solution)/shard_map/outputs_home/ppermute | solution.py:449
  137.6 27.6 %collective-permute-start.15 = (bf16[4,2,128,128]{3,2,1,0:T(8,128)(2,1)S(1)}, bf16[4,2,128,128]{3,2,1,0:T(8,128)(2,1)S(1)}, u32[]{:S(2)}, u32[]{:S(2)}) collective-permute-start(bf16[4,2,128,128]{3,2,1,0:T(8,128)(2,1)S(1)} %get-tuple-element.65), channel_id=1, source_target_pairs={{0,32},{8,0},{16,40},{24,8},{32,48},{40,16},{48,56},{56,24},{64,96... | collective-permute-start | bytes 786440 | tf_op jit(solution)/shard_map/outputs_home/ppermute | solution.py:449
  138.3 18.3 %collective-permute-start.16 = (bf16[4,128,128]{2,1,0:T(8,128)(2,1)S(1)}, bf16[4,128,128]{2,1,0:T(8,128)(2,1)S(1)}, u32[]{:S(2)}, u32[]{:S(2)}) collective-permute-start(bf16[4,128,128]{2,1,0:T(8,128)(2,1)S(1)} %get-tuple-element.66), channel_id=1, source_target_pairs={{0,16},{8,48},{16,24},{24,56},{32,0},{40,32},{48,8},{56,40},{64,80... | collective-permute-start | bytes 393224 | tf_op jit(solution)/shard_map/outputs_home/ppermute | solution.py:449
  145.4 19.7 %collective-permute-start.17 = (bf16[4,128,128]{2,1,0:T(8,128)(2,1)S(1)}, bf16[4,128,128]{2,1,0:T(8,128)(2,1)S(1)}, u32[]{:S(2)}, u32[]{:S(2)}) collective-permute-start(bf16[4,128,128]{2,1,0:T(8,128)(2,1)S(1)} %get-tuple-element.67), channel_id=1, source_target_pairs={{0,48},{8,16},{16,56},{24,24},{32,32},{40,0},{48,40},{56,8},{64,11... | collective-permute-start | bytes 393224 | tf_op jit(solution)/shard_map/outputs_home/ppermute | solution.py:449

commit v12 on v6

--- a/solution.py
+++ b/solution.py
@@ -172,26 +172,6 @@
         compiler_params=pltpu.CompilerParams(vmem_limit_bytes=16 << 20),
         name="gather",
     )(table, *received)
-
-
-def pack_kernel(query, key, value, out):
-    for kind, slab in enumerate((query, key, value)):
-        for group in range(8):
-            for head in range(HEADS_HERE):
-                at = (group * HEADS_HERE + head) * HEAD_DIM
-                lines = slab[0, :, :, at : at + HEAD_DIM]
-                out[group, kind, head] = lines.reshape(32, HEAD_DIM)
-
-
-def pack(query, key, value):
-    return pl.pallas_call(
-        pack_kernel,
-        out_shape=jax.ShapeDtypeStruct((8, 3, HEADS_HERE, 32, HEAD_DIM), LOW),
-        in_specs=whole(3),
-        out_specs=whole(1)[0],
-        compiler_params=pltpu.CompilerParams(vmem_limit_bytes=16 << 20),
-        name="pack",
-    )(query, key, value)
 
 
 def deal_kernel(swapped, out):
@@ -469,8 +449,11 @@
         grads = send_all(spread(place, upstream), [flipped(path) for path in to_owner])
 
     with jax.named_scope("heads"):
-        lines = pack(query_slab, key_slab, value_slab)
-        swapped = lax.all_to_all(lines, "head", 0, 0, tiled=True)
+        lines = [
+            slab.reshape(8, 4, 40, 128).transpose(2, 0, 1, 3).reshape(8, 5, 32, 128)
+            for slab in (query_slab, key_slab, value_slab)
+        ]
+        swapped = lax.all_to_all(jnp.stack(lines, axis=1), "head", 0, 0, tiled=True)
     with jax.named_scope("tiles"):
         dealt, early = lax.optimization_barrier((deal(swapped), grads[:EARLY]))
         got = lax.all_to_all(dealt, "tile", 0, 0, tiled=True)

time: 159 us -> 157 us (0.987)
    unnamed x8 -> x6, local copies, waits for them, and re-layouts: 2.91 us -> 0.01 us
    reshape x0 -> x6, local copies, waits for them, and re-layouts: none -> 1.79 us  [local(): slab.reshape(8, 4, 40, 128).transpose(2, 0, 1, 3).reshape(8, 5, 32, 128)]
where the time goes in v12:
time: 157 us; the launch traced here: 156 us
  starting transfers between devices  86.9 us (55%)
  waiting for transfers between devices  50 us (32%)
  Pallas kernels  13.8 us (9%)
  local copies, waits for them, and re-layouts  3.23 us (2%)
    ppermute x18, starting transfers between devices, send_all(): lax.ppermute(part, 'tile', path)  71.7 us
    ppermute x18, waiting for transfers between devices, send_all(): lax.ppermute(part, 'tile', path)  29.3 us
    all_to_all x1, waiting for transfers between devices, local(): got = lax.all_to_all(dealt, 'tile', 0, 0, tiled=True)  20.6 us
    all_to_all x1, starting transfers between devices, local(): got = lax.all_to_all(dealt, 'tile', 0, 0, tiled=True)  10.8 us
    pallas_call x1, Pallas kernels, attend(): pl.pallas_call(attend_kernel, out_shape=[jax.ShapeDtypeStruct((2, 2, 5, T...  8.12 us
    all_to_all x1, starting transfers between devices, local(): swapped = lax.all_to_all(jnp.stack(lines, axis=1), 'head', 0, 0, tiled=True)  4.43 us
  transfers between devices with their start and end apart: 20, of which 9 were waited for; matrix products, arithmetic and copies ran while one was open for 1% of the time, Pallas kernels for 2%

profile of v12, /device:TPU:40, one launch (start us, length us, event | category | flops | bytes accessed | tf_op | source)
XLA Modules:
  0.0 156.0 jit_solution(1021452190775596880)
XLA Ops:
  0.7 1.2 reshape.32
  1.8 0.1 copy.9
  2.0 0.1 reshape.34
  2.1 0.1 copy.10
  2.2 0.1 reshape.36
  2.4 0.1 copy.11
  2.5 1.1 pad_maximum_fusion
  3.6 4.4 %all-to-all-start = ((bf16[8,3,5,32,128]{4,3,2,1,0:T(8,128)(2,1)}), bf16[8,3,5,32,128]{4,3,2,1,0:T(8,128)(2,1)S(1)}, u32[]{:S(2)}, u32[]{:S(2)}) async-start(bf16[8,3,5,32,128]{4,3,2,1,0:T(8,128)(2,1)} %pad_maximum_fusion), calls=%async_computation | async-start | bytes 1966080 | tf_op jit(solution)/shard_map/heads/all_to_all | solution.py:456
  8.0 0.7 dynamic-slice_bitcast_fusion.table
  8.7 0.9 spread.1
  9.6 5.2 %collective-permute-start = (bf16[2,128,128]{2,1,0:T(8,128)(2,1)S(1)}, bf16[2,128,128]{2,1,0:T(8,128)(2,1)S(1)}, u32[]{:S(2)}, u32[]{:S(2)}) collective-permute-start(bf16[2,128,128]{2,1,0:T(8,128)(2,1)S(1)} %get-tuple-element.36), channel_id=1, source_target_pairs={{48,0},{16,8},{40,16},{8,24},{32,32},{0,40},{56,48},{24,56},{112,6... | collective-permute-start | bytes 196616 | tf_op jit(solution)/shard_map/upstream_to_units/ppermute | solution.py:439
  14.8 1.9 %collective-permute-start.1 = (bf16[2,128,128]{2,1,0:T(8,128)(2,1)S(1)}, bf16[2,128,128]{2,1,0:T(8,128)(2,1)S(1)}, u32[]{:S(2)}, u32[]{:S(2)}) collective-permute-start(bf16[2,128,128]{2,1,0:T(8,128)(2,1)S(1)} %get-tuple-element.37), channel_id=1, source_target_pairs={{16,0},{48,8},{8,16},{40,24},{0,32},{32,40},{24,48},{56,56},{80,64... | collective-permute-start | bytes 196616 | tf_op jit(solution)/shard_map/upstream_to_units/ppermute | solution.py:439
  16.7 10.0 %collective-permute-start.2 = (bf16[2,128,128]{2,1,0:T(8,128)(2,1)S(1)}, bf16[2,128,128]{2,1,0:T(8,128)(2,1)S(1)}, u32[]{:S(2)}, u32[]{:S(2)}) collective-permute-start(bf16[2,128,128]{2,1,0:T(8,128)(2,1)S(1)} %get-tuple-element.38), channel_id=1, source_target_pairs={{40,0},{24,8},{32,16},{16,24},{56,32},{8,40},{48,48},{0,56},{104,6... | collective-permute-start | bytes 196616 | tf_op jit(solution)/shard_map/upstream_to_units/ppermute | solution.py:439
  26.7 0.0 all-to-all-done.swapped
  26.7 1.2 deal.1
  28.0 0.0 collective-permute-done.refs_0_
  28.0 0.0 collective-permute-done.1.refs_1_
  28.0 0.6 collective-permute-done.2.refs_2_
  28.6 10.8 %all-to-all-start.1 = ((bf16[32,19,8,128]{3,2,1,0:T(8,128)(2,1)}), bf16[32,19,8,128]{3,2,1,0:T(8,128)(2,1)S(1)}, u32[]{:S(2)}, u32[]{:S(2)}) async-start(bf16[32,19,8,128]{3,2,1,0:T(8,128)(2,1)} %deal.1), calls=%async_computation.1 | async-start | bytes 2490368 | tf_op jit(solution)/shard_map/tiles/all_to_all | solution.py:459
  39.4 2.5 %collective-permute-start.3 = (bf16[2,128,128]{2,1,0:T(8,128)(2,1)S(1)}, bf16[2,128,128]{2,1,0:T(8,128)(2,1)S(1)}, u32[]{:S(2)}, u32[]{:S(2)}) collective-permute-start(bf16[2,128,128]{2,1,0:T(8,128)(2,1)S(1)} %get-tuple-element.40), channel_id=1, source_target_pairs={{8,0},{56,8},{0,16},{48,24},{24,32},{40,40},{16,48},{32,56},{72,64... | collective-permute-start | bytes 196616 | tf_op jit(solution)/shard_map/upstream_to_units/ppermute | solution.py:439
  41.9 5.5 %collective-permute-start.4 = (bf16[128,128]{1,0:T(8,128)(2,1)S(1)}, bf16[128,128]{1,0:T(8,128)(2,1)S(1)}, u32[]{:S(2)}, u32[]{:S(2)}) collective-permute-start(bf16[128,128]{1,0:T(8,128)(2,1)S(1)} %get-tuple-element.41), channel_id=1, source_target_pairs={{32,0},{0,8},{56,16},{24,24},{48,32},{16,40},{40,48},{8,56},{96,64... | collective-permute-start | bytes 98312 | tf_op jit(solution)/shard_map/upstream_to_units/ppermute | solution.py:439
  47.3 4.3 %collective-permute-start.5 = (bf16[128,128]{1,0:T(8,128)(2,1)S(1)}, bf16[128,128]{1,0:T(8,128)(2,1)S(1)}, u32[]{:S(2)}, u32[]{:S(2)}) collective-permute-start(bf16[128,128]{1,0:T(8,128)(2,1)S(1)} %get-tuple-element.42), channel_id=1, source_target_pairs={{0,0},{32,8},{24,16},{56,24},{16,32},{48,40},{8,48},{40,56},{64,64... | collective-permute-start | bytes 98312 | tf_op jit(solution)/shard_map/upstream_to_units/ppermute | solution.py:439
  51.6 20.6 %all-to-all-done.1 = bf16[32,19,8,128]{3,2,1,0:T(8,128)(2,1)S(1)} async-done(((bf16[32,19,8,128]{3,2,1,0:T(8,128)(2,1)}), bf16[32,19,8,128]{3,2,1,0:T(8,128)(2,1)S(1)}, u32[]{:S(2)}, u32[]{:S(2)}) %all-to-all-start.1) | async-done | bytes 1245216 | tf_op jit(solution)/shard_map/tiles/all_to_all | solution.py:459
  72.3 0.7 copy.12
  73.0 0.1 slice_bitcast_fusion
  73.0 2.5 %collective-permute-start.7 = (bf16[14,128,128]{2,1,0:T(8,128)(2,1)S(1)}, bf16[14,128,128]{2,1,0:T(8,128)(2,1)S(1)}, u32[]{:S(2)}, u32[]{:S(2)}) collective-permute-start(bf16[14,128,128]{2,1,0:T(8,128)(2,1)S(1)} %get-tuple-element.68), channel_id=1, source_target_pairs={{64,0},{72,8},{80,16},{88,24},{96,32},{104,40},{112,48},{120,56},{... | collective-permute-start | bytes 1376264 | tf_op jit(solution)/shard_map/halos/ppermute | solution.py:439
  75.5 3.4 %collective-permute-start.6 = (bf16[14,128,128]{2,1,0:T(8,128)(2,1)S(1)}, bf16[14,128,128]{2,1,0:T(8,128)(2,1)S(1)}, u32[]{:S(2)}, u32[]{:S(2)}) collective-permute-start(bf16[14,128,128]{2,1,0:T(8,128)(2,1)S(1)} %get-tuple-element.69), channel_id=1, source_target_pairs={{0,64},{8,72},{16,80},{24,88},{32,96},{40,104},{48,112},{56,120},{... | collective-permute-start | bytes 1376264 | tf_op jit(solution)/shard_map/halos/ppermute | solution.py:439
  78.9 4.5 %collective-permute-done.7.below = bf16[14,128,128]{2,1,0:T(8,128)(2,1)S(1)} collective-permute-done((bf16[14,128,128]{2,1,0:T(8,128)(2,1)S(1)}, bf16[14,128,128]{2,1,0:T(8,128)(2,1)S(1)}, u32[]{:S(2)}, u32[]{:S(2)}) %collective-permute-start.7) | collective-permute-done | bytes 458784 | tf_op jit(solution)/shard_map/halos/ppermute | solution.py:439
  83.4 2.5 %collective-permute-done.6.above = bf16[14,128,128]{2,1,0:T(8,128)(2,1)S(1)} collective-permute-done((bf16[14,128,128]{2,1,0:T(8,128)(2,1)S(1)}, bf16[14,128,128]{2,1,0:T(8,128)(2,1)S(1)}, u32[]{:S(2)}, u32[]{:S(2)}) %collective-permute-start.6) | collective-permute-done | bytes 458784 | tf_op jit(solution)/shard_map/halos/ppermute | solution.py:439
  85.9 8.1 %attend.1 = (bf16[2,2,5,128,128]{4,3,2,1,0:T(8,128)(2,1)S(1)}, f32[2,2,7,128,128]{4,3,2,1,0:T(8,128)S(1)}, bf16[2,7,128,128]{3,2,1,0:T(8,128)(2,1)S(1)}, bf16[2,7,128,128]{3,2,1,0:T(8,128)(2,1)S(1)}) custom-call(s32[14]{0:T(128)S(1)} %dynamic-slice_bitcast_fusion.table, bf16[2,19,128,128]{3,2,1,0:T(8,128)(2,1)S(1)} %bitcast.20, ...), custom_call_target="tpu_custom_call" | custom-call | flops 3000000000 | bytes 8000000 | tf_op jit(solution)/shard_map/attention/attend/pallas_call | solution.py:348
  94.0 3.4 %collective-permute-start.8 = (bf16[2,7,128,128]{3,2,1,0:T(8,128)(2,1)S(1)}, bf16[2,7,128,128]{3,2,1,0:T(8,128)(2,1)S(1)}, u32[]{:S(2)}, u32[]{:S(2)}) collective-permute-start(bf16[2,7,128,128]{3,2,1,0:T(8,128)(2,1)S(1)} %get-tuple-element.52), channel_id=1, source_target_pairs={{0,64},{8,72},{16,80},{24,88},{32,96},{40,104},{48,112},{56,120},{... | collective-permute-start | bytes 1376264 | tf_op jit(solution)/shard_map/row_terms/ppermute | solution.py:439
  97.4 2.5 %collective-permute-start.9 = (bf16[2,7,128,128]{3,2,1,0:T(8,128)(2,1)S(1)}, bf16[2,7,128,128]{3,2,1,0:T(8,128)(2,1)S(1)}, u32[]{:S(2)}, u32[]{:S(2)}) collective-permute-start(bf16[2,7,128,128]{3,2,1,0:T(8,128)(2,1)S(1)} %get-tuple-element.53), channel_id=1, source_target_pairs={{64,0},{72,8},{80,16},{88,24},{96,32},{104,40},{112,48},{120,56},{... | collective-permute-start | bytes 1376264 | tf_op jit(solution)/shard_map/row_terms/ppermute | solution.py:439
  99.9 4.5 %collective-permute-done.8.above = bf16[2,7,128,128]{3,2,1,0:T(8,128)(2,1)S(1)} collective-permute-done((bf16[2,7,128,128]{3,2,1,0:T(8,128)(2,1)S(1)}, bf16[2,7,128,128]{3,2,1,0:T(8,128)(2,1)S(1)}, u32[]{:S(2)}, u32[]{:S(2)}) %collective-permute-start.8) | collective-permute-done | bytes 458784 | tf_op jit(solution)/shard_map/row_terms/ppermute | solution.py:439
  104.4 3.4 %collective-permute-done.9.below = bf16[2,7,128,128]{3,2,1,0:T(8,128)(2,1)S(1)} collective-permute-done((bf16[2,7,128,128]{3,2,1,0:T(8,128)(2,1)S(1)}, bf16[2,7,128,128]{3,2,1,0:T(8,128)(2,1)S(1)}, u32[]{:S(2)}, u32[]{:S(2)}) %collective-permute-start.9) | collective-permute-done | bytes 458784 | tf_op jit(solution)/shard_map/row_terms/ppermute | solution.py:439
  107.8 0.7 rims.1
  108.5 4.2 %collective-permute-start.12 = (bf16[4,2,128,128]{3,2,1,0:T(8,128)(2,1)S(1)}, bf16[4,2,128,128]{3,2,1,0:T(8,128)(2,1)S(1)}, u32[]{:S(2)}, u32[]{:S(2)}) collective-permute-start(bf16[4,2,128,128]{3,2,1,0:T(8,128)(2,1)S(1)} %get-tuple-element.60), channel_id=1, source_target_pairs={{0,40},{8,24},{16,32},{24,16},{32,56},{40,8},{48,48},{56,0},{64,10... | collective-permute-start | bytes 786440 | tf_op jit(solution)/shard_map/column_terms/ppermute | solution.py:439
  112.6 5.1 %collective-permute-start.13 = (bf16[4,2,128,128]{3,2,1,0:T(8,128)(2,1)S(1)}, bf16[4,2,128,128]{3,2,1,0:T(8,128)(2,1)S(1)}, u32[]{:S(2)}, u32[]{:S(2)}) collective-permute-start(bf16[4,2,128,128]{3,2,1,0:T(8,128)(2,1)S(1)} %get-tuple-element.61), channel_id=1, source_target_pairs={{0,8},{8,56},{16,0},{24,48},{32,24},{40,40},{48,16},{56,32},{64,72... | collective-permute-start | bytes 786440 | tf_op jit(solution)/shard_map/column_terms/ppermute | solution.py:439
  117.8 1.9 %collective-permute-start.10 = (bf16[2,2,128,128]{3,2,1,0:T(8,128)(2,1)S(1)}, bf16[2,2,128,128]{3,2,1,0:T(8,128)(2,1)S(1)}, u32[]{:S(2)}, u32[]{:S(2)}) collective-permute-start(bf16[2,2,128,128]{3,2,1,0:T(8,128)(2,1)S(1)} %get-tuple-element.54), channel_id=1, source_target_pairs={{0,56},{8,0},{16,8},{24,16},{32,24},{40,32},{56,48},{64,120},{72,6... | collective-permute-start | bytes 393224 | tf_op jit(solution)/shard_map/column_terms/ppermute | solution.py:439
  119.7 3.9 %collective-permute-start.11 = (bf16[2,2,128,128]{3,2,1,0:T(8,128)(2,1)S(1)}, bf16[2,2,128,128]{3,2,1,0:T(8,128)(2,1)S(1)}, u32[]{:S(2)}, u32[]{:S(2)}) collective-permute-start(bf16[2,2,128,128]{3,2,1,0:T(8,128)(2,1)S(1)} %get-tuple-element.55), channel_id=1, source_target_pairs={{0,8},{8,16},{16,24},{24,32},{32,40},{48,56},{56,0},{64,72},{72,80... | collective-permute-start | bytes 393224 | tf_op jit(solution)/shard_map/column_terms/ppermute | solution.py:439
  123.6 3.3 %collective-permute-done.10.before = bf16[2,2,128,128]{3,2,1,0:T(8,128)(2,1)S(1)} collective-permute-done((bf16[2,2,128,128]{3,2,1,0:T(8,128)(2,1)S(1)}, bf16[2,2,128,128]{3,2,1,0:T(8,128)(2,1)S(1)}, u32[]{:S(2)}, u32[]{:S(2)}) %collective-permute-start.10) | collective-permute-done | bytes 131104 | tf_op jit(solution)/shard_map/column_terms/ppermute | solution.py:439
  127.0 2.5 %collective-permute-done.11.after = bf16[2,2,128,128]{3,2,1,0:T(8,128)(2,1)S(1)} collective-permute-done((bf16[2,2,128,128]{3,2,1,0:T(8,128)(2,1)S(1)}, bf16[2,2,128,128]{3,2,1,0:T(8,128)(2,1)S(1)}, u32[]{:S(2)}, u32[]{:S(2)}) %collective-permute-start.11) | collective-permute-done | bytes 131104 | tf_op jit(solution)/shard_map/column_terms/ppermute | solution.py:439
  129.4 0.7 combine.1
  130.2 2.5 %collective-permute-start.14 = (bf16[4,2,128,128]{3,2,1,0:T(8,128)(2,1)S(1)}, bf16[4,2,128,128]{3,2,1,0:T(8,128)(2,1)S(1)}, u32[]{:S(2)}, u32[]{:S(2)}) collective-permute-start(bf16[4,2,128,128]{3,2,1,0:T(8,128)(2,1)S(1)} %get-tuple-element.64), channel_id=1, source_target_pairs={{0,48},{8,16},{16,40},{24,8},{32,32},{40,0},{48,56},{56,24},{64,11... | collective-permute-start | bytes 786440 | tf_op jit(solution)/shard_map/outputs_home/ppermute | solution.py:439
  132.7 5.1 %collective-permute-start.15 = (bf16[4,2,128,128]{3,2,1,0:T(8,128)(2,1)S(1)}, bf16[4,2,128,128]{3,2,1,0:T(8,128)(2,1)S(1)}, u32[]{:S(2)}, u32[]{:S(2)}) collective-permute-start(bf16[4,2,128,128]{3,2,1,0:T(8,128)(2,1)S(1)} %get-tuple-element.65), channel_id=1, source_target_pairs={{0,16},{8,48},{16,8},{24,40},{32,0},{40,32},{48,24},{56,56},{64,80... | collective-permute-start | bytes 786440 | tf_op jit(solution)/shard_map/outputs_home/ppermute | solution.py:439
  137.8 1.9 %collective-permute-start.16 = (bf16[4,128,128]{2,1,0:T(8,128)(2,1)S(1)}, bf16[4,128,128]{2,1,0:T(8,128)(2,1)S(1)}, u32[]{:S(2)}, u32[]{:S(2)}) collective-permute-start(bf16[4,128,128]{2,1,0:T(8,128)(2,1)S(1)} %get-tuple-element.66), channel_id=1, source_target_pairs={{0,32},{8,0},{16,56},{24,24},{32,48},{40,16},{48,40},{56,8},{64,96... | collective-permute-start | bytes 393224 | tf_op jit(solution)/shard_map/outputs_home/ppermute | solution.py:439
  139.7 6.1 %collective-permute-start.17 = (bf16[4,128,128]{2,1,0:T(8,128)(2,1)S(1)}, bf16[4,128,128]{2,1,0:T(8,128)(2,1)S(1)}, u32[]{:S(2)}, u32[]{:S(2)}) collective-permute-start(bf16[4,128,128]{2,1,0:T(8,128)(2,1)S(1)} %get-tuple-element.67), channel_id=1, source_target_pairs={{0,0},{8,32},{16,24},{24,56},{32,16},{40,48},{48,8},{56,40},{64,64... | collective-permute-start | bytes 393224 | tf_op jit(solution)/shard_map/outputs_home/ppermute | solution.py:439
  145.8 8.0 %collective-permute-done.16.refs_4_ = bf16[4,128,128]{2,1,0:T(8,128)(2,1)S(1)} collective-permute-done((bf16[4,128,128]{2,1,0:T(8,128)(2,1)S(1)}, bf16[4,128,128]{2,1,0:T(8,128)(2,1)S(1)}, u32[]{:S(2)}, u32[]{:S(2)}) %collective-permute-start.16) | collective-permute-done | bytes 131104 | tf_op jit(solution)/shard_map/outputs_home/ppermute | solution.py:439
  153.8 2.1 %gather.1 = (bf16[256,640]{1,0:T(8,128)(2,1)}, bf16[256,640]{1,0:T(8,128)(2,1)}, bf16[256,640]{1,0:T(8,128)(2,1)}, bf16[256,640]{1,0:T(8,128)(2,1)}) custom-call(s32[14]{0:T(128)S(1)} %dynamic-slice_bitcast_fusion.table, bf16[4,2,128,128]{3,2,1,0:T(8,128)(2,1)S(1)} %collective-permute-done.12.refs_0_, ...), custom_call_target="tpu_custom_call" | custom-call | tf_op jit(solution)/shard_map/settle/gather/pallas_call | solution.py:167
  (14 shorter events, 0.0 us)
Async XLA Ops:
  0.6 1.3 copy-start.1
  0.6 1.6 %copy-start.2 = (bf16[1,8,4,5120]{3,2,1,0:T(4,128)(2,1)S(1)}, bf16[1,8,4,5120]{3,2,1,0:T(4,128)(2,1)}, u32[]{:S(2)}) copy-start(bf16[1,8,4,5120]{3,2,1,0:T(4,128)(2,1)} %param.7) | copy-start | bytes 983044
  3.6 5.1 %copy-start = (bf16[256,640]{1,0:T(8,128)(2,1)S(1)}, bf16[256,640]{1,0:T(8,128)(2,1)}, u32[]{:S(2)}) copy-start(bf16[256,640]{1,0:T(8,128)(2,1)} %upstream.1) | copy-start | bytes 983044
  3.6 23.1 %all-to-all-start = ((bf16[8,3,5,32,128]{4,3,2,1,0:T(8,128)(2,1)}), bf16[8,3,5,32,128]{4,3,2,1,0:T(8,128)(2,1)S(1)}, u32[]{:S(2)}, u32[]{:S(2)}) async-start(bf16[8,3,5,32,128]{4,3,2,1,0:T(8,128)(2,1)} %pad_maximum_fusion), calls=%async_computation | async-start | bytes 1966080 | tf_op jit(solution)/shard_map/heads/all_to_all | solution.py:456
  9.6 18.3 %collective-permute-start = (bf16[2,128,128]{2,1,0:T(8,128)(2,1)S(1)}, bf16[2,128,128]{2,1,0:T(8,128)(2,1)S(1)}, u32[]{:S(2)}, u32[]{:S(2)}) collective-permute-start(bf16[2,128,128]{2,1,0:T(8,128)(2,1)S(1)} %get-tuple-element.36), channel_id=1, source_target_pairs={{48,0},{16,8},{40,16},{8,24},{32,32},{0,40},{56,48},{24,56},{112,6... | collective-permute-start | bytes 196616 | tf_op jit(solution)/shard_map/upstream_to_units/ppermute | solution.py:439
  14.8 13.2 %collective-permute-start.1 = (bf16[2,128,128]{2,1,0:T(8,128)(2,1)S(1)}, bf16[2,128,128]{2,1,0:T(8,128)(2,1)S(1)}, u32[]{:S(2)}, u32[]{:S(2)}) collective-permute-start(bf16[2,128,128]{2,1,0:T(8,128)(2,1)S(1)} %get-tuple-element.37), channel_id=1, source_target_pairs={{16,0},{48,8},{8,16},{40,24},{0,32},{32,40},{24,48},{56,56},{80,64... | collective-permute-start | bytes 196616 | tf_op jit(solution)/shard_map/upstream_to_units/ppermute | solution.py:439
  16.7 11.9 %collective-permute-start.2 = (bf16[2,128,128]{2,1,0:T(8,128)(2,1)S(1)}, bf16[2,128,128]{2,1,0:T(8,128)(2,1)S(1)}, u32[]{:S(2)}, u32[]{:S(2)}) collective-permute-start(bf16[2,128,128]{2,1,0:T(8,128)(2,1)S(1)} %get-tuple-element.38), channel_id=1, source_target_pairs={{40,0},{24,8},{32,16},{16,24},{56,32},{8,40},{48,48},{0,56},{104,6... | collective-permute-start | bytes 196616 | tf_op jit(solution)/shard_map/upstream_to_units/ppermute | solution.py:439
  28.6 43.7 %all-to-all-start.1 = ((bf16[32,19,8,128]{3,2,1,0:T(8,128)(2,1)}), bf16[32,19,8,128]{3,2,1,0:T(8,128)(2,1)S(1)}, u32[]{:S(2)}, u32[]{:S(2)}) async-start(bf16[32,19,8,128]{3,2,1,0:T(8,128)(2,1)} %deal.1), calls=%async_computation.1 | async-start | bytes 2490368 | tf_op jit(solution)/shard_map/tiles/all_to_all | solution.py:459
  39.4 33.6 %collective-permute-start.3 = (bf16[2,128,128]{2,1,0:T(8,128)(2,1)S(1)}, bf16[2,128,128]{2,1,0:T(8,128)(2,1)S(1)}, u32[]{:S(2)}, u32[]{:S(2)}) collective-permute-start(bf16[2,128,128]{2,1,0:T(8,128)(2,1)S(1)} %get-tuple-element.40), channel_id=1, source_target_pairs={{8,0},{56,8},{0,16},{48,24},{24,32},{40,40},{16,48},{32,56},{72,64... | collective-permute-start | bytes 196616 | tf_op jit(solution)/shard_map/upstream_to_units/ppermute | solution.py:439
  41.9 31.1 %collective-permute-start.4 = (bf16[128,128]{1,0:T(8,128)(2,1)S(1)}, bf16[128,128]{1,0:T(8,128)(2,1)S(1)}, u32[]{:S(2)}, u32[]{:S(2)}) collective-permute-start(bf16[128,128]{1,0:T(8,128)(2,1)S(1)} %get-tuple-element.41), channel_id=1, source_target_pairs={{32,0},{0,8},{56,16},{24,24},{48,32},{16,40},{40,48},{8,56},{96,64... | collective-permute-start | bytes 98312 | tf_op jit(solution)/shard_map/upstream_to_units/ppermute | solution.py:439
  47.3 25.6 %collective-permute-start.5 = (bf16[128,128]{1,0:T(8,128)(2,1)S(1)}, bf16[128,128]{1,0:T(8,128)(2,1)S(1)}, u32[]{:S(2)}, u32[]{:S(2)}) collective-permute-start(bf16[128,128]{1,0:T(8,128)(2,1)S(1)} %get-tuple-element.42), channel_id=1, source_target_pairs={{0,0},{32,8},{24,16},{56,24},{16,32},{48,40},{8,48},{40,56},{64,64... | collective-permute-start | bytes 98312 | tf_op jit(solution)/shard_map/upstream_to_units/ppermute | solution.py:439
  73.0 10.4 %collective-permute-start.7 = (bf16[14,128,128]{2,1,0:T(8,128)(2,1)S(1)}, bf16[14,128,128]{2,1,0:T(8,128)(2,1)S(1)}, u32[]{:S(2)}, u32[]{:S(2)}) collective-permute-start(bf16[14,128,128]{2,1,0:T(8,128)(2,1)S(1)} %get-tuple-element.68), channel_id=1, source_target_pairs={{64,0},{72,8},{80,16},{88,24},{96,32},{104,40},{112,48},{120,56},{... | collective-permute-start | bytes 1376264 | tf_op jit(solution)/shard_map/halos/ppermute | solution.py:439
  75.5 10.4 %collective-permute-start.6 = (bf16[14,128,128]{2,1,0:T(8,128)(2,1)S(1)}, bf16[14,128,128]{2,1,0:T(8,128)(2,1)S(1)}, u32[]{:S(2)}, u32[]{:S(2)}) collective-permute-start(bf16[14,128,128]{2,1,0:T(8,128)(2,1)S(1)} %get-tuple-element.69), channel_id=1, source_target_pairs={{0,64},{8,72},{16,80},{24,88},{32,96},{40,104},{48,112},{56,120},{... | collective-permute-start | bytes 1376264 | tf_op jit(solution)/shard_map/halos/ppermute | solution.py:439
  94.0 10.4 %collective-permute-start.8 = (bf16[2,7,128,128]{3,2,1,0:T(8,128)(2,1)S(1)}, bf16[2,7,128,128]{3,2,1,0:T(8,128)(2,1)S(1)}, u32[]{:S(2)}, u32[]{:S(2)}) collective-permute-start(bf16[2,7,128,128]{3,2,1,0:T(8,128)(2,1)S(1)} %get-tuple-element.52), channel_id=1, source_target_pairs={{0,64},{8,72},{16,80},{24,88},{32,96},{40,104},{48,112},{56,120},{... | collective-permute-start | bytes 1376264 | tf_op jit(solution)/shard_map/row_terms/ppermute | solution.py:439
  97.4 10.4 %collective-permute-start.9 = (bf16[2,7,128,128]{3,2,1,0:T(8,128)(2,1)S(1)}, bf16[2,7,128,128]{3,2,1,0:T(8,128)(2,1)S(1)}, u32[]{:S(2)}, u32[]{:S(2)}) collective-permute-start(bf16[2,7,128,128]{3,2,1,0:T(8,128)(2,1)S(1)} %get-tuple-element.53), channel_id=1, source_target_pairs={{64,0},{72,8},{80,16},{88,24},{96,32},{104,40},{112,48},{120,56},{... | collective-permute-start | bytes 1376264 | tf_op jit(solution)/shard_map/row_terms/ppermute | solution.py:439
  108.5 21.7 %collective-permute-start.12 = (bf16[4,2,128,128]{3,2,1,0:T(8,128)(2,1)S(1)}, bf16[4,2,128,128]{3,2,1,0:T(8,128)(2,1)S(1)}, u32[]{:S(2)}, u32[]{:S(2)}) collective-permute-start(bf16[4,2,128,128]{3,2,1,0:T(8,128)(2,1)S(1)} %get-tuple-element.60), channel_id=1, source_target_pairs={{0,40},{8,24},{16,32},{24,16},{32,56},{40,8},{48,48},{56,0},{64,10... | collective-permute-start | bytes 786440 | tf_op jit(solution)/shard_map/column_terms/ppermute | solution.py:439
  112.6 17.5 %collective-permute-start.13 = (bf16[4,2,128,128]{3,2,1,0:T(8,128)(2,1)S(1)}, bf16[4,2,128,128]{3,2,1,0:T(8,128)(2,1)S(1)}, u32[]{:S(2)}, u32[]{:S(2)}) collective-permute-start(bf16[4,2,128,128]{3,2,1,0:T(8,128)(2,1)S(1)} %get-tuple-element.61), channel_id=1, source_target_pairs={{0,8},{8,56},{16,0},{24,48},{32,24},{40,40},{48,16},{56,32},{64,72... | collective-permute-start | bytes 786440 | tf_op jit(solution)/shard_map/column_terms/ppermute | solution.py:439
  117.8 9.2 %collective-permute-start.10 = (bf16[2,2,128,128]{3,2,1,0:T(8,128)(2,1)S(1)}, bf16[2,2,128,128]{3,2,1,0:T(8,128)(2,1)S(1)}, u32[]{:S(2)}, u32[]{:S(2)}) collective-permute-start(bf16[2,2,128,128]{3,2,1,0:T(8,128)(2,1)S(1)} %get-tuple-element.54), channel_id=1, source_target_pairs={{0,56},{8,0},{16,8},{24,16},{32,24},{40,32},{56,48},{64,120},{72,6... | collective-permute-start | bytes 393224 | tf_op jit(solution)/shard_map/column_terms/ppermute | solution.py:439
  119.7 9.8 %collective-permute-start.11 = (bf16[2,2,128,128]{3,2,1,0:T(8,128)(2,1)S(1)}, bf16[2,2,128,128]{3,2,1,0:T(8,128)(2,1)S(1)}, u32[]{:S(2)}, u32[]{:S(2)}) collective-permute-start(bf16[2,2,128,128]{3,2,1,0:T(8,128)(2,1)S(1)} %get-tuple-element.55), channel_id=1, source_target_pairs={{0,8},{8,16},{16,24},{24,32},{32,40},{48,56},{56,0},{64,72},{72,80... | collective-permute-start | bytes 393224 | tf_op jit(solution)/shard_map/column_terms/ppermute | solution.py:439
  130.2 23.6 %collective-permute-start.14 = (bf16[4,2,128,128]{3,2,1,0:T(8,128)(2,1)S(1)}, bf16[4,2,128,128]{3,2,1,0:T(8,128)(2,1)S(1)}, u32[]{:S(2)}, u32[]{:S(2)}) collective-permute-start(bf16[4,2,128,128]{3,2,1,0:T(8,128)(2,1)S(1)} %get-tuple-element.64), channel_id=1, source_target_pairs={{0,48},{8,16},{16,40},{24,8},{32,32},{40,0},{48,56},{56,24},{64,11... | collective-permute-start | bytes 786440 | tf_op jit(solution)/shard_map/outputs_home/ppermute | solution.py:439
  132.7 21.2 %collective-permute-start.15 = (bf16[4,2,128,128]{3,2,1,0:T(8,128)(2,1)S(1)}, bf16[4,2,128,128]{3,2,1,0:T(8,128)(2,1)S(1)}, u32[]{:S(2)}, u32[]{:S(2)}) collective-permute-start(bf16[4,2,128,128]{3,2,1,0:T(8,128)(2,1)S(1)} %get-tuple-element.65), channel_id=1, source_target_pairs={{0,16},{8,48},{16,8},{24,40},{32,0},{40,32},{48,24},{56,56},{64,80... | collective-permute-start | bytes 786440 | tf_op jit(solution)/shard_map/outputs_home/ppermute | solution.py:439
  137.8 16.0 %collective-permute-start.16 = (bf16[4,128,128]{2,1,0:T(8,128)(2,1)S(1)}, bf16[4,128,128]{2,1,0:T(8,128)(2,1)S(1)}, u32[]{:S(2)}, u32[]{:S(2)}) collective-permute-start(bf16[4,128,128]{2,1,0:T(8,128)(2,1)S(1)} %get-tuple-element.66), channel_id=1, source_target_pairs={{0,32},{8,0},{16,56},{24,24},{32,48},{40,16},{48,40},{56,8},{64,96... | collective-permute-start | bytes 393224 | tf_op jit(solution)/shard_map/outputs_home/ppermute | solution.py:439
  139.7 14.1 %collective-permute-start.17 = (bf16[4,128,128]{2,1,0:T(8,128)(2,1)S(1)}, bf16[4,128,128]{2,1,0:T(8,128)(2,1)S(1)}, u32[]{:S(2)}, u32[]{:S(2)}) collective-permute-start(bf16[4,128,128]{2,1,0:T(8,128)(2,1)S(1)} %get-tuple-element.67), channel_id=1, source_target_pairs={{0,0},{8,32},{16,24},{24,56},{32,16},{40,48},{48,8},{56,40},{64,64... | collective-permute-start | bytes 393224 | tf_op jit(solution)/shard_map/outputs_home/ppermute | solution.py:439

commit v13 on v12

--- a/solution.py
+++ b/solution.py
@@ -63,7 +63,7 @@
 
 ROW_STEPS = ((1, 0), (-1, 0))
 COLUMN_STEPS = ((0, 1), (0, -1))
-EARLY = 3
+EARLY = 2
 OWNER_STEPS = tuple((which, turn) for which in range(3) for turn in range(2))
 
 

time: 157 us -> 157 us (level)
  waiting for transfers between devices: 50 us -> 55.8 us
  starting transfers between devices: 86.9 us -> 81.4 us
    all_to_all x1, waiting for transfers between devices: 0.01 us -> 6.55 us  [local(): swapped = lax.all_to_all(jnp.stack(lines, axis=1), 'head', 0, 0, tiled=True)]
    ppermute x18, starting transfers between devices: 71.7 us -> 65.8 us  [send_all(): lax.ppermute(part, 'tile', path)]
    all_to_all x1, waiting for transfers between devices: 20.6 us -> 15 us  [local(): got = lax.all_to_all(dealt, 'tile', 0, 0, tiled=True)]
    ppermute x18, waiting for transfers between devices: 29.3 us -> 34.2 us  [send_all(): lax.ppermute(part, 'tile', path)]
  transfers between devices with their start and end apart: 20 -> 20, of which waited for: 9 -> 10; matrix products, arithmetic and copies ran while one was open for 1% -> 1% of each run, Pallas kernels for 2% -> 2%
where the time goes in v13:
time: 157 us; the launch traced here: 156 us
  starting transfers between devices  81.4 us (52%)
  waiting for transfers between devices  55.8 us (36%)
  Pallas kernels  13.8 us (9%)
  local copies, waits for them, and re-layouts  3.23 us (2%)
    ppermute x18, starting transfers between devices, send_all(): lax.ppermute(part, 'tile', path)  65.8 us
    ppermute x18, waiting for transfers between devices, send_all(): lax.ppermute(part, 'tile', path)  34.2 us
    all_to_all x1, waiting for transfers between devices, local(): got = lax.all_to_all(dealt, 'tile', 0, 0, tiled=True)  15 us
    all_to_all x1, starting transfers between devices, local(): got = lax.all_to_all(dealt, 'tile', 0, 0, tiled=True)  11.2 us
    pallas_call x1, Pallas kernels, attend(): pl.pallas_call(attend_kernel, out_shape=[jax.ShapeDtypeStruct((2, 2, 5, T...  8.13 us
    all_to_all x1, waiting for transfers between devices, local(): swapped = lax.all_to_all(jnp.stack(lines, axis=1), 'head', 0, 0, tiled=True)  6.55 us
    all_to_all x1, starting transfers between devices, local(): swapped = lax.all_to_all(jnp.stack(lines, axis=1), 'head', 0, 0, tiled=True)  4.43 us
  transfers between devices with their start and end apart: 20, of which 10 were waited for; matrix products, arithmetic and copies ran while one was open for 1% of the time, Pallas kernels for 2%

profile of v13, /device:TPU:40, one launch (start us, length us, event | category | flops | bytes accessed | tf_op | source)
XLA Modules:
  0.0 156.3 jit_solution(851102340826285082)
XLA Ops:
  0.7 1.2 reshape.32
  1.8 0.1 copy.9
  2.0 0.1 reshape.34
  2.1 0.1 copy.10
  2.2 0.1 reshape.36
  2.4 0.1 copy.11
  2.5 1.1 pad_maximum_fusion
  3.6 4.4 %all-to-all-start = ((bf16[8,3,5,32,128]{4,3,2,1,0:T(8,128)(2,1)}), bf16[8,3,5,32,128]{4,3,2,1,0:T(8,128)(2,1)S(1)}, u32[]{:S(2)}, u32[]{:S(2)}) async-start(bf16[8,3,5,32,128]{4,3,2,1,0:T(8,128)(2,1)} %pad_maximum_fusion), calls=%async_computation | async-start | bytes 1966080 | tf_op jit(solution)/shard_map/heads/all_to_all | solution.py:456
  8.0 0.7 dynamic-slice_bitcast_fusion.table
  8.7 0.9 spread.1
  9.6 5.2 %collective-permute-start = (bf16[2,128,128]{2,1,0:T(8,128)(2,1)S(1)}, bf16[2,128,128]{2,1,0:T(8,128)(2,1)S(1)}, u32[]{:S(2)}, u32[]{:S(2)}) collective-permute-start(bf16[2,128,128]{2,1,0:T(8,128)(2,1)S(1)} %get-tuple-element.36), channel_id=1, source_target_pairs={{48,0},{16,8},{40,16},{8,24},{32,32},{0,40},{56,48},{24,56},{112,6... | collective-permute-start | bytes 196616 | tf_op jit(solution)/shard_map/upstream_to_units/ppermute | solution.py:439
  14.8 1.9 %collective-permute-start.1 = (bf16[2,128,128]{2,1,0:T(8,128)(2,1)S(1)}, bf16[2,128,128]{2,1,0:T(8,128)(2,1)S(1)}, u32[]{:S(2)}, u32[]{:S(2)}) collective-permute-start(bf16[2,128,128]{2,1,0:T(8,128)(2,1)S(1)} %get-tuple-element.37), channel_id=1, source_target_pairs={{16,0},{48,8},{8,16},{40,24},{0,32},{32,40},{24,48},{56,56},{80,64... | collective-permute-start | bytes 196616 | tf_op jit(solution)/shard_map/upstream_to_units/ppermute | solution.py:439
  16.7 6.5 %all-to-all-done.swapped = bf16[8,3,5,32,128]{4,3,2,1,0:T(8,128)(2,1)S(1)} async-done(((bf16[8,3,5,32,128]{4,3,2,1,0:T(8,128)(2,1)}), bf16[8,3,5,32,128]{4,3,2,1,0:T(8,128)(2,1)S(1)}, u32[]{:S(2)}, u32[]{:S(2)}) %all-to-all-start) | async-done | bytes 983072 | tf_op jit(solution)/shard_map/heads/all_to_all | solution.py:456
  23.3 1.2 deal.1
  24.5 11.2 %all-to-all-start.1 = ((bf16[32,19,8,128]{3,2,1,0:T(8,128)(2,1)}), bf16[32,19,8,128]{3,2,1,0:T(8,128)(2,1)S(1)}, u32[]{:S(2)}, u32[]{:S(2)}) async-start(bf16[32,19,8,128]{3,2,1,0:T(8,128)(2,1)} %deal.1), calls=%async_computation.1 | async-start | bytes 2490368 | tf_op jit(solution)/shard_map/tiles/all_to_all | solution.py:459
  35.8 6.4 %collective-permute-start.2 = (bf16[2,128,128]{2,1,0:T(8,128)(2,1)S(1)}, bf16[2,128,128]{2,1,0:T(8,128)(2,1)S(1)}, u32[]{:S(2)}, u32[]{:S(2)}) collective-permute-start(bf16[2,128,128]{2,1,0:T(8,128)(2,1)S(1)} %get-tuple-element.39), channel_id=1, source_target_pairs={{40,0},{24,8},{32,16},{16,24},{56,32},{8,40},{48,48},{0,56},{104,6... | collective-permute-start | bytes 196616 | tf_op jit(solution)/shard_map/upstream_to_units/ppermute | solution.py:439
  42.2 1.9 %collective-permute-start.3 = (bf16[2,128,128]{2,1,0:T(8,128)(2,1)S(1)}, bf16[2,128,128]{2,1,0:T(8,128)(2,1)S(1)}, u32[]{:S(2)}, u32[]{:S(2)}) collective-permute-start(bf16[2,128,128]{2,1,0:T(8,128)(2,1)S(1)} %get-tuple-element.40), channel_id=1, source_target_pairs={{8,0},{56,8},{0,16},{48,24},{24,32},{40,40},{16,48},{32,56},{72,64... | collective-permute-start | bytes 196616 | tf_op jit(solution)/shard_map/upstream_to_units/ppermute | solution.py:439
  44.1 6.0 %collective-permute-start.4 = (bf16[128,128]{1,0:T(8,128)(2,1)S(1)}, bf16[128,128]{1,0:T(8,128)(2,1)S(1)}, u32[]{:S(2)}, u32[]{:S(2)}) collective-permute-start(bf16[128,128]{1,0:T(8,128)(2,1)S(1)} %get-tuple-element.41), channel_id=1, source_target_pairs={{32,0},{0,8},{56,16},{24,24},{48,32},{16,40},{40,48},{8,56},{96,64... | collective-permute-start | bytes 98312 | tf_op jit(solution)/shard_map/upstream_to_units/ppermute | solution.py:439
  50.1 3.1 %collective-permute-start.5 = (bf16[128,128]{1,0:T(8,128)(2,1)S(1)}, bf16[128,128]{1,0:T(8,128)(2,1)S(1)}, u32[]{:S(2)}, u32[]{:S(2)}) collective-permute-start(bf16[128,128]{1,0:T(8,128)(2,1)S(1)} %get-tuple-element.42), channel_id=1, source_target_pairs={{0,0},{32,8},{24,16},{56,24},{16,32},{48,40},{8,48},{40,56},{64,64... | collective-permute-start | bytes 98312 | tf_op jit(solution)/shard_map/upstream_to_units/ppermute | solution.py:439
  53.2 15.0 %all-to-all-done.1 = bf16[32,19,8,128]{3,2,1,0:T(8,128)(2,1)S(1)} async-done(((bf16[32,19,8,128]{3,2,1,0:T(8,128)(2,1)}), bf16[32,19,8,128]{3,2,1,0:T(8,128)(2,1)S(1)}, u32[]{:S(2)}, u32[]{:S(2)}) %all-to-all-start.1) | async-done | bytes 1245216 | tf_op jit(solution)/shard_map/tiles/all_to_all | solution.py:459
  68.2 0.7 copy.12
  68.9 0.0 collective-permute-done.4.refs_4_
  68.9 0.3 collective-permute-done.5.refs_5_
  69.2 0.0 collective-permute-done.2.refs_2_
  69.2 0.1 slice_bitcast_fusion
  69.3 2.6 %collective-permute-start.7 = (bf16[14,128,128]{2,1,0:T(8,128)(2,1)S(1)}, bf16[14,128,128]{2,1,0:T(8,128)(2,1)S(1)}, u32[]{:S(2)}, u32[]{:S(2)}) collective-permute-start(bf16[14,128,128]{2,1,0:T(8,128)(2,1)S(1)} %get-tuple-element.68), channel_id=1, source_target_pairs={{64,0},{72,8},{80,16},{88,24},{96,32},{104,40},{112,48},{120,56},{... | collective-permute-start | bytes 1376264 | tf_op jit(solution)/shard_map/halos/ppermute | solution.py:439
  71.9 3.2 %collective-permute-start.6 = (bf16[14,128,128]{2,1,0:T(8,128)(2,1)S(1)}, bf16[14,128,128]{2,1,0:T(8,128)(2,1)S(1)}, u32[]{:S(2)}, u32[]{:S(2)}) collective-permute-start(bf16[14,128,128]{2,1,0:T(8,128)(2,1)S(1)} %get-tuple-element.69), channel_id=1, source_target_pairs={{0,64},{8,72},{16,80},{24,88},{32,96},{40,104},{48,112},{56,120},{... | collective-permute-start | bytes 1376264 | tf_op jit(solution)/shard_map/halos/ppermute | solution.py:439
  75.1 7.4 %collective-permute-done.7.below = bf16[14,128,128]{2,1,0:T(8,128)(2,1)S(1)} collective-permute-done((bf16[14,128,128]{2,1,0:T(8,128)(2,1)S(1)}, bf16[14,128,128]{2,1,0:T(8,128)(2,1)S(1)}, u32[]{:S(2)}, u32[]{:S(2)}) %collective-permute-start.7) | collective-permute-done | bytes 458784 | tf_op jit(solution)/shard_map/halos/ppermute | solution.py:439
  82.5 2.0 %collective-permute-done.6.above = bf16[14,128,128]{2,1,0:T(8,128)(2,1)S(1)} collective-permute-done((bf16[14,128,128]{2,1,0:T(8,128)(2,1)S(1)}, bf16[14,128,128]{2,1,0:T(8,128)(2,1)S(1)}, u32[]{:S(2)}, u32[]{:S(2)}) %collective-permute-start.6) | collective-permute-done | bytes 458784 | tf_op jit(solution)/shard_map/halos/ppermute | solution.py:439
  84.6 8.1 %attend.1 = (bf16[2,2,5,128,128]{4,3,2,1,0:T(8,128)(2,1)S(1)}, f32[2,2,7,128,128]{4,3,2,1,0:T(8,128)S(1)}, bf16[2,7,128,128]{3,2,1,0:T(8,128)(2,1)S(1)}, bf16[2,7,128,128]{3,2,1,0:T(8,128)(2,1)S(1)}) custom-call(s32[14]{0:T(128)S(1)} %dynamic-slice_bitcast_fusion.table, bf16[2,19,128,128]{3,2,1,0:T(8,128)(2,1)S(1)} %bitcast.20, ...), custom_call_target="tpu_custom_call" | custom-call | flops 3000000000 | bytes 8000000 | tf_op jit(solution)/shard_map/attention/attend/pallas_call | solution.py:348
  92.7 3.5 %collective-permute-start.8 = (bf16[2,7,128,128]{3,2,1,0:T(8,128)(2,1)S(1)}, bf16[2,7,128,128]{3,2,1,0:T(8,128)(2,1)S(1)}, u32[]{:S(2)}, u32[]{:S(2)}) collective-permute-start(bf16[2,7,128,128]{3,2,1,0:T(8,128)(2,1)S(1)} %get-tuple-element.52), channel_id=1, source_target_pairs={{0,64},{8,72},{16,80},{24,88},{32,96},{40,104},{48,112},{56,120},{... | collective-permute-start | bytes 1376264 | tf_op jit(solution)/shard_map/row_terms/ppermute | solution.py:439
  96.2 2.3 %collective-permute-start.9 = (bf16[2,7,128,128]{3,2,1,0:T(8,128)(2,1)S(1)}, bf16[2,7,128,128]{3,2,1,0:T(8,128)(2,1)S(1)}, u32[]{:S(2)}, u32[]{:S(2)}) collective-permute-start(bf16[2,7,128,128]{3,2,1,0:T(8,128)(2,1)S(1)} %get-tuple-element.53), channel_id=1, source_target_pairs={{64,0},{72,8},{80,16},{88,24},{96,32},{104,40},{112,48},{120,56},{... | collective-permute-start | bytes 1376264 | tf_op jit(solution)/shard_map/row_terms/ppermute | solution.py:439
  98.6 5.8 %collective-permute-done.8.above = bf16[2,7,128,128]{3,2,1,0:T(8,128)(2,1)S(1)} collective-permute-done((bf16[2,7,128,128]{3,2,1,0:T(8,128)(2,1)S(1)}, bf16[2,7,128,128]{3,2,1,0:T(8,128)(2,1)S(1)}, u32[]{:S(2)}, u32[]{:S(2)}) %collective-permute-start.8) | collective-permute-done | bytes 458784 | tf_op jit(solution)/shard_map/row_terms/ppermute | solution.py:439
  104.4 3.6 %collective-permute-done.9.below = bf16[2,7,128,128]{3,2,1,0:T(8,128)(2,1)S(1)} collective-permute-done((bf16[2,7,128,128]{3,2,1,0:T(8,128)(2,1)S(1)}, bf16[2,7,128,128]{3,2,1,0:T(8,128)(2,1)S(1)}, u32[]{:S(2)}, u32[]{:S(2)}) %collective-permute-start.9) | collective-permute-done | bytes 458784 | tf_op jit(solution)/shard_map/row_terms/ppermute | solution.py:439
  108.0 0.7 rims.1
  108.7 4.0 %collective-permute-start.12 = (bf16[4,2,128,128]{3,2,1,0:T(8,128)(2,1)S(1)}, bf16[4,2,128,128]{3,2,1,0:T(8,128)(2,1)S(1)}, u32[]{:S(2)}, u32[]{:S(2)}) collective-permute-start(bf16[4,2,128,128]{3,2,1,0:T(8,128)(2,1)S(1)} %get-tuple-element.60), channel_id=1, source_target_pairs={{0,40},{8,24},{16,32},{24,16},{32,56},{40,8},{48,48},{56,0},{64,10... | collective-permute-start | bytes 786440 | tf_op jit(solution)/shard_map/column_terms/ppermute | solution.py:439
  112.7 4.1 %collective-permute-start.13 = (bf16[4,2,128,128]{3,2,1,0:T(8,128)(2,1)S(1)}, bf16[4,2,128,128]{3,2,1,0:T(8,128)(2,1)S(1)}, u32[]{:S(2)}, u32[]{:S(2)}) collective-permute-start(bf16[4,2,128,128]{3,2,1,0:T(8,128)(2,1)S(1)} %get-tuple-element.61), channel_id=1, source_target_pairs={{0,8},{8,56},{16,0},{24,48},{32,24},{40,40},{48,16},{56,32},{64,72... | collective-permute-start | bytes 786440 | tf_op jit(solution)/shard_map/column_terms/ppermute | solution.py:439
  116.8 2.3 %collective-permute-start.10 = (bf16[2,2,128,128]{3,2,1,0:T(8,128)(2,1)S(1)}, bf16[2,2,128,128]{3,2,1,0:T(8,128)(2,1)S(1)}, u32[]{:S(2)}, u32[]{:S(2)}) collective-permute-start(bf16[2,2,128,128]{3,2,1,0:T(8,128)(2,1)S(1)} %get-tuple-element.54), channel_id=1, source_target_pairs={{0,56},{8,0},{16,8},{24,16},{32,24},{40,32},{56,48},{64,120},{72,6... | collective-permute-start | bytes 393224 | tf_op jit(solution)/shard_map/column_terms/ppermute | solution.py:439
  119.1 3.5 %collective-permute-start.11 = (bf16[2,2,128,128]{3,2,1,0:T(8,128)(2,1)S(1)}, bf16[2,2,128,128]{3,2,1,0:T(8,128)(2,1)S(1)}, u32[]{:S(2)}, u32[]{:S(2)}) collective-permute-start(bf16[2,2,128,128]{3,2,1,0:T(8,128)(2,1)S(1)} %get-tuple-element.55), channel_id=1, source_target_pairs={{0,8},{8,16},{16,24},{24,32},{32,40},{48,56},{56,0},{64,72},{72,80... | collective-permute-start | bytes 393224 | tf_op jit(solution)/shard_map/column_terms/ppermute | solution.py:439
  122.7 5.2 %collective-permute-done.10.before = bf16[2,2,128,128]{3,2,1,0:T(8,128)(2,1)S(1)} collective-permute-done((bf16[2,2,128,128]{3,2,1,0:T(8,128)(2,1)S(1)}, bf16[2,2,128,128]{3,2,1,0:T(8,128)(2,1)S(1)}, u32[]{:S(2)}, u32[]{:S(2)}) %collective-permute-start.10) | collective-permute-done | bytes 131104 | tf_op jit(solution)/shard_map/column_terms/ppermute | solution.py:439
  127.8 2.0 %collective-permute-done.11.after = bf16[2,2,128,128]{3,2,1,0:T(8,128)(2,1)S(1)} collective-permute-done((bf16[2,2,128,128]{3,2,1,0:T(8,128)(2,1)S(1)}, bf16[2,2,128,128]{3,2,1,0:T(8,128)(2,1)S(1)}, u32[]{:S(2)}, u32[]{:S(2)}) %collective-permute-start.11) | collective-permute-done | bytes 131104 | tf_op jit(solution)/shard_map/column_terms/ppermute | solution.py:439
  129.9 0.7 combine.1
  130.6 2.3 %collective-permute-start.14 = (bf16[4,2,128,128]{3,2,1,0:T(8,128)(2,1)S(1)}, bf16[4,2,128,128]{3,2,1,0:T(8,128)(2,1)S(1)}, u32[]{:S(2)}, u32[]{:S(2)}) collective-permute-start(bf16[4,2,128,128]{3,2,1,0:T(8,128)(2,1)S(1)} %get-tuple-element.64), channel_id=1, source_target_pairs={{0,48},{8,16},{16,40},{24,8},{32,32},{40,0},{48,56},{56,24},{64,11... | collective-permute-start | bytes 786440 | tf_op jit(solution)/shard_map/outputs_home/ppermute | solution.py:439
  133.0 4.5 %collective-permute-start.15 = (bf16[4,2,128,128]{3,2,1,0:T(8,128)(2,1)S(1)}, bf16[4,2,128,128]{3,2,1,0:T(8,128)(2,1)S(1)}, u32[]{:S(2)}, u32[]{:S(2)}) collective-permute-start(bf16[4,2,128,128]{3,2,1,0:T(8,128)(2,1)S(1)} %get-tuple-element.65), channel_id=1, source_target_pairs={{0,16},{8,48},{16,8},{24,40},{32,0},{40,32},{48,24},{56,56},{64,80... | collective-permute-start | bytes 786440 | tf_op jit(solution)/shard_map/outputs_home/ppermute | solution.py:439
  137.5 1.9 %collective-permute-start.16 = (bf16[4,128,128]{2,1,0:T(8,128)(2,1)S(1)}, bf16[4,128,128]{2,1,0:T(8,128)(2,1)S(1)}, u32[]{:S(2)}, u32[]{:S(2)}) collective-permute-start(bf16[4,128,128]{2,1,0:T(8,128)(2,1)S(1)} %get-tuple-element.66), channel_id=1, source_target_pairs={{0,32},{8,0},{16,56},{24,24},{32,48},{40,16},{48,40},{56,8},{64,96... | collective-permute-start | bytes 393224 | tf_op jit(solution)/shard_map/outputs_home/ppermute | solution.py:439
  139.4 6.8 %collective-permute-start.17 = (bf16[4,128,128]{2,1,0:T(8,128)(2,1)S(1)}, bf16[4,128,128]{2,1,0:T(8,128)(2,1)S(1)}, u32[]{:S(2)}, u32[]{:S(2)}) collective-permute-start(bf16[4,128,128]{2,1,0:T(8,128)(2,1)S(1)} %get-tuple-element.67), channel_id=1, source_target_pairs={{0,0},{8,32},{16,24},{24,56},{32,16},{40,48},{48,8},{56,40},{64,64... | collective-permute-start | bytes 393224 | tf_op jit(solution)/shard_map/outputs_home/ppermute | solution.py:439
  146.2 7.9 %collective-permute-done.16.refs_4_ = bf16[4,128,128]{2,1,0:T(8,128)(2,1)S(1)} collective-permute-done((bf16[4,128,128]{2,1,0:T(8,128)(2,1)S(1)}, bf16[4,128,128]{2,1,0:T(8,128)(2,1)S(1)}, u32[]{:S(2)}, u32[]{:S(2)}) %collective-permute-start.16) | collective-permute-done | bytes 131104 | tf_op jit(solution)/shard_map/outputs_home/ppermute | solution.py:439
  154.2 2.1 %gather.1 = (bf16[256,640]{1,0:T(8,128)(2,1)}, bf16[256,640]{1,0:T(8,128)(2,1)}, bf16[256,640]{1,0:T(8,128)(2,1)}, bf16[256,640]{1,0:T(8,128)(2,1)}) custom-call(s32[14]{0:T(128)S(1)} %dynamic-slice_bitcast_fusion.table, bf16[4,2,128,128]{3,2,1,0:T(8,128)(2,1)S(1)} %collective-permute-done.12.refs_0_, ...), custom_call_target="tpu_custom_call" | custom-call | tf_op jit(solution)/shard_map/settle/gather/pallas_call | solution.py:167
  (14 shorter events, 0.0 us)
Async XLA Ops:
  0.6 1.3 copy-start.1
  0.6 1.6 %copy-start.2 = (bf16[1,8,4,5120]{3,2,1,0:T(4,128)(2,1)S(1)}, bf16[1,8,4,5120]{3,2,1,0:T(4,128)(2,1)}, u32[]{:S(2)}) copy-start(bf16[1,8,4,5120]{3,2,1,0:T(4,128)(2,1)} %param.7) | copy-start | bytes 983044
  3.6 5.1 %copy-start = (bf16[256,640]{1,0:T(8,128)(2,1)S(1)}, bf16[256,640]{1,0:T(8,128)(2,1)}, u32[]{:S(2)}) copy-start(bf16[256,640]{1,0:T(8,128)(2,1)} %upstream.1) | copy-start | bytes 983044
  3.6 19.7 %all-to-all-start = ((bf16[8,3,5,32,128]{4,3,2,1,0:T(8,128)(2,1)}), bf16[8,3,5,32,128]{4,3,2,1,0:T(8,128)(2,1)S(1)}, u32[]{:S(2)}, u32[]{:S(2)}) async-start(bf16[8,3,5,32,128]{4,3,2,1,0:T(8,128)(2,1)} %pad_maximum_fusion), calls=%async_computation | async-start | bytes 1966080 | tf_op jit(solution)/shard_map/heads/all_to_all | solution.py:456
  9.6 14.9 %collective-permute-start = (bf16[2,128,128]{2,1,0:T(8,128)(2,1)S(1)}, bf16[2,128,128]{2,1,0:T(8,128)(2,1)S(1)}, u32[]{:S(2)}, u32[]{:S(2)}) collective-permute-start(bf16[2,128,128]{2,1,0:T(8,128)(2,1)S(1)} %get-tuple-element.36), channel_id=1, source_target_pairs={{48,0},{16,8},{40,16},{8,24},{32,32},{0,40},{56,48},{24,56},{112,6... | collective-permute-start | bytes 196616 | tf_op jit(solution)/shard_map/upstream_to_units/ppermute | solution.py:439
  14.8 9.7 %collective-permute-start.1 = (bf16[2,128,128]{2,1,0:T(8,128)(2,1)S(1)}, bf16[2,128,128]{2,1,0:T(8,128)(2,1)S(1)}, u32[]{:S(2)}, u32[]{:S(2)}) collective-permute-start(bf16[2,128,128]{2,1,0:T(8,128)(2,1)S(1)} %get-tuple-element.37), channel_id=1, source_target_pairs={{16,0},{48,8},{8,16},{40,24},{0,32},{32,40},{24,48},{56,56},{80,64... | collective-permute-start | bytes 196616 | tf_op jit(solution)/shard_map/upstream_to_units/ppermute | solution.py:439
  24.5 43.7 %all-to-all-start.1 = ((bf16[32,19,8,128]{3,2,1,0:T(8,128)(2,1)}), bf16[32,19,8,128]{3,2,1,0:T(8,128)(2,1)S(1)}, u32[]{:S(2)}, u32[]{:S(2)}) async-start(bf16[32,19,8,128]{3,2,1,0:T(8,128)(2,1)} %deal.1), calls=%async_computation.1 | async-start | bytes 2490368 | tf_op jit(solution)/shard_map/tiles/all_to_all | solution.py:459
  35.8 33.4 %collective-permute-start.2 = (bf16[2,128,128]{2,1,0:T(8,128)(2,1)S(1)}, bf16[2,128,128]{2,1,0:T(8,128)(2,1)S(1)}, u32[]{:S(2)}, u32[]{:S(2)}) collective-permute-start(bf16[2,128,128]{2,1,0:T(8,128)(2,1)S(1)} %get-tuple-element.39), channel_id=1, source_target_pairs={{40,0},{24,8},{32,16},{16,24},{56,32},{8,40},{48,48},{0,56},{104,6... | collective-permute-start | bytes 196616 | tf_op jit(solution)/shard_map/upstream_to_units/ppermute | solution.py:439
  42.2 27.0 %collective-permute-start.3 = (bf16[2,128,128]{2,1,0:T(8,128)(2,1)S(1)}, bf16[2,128,128]{2,1,0:T(8,128)(2,1)S(1)}, u32[]{:S(2)}, u32[]{:S(2)}) collective-permute-start(bf16[2,128,128]{2,1,0:T(8,128)(2,1)S(1)} %get-tuple-element.40), channel_id=1, source_target_pairs={{8,0},{56,8},{0,16},{48,24},{24,32},{40,40},{16,48},{32,56},{72,64... | collective-permute-start | bytes 196616 | tf_op jit(solution)/shard_map/upstream_to_units/ppermute | solution.py:439
  44.1 24.8 %collective-permute-start.4 = (bf16[128,128]{1,0:T(8,128)(2,1)S(1)}, bf16[128,128]{1,0:T(8,128)(2,1)S(1)}, u32[]{:S(2)}, u32[]{:S(2)}) collective-permute-start(bf16[128,128]{1,0:T(8,128)(2,1)S(1)} %get-tuple-element.41), channel_id=1, source_target_pairs={{32,0},{0,8},{56,16},{24,24},{48,32},{16,40},{40,48},{8,56},{96,64... | collective-permute-start | bytes 98312 | tf_op jit(solution)/shard_map/upstream_to_units/ppermute | solution.py:439
  50.1 19.0 %collective-permute-start.5 = (bf16[128,128]{1,0:T(8,128)(2,1)S(1)}, bf16[128,128]{1,0:T(8,128)(2,1)S(1)}, u32[]{:S(2)}, u32[]{:S(2)}) collective-permute-start(bf16[128,128]{1,0:T(8,128)(2,1)S(1)} %get-tuple-element.42), channel_id=1, source_target_pairs={{0,0},{32,8},{24,16},{56,24},{16,32},{48,40},{8,48},{40,56},{64,64... | collective-permute-start | bytes 98312 | tf_op jit(solution)/shard_map/upstream_to_units/ppermute | solution.py:439
  69.3 13.3 %collective-permute-start.7 = (bf16[14,128,128]{2,1,0:T(8,128)(2,1)S(1)}, bf16[14,128,128]{2,1,0:T(8,128)(2,1)S(1)}, u32[]{:S(2)}, u32[]{:S(2)}) collective-permute-start(bf16[14,128,128]{2,1,0:T(8,128)(2,1)S(1)} %get-tuple-element.68), channel_id=1, source_target_pairs={{64,0},{72,8},{80,16},{88,24},{96,32},{104,40},{112,48},{120,56},{... | collective-permute-start | bytes 1376264 | tf_op jit(solution)/shard_map/halos/ppermute | solution.py:439
  71.9 12.7 %collective-permute-start.6 = (bf16[14,128,128]{2,1,0:T(8,128)(2,1)S(1)}, bf16[14,128,128]{2,1,0:T(8,128)(2,1)S(1)}, u32[]{:S(2)}, u32[]{:S(2)}) collective-permute-start(bf16[14,128,128]{2,1,0:T(8,128)(2,1)S(1)} %get-tuple-element.69), channel_id=1, source_target_pairs={{0,64},{8,72},{16,80},{24,88},{32,96},{40,104},{48,112},{56,120},{... | collective-permute-start | bytes 1376264 | tf_op jit(solution)/shard_map/halos/ppermute | solution.py:439
  92.7 11.7 %collective-permute-start.8 = (bf16[2,7,128,128]{3,2,1,0:T(8,128)(2,1)S(1)}, bf16[2,7,128,128]{3,2,1,0:T(8,128)(2,1)S(1)}, u32[]{:S(2)}, u32[]{:S(2)}) collective-permute-start(bf16[2,7,128,128]{3,2,1,0:T(8,128)(2,1)S(1)} %get-tuple-element.52), channel_id=1, source_target_pairs={{0,64},{8,72},{16,80},{24,88},{32,96},{40,104},{48,112},{56,120},{... | collective-permute-start | bytes 1376264 | tf_op jit(solution)/shard_map/row_terms/ppermute | solution.py:439
  96.2 11.8 %collective-permute-start.9 = (bf16[2,7,128,128]{3,2,1,0:T(8,128)(2,1)S(1)}, bf16[2,7,128,128]{3,2,1,0:T(8,128)(2,1)S(1)}, u32[]{:S(2)}, u32[]{:S(2)}) collective-permute-start(bf16[2,7,128,128]{3,2,1,0:T(8,128)(2,1)S(1)} %get-tuple-element.53), channel_id=1, source_target_pairs={{64,0},{72,8},{80,16},{88,24},{96,32},{104,40},{112,48},{120,56},{... | collective-permute-start | bytes 1376264 | tf_op jit(solution)/shard_map/row_terms/ppermute | solution.py:439
  108.7 21.9 %collective-permute-start.12 = (bf16[4,2,128,128]{3,2,1,0:T(8,128)(2,1)S(1)}, bf16[4,2,128,128]{3,2,1,0:T(8,128)(2,1)S(1)}, u32[]{:S(2)}, u32[]{:S(2)}) collective-permute-start(bf16[4,2,128,128]{3,2,1,0:T(8,128)(2,1)S(1)} %get-tuple-element.60), channel_id=1, source_target_pairs={{0,40},{8,24},{16,32},{24,16},{32,56},{40,8},{48,48},{56,0},{64,10... | collective-permute-start | bytes 786440 | tf_op jit(solution)/shard_map/column_terms/ppermute | solution.py:439
  112.7 17.9 %collective-permute-start.13 = (bf16[4,2,128,128]{3,2,1,0:T(8,128)(2,1)S(1)}, bf16[4,2,128,128]{3,2,1,0:T(8,128)(2,1)S(1)}, u32[]{:S(2)}, u32[]{:S(2)}) collective-permute-start(bf16[4,2,128,128]{3,2,1,0:T(8,128)(2,1)S(1)} %get-tuple-element.61), channel_id=1, source_target_pairs={{0,8},{8,56},{16,0},{24,48},{32,24},{40,40},{48,16},{56,32},{64,72... | collective-permute-start | bytes 786440 | tf_op jit(solution)/shard_map/column_terms/ppermute | solution.py:439
  116.8 11.0 %collective-permute-start.10 = (bf16[2,2,128,128]{3,2,1,0:T(8,128)(2,1)S(1)}, bf16[2,2,128,128]{3,2,1,0:T(8,128)(2,1)S(1)}, u32[]{:S(2)}, u32[]{:S(2)}) collective-permute-start(bf16[2,2,128,128]{3,2,1,0:T(8,128)(2,1)S(1)} %get-tuple-element.54), channel_id=1, source_target_pairs={{0,56},{8,0},{16,8},{24,16},{32,24},{40,32},{56,48},{64,120},{72,6... | collective-permute-start | bytes 393224 | tf_op jit(solution)/shard_map/column_terms/ppermute | solution.py:439
  119.1 10.7 %collective-permute-start.11 = (bf16[2,2,128,128]{3,2,1,0:T(8,128)(2,1)S(1)}, bf16[2,2,128,128]{3,2,1,0:T(8,128)(2,1)S(1)}, u32[]{:S(2)}, u32[]{:S(2)}) collective-permute-start(bf16[2,2,128,128]{3,2,1,0:T(8,128)(2,1)S(1)} %get-tuple-element.55), channel_id=1, source_target_pairs={{0,8},{8,16},{16,24},{24,32},{32,40},{48,56},{56,0},{64,72},{72,80... | collective-permute-start | bytes 393224 | tf_op jit(solution)/shard_map/column_terms/ppermute | solution.py:439
  130.6 23.5 %collective-permute-start.14 = (bf16[4,2,128,128]{3,2,1,0:T(8,128)(2,1)S(1)}, bf16[4,2,128,128]{3,2,1,0:T(8,128)(2,1)S(1)}, u32[]{:S(2)}, u32[]{:S(2)}) collective-permute-start(bf16[4,2,128,128]{3,2,1,0:T(8,128)(2,1)S(1)} %get-tuple-element.64), channel_id=1, source_target_pairs={{0,48},{8,16},{16,40},{24,8},{32,32},{40,0},{48,56},{56,24},{64,11... | collective-permute-start | bytes 786440 | tf_op jit(solution)/shard_map/outputs_home/ppermute | solution.py:439
  133.0 21.2 %collective-permute-start.15 = (bf16[4,2,128,128]{3,2,1,0:T(8,128)(2,1)S(1)}, bf16[4,2,128,128]{3,2,1,0:T(8,128)(2,1)S(1)}, u32[]{:S(2)}, u32[]{:S(2)}) collective-permute-start(bf16[4,2,128,128]{3,2,1,0:T(8,128)(2,1)S(1)} %get-tuple-element.65), channel_id=1, source_target_pairs={{0,16},{8,48},{16,8},{24,40},{32,0},{40,32},{48,24},{56,56},{64,80... | collective-permute-start | bytes 786440 | tf_op jit(solution)/shard_map/outputs_home/ppermute | solution.py:439
  137.5 16.7 %collective-permute-start.16 = (bf16[4,128,128]{2,1,0:T(8,128)(2,1)S(1)}, bf16[4,128,128]{2,1,0:T(8,128)(2,1)S(1)}, u32[]{:S(2)}, u32[]{:S(2)}) collective-permute-start(bf16[4,128,128]{2,1,0:T(8,128)(2,1)S(1)} %get-tuple-element.66), channel_id=1, source_target_pairs={{0,32},{8,0},{16,56},{24,24},{32,48},{40,16},{48,40},{56,8},{64,96... | collective-permute-start | bytes 393224 | tf_op jit(solution)/shard_map/outputs_home/ppermute | solution.py:439
  139.4 14.7 %collective-permute-start.17 = (bf16[4,128,128]{2,1,0:T(8,128)(2,1)S(1)}, bf16[4,128,128]{2,1,0:T(8,128)(2,1)S(1)}, u32[]{:S(2)}, u32[]{:S(2)}) collective-permute-start(bf16[4,128,128]{2,1,0:T(8,128)(2,1)S(1)} %get-tuple-element.67), channel_id=1, source_target_pairs={{0,0},{8,32},{16,24},{24,56},{32,16},{40,48},{48,8},{56,40},{64,64... | collective-permute-start | bytes 393224 | tf_op jit(solution)/shard_map/outputs_home/ppermute | solution.py:439
